TPU v7x, 32 devices: a whole 2x2x4 slice. The times are simulated.
32 devices in a mesh: row: 2 (over y), col: 16 (over z, x, core).
Axes of the slice: x: 2, y: 2, z: 4, core: 2. Of those that a mesh axis runs over, the one named last changes fastest.
Arguments:
- phase_codes: int32 [64, 32768], P('row', 'col'), may hold values from 0 to 4095
- aperture: int32 [64, 32768], P('row', 'col'), may hold values from 0 to 1
- tile_offsets: int32 [4, 64], P('row', 'col'), may hold values from 0 to 4095
Outputs:
- psf_field: float32 [2, 64, 131072], P(None, 'row', 'col')
All inputs are finite; a program needn't handle non-finite values.
Results may differ from a plain program's by a relative error of at most 0.00013.
Values sent between devices are 32-bit elements; how exact they have to be, the bound alone decides.
No kernel may reach another device: no remote copies, remote signals or barrier semaphores. Data moves between devices by JAX's collectives and lax.ppermute only.
A program may use at most 64 MiB of HBM per device.

v0:
```python
import math

import jax
import jax.numpy as jnp
import numpy as np
from jax import lax
from jax.sharding import PartitionSpec as P

LEVELS = 4096
TILE_R = 16
TILE_C = 512


def bit_reverse_table(number):
    bit_width = number.bit_length() - 1
    entries = np.arange(number)
    result = np.zeros(number, np.int64)
    for place_bit in range(bit_width):
        result = result | (entries >> place_bit & 1) << bit_width - 1 - place_bit
    return result


def angle_table(first_idx, second_idx, modulus):
    product = first_idx[:, None] * second_idx[None, :] % modulus
    return product.astype(jnp.float32) * (2.0 * math.pi / modulus)


def per_device(phase_codes, aperture, tile_offsets):
    n_col = lax.axis_size("col")
    n_row = lax.axis_size("row")
    bit_count = n_col.bit_length() - 1
    col_index = lax.axis_index("col")
    row_index = lax.axis_index("row")
    row_dev, pupil_dev = phase_codes.shape
    tile_rows, tile_cols = tile_offsets.shape
    running = jnp.cumsum(tile_offsets, axis=0) % LEVELS
    totals = running[-1, :]
    every_total = lax.all_gather(totals[None, :], "row", axis=0, tiled=True)
    earlier = jnp.arange(every_total.shape[0], dtype=jnp.int32) < row_index
    before = jnp.sum(jnp.where(earlier[:, None], every_total, 0), axis=0) % LEVELS
    piston = (before[None, :] + running) % LEVELS
    codes = phase_codes.reshape(tile_rows, TILE_R, tile_cols, TILE_C) + piston[:, None, :, None]
    codes = (codes % LEVELS).reshape(row_dev, pupil_dev)
    theta = codes.astype(jnp.float32) * (2.0 * math.pi / LEVELS)
    amplitude = aperture.astype(jnp.float32)
    field = jnp.stack([amplitude * jnp.cos(theta), amplitude * jnp.sin(theta)])
    open_count = lax.psum(jnp.sum(aperture), ("row", "col"))
    scale = jnp.sqrt(jnp.float32(row_dev * n_row) / open_count.astype(jnp.float32))
    fold = pupil_dev // n_col
    arranged = field.reshape((2, row_dev, fold) + (2,) * bit_count)
    axis_order = (0, 1) + tuple(range(bit_count + 2, 2, -1)) + (2,)
    arranged = jnp.transpose(arranged, axis_order).reshape(2, row_dev, n_col, fold)
    received = lax.all_to_all(arranged, "col", split_axis=2, concat_axis=3, tiled=True)
    freq_len = fold * n_col
    pad_len = 4 * freq_len
    pupil_part = received.reshape(2, row_dev, freq_len)
    idx_f = jnp.arange(freq_len, dtype=jnp.int32)
    pre_angle = angle_table(jnp.arange(4, dtype=jnp.int32), idx_f, pad_len)
    pre_cos = jnp.cos(pre_angle)[None, :, :]
    pre_sin = jnp.sin(pre_angle)[None, :, :]
    real_in = pupil_part[0][:, None, :]
    imag_in = pupil_part[1][:, None, :]
    shifted = jnp.stack(
        [real_in * pre_cos + imag_in * pre_sin, imag_in * pre_cos - real_in * pre_sin]
    )
    main_angle = angle_table(idx_f, idx_f, freq_len)
    with_cos = jnp.einsum(
        "xraf,sf->xras", shifted, jnp.cos(main_angle), precision=lax.Precision.HIGHEST
    )
    with_sin = jnp.einsum(
        "xraf,sf->xras", shifted, jnp.sin(main_angle), precision=lax.Precision.HIGHEST
    )
    spec_re = jnp.transpose(with_cos[0] + with_sin[1], (0, 2, 1)).reshape(row_dev, pad_len)
    spec_im = jnp.transpose(with_cos[1] - with_sin[0], (0, 2, 1)).reshape(row_dev, pad_len)
    own_residue = jnp.zeros((), jnp.int32)
    for place_bit in range(bit_count):
        own_residue = own_residue + col_index // 2**place_bit % 2 * 2 ** (bit_count - 1 - place_bit)
    total_len = pad_len * n_col
    twist = own_residue * jnp.arange(pad_len, dtype=jnp.int32) % total_len
    twist_angle = twist.astype(jnp.float32) * (2.0 * math.pi / total_len)
    tw_cos = jnp.cos(twist_angle)[None, :]
    tw_sin = jnp.sin(twist_angle)[None, :]
    spectrum = jnp.stack([spec_re * tw_cos + spec_im * tw_sin, spec_im * tw_cos - spec_re * tw_sin])
    residue_ids = jnp.asarray(bit_reverse_table(n_col), jnp.int32)
    mix_angle = angle_table(jnp.arange(n_col, dtype=jnp.int32), residue_ids, n_col)
    mix_cos = jnp.cos(mix_angle)
    mix_sin = jnp.sin(mix_angle)
    block = lax.all_to_all(
        spectrum.reshape(2, row_dev, 1, pad_len), "col", split_axis=3, concat_axis=2, tiled=True
    )
    block_cos = jnp.einsum("cd,xrdt->xrct", mix_cos, block, precision=lax.Precision.HIGHEST)
    block_sin = jnp.einsum("cd,xrdt->xrct", mix_sin, block, precision=lax.Precision.HIGHEST)
    mixed = jnp.stack([block_cos[0] + block_sin[1], block_cos[1] - block_sin[0]])
    gathered = lax.all_to_all(mixed, "col", split_axis=2, concat_axis=3, tiled=True)
    spectrum = gathered.reshape(2, row_dev, pad_len)
    return spectrum * scale


def solution(mesh):
    placed = (P("row", "col"), P("row", "col"), P("row", "col"))
    return jax.shard_map(
        per_device, mesh=mesh, in_specs=placed, out_specs=P(None, "row", "col"), check_vma=False
    )
```

profile of v0, /device:TPU:0, one launch (start us, length us, event | category | flops | bytes accessed | tf_op | source)
XLA Modules:
  0.0 406.1 jit_solution(8304330803975853928)
XLA Ops:
  0.0 0.7 reduce_window_sum.11
  0.7 5.1 %all-gather = s32[2,1,4]{2,1,0:T(1,128)S(1)} all-gather(s32[1,1,4]{2,1,0:T(1,128)S(1)} %slice_bitcast_fusion), channel_id=1, replica_groups=mesh['row'=2,'col'=16] {'row'}, dimensions={0}, use_global_device_ids=true | all-gather | bytes 48 | tf_op jit(solution)/shard_map/all_gather | solution.py:38
  6.2 2.1 cosine_multiply_fusion
  8.3 0.3 copy.50
  8.6 1.3 copy.51
  9.9 2.3 maximum_bitcast_fusion.1
  12.2 2.4 copy.66
  14.7 6.6 %all-to-all-start = ((f32[2,32,16,128]{3,1,0,2:T(8,128)}), f32[2,32,16,128]{3,1,0,2:T(8,128)S(1)}, u32[]{:S(2)}, u32[]{:S(2)}) async-start(f32[2,32,16,128]{3,1,0,2:T(8,128)} %bitcast.6), calls=%async_computation | async-start | bytes 1048576 | tf_op jit(solution)/shard_map/all_to_all | solution.py:53
  21.5 0.3 fusion.30
  21.8 13.9 %all-to-all-done = f32[2,32,16,128]{3,1,0,2:T(8,128)S(1)} async-done(((f32[2,32,16,128]{3,1,0,2:T(8,128)}), f32[2,32,16,128]{3,1,0,2:T(8,128)S(1)}, u32[]{:S(2)}, u32[]{:S(2)}) %all-to-all-start) | async-done | bytes 524320 | tf_op jit(solution)/shard_map/all_to_all | solution.py:53
  36.3 0.3 multiply_add_fusion.1
  37.0 76.2 %fusion.5 = f32[2,32,4,2048]{3,1,2,0:T(8,128)S(1)} fusion(f32[2,32,4,2048]{3,1,2,0:T(8,128)S(1)} %pad_maximum_fusion.11), kind=kOutput, calls=%fused_computation.8 | convolution fusion | flops 12943622144 | bytes 4194304 | tf_op jit(solution)/shard_map/xraf,sf->xras/dot_general | solution.py:67
  113.2 77.1 %fusion.3 = f32[2,32,4,2048]{3,1,2,0:T(8,128)S(1)} fusion(f32[2,32,4,2048]{3,1,2,0:T(8,128)S(1)} %pad_maximum_fusion.10), kind=kOutput, calls=%fused_computation.6 | convolution fusion | flops 12943622144 | bytes 4194304 | tf_op jit(solution)/shard_map/xraf,sf->xras/dot_general | solution.py:70
  190.6 3.1 copy.56
  193.7 3.1 copy.57
  196.8 7.0 %multiply_add_fusion = (f32[1,32,8192]{1,2,0:T(8,128)S(1)}, f32[1,32,8192]{1,2,0:T(8,128)S(1)}) fusion(f32[1,32,8192]{1,2,0:T(8,128)} %bitcast.77, f32[1,32,8192]{1,2,0:T(8,128)} %bitcast.76, f32[8192]{0:T(1024)S(1)} %get-tuple-element.21, f32[8192]{0:T(1024)S(1)} %get-tuple-element.22), kind=kLoop, calls=%fused_computation.17 | loop fusion | flops 1572864 | bytes 4259840 | tf_op jit(solution)/shard_map/add | solution.py:83
  203.8 0.5 maximum_bitcast_fusion
  204.3 31.5 %copy.75 = f32[2,32,1,8192]{1,0,2,3:T(2,128)} copy(f32[2,32,1,8192]{1,3,0,2:T(8,128)S(1)} %maximum_bitcast_fusion) | data formatting | bytes 4194304 | tf_op jit(solution)/shard_map/reshape | solution.py:89
  235.8 10.3 %reshape.314 = f32[16,1,32768]{2,1,0:T(1,128)S(1)} reshape(f32[8192,1,2,32]{3,2,1,0:T(2,128)} %bitcast.75) | data formatting | bytes 4194304
  246.2 51.3 %all_to_all.30 = f32[16,1,32768]{2,1,0:T(1,128)} all-to-all(f32[16,1,32768]{2,1,0:T(1,128)S(1)} %reshape.314), channel_id=1, replica_groups=mesh['row'=2,'col'=16] {'col'}, dimensions={0} | all-to-all | bytes 4194304 | tf_op jit(solution)/shard_map/all_to_all | solution.py:88
  297.5 0.5 broadcast.421
  298.0 7.3 %reduce = f32[16,32768]{1,0:T(8,128)S(1)} reduce(f32[16,1,32768]{2,1,0:T(1,128)} %all_to_all.30, f32[]{:T(128)} %broadcast.421), dimensions={1}, to_apply=%all_to_all.9.reduce_sub_computation | reduce | bytes 4194308 | tf_op jit(solution)/shard_map/all_to_all | solution.py:88
  305.3 9.0 %reshape.315 = f32[8192,1,2,32]{3,2,1,0:T(2,128)} reshape(f32[16,32768]{1,0:T(8,128)S(1)} %reduce) | data formatting | bytes 4194304
  314.3 7.1 %copy.67 = f32[2,32,16,512]{3,2,1,0:T(8,128)S(1)} copy(f32[2,32,16,512]{1,0,3,2:T(2,128)} %bitcast.74) | data formatting | bytes 4194304 | tf_op jit(solution)/shard_map/all_to_all | solution.py:88
  321.4 2.0 convolution_bitcast_fusion
  323.4 2.1 convolution_bitcast_fusion.1
  325.5 0.7 slice_add_fusion
  326.4 2.5 copy.60
  329.0 5.1 %all-to-all-start.2 = ((f32[2,32,16,512]{3,1,0,2:T(8,128)}), f32[2,32,16,512]{3,1,0,2:T(8,128)S(1)}, u32[]{:S(2)}, u32[]{:S(2)}) async-start(f32[2,32,16,512]{3,1,0,2:T(8,128)} %copy.60), calls=%async_computation.2 | async-start | bytes 4194304 | tf_op jit(solution)/shard_map/all_to_all | solution.py:94
  334.1 0.7 reduce_sum.19
  334.8 68.6 %psum.7 = s32[]{:T(128)} all-reduce(s32[]{:T(128)} %reduce_sum.19), channel_id=1, replica_groups=mesh['row'=2,'col'=16] {'row','col'}, use_global_device_ids=true, to_apply=%region_3.4 | all-reduce | flops 1 | bytes 8 | tf_op jit(solution)/shard_map/psum | solution.py:47
  404.3 1.5 copy.68
  (23 shorter events, 2.1 us)
Async XLA Ops:
  14.7 21.1 %all-to-all-start = ((f32[2,32,16,128]{3,1,0,2:T(8,128)}), f32[2,32,16,128]{3,1,0,2:T(8,128)S(1)}, u32[]{:S(2)}, u32[]{:S(2)}) async-start(f32[2,32,16,128]{3,1,0,2:T(8,128)} %bitcast.6), calls=%async_computation | async-start | bytes 1048576 | tf_op jit(solution)/shard_map/all_to_all | solution.py:53
  314.3 7.1 %copy-start.1 = (s32[16]{0:T(128)S(1)}, s32[16]{0:T(128)}, u32[]{:S(2)}) copy-start(s32[16]{0:T(128)} %constant.187.clone) | copy-start | bytes 196
  326.4 7.7 %copy-start = (s32[32,2048]{1,0:T(8,128)S(1)}, s32[32,2048]{1,0:T(8,128)}, u32[]{:S(2)}) copy-start(s32[32,2048]{1,0:T(8,128)} %param.5) | copy-start | bytes 786436
  329.0 75.1 %all-to-all-start.2 = ((f32[2,32,16,512]{3,1,0,2:T(8,128)}), f32[2,32,16,512]{3,1,0,2:T(8,128)S(1)}, u32[]{:S(2)}, u32[]{:S(2)}) async-start(f32[2,32,16,512]{3,1,0,2:T(8,128)} %copy.60), calls=%async_computation.2 | async-start | bytes 4194304 | tf_op jit(solution)/shard_map/all_to_all | solution.py:94
where the time goes:
time: 410 us; the launch traced here: 406 us
  matrix products  157 us (38%)
  blocking collectives  125 us (30%)
  local copies, waits for them, and re-layouts  73.5 us (18%)
  other arithmetic  23.2 us (6%)
  waiting for transfers between devices  13.9 us (3%)
  starting transfers between devices  11.7 us (3%)
    dot_general x1, matrix products, per_device(): jnp.einsum('xraf,sf->xras', shifted, jnp.sin(main_angle), precision=lax.P...  77.1 us
    dot_general x1, matrix products, per_device(): jnp.einsum('xraf,sf->xras', shifted, jnp.cos(main_angle), precision=lax.P...  76.2 us
    psum x1, blocking collectives, per_device(): open_count = lax.psum(jnp.sum(aperture), ('row', 'col'))  68.6 us
    all_to_all x1, blocking collectives, per_device(): lax.all_to_all(spectrum.reshape(2, row_dev, 1, pad_len), 'col', split_axi...  51.3 us
    reshape x1, local copies, waits for them, and re-layouts, per_device(): spectrum.reshape(2, row_dev, 1, pad_len)  31.5 us
    unnamed x8, local copies, waits for them, and re-layouts  19.4 us
    all_to_all x1, waiting for transfers between devices, per_device(): lax.all_to_all(arranged, 'col', split_axis=2, concat_axis=3, tiled=True)  13.9 us
  transfers between devices with their start and end apart: 2, of which 1 were waited for; matrix products, arithmetic and copies ran while one was open for 0% of the time, Pallas kernels for 0%

commit v1 on v0

v1 whole, which is shorter than its diff:
```python
import math
from functools import partial

import jax
import jax.numpy as jnp
import ml_dtypes
import numpy as np
from jax import lax
from jax.experimental import pallas as pl
from jax.experimental.pallas import tpu as pltpu
from jax.sharding import PartitionSpec as P

LEVELS = 4096
TILE_R = 16
TILE_C = 512
LANES = 128
SUBS = 8
INNER = 256
PAD = 4
GROUP = 8


class Plan:
    def __init__(self, row_dev, pupil_dev, n_col, n_row):
        self.row_dev = row_dev
        self.pupil_dev = pupil_dev
        self.n_col = n_col
        self.n_row = n_row
        self.rows_all = row_dev * n_row
        self.group = min(GROUP, n_col)
        self.n_groups = n_col // self.group
        self.rows = row_dev // self.group
        self.n_pupil = pupil_dev * n_col
        self.n_pad = PAD * self.n_pupil
        self.n1 = self.n_pupil // INNER
        self.k1 = PAD * self.n1
        self.n1_dev = pupil_dev // INNER
        self.k2_group = INNER // self.n_groups
        self.k2_dev = INNER // n_col
        self.freq_tiles = PAD * pupil_dev // LANES
        self.k1_tiles = self.k1 // LANES
        self.lane_parts = INNER // LANES
        self.chunk = self.rows * 2 * self.lane_parts * self.n1_dev


def split_bf16(table):
    high = table.astype(ml_dtypes.bfloat16)
    low = (table - high.astype(np.float64)).astype(ml_dtypes.bfloat16)
    return high, low


def outer_tables(plan):
    angle = np.arange(plan.n1)[:, None] * np.arange(plan.k1)[None, :] % plan.k1
    angle = angle * (2.0 * np.pi / plan.k1)
    cos, sin = np.cos(angle), np.sin(angle)
    return split_bf16(np.block([[cos, -sin], [sin, cos]]))


def inner_tables(plan):
    angle = np.arange(INNER)[:, None] * np.arange(INNER)[None, :] % INNER
    angle = angle * (2.0 * np.pi / INNER)
    cos, sin = np.cos(angle), np.sin(angle)
    by_group = []
    for g in range(plan.n_groups):
        part = slice(g * plan.k2_group, (g + 1) * plan.k2_group)
        by_group.append(np.block([[cos[part], sin[part]], [-sin[part], cos[part]]]))
    return split_bf16(np.stack(by_group))


def twist_tables(plan):
    angle = np.arange(INNER)[:, None] * np.arange(plan.k1)[None, :] * (2.0 * np.pi / plan.n_pad)
    return np.cos(angle).astype(np.float32), np.sin(angle).astype(np.float32)


def field_kernel(plan, piston_ref, count_ref, codes_ref, mask_ref, out_ref):
    for t in range(plan.row_dev // SUBS):
        for j in range(plan.pupil_dev // LANES):
            rows = slice(t * SUBS, (t + 1) * SUBS)
            lanes = slice(j * LANES, (j + 1) * LANES)
            piston = piston_ref[t * SUBS // TILE_R, j * LANES // TILE_C]
            code = (codes_ref[rows, lanes] + piston) & (LEVELS - 1)
            quadrant = (code + LEVELS // 8) >> 10
            rest = (code - (quadrant << 10)).astype(jnp.float32) * (2.0 * math.pi / LEVELS)
            sq = rest * rest
            cos = 1.0 + sq * (-1.0 / 2 + sq * (1.0 / 24 + sq * (-1.0 / 720 + sq * (1.0 / 40320))))
            sin = rest * (1.0 + sq * (-1.0 / 6 + sq * (1.0 / 120 + sq * (-1.0 / 5040 + sq * (1.0 / 362880)))))
            amplitude = mask_ref[rows, lanes].astype(jnp.float32)
            swap = (quadrant & 1) == 1
            real = jnp.where(swap, sin, cos) * jnp.where(((quadrant + 1) & 2) == 2, -amplitude, amplitude)
            imag = jnp.where(swap, cos, sin) * jnp.where((quadrant & 2) == 2, -amplitude, amplitude)
            for part, value in enumerate((real, imag)):
                start = (part * plan.lane_parts + j % plan.lane_parts) * plan.n1_dev + j // plan.lane_parts
                step = 2 * plan.lane_parts * plan.n1_dev
                take = min(plan.rows, SUBS)
                for d in range(SUBS // take):
                    row = t * SUBS + d * take
                    dest, first = row // plan.rows, row % plan.rows
                    for g in range(plan.n_groups):
                        out_ref[g * plan.group + dest, pl.ds(first * step + start, take, stride=step), :] = value[
                            d * take : (d + 1) * take
                        ]
    count = count_ref[0, 0].astype(jnp.float32)
    for dest in range(plan.n_col):
        out_ref[dest, plan.chunk :, :] = jnp.full((SUBS, LANES), count, jnp.float32)


def transform_kernel(plan, group_ref, x_ref, tail_ref, w1h_ref, w1l_ref, tc_ref, ts_ref, w2h_ref, w2l_ref, out_ref):
    del group_ref
    r = pl.program_id(0)
    halves = []
    for part in range(2):
        pieces = []
        for lt in range(plan.lane_parts):
            at = (part * plan.lane_parts + lt) * plan.n1_dev
            pieces.append(x_ref[:, at : at + plan.n1_dev, :].reshape(plan.n1, LANES))
        halves.append(jnp.concatenate(pieces, axis=1))
    x = jnp.concatenate(halves, axis=0)
    xh = x.astype(jnp.bfloat16)
    xl = (x - xh.astype(jnp.float32)).astype(jnp.bfloat16)

    def outer(a, b):
        return lax.dot_general(a, b, (((0,), (0,)), ((), ())), preferred_element_type=jnp.float32)

    y = outer(xh, w1h_ref[...]) + outer(xl, w1h_ref[...]) + outer(xh, w1l_ref[...])
    yr, yi = y[:, : plan.k1], y[:, plan.k1 :]
    tc, ts = tc_ref[...], ts_ref[...]
    b = jnp.concatenate([yr * tc + yi * ts, yi * tc - yr * ts], axis=0)
    bh = b.astype(jnp.bfloat16)
    bl = (b - bh.astype(jnp.float32)).astype(jnp.bfloat16)

    def inner(a, b):
        return jnp.dot(a, b, preferred_element_type=jnp.float32)

    z = inner(w2h_ref[0], bh) + inner(w2l_ref[0], bh) + inner(w2h_ref[0], bl)
    count = jnp.sum(tail_ref[:, 0, :], axis=0, keepdims=True)
    scale = jnp.sqrt(float(plan.rows_all) / count)
    take = min(plan.k2_dev, SUBS)
    step = plan.k1_tiles * plan.rows
    for part in range(2):
        for k2 in range(0, plan.k2_group, take):
            dest, k2_in = k2 // plan.k2_dev, k2 % plan.k2_dev
            for j in range(plan.k1_tiles):
                at = (part * plan.freq_tiles + k2_in * plan.k1_tiles + j) * plan.rows
                row = part * plan.k2_group + k2
                value = z[row : row + take, j * LANES : (j + 1) * LANES] * scale
                out_ref[dest, pl.ds(at + r, take, stride=step), :] = value


def merge_kernel(plan, in_ref, out_ref):
    per = SUBS // plan.rows
    for f in range(plan.freq_tiles):
        for d in range(per):
            out_ref[0, d * plan.rows : (d + 1) * plan.rows, f * LANES : (f + 1) * LANES] = in_ref[
                d, f * plan.rows : (f + 1) * plan.rows, :
            ]


def per_device(phase_codes, aperture, tile_offsets):
    n_col = lax.axis_size("col")
    n_row = lax.axis_size("row")
    row_index = lax.axis_index("row")
    plan = Plan(*phase_codes.shape, n_col, n_row)
    tile_rows, tile_cols = tile_offsets.shape

    running = [tile_offsets[0]]
    for i in range(1, tile_rows):
        running.append(running[-1] + tile_offsets[i])
    count = jnp.sum(aperture)
    info = jnp.concatenate([running[-1], count[None]])[None, :]
    before = jnp.zeros((tile_cols,), jnp.int32)
    for d in range(1, n_row):
        other = lax.ppermute(info, "row", [(i, (i + d) % n_row) for i in range(n_row)])
        before = before + jnp.where(row_index >= d, other[0, :tile_cols], 0)
        count = count + other[0, tile_cols]
    piston = jnp.stack(running) + before[None, :]

    smem = pl.BlockSpec(memory_space=pltpu.SMEM)
    vmem = pl.BlockSpec(memory_space=pltpu.VMEM)
    packed = pl.pallas_call(
        partial(field_kernel, plan),
        out_shape=jax.ShapeDtypeStruct((n_col, plan.chunk + SUBS, LANES), jnp.float32),
        in_specs=[smem, smem, vmem, vmem],
        out_specs=vmem,
        compiler_params=pltpu.CompilerParams(vmem_limit_bytes=40 * 2**20),
        name="field",
    )(piston, count.reshape(1, 1), phase_codes, aperture)
    received = lax.all_to_all(packed, "col", split_axis=0, concat_axis=0, tiled=True)

    w1h, w1l = outer_tables(plan)
    w2h, w2l = inner_tables(plan)
    tc, ts = twist_tables(plan)
    group = (lax.axis_index("col") // plan.group).reshape(1).astype(jnp.int32)
    chunk_row = plan.chunk // plan.rows
    whole = lambda a: pl.BlockSpec(a.shape, lambda r, g: (0,) * a.ndim)
    mine = lambda a: pl.BlockSpec((1,) + a.shape[1:], lambda r, g: (g[0], 0, 0))
    out_rows = 2 * plan.freq_tiles * plan.rows
    spectrum = pl.pallas_call(
        partial(transform_kernel, plan),
        out_shape=jax.ShapeDtypeStruct((plan.group, out_rows, LANES), jnp.float32),
        grid_spec=pltpu.PrefetchScalarGridSpec(
            num_scalar_prefetch=1,
            grid=(plan.rows,),
            in_specs=[
                pl.BlockSpec((n_col, chunk_row, LANES), lambda r, g: (0, r, 0)),
                pl.BlockSpec((n_col, SUBS, LANES), lambda r, g: (0, plan.chunk // SUBS, 0)),
                whole(w1h),
                whole(w1l),
                whole(tc),
                whole(ts),
                mine(w2h),
                mine(w2l),
            ],
            out_specs=pl.BlockSpec((plan.group, out_rows, LANES), lambda r, g: (0, 0, 0)),
        ),
        compiler_params=pltpu.CompilerParams(vmem_limit_bytes=48 * 2**20),
        name="transform",
    )(group, received, received, w1h, w1l, tc, ts, w2h, w2l)

    groups = [[g * plan.group + i for i in range(plan.group)] for g in range(plan.n_groups)]
    blocks = lax.all_to_all(
        spectrum, "col", split_axis=0, concat_axis=0, tiled=True, axis_index_groups=groups
    )
    per = SUBS // plan.rows
    half = plan.freq_tiles * plan.rows
    return pl.pallas_call(
        partial(merge_kernel, plan),
        out_shape=jax.ShapeDtypeStruct((2, plan.row_dev, plan.freq_tiles * LANES), jnp.float32),
        grid=(2, plan.row_dev // SUBS),
        in_specs=[pl.BlockSpec((per, half, LANES), lambda c, t: (t, c, 0))],
        out_specs=pl.BlockSpec((1, SUBS, plan.freq_tiles * LANES), lambda c, t: (c, t, 0)),
        name="merge",
    )(blocks)


def solution(mesh):
    placed = (P("row", "col"), P("row", "col"), P("row", "col"))
    return jax.shard_map(
        per_device, mesh=mesh, in_specs=placed, out_specs=P(None, "row", "col"), check_vma=False
    )
```

time: 410 us -> 92 us (0.22)
  matrix products: 157 us -> 0 us
  blocking collectives: 125 us -> 32.5 us
  local copies, waits for them, and re-layouts: 73.5 us -> 4.62 us
  other arithmetic: 23.2 us -> 3.14 us
  Pallas kernels: 0 us -> 14.9 us
  waiting for transfers between devices: 13.9 us -> 25.5 us
    dot_general x4 -> x0, matrix products: 157 us -> none  [the longest x1 77.1 us: per_device(): jnp.einsum('xraf,sf->xras', shifted, jnp.sin(main_angle), precision=lax.P...]
    psum x1 -> x0, blocking collectives: 68.6 us -> none  [per_device(): open_count = lax.psum(jnp.sum(aperture), ('row', 'col'))]
    reshape x2 -> x0, local copies, waits for them, and re-layouts: 33.9 us -> none  [the longest x1 31.5 us: per_device(): spectrum.reshape(2, row_dev, 1, pad_len)]
    all_to_all x1, blocking collectives: 51.3 us -> 32.5 us  [per_device(): lax.all_to_all(spectrum, 'col', split_axis=0, concat_axis=0, tiled=True,...]
    unnamed x8 -> x16, local copies, waits for them, and re-layouts: 19.4 us -> 3.99 us
    pallas_call x0 -> x3, Pallas kernels: none -> 14.9 us  [the longest x1 6.66 us: per_device(): pl.pallas_call(partial(transform_kernel, plan), out_shape=jax.ShapeDtypeS...]
    all_to_all x2 -> x1, waiting for transfers between devices: 13.9 us -> 24 us  [per_device(): lax.all_to_all(packed, 'col', split_axis=0, concat_axis=0, tiled=True)]
    add x3 -> x2, other arithmetic: 7.94 us -> 0.02 us  [per_device(): piston = jnp.stack(running) + before[None, :]]
  transfers between devices with their start and end apart: 2 -> 2, of which waited for: 1 -> 2; matrix products, arithmetic and copies ran while one was open for 0% -> 0% of each run, Pallas kernels for 0% -> 0%
where the time goes in v1:
time: 92 us; the launch traced here: 91.4 us
  blocking collectives  32.5 us (35%)
  waiting for transfers between devices  25.5 us (28%)
  Pallas kernels  14.9 us (16%)
  starting transfers between devices  9.38 us (10%)
  local copies, waits for them, and re-layouts  4.62 us (5%)
  other arithmetic  3.14 us (3%)
  between operations  1.35 us (1%)
    all_to_all x1, blocking collectives, per_device(): lax.all_to_all(spectrum, 'col', split_axis=0, concat_axis=0, tiled=True,...  32.5 us
    all_to_all x1, waiting for transfers between devices, per_device(): lax.all_to_all(packed, 'col', split_axis=0, concat_axis=0, tiled=True)  24 us
    pallas_call x1, Pallas kernels, per_device(): pl.pallas_call(partial(transform_kernel, plan), out_shape=jax.ShapeDtypeS...  6.66 us
    all_to_all x1, starting transfers between devices, per_device(): lax.all_to_all(packed, 'col', split_axis=0, concat_axis=0, tiled=True)  6.41 us
    pallas_call x1, Pallas kernels, per_device(): pl.pallas_call(partial(merge_kernel, plan), out_shape=jax.ShapeDtypeStruc...  5.79 us
    unnamed x16, local copies, waits for them, and re-layouts  3.99 us
    ppermute x1, starting transfers between devices, per_device(): lax.ppermute(info, 'row', [(i, (i + d) % n_row) for i in range(n_row)])  2.97 us
    pallas_call x1, Pallas kernels, per_device(): pl.pallas_call(partial(field_kernel, plan), out_shape=jax.ShapeDtypeStruc...  2.46 us
  transfers between devices with their start and end apart: 2, of which 2 were waited for; matrix products, arithmetic and copies ran while one was open for 0% of the time, Pallas kernels for 0%

profile of v1, /device:TPU:0, one launch (start us, length us, event | category | flops | bytes accessed | tf_op | source)
XLA Modules:
  0.0 91.4 jit_solution(47785471130826960)
XLA Ops:
  0.0 0.8 fusion.1
  0.8 1.7 %reduce_sum.9 = s32[]{:T(128)} reduce(s32[32,2048]{1,0:T(8,128)} %mask_ref.1, s32[]{:T(128)} %constant.33.clone.1), dimensions={0,1}, to_apply=%region_0.0 | reduce | flops 65535 | bytes 262152 | tf_op jit(solution)/shard_map/reduce_sum | solution.py:168
  2.4 0.7 add_bitcast_fusion
  3.1 3.0 %collective-permute-start = (s32[1,5]{1,0:T(1,128)S(1)}, s32[1,5]{1,0:T(1,128)S(1)}, u32[]{:S(2)}, u32[]{:S(2)}) collective-permute-start(s32[1,5]{1,0:T(1,128)S(1)} %add_bitcast_fusion), channel_id=1, source_target_pairs={{0,16},{16,0},{1,17},{17,1},{2,18},{18,2},{3,19},{19,3},{4,20},{20... | collective-permute-start | bytes 68 | tf_op jit(solution)/shard_map/ppermute | solution.py:172
  6.1 1.5 %collective-permute-done = s32[1,5]{1,0:T(1,128)S(1)} collective-permute-done((s32[1,5]{1,0:T(1,128)S(1)}, s32[1,5]{1,0:T(1,128)S(1)}, u32[]{:S(2)}, u32[]{:S(2)}) %collective-permute-start) | collective-permute-done | bytes 52 | tf_op jit(solution)/shard_map/ppermute | solution.py:172
  7.6 0.6 slice.15
  9.6 0.0 copy-start
  9.6 0.9 %copy-done = s32[32,2048]{1,0:T(8,128)S(1)} copy-done((s32[32,2048]{1,0:T(8,128)S(1)}, s32[32,2048]{1,0:T(8,128)}, u32[]{:S(2)}) %copy-start) | copy-done | bytes 262168
  10.5 0.0 copy-start.7
  10.5 0.9 %copy-done.7 = s32[32,2048]{1,0:T(8,128)S(1)} copy-done((s32[32,2048]{1,0:T(8,128)S(1)}, s32[32,2048]{1,0:T(8,128)}, u32[]{:S(2)}) %copy-start.7) | copy-done | bytes 262168
  11.5 0.0 copy-start.1
  11.5 0.0 copy-start.2
  11.5 0.0 copy-start.3
  11.5 0.0 copy-start.4
  11.5 2.5 %field.1 = f32[16,136,128]{2,1,0:T(8,128)} custom-call(s32[2,4]{1,0:T(2,128)S(1)} %add_add_fusion.piston_ref, s32[1,1]{1,0:T(1,128)} %bitcast.6.count_ref, s32[32,2048]{1,0:T(8,128)S(1)} %copy-done.7, s32[32,2048]{1,0:T(8,128)S(1)} %copy-done), custom_call_target="tpu_custom_call" | custom-call | tf_op jit(solution)/shard_map/field/pallas_call | solution.py:179
  13.9 6.4 %all-to-all-start = ((f32[16,136,128]{2,1,0:T(8,128)}), f32[16,136,128]{2,1,0:T(8,128)S(1)}, u32[]{:S(2)}, u32[]{:S(2)}) async-start(f32[16,136,128]{2,1,0:T(8,128)} %field.1), calls=%async_computation | async-start | bytes 2228224 | tf_op jit(solution)/shard_map/all_to_all | solution.py:187
  20.4 24.0 %all-to-all-done.x_ref.tail_ref = f32[16,136,128]{2,1,0:T(8,128)S(1)} async-done(((f32[16,136,128]{2,1,0:T(8,128)}), f32[16,136,128]{2,1,0:T(8,128)S(1)}, u32[]{:S(2)}, u32[]{:S(2)}) %all-to-all-start) | async-done | bytes 1114144 | tf_op jit(solution)/shard_map/all_to_all | solution.py:187
  44.4 0.0 copy-done.1
  44.4 0.0 copy-done.2
  44.4 0.0 copy-done.3
  44.4 0.0 copy-done.4
  44.4 0.0 copy-start.5
  44.4 1.0 %copy-done.5 = bf16[256,1024]{1,0:T(8,128)(2,1)S(1)} copy-done((bf16[256,1024]{1,0:T(8,128)(2,1)S(1)}, bf16[256,1024]{1,0:T(8,128)(2,1)}, u32[]{:S(2)}) %copy-start.5) | copy-done | bytes 524312
  45.4 0.0 copy-start.6
  45.5 1.0 %copy-done.6 = bf16[256,1024]{1,0:T(8,128)(2,1)S(1)} copy-done((bf16[256,1024]{1,0:T(8,128)(2,1)S(1)}, bf16[256,1024]{1,0:T(8,128)(2,1)}, u32[]{:S(2)}) %copy-start.6) | copy-done | bytes 524312
  46.5 6.7 %transform.1 = f32[8,512,128]{2,1,0:T(8,128)} custom-call(s32[1]{0:T(128)} %bitcast.group_ref, f32[16,136,128]{2,1,0:T(8,128)S(1)} %all-to-all-done.x_ref.tail_ref, f32[16,136,128]{2,1,0:T(8,128)S(1)} %all-to-all-done.x_ref.tail_ref, bf16[256,1024]{1,0:T(8,128)(2,1)S(1)} %copy-done.6, bf16[256,1024]{1,0:T(8,128)(2,1)S(1)} %copy-done.5, ...), custom_call_target="tpu_custom_call" | custom-call | tf_op jit(solution)/shard_map/transform/pallas_call | solution.py:197
  53.2 32.5 %all_to_all.10.in_ref = f32[8,512,128]{2,1,0:T(8,128)} all-to-all(f32[8,512,128]{2,1,0:T(8,128)} %transform.1), channel_id=1, replica_groups={{0,1,2,3,4,5,6,7},{8,9,10,11,12,13,14,15},{16,17,18,19,20,21,22,23},{24..., dimensions={0} | all-to-all | bytes 4194304 | tf_op jit(solution)/shard_map/all_to_all | solution.py:220
  85.6 5.8 %merge.1 = f32[2,32,8192]{2,1,0:T(8,128)} custom-call(f32[8,512,128]{2,1,0:T(8,128)} %all_to_all.10.in_ref), custom_call_target="tpu_custom_call" | custom-call | tf_op jit(solution)/shard_map/merge/pallas_call | solution.py:225
  (2 shorter events, 0.0 us)
Async XLA Ops:
  3.1 4.5 %collective-permute-start = (s32[1,5]{1,0:T(1,128)S(1)}, s32[1,5]{1,0:T(1,128)S(1)}, u32[]{:S(2)}, u32[]{:S(2)}) collective-permute-start(s32[1,5]{1,0:T(1,128)S(1)} %add_bitcast_fusion), channel_id=1, source_target_pairs={{0,16},{16,0},{1,17},{17,1},{2,18},{18,2},{3,19},{19,3},{4,20},{20... | collective-permute-start | bytes 68 | tf_op jit(solution)/shard_map/ppermute | solution.py:172
  9.6 1.0 %copy-start = (s32[32,2048]{1,0:T(8,128)S(1)}, s32[32,2048]{1,0:T(8,128)}, u32[]{:S(2)}) copy-start(s32[32,2048]{1,0:T(8,128)} %mask_ref.1) | copy-start | bytes 786436
  10.5 0.9 %copy-start.7 = (s32[32,2048]{1,0:T(8,128)S(1)}, s32[32,2048]{1,0:T(8,128)}, u32[]{:S(2)}) copy-start(s32[32,2048]{1,0:T(8,128)} %codes_ref.1) | copy-start | bytes 786436
  11.5 32.9 %copy-start.1 = (bf16[2,256,512]{2,1,0:T(8,128)(2,1)S(1)}, bf16[2,256,512]{2,1,0:T(8,128)(2,1)}, u32[]{:S(2)}) copy-start(bf16[2,256,512]{2,1,0:T(8,128)(2,1)} %constant.44.clone.w2l_ref) | copy-start | bytes 1572868
  11.5 32.9 %copy-start.2 = (bf16[2,256,512]{2,1,0:T(8,128)(2,1)S(1)}, bf16[2,256,512]{2,1,0:T(8,128)(2,1)}, u32[]{:S(2)}) copy-start(bf16[2,256,512]{2,1,0:T(8,128)(2,1)} %constant.43.clone.w2h_ref) | copy-start | bytes 1572868
  11.5 32.9 %copy-start.3 = (f32[256,512]{1,0:T(8,128)S(1)}, f32[256,512]{1,0:T(8,128)}, u32[]{:S(2)}) copy-start(f32[256,512]{1,0:T(8,128)} %constant.42.clone.ts_ref) | copy-start | bytes 1572868
  11.5 32.9 %copy-start.4 = (f32[256,512]{1,0:T(8,128)S(1)}, f32[256,512]{1,0:T(8,128)}, u32[]{:S(2)}) copy-start(f32[256,512]{1,0:T(8,128)} %constant.41.clone.tc_ref) | copy-start | bytes 1572868
  13.9 30.4 %all-to-all-start = ((f32[16,136,128]{2,1,0:T(8,128)}), f32[16,136,128]{2,1,0:T(8,128)S(1)}, u32[]{:S(2)}, u32[]{:S(2)}) async-start(f32[16,136,128]{2,1,0:T(8,128)} %field.1), calls=%async_computation | async-start | bytes 2228224 | tf_op jit(solution)/shard_map/all_to_all | solution.py:187
  44.4 1.0 %copy-start.5 = (bf16[256,1024]{1,0:T(8,128)(2,1)S(1)}, bf16[256,1024]{1,0:T(8,128)(2,1)}, u32[]{:S(2)}) copy-start(bf16[256,1024]{1,0:T(8,128)(2,1)} %constant.40.clone.w1l_ref) | copy-start | bytes 1572868
  45.4 1.0 %copy-start.6 = (bf16[256,1024]{1,0:T(8,128)(2,1)S(1)}, bf16[256,1024]{1,0:T(8,128)(2,1)}, u32[]{:S(2)}) copy-start(bf16[256,1024]{1,0:T(8,128)(2,1)} %constant.39.clone.w1h_ref) | copy-start | bytes 1572868

commit v2 on v1

v2 whole, which is shorter than its diff:
```python
import math
from functools import partial

import jax
import jax.numpy as jnp
import ml_dtypes
import numpy as np
from jax import lax
from jax.experimental import pallas as pl
from jax.experimental.pallas import tpu as pltpu
from jax.sharding import PartitionSpec as P

LEVELS = 4096
TILE_R = 16
TILE_C = 512
LANES = 128
SUBS = 8
INNER = 256
PAD = 4
SPLITS = (2, 2)
GROUP = 8


class Plan:
    def __init__(self, row_dev, pupil_dev, n_col, n_row):
        self.row_dev = row_dev
        self.pupil_dev = pupil_dev
        self.n_col = n_col
        self.n_row = n_row
        self.rows_all = row_dev * n_row
        self.group = min(GROUP, n_col)
        self.n_groups = n_col // self.group
        self.rows = row_dev // self.group
        self.n_pupil = pupil_dev * n_col
        self.n_pad = PAD * self.n_pupil
        self.n1 = self.n_pupil // INNER
        self.k1 = PAD * self.n1
        self.n1_dev = pupil_dev // INNER
        self.k2_group = INNER // self.n_groups
        self.k2_dev = INNER // n_col
        self.freq_tiles = PAD * pupil_dev // LANES
        self.k1_tiles = self.k1 // LANES
        self.lane_parts = INNER // LANES
        self.chunk = self.rows * 2 * self.lane_parts * self.n1_dev


def split_bf16(table):
    high = table.astype(ml_dtypes.bfloat16)
    low = (table - high.astype(np.float64)).astype(ml_dtypes.bfloat16)
    return np.stack([high, low])


def outer_tables(plan):
    angle = np.arange(plan.n1)[:, None] * np.arange(plan.k1)[None, :] % plan.k1
    angle = angle * (2.0 * np.pi / plan.k1)
    cos, sin = np.cos(angle), np.sin(angle)
    return split_bf16(np.block([[cos, -sin], [sin, cos]]))


def inner_tables(plan):
    angle = np.arange(INNER)[:, None] * np.arange(INNER)[None, :] % INNER
    angle = angle * (2.0 * np.pi / INNER)
    cos, sin = np.cos(angle), np.sin(angle)
    by_dest = []
    for q in range(plan.n_col):
        part = slice(q * plan.k2_dev, (q + 1) * plan.k2_dev)
        by_dest.append(np.block([[cos[part], sin[part]], [-sin[part], cos[part]]]))
    return split_bf16(np.stack(by_dest))


def twist_tables(plan):
    angle = np.arange(INNER)[:, None] * np.arange(plan.k1)[None, :] * (2.0 * np.pi / plan.n_pad)
    return np.stack([np.cos(angle), np.sin(angle)]).astype(np.float32)


def field_kernel(plan, row_ref, tiles_ref, *refs):
    others, (codes_ref, mask_ref, all_mask_ref, out_ref, open_ref) = refs[: plan.n_row - 1], refs[plan.n_row - 1 :]
    step_id = pl.program_id(0)
    tile_cols = plan.pupil_dev // TILE_C

    @pl.when(step_id == 0)
    def _():
        total = jnp.zeros((SUBS, LANES), jnp.int32)
        for t in range(plan.row_dev // SUBS):
            for j in range(plan.pupil_dev // LANES):
                total = total + all_mask_ref[t * SUBS : (t + 1) * SUBS, j * LANES : (j + 1) * LANES]
        open_ref[...] = total.astype(jnp.float32)

    pistons = []
    for i in range(tile_cols):
        piston = jnp.int32(0)
        for d, other in enumerate(others):
            column = other[0, i]
            for k in range(1, plan.row_dev // TILE_R):
                column = column + other[k, i]
            piston = piston + jnp.where(row_ref[0] > d, column, 0)
        for k in range(plan.row_dev // TILE_R):
            piston = piston + jnp.where(step_id >= k, tiles_ref[k, i], 0)
        pistons.append(piston)
    take = min(plan.rows, SUBS)
    stride = 2 * plan.lane_parts * plan.n1_dev
    for t in range(TILE_R // SUBS):
        for j in range(plan.pupil_dev // LANES):
            rows = slice(t * SUBS, (t + 1) * SUBS)
            lanes = slice(j * LANES, (j + 1) * LANES)
            code = (codes_ref[rows, lanes] + pistons[j * LANES // TILE_C]) & (LEVELS - 1)
            quadrant = (code + LEVELS // 8) >> 10
            rest = (code - (quadrant << 10)).astype(jnp.float32) * (2.0 * math.pi / LEVELS)
            sq = rest * rest
            cos = 1.0 + sq * (-1.0 / 2 + sq * (1.0 / 24 + sq * (-1.0 / 720 + sq * (1.0 / 40320))))
            sin = rest * (1.0 + sq * (-1.0 / 6 + sq * (1.0 / 120 + sq * (-1.0 / 5040 + sq * (1.0 / 362880)))))
            amplitude = mask_ref[rows, lanes].astype(jnp.float32)
            swap = (quadrant & 1) == 1
            real = jnp.where(swap, sin, cos) * jnp.where(((quadrant + 1) & 2) == 2, -amplitude, amplitude)
            imag = jnp.where(swap, cos, sin) * jnp.where((quadrant & 2) == 2, -amplitude, amplitude)
            for part, value in enumerate((real, imag)):
                start = (part * plan.lane_parts + j % plan.lane_parts) * plan.n1_dev + j // plan.lane_parts
                for d in range(SUBS // take):
                    row = t * SUBS + d * take
                    dest, first = row // plan.rows, row % plan.rows
                    for g in range(plan.n_groups):
                        out_ref[g, dest, pl.ds(first * stride + start, take, stride=stride), :] = value[
                            d * take : (d + 1) * take
                        ]
    for g in range(plan.n_groups):
        for dest in range(TILE_R // plan.rows):
            out_ref[g, dest, plan.chunk :, :] = open_ref[...]


def transform_kernel(plan, first, rows, with_count, me_ref, x_ref, w1_ref, twist_ref, w2_ref, *refs):
    chunk_row = plan.chunk // plan.rows
    me = me_ref[0]

    def outer(a, b):
        return lax.dot_general(a, b, (((0,), (0,)), ((), ())), preferred_element_type=jnp.float32)

    def inner(a, b):
        return jnp.dot(a, b, preferred_element_type=jnp.float32)

    if with_count:
        refs[plan.group][...] = jnp.sum(x_ref[:, plan.chunk :, :], axis=0)
    w2 = [jnp.concatenate([w2_ref[s, me ^ b] for b in range(plan.group)], axis=0) for s in range(2)]
    tc, ts = twist_ref[0], twist_ref[1]
    for r in range(rows):
        halves = []
        for part in range(2):
            pieces = []
            for lt in range(plan.lane_parts):
                at = (first + r) * chunk_row + (part * plan.lane_parts + lt) * plan.n1_dev
                pieces.append(x_ref[:, at : at + plan.n1_dev, :].reshape(plan.n1, LANES))
            halves.append(jnp.concatenate(pieces, axis=1))
        x = jnp.concatenate(halves, axis=0)
        xh = x.astype(jnp.bfloat16)
        xl = (x - xh.astype(jnp.float32)).astype(jnp.bfloat16)
        y = outer(xh, w1_ref[0]) + outer(xl, w1_ref[0]) + outer(xh, w1_ref[1])
        yr, yi = y[:, : plan.k1], y[:, plan.k1 :]
        f = jnp.concatenate([yr * tc + yi * ts, yi * tc - yr * ts], axis=0)
        fh = f.astype(jnp.bfloat16)
        fl = (f - fh.astype(jnp.float32)).astype(jnp.bfloat16)
        z = inner(w2[0], fh) + inner(w2[1], fh) + inner(w2[0], fl)
        size = 2 * plan.k2_dev
        for b in range(plan.group):
            refs[b][r] = z[b * size : (b + 1) * size].reshape(2, plan.k2_dev, plan.k1)


def merge_kernel(plan, splits, at_ref, *refs):
    del at_ref
    n = len(splits)
    even, odd, parity_ref, counts = refs[:n], refs[n : 2 * n], refs[2 * n], refs[2 * n + 1 : 2 * n + 1 + plan.n_row]
    out_ref, tile_ref = refs[-2], refs[-1]
    total = counts[0][...]
    for other in counts[1:]:
        total = total + other[...]
    total = jnp.sum(jnp.sum(total, axis=0, keepdims=True), axis=1, keepdims=True)
    scale = jnp.sqrt(float(plan.rows_all) / total)
    swapped = parity_ref[0] == 1
    take = min(plan.k2_dev, SUBS)
    for i, rows in enumerate(splits):
        for r in range(rows):
            for k2 in range(0, plan.k2_dev, take):
                for j in range(plan.k1_tiles):
                    lanes = slice(j * LANES, (j + 1) * LANES)
                    a = even[i][r, 0, k2 : k2 + take, lanes] * scale
                    b = odd[i][r, 0, k2 : k2 + take, lanes] * scale
                    at = (k2 * plan.k1_tiles + j) * SUBS + sum(splits[:i]) + r
                    stride = plan.k1_tiles * SUBS
                    tile_ref[pl.ds(at, take, stride=stride), :] = jnp.where(swapped, b, a)
                    tile_ref[pl.ds(at + plan.rows, take, stride=stride), :] = jnp.where(swapped, a, b)
    for f in range(plan.freq_tiles):
        out_ref[0, :, f * LANES : (f + 1) * LANES] = tile_ref[f * SUBS : (f + 1) * SUBS, :]


def per_device(phase_codes, aperture, tile_offsets):
    n_col = lax.axis_size("col")
    n_row = lax.axis_size("row")
    plan = Plan(*phase_codes.shape, n_col, n_row)
    row_index = lax.axis_index("row").astype(jnp.int32).reshape(1)
    col_index = lax.axis_index("col").astype(jnp.int32).reshape(1)
    me = col_index

    def along_rows(value):
        return [lax.ppermute(value, "row", [(i, (i + d) % n_row) for i in range(n_row)]) for d in range(1, n_row)]

    smem = pl.BlockSpec(memory_space=pltpu.SMEM)
    vmem = pl.BlockSpec(memory_space=pltpu.VMEM)
    others = along_rows(tile_offsets)
    steps = plan.row_dev // TILE_R
    block = (plan.n_groups, plan.group // steps, plan.chunk + SUBS, LANES)
    packed = pl.pallas_call(
        partial(field_kernel, plan),
        out_shape=jax.ShapeDtypeStruct((plan.n_groups, plan.group, plan.chunk + SUBS, LANES), jnp.float32),
        grid=(steps,),
        in_specs=[smem, smem]
        + [smem] * (n_row - 1)
        + [
            pl.BlockSpec((TILE_R, plan.pupil_dev), lambda t: (t, 0)),
            pl.BlockSpec((TILE_R, plan.pupil_dev), lambda t: (t, 0)),
            pl.BlockSpec((plan.row_dev, plan.pupil_dev), lambda t: (0, 0)),
        ],
        out_specs=pl.BlockSpec(block, lambda t: (0, t, 0, 0)),
        scratch_shapes=[pltpu.VMEM((SUBS, LANES), jnp.float32)],
        name="field",
    )(row_index, tile_offsets, *others, phase_codes, aperture, aperture)
    packed = packed.reshape(n_col, plan.chunk + SUBS, LANES)
    received = lax.all_to_all(packed, "col", split_axis=0, concat_axis=0, tiled=True)

    w1, w2, twist = outer_tables(plan), inner_tables(plan), twist_tables(plan)
    splits = SPLITS if sum(SPLITS) == plan.rows else (plan.rows,)
    chunks = []
    for i, rows in enumerate(splits):
        shapes = [jax.ShapeDtypeStruct((rows, 2, plan.k2_dev, plan.k1), jnp.float32)] * plan.group
        if i == 0:
            shapes = shapes + [jax.ShapeDtypeStruct((SUBS, LANES), jnp.float32)]
        made = pl.pallas_call(
            partial(transform_kernel, plan, sum(splits[:i]), rows, i == 0),
            out_shape=shapes,
            in_specs=[smem, vmem, vmem, vmem, vmem],
            out_specs=[vmem] * len(shapes),
            compiler_params=pltpu.CompilerParams(vmem_limit_bytes=24 * 2**20),
            name="transform",
        )(me, received, w1, twist, w2)
        if i == 0:
            counts = [made[-1]] + along_rows(made[-1])
        chunks.append(
            [made[0]]
            + [lax.ppermute(made[b], "col", [(q, q ^ b) for q in range(n_col)]) for b in range(1, plan.group)]
        )

    inside = col_index % plan.group
    parity = inside % 2
    out = None
    for b in range(plan.group - 2, -1, -2):
        tile = (inside // 2) ^ (b // 2)
        pair = [c[b] for c in chunks] + [c[b + 1] for c in chunks]
        in_specs = [pl.BlockSpec((rows, 1, plan.k2_dev, plan.k1), lambda c, t: (0, c, 0, 0)) for rows in splits] * 2
        in_specs = in_specs + [smem] + [pl.BlockSpec((SUBS, LANES), lambda c, t: (0, 0))] * n_row
        args = [tile, *pair, parity, *counts]
        aliases = {}
        kernel = partial(merge_kernel, plan, splits)
        if out is not None:
            in_specs = in_specs + [pl.BlockSpec(memory_space=pl.ANY)]
            args = args + [out]
            aliases = {len(args) - 1: 0}
        out = pl.pallas_call(
            kernel,
            out_shape=jax.ShapeDtypeStruct((2, plan.row_dev, plan.freq_tiles * LANES), jnp.float32),
            grid_spec=pltpu.PrefetchScalarGridSpec(
                num_scalar_prefetch=1,
                grid=(2,),
                in_specs=in_specs,
                out_specs=pl.BlockSpec((1, SUBS, plan.freq_tiles * LANES), lambda c, t: (c, t[0], 0)),
                scratch_shapes=[pltpu.VMEM((plan.freq_tiles * SUBS, LANES), jnp.float32)],
            ),
            input_output_aliases=aliases,
            name="merge",
        )(*args)
    return out


def solution(mesh):
    placed = (P("row", "col"), P("row", "col"), P("row", "col"))
    return jax.shard_map(
        per_device, mesh=mesh, in_specs=placed, out_specs=P(None, "row", "col"), check_vma=False
    )
```

time: 92 us -> 83.4 us (0.907)
  blocking collectives: 32.5 us -> 0 us
  starting transfers between devices: 9.38 us -> 27.5 us
  waiting for transfers between devices: 25.5 us -> 33.2 us
  other arithmetic: 3.14 us -> 0 us
  Pallas kernels: 14.9 us -> 17.7 us
  between operations: 1.35 us -> 0.13 us
    all_to_all x1 -> x0, blocking collectives: 32.5 us -> none  [per_device(): lax.all_to_all(spectrum, 'col', split_axis=0, concat_axis=0, tiled=True,...]
    ppermute x1 -> x16, starting transfers between devices: 2.97 us -> 21 us  [the longest x14 16.5 us: per_device(): lax.ppermute(made[b], 'col', [(q, q ^ b) for q in range(n_col)])]
    ppermute x1 -> x16, waiting for transfers between devices: 1.52 us -> 9.19 us  [the longest x14 5.34 us: per_device(): lax.ppermute(made[b], 'col', [(q, q ^ b) for q in range(n_col)])]
    pallas_call x2 -> x6, Pallas kernels: 12.5 us -> 14.7 us  [the longest x4 8.79 us: per_device(): pl.pallas_call(kernel, out_shape=jax.ShapeDtypeStruct((2, plan.row_dev, p...]
    reduce_sum x1 -> x0, other arithmetic: 1.65 us -> none  [per_device(): count = jnp.sum(aperture)]
    unnamed x16 -> x44, local copies, waits for them, and re-layouts: 3.99 us -> 4.46 us
  transfers between devices with their start and end apart: 2 -> 17, of which waited for: 2 -> 7; matrix products, arithmetic and copies ran while one was open for 0% -> 0% of each run, Pallas kernels for 0% -> 12%
where the time goes in v2:
time: 83.4 us; the launch traced here: 82.9 us
  waiting for transfers between devices  33.2 us (40%)
  starting transfers between devices  27.5 us (33%)
  Pallas kernels  17.7 us (21%)
  local copies, waits for them, and re-layouts  4.46 us (5%)
    all_to_all x1, waiting for transfers between devices, per_device(): lax.all_to_all(packed, 'col', split_axis=0, concat_axis=0, tiled=True)  24 us
    ppermute x14, starting transfers between devices, per_device(): lax.ppermute(made[b], 'col', [(q, q ^ b) for q in range(n_col)])  16.5 us
    pallas_call x4, Pallas kernels, per_device(): pl.pallas_call(kernel, out_shape=jax.ShapeDtypeStruct((2, plan.row_dev, p...  8.79 us
    all_to_all x1, starting transfers between devices, per_device(): lax.all_to_all(packed, 'col', split_axis=0, concat_axis=0, tiled=True)  6.41 us
    pallas_call x2, Pallas kernels, per_device(): pl.pallas_call(partial(transform_kernel, plan, sum(splits[:i]), rows, i =...  5.91 us
    ppermute x14, waiting for transfers between devices, per_device(): lax.ppermute(made[b], 'col', [(q, q ^ b) for q in range(n_col)])  5.34 us
    ppermute x2, starting transfers between devices, along_rows(): lax.ppermute(value, 'row', [(i, (i + d) % n_row) for i in range(n_row)])  4.49 us
    unnamed x44, local copies, waits for them, and re-layouts  4.46 us
  transfers between devices with their start and end apart: 17, of which 7 were waited for; matrix products, arithmetic and copies ran while one was open for 0% of the time, Pallas kernels for 12%

profile of v2, /device:TPU:0, one launch (start us, length us, event | category | flops | bytes accessed | tf_op | source)
XLA Modules:
  0.0 82.9 jit_solution(11331346168025317866)
XLA Ops:
  0.0 3.0 %collective-permute-start = (s32[2,4]{1,0:T(2,128)}, s32[2,4]{1,0:T(2,128)S(1)}, u32[]{:S(2)}, u32[]{:S(2)}) collective-permute-start(s32[2,4]{1,0:T(2,128)} %tiles_ref.1), channel_id=1, source_target_pairs={{0,16},{16,0},{1,17},{17,1},{2,18},{18,2},{3,19},{19,3},{4,20},{20... | collective-permute-start | bytes 104 | tf_op jit(solution)/shard_map/ppermute | solution.py:202
  3.0 1.8 %collective-permute-done.refs_0_ = s32[2,4]{1,0:T(2,128)S(1)} collective-permute-done((s32[2,4]{1,0:T(2,128)}, s32[2,4]{1,0:T(2,128)S(1)}, u32[]{:S(2)}, u32[]{:S(2)}) %collective-permute-start) | collective-permute-done | bytes 64 | tf_op jit(solution)/shard_map/ppermute | solution.py:202
  5.3 3.0 %field.1 = f32[2,8,136,128]{3,2,1,0:T(8,128)} custom-call(s32[1]{0:T(128)} %bitcast.1.row_ref, s32[2,4]{1,0:T(2,128)} %tiles_ref.1, s32[2,4]{1,0:T(2,128)} %copy-done.21, s32[32,2048]{1,0:T(8,128)} %refs_1_.1, s32[32,2048]{1,0:T(8,128)} %refs_3_.1, s32[32,2048]{1,0:T(8,128)} %refs_3_.1), custom_call_target="tpu_custom_call" | custom-call | tf_op jit(solution)/shard_map/field/pallas_call | solution.py:209
  8.2 6.4 %all-to-all-start = ((f32[16,136,128]{2,1,0:T(8,128)}), f32[16,136,128]{2,1,0:T(8,128)S(1)}, u32[]{:S(2)}, u32[]{:S(2)}) async-start(f32[16,136,128]{2,1,0:T(8,128)} %bitcast.3), calls=%async_computation | async-start | bytes 2228224 | tf_op jit(solution)/shard_map/all_to_all | solution.py:225
  14.6 24.0 %all-to-all-done.x_ref = f32[16,136,128]{2,1,0:T(8,128)S(1)} async-done(((f32[16,136,128]{2,1,0:T(8,128)}), f32[16,136,128]{2,1,0:T(8,128)S(1)}, u32[]{:S(2)}, u32[]{:S(2)}) %all-to-all-start) | async-done | bytes 1114144 | tf_op jit(solution)/shard_map/all_to_all | solution.py:225
  38.7 1.2 %copy-done.2 = bf16[2,16,32,512]{3,2,1,0:T(8,128)(2,1)S(1)} copy-done((bf16[2,16,32,512]{3,2,1,0:T(8,128)(2,1)S(1)}, bf16[2,16,32,512]{3,2,1,0:T(8,128)(2,1)}, u32[]{:S(2)}) %copy-start.2) | copy-done | bytes 1048600
  39.9 2.9 %transform.2 = (f32[2,2,16,512]{3,2,1,0:T(8,128)S(1)}, f32[2,2,16,512]{3,2,1,0:T(8,128)S(1)}, f32[2,2,16,512]{3,2,1,0:T(8,128)S(1)}, f32[2,2,16,512]{3,2,1,0:T(8...) custom-call(s32[1]{0:T(128)} %bitcast.me_ref, ...), custom_call_target="tpu_custom_call" | custom-call | tf_op jit(solution)/shard_map/transform/pallas_call | solution.py:234
  42.8 5.0 %collective-permute-start.12 = (f32[2,2,16,512]{3,2,1,0:T(8,128)S(1)}, f32[2,2,16,512]{3,2,1,0:T(8,128)S(1)}, u32[]{:S(2)}, u32[]{:S(2)}) collective-permute-start(f32[2,2,16,512]{3,2,1,0:T(8,128)S(1)} %get-tuple-element.35), channel_id=1, source_target_pairs={{0,6},{1,7},{2,4},{3,5},{4,2},{5,3},{6,0},{7,1},{8,14},{9,15},{10,... | collective-permute-start | bytes 393224 | tf_op jit(solution)/shard_map/ppermute | solution.py:246
  47.8 3.0 %transform.3 = (f32[2,2,16,512]{3,2,1,0:T(8,128)S(1)}, f32[2,2,16,512]{3,2,1,0:T(8,128)S(1)}, f32[2,2,16,512]{3,2,1,0:T(8,128)}, f32[2,2,16,512]{3,2,1,0:T(8,128...) custom-call(s32[1]{0:T(128)} %bitcast.me_ref, ...), custom_call_target="tpu_custom_call" | custom-call | tf_op jit(solution)/shard_map/transform/pallas_call | solution.py:234
  50.8 0.6 copy-done.4
  51.5 2.5 %collective-permute-start.13 = (f32[2,2,16,512]{3,2,1,0:T(8,128)S(1)}, f32[2,2,16,512]{3,2,1,0:T(8,128)S(1)}, u32[]{:S(2)}, u32[]{:S(2)}) collective-permute-start(f32[2,2,16,512]{3,2,1,0:T(8,128)S(1)} %get-tuple-element.36), channel_id=1, source_target_pairs={{0,6},{1,7},{2,4},{3,5},{4,2},{5,3},{6,0},{7,1},{8,14},{9,15},{10,... | collective-permute-start | bytes 393224 | tf_op jit(solution)/shard_map/ppermute | solution.py:246
  54.1 1.5 %collective-permute-start.3 = (f32[8,128]{1,0:T(8,128)S(1)}, f32[8,128]{1,0:T(8,128)S(1)}, u32[]{:S(2)}, u32[]{:S(2)}) collective-permute-start(f32[8,128]{1,0:T(8,128)S(1)} %get-tuple-element.26.refs_5_), channel_id=1, source_target_pairs={{0,16},{16,0},{1,17},{17,1},{2,18},{18,2},{3,19},{19,3},{4,20},{20... | collective-permute-start | bytes 12296 | tf_op jit(solution)/shard_map/ppermute | solution.py:202
  55.7 2.1 %collective-permute-done.3.refs_6_ = f32[8,128]{1,0:T(8,128)S(1)} collective-permute-done((f32[8,128]{1,0:T(8,128)S(1)}, f32[8,128]{1,0:T(8,128)S(1)}, u32[]{:S(2)}, u32[]{:S(2)}) %collective-permute-start.3) | collective-permute-done | bytes 4128 | tf_op jit(solution)/shard_map/ppermute | solution.py:202
  57.8 0.6 collective-permute-start.10
  58.4 0.6 collective-permute-start.8
  59.0 1.4 %collective-permute-start.11 = (f32[2,2,16,512]{3,2,1,0:T(8,128)S(1)}, f32[2,2,16,512]{3,2,1,0:T(8,128)S(1)}, u32[]{:S(2)}, u32[]{:S(2)}) collective-permute-start(f32[2,2,16,512]{3,2,1,0:T(8,128)S(1)} %get-tuple-element.34), channel_id=1, source_target_pairs={{0,5},{1,4},{2,7},{3,6},{4,1},{5,0},{6,3},{7,2},{8,13},{9,12},{10,... | collective-permute-start | bytes 393224 | tf_op jit(solution)/shard_map/ppermute | solution.py:246
  60.4 0.9 %collective-permute-start.9 = (f32[2,2,16,512]{3,2,1,0:T(8,128)S(1)}, f32[2,2,16,512]{3,2,1,0:T(8,128)S(1)}, u32[]{:S(2)}, u32[]{:S(2)}) collective-permute-start(f32[2,2,16,512]{3,2,1,0:T(8,128)S(1)} %get-tuple-element.32), channel_id=1, source_target_pairs={{0,4},{1,5},{2,6},{3,7},{4,0},{5,1},{6,2},{7,3},{8,12},{9,13},{10,... | collective-permute-start | bytes 393224 | tf_op jit(solution)/shard_map/ppermute | solution.py:246
  61.3 1.5 %collective-permute-start.4 = (f32[2,2,16,512]{3,2,1,0:T(8,128)S(1)}, f32[2,2,16,512]{3,2,1,0:T(8,128)S(1)}, u32[]{:S(2)}, u32[]{:S(2)}) collective-permute-start(f32[2,2,16,512]{3,2,1,0:T(8,128)S(1)} %get-tuple-element.27), channel_id=1, source_target_pairs={{0,2},{1,3},{2,0},{3,1},{4,6},{5,7},{6,4},{7,5},{8,10},{9,11},{10,... | collective-permute-start | bytes 393224 | tf_op jit(solution)/shard_map/ppermute | solution.py:246
  62.8 0.8 collective-permute-done.10.refs_2_
  63.6 0.9 %collective-permute-start.6 = (f32[2,2,16,512]{3,2,1,0:T(8,128)}, f32[2,2,16,512]{3,2,1,0:T(8,128)S(1)}, u32[]{:S(2)}, u32[]{:S(2)}) collective-permute-start(f32[2,2,16,512]{3,2,1,0:T(8,128)} %get-tuple-element.29), channel_id=1, source_target_pairs={{0,3},{1,2},{2,1},{3,0},{4,7},{5,6},{6,5},{7,4},{8,11},{9,10},{10,... | collective-permute-start | bytes 393224 | tf_op jit(solution)/shard_map/ppermute | solution.py:246
  64.5 1.8 %collective-permute-done.8.refs_0_ = f32[2,2,16,512]{3,2,1,0:T(8,128)S(1)} collective-permute-done((f32[2,2,16,512]{3,2,1,0:T(8,128)S(1)}, f32[2,2,16,512]{3,2,1,0:T(8,128)S(1)}, u32[]{:S(2)}, u32[]{:S(2)}) %collective-permute-start.8) | collective-permute-done | bytes 131104 | tf_op jit(solution)/shard_map/ppermute | solution.py:246
  66.3 1.6 %collective-permute-start.5 = (f32[2,2,16,512]{3,2,1,0:T(8,128)}, f32[2,2,16,512]{3,2,1,0:T(8,128)S(1)}, u32[]{:S(2)}, u32[]{:S(2)}) collective-permute-start(f32[2,2,16,512]{3,2,1,0:T(8,128)} %get-tuple-element.28), channel_id=1, source_target_pairs={{0,2},{1,3},{2,0},{3,1},{4,6},{5,7},{6,4},{7,5},{8,10},{9,11},{10,... | collective-permute-start | bytes 393224 | tf_op jit(solution)/shard_map/ppermute | solution.py:246
  67.8 1.4 %collective-permute-done.11.refs_3_ = f32[2,2,16,512]{3,2,1,0:T(8,128)S(1)} collective-permute-done((f32[2,2,16,512]{3,2,1,0:T(8,128)S(1)}, f32[2,2,16,512]{3,2,1,0:T(8,128)S(1)}, u32[]{:S(2)}, u32[]{:S(2)}) %collective-permute-start.11) | collective-permute-done | bytes 131104 | tf_op jit(solution)/shard_map/ppermute | solution.py:246
  69.2 0.9 %collective-permute-start.7 = (f32[2,2,16,512]{3,2,1,0:T(8,128)}, f32[2,2,16,512]{3,2,1,0:T(8,128)S(1)}, u32[]{:S(2)}, u32[]{:S(2)}) collective-permute-start(f32[2,2,16,512]{3,2,1,0:T(8,128)} %get-tuple-element.30), channel_id=1, source_target_pairs={{0,3},{1,2},{2,1},{3,0},{4,7},{5,6},{6,5},{7,4},{8,11},{9,10},{10,... | collective-permute-start | bytes 393224 | tf_op jit(solution)/shard_map/ppermute | solution.py:246
  70.1 1.4 %collective-permute-done.9.refs_1_ = f32[2,2,16,512]{3,2,1,0:T(8,128)S(1)} collective-permute-done((f32[2,2,16,512]{3,2,1,0:T(8,128)S(1)}, f32[2,2,16,512]{3,2,1,0:T(8,128)S(1)}, u32[]{:S(2)}, u32[]{:S(2)}) %collective-permute-start.9) | collective-permute-done | bytes 131104 | tf_op jit(solution)/shard_map/ppermute | solution.py:246
  72.0 2.2 %merge.4.refs_7_ = f32[2,32,8192]{2,1,0:T(8,128)} custom-call(s32[1]{0:T(128)S(6)} %xor.11.at_ref, f32[2,2,16,512]{3,2,1,0:T(8,128)} %copy-done.6, f32[2,2,16,512]{3,2,1,0:T(8,128)} %copy-done.8, f32[2,2,16,512]{3,2,1,0:T(8,128)} %copy-done.7, f32[2,2,16,512]{3,2,1,0:T(8,128)} %copy-done.9, s32[1]{0:T(128)S(6)} %select_n.21.refs_4_, f32[8,128]{1,0:T(8,128)} %copy-done.5, ...), custom_call_target="tpu_custom_call" | custom-call | tf_op jit(solution)/shard_map/merge/pallas_call | solution.py:264
  74.3 2.2 %merge.5.refs_7_ = f32[2,32,8192]{2,1,0:T(8,128)} custom-call(s32[1]{0:T(128)S(6)} %xor.10.at_ref, f32[2,2,16,512]{3,2,1,0:T(8,128)} %copy-done.11, f32[2,2,16,512]{3,2,1,0:T(8,128)} %copy-done.15, f32[2,2,16,512]{3,2,1,0:T(8,128)} %copy-done.10, f32[2,2,16,512]{3,2,1,0:T(8,128)} %copy-done.13, ...), custom_call_target="tpu_custom_call", output_to_operand_aliasing={{}: (8, {})} | custom-call | tf_op jit(solution)/shard_map/merge/pallas_call | solution.py:264
  76.5 0.6 copy-done.14
  77.2 0.6 copy-done.19
  77.8 2.2 %merge.6.refs_7_ = f32[2,32,8192]{2,1,0:T(8,128)} custom-call(s32[1]{0:T(128)S(6)} %xor.9.at_ref, f32[2,2,16,512]{3,2,1,0:T(8,128)} %copy-done.12, f32[2,2,16,512]{3,2,1,0:T(8,128)} %copy-done.17, f32[2,2,16,512]{3,2,1,0:T(8,128)} %copy-done.14, f32[2,2,16,512]{3,2,1,0:T(8,128)} %copy-done.19, ...), custom_call_target="tpu_custom_call", output_to_operand_aliasing={{}: (8, {})} | custom-call | tf_op jit(solution)/shard_map/merge/pallas_call | solution.py:264
  80.1 0.6 copy-done.16
  80.7 2.2 %merge.7 = f32[2,32,8192]{2,1,0:T(8,128)} custom-call(s32[1]{0:T(128)S(6)} %select_n.20.at_ref, f32[2,2,16,512]{3,2,1,0:T(8,128)} %copy-done.3, f32[2,2,16,512]{3,2,1,0:T(8,128)} %copy-done.4, f32[2,2,16,512]{3,2,1,0:T(8,128)} %copy-done.16, f32[2,2,16,512]{3,2,1,0:T(8,128)} %copy-done.18, s32[1]{0:T(128)S(6)} %select_n.21.refs_4_, ...), custom_call_target="tpu_custom_call", output_to_operand_aliasing={{}: (8, {})} | custom-call | tf_op jit(solution)/shard_map/merge/pallas_call | solution.py:264
  (53 shorter events, 1.4 us)
Async XLA Ops:
  0.0 38.7 %copy-start = (bf16[2,256,1024]{2,1,0:T(8,128)(2,1)S(1)}, bf16[2,256,1024]{2,1,0:T(8,128)(2,1)}, u32[]{:S(2)}) copy-start(bf16[2,256,1024]{2,1,0:T(8,128)(2,1)} %constant.72.clone.w1_ref) | copy-start | bytes 3145732
  0.0 38.7 %copy-start.1 = (f32[2,256,512]{2,1,0:T(8,128)S(1)}, f32[2,256,512]{2,1,0:T(8,128)}, u32[]{:S(2)}) copy-start(f32[2,256,512]{2,1,0:T(8,128)} %constant.73.clone.twist_ref) | copy-start | bytes 3145732
  0.0 4.7 %collective-permute-start = (s32[2,4]{1,0:T(2,128)}, s32[2,4]{1,0:T(2,128)S(1)}, u32[]{:S(2)}, u32[]{:S(2)}) collective-permute-start(s32[2,4]{1,0:T(2,128)} %tiles_ref.1), channel_id=1, source_target_pairs={{0,16},{16,0},{1,17},{17,1},{2,18},{18,2},{3,19},{19,3},{4,20},{20... | collective-permute-start | bytes 104 | tf_op jit(solution)/shard_map/ppermute | solution.py:202
  8.2 30.4 %all-to-all-start = ((f32[16,136,128]{2,1,0:T(8,128)}), f32[16,136,128]{2,1,0:T(8,128)S(1)}, u32[]{:S(2)}, u32[]{:S(2)}) async-start(f32[16,136,128]{2,1,0:T(8,128)} %bitcast.3), calls=%async_computation | async-start | bytes 2228224 | tf_op jit(solution)/shard_map/all_to_all | solution.py:225
  38.7 1.2 %copy-start.2 = (bf16[2,16,32,512]{3,2,1,0:T(8,128)(2,1)S(1)}, bf16[2,16,32,512]{3,2,1,0:T(8,128)(2,1)}, u32[]{:S(2)}) copy-start(bf16[2,16,32,512]{3,2,1,0:T(8,128)(2,1)} %constant.74.clone.w2_ref) | copy-start | bytes 3145732
  42.8 8.0 %copy-start.3 = (f32[2,2,16,512]{3,2,1,0:T(8,128)}, f32[2,2,16,512]{3,2,1,0:T(8,128)S(1)}, u32[]{:S(2)}) copy-start(f32[2,2,16,512]{3,2,1,0:T(8,128)S(1)} %get-tuple-element.22.refs_0_) | copy-start | bytes 393220
  42.8 11.3 %copy-start.5 = (f32[8,128]{1,0:T(8,128)}, f32[8,128]{1,0:T(8,128)S(1)}, u32[]{:S(2)}) copy-start(f32[8,128]{1,0:T(8,128)S(1)} %get-tuple-element.26.refs_5_) | copy-start | bytes 12292
  42.8 15.6 %collective-permute-start.12 = (f32[2,2,16,512]{3,2,1,0:T(8,128)S(1)}, f32[2,2,16,512]{3,2,1,0:T(8,128)S(1)}, u32[]{:S(2)}, u32[]{:S(2)}) collective-permute-start(f32[2,2,16,512]{3,2,1,0:T(8,128)S(1)} %get-tuple-element.35), channel_id=1, source_target_pairs={{0,6},{1,7},{2,4},{3,5},{4,2},{5,3},{6,0},{7,1},{8,14},{9,15},{10,... | collective-permute-start | bytes 393224 | tf_op jit(solution)/shard_map/ppermute | solution.py:246
  47.8 11.1 %collective-permute-start.14 = (f32[2,2,16,512]{3,2,1,0:T(8,128)S(1)}, f32[2,2,16,512]{3,2,1,0:T(8,128)S(1)}, u32[]{:S(2)}, u32[]{:S(2)}) collective-permute-start(f32[2,2,16,512]{3,2,1,0:T(8,128)S(1)} %get-tuple-element.37), channel_id=1, source_target_pairs={{0,7},{1,6},{2,5},{3,4},{4,3},{5,2},{6,1},{7,0},{8,15},{9,14},{10,... | collective-permute-start | bytes 393224 | tf_op jit(solution)/shard_map/ppermute | solution.py:246
  51.5 8.9 %collective-permute-start.13 = (f32[2,2,16,512]{3,2,1,0:T(8,128)S(1)}, f32[2,2,16,512]{3,2,1,0:T(8,128)S(1)}, u32[]{:S(2)}, u32[]{:S(2)}) collective-permute-start(f32[2,2,16,512]{3,2,1,0:T(8,128)S(1)} %get-tuple-element.36), channel_id=1, source_target_pairs={{0,6},{1,7},{2,4},{3,5},{4,2},{5,3},{6,0},{7,1},{8,14},{9,15},{10,... | collective-permute-start | bytes 393224 | tf_op jit(solution)/shard_map/ppermute | solution.py:246
  54.0 7.3 %collective-permute-start.15 = (f32[2,2,16,512]{3,2,1,0:T(8,128)S(1)}, f32[2,2,16,512]{3,2,1,0:T(8,128)S(1)}, u32[]{:S(2)}, u32[]{:S(2)}) collective-permute-start(f32[2,2,16,512]{3,2,1,0:T(8,128)S(1)} %get-tuple-element.38), channel_id=1, source_target_pairs={{0,7},{1,6},{2,5},{3,4},{4,3},{5,2},{6,1},{7,0},{8,15},{9,14},{10,... | collective-permute-start | bytes 393224 | tf_op jit(solution)/shard_map/ppermute | solution.py:246
  54.1 3.6 %collective-permute-start.3 = (f32[8,128]{1,0:T(8,128)S(1)}, f32[8,128]{1,0:T(8,128)S(1)}, u32[]{:S(2)}, u32[]{:S(2)}) collective-permute-start(f32[8,128]{1,0:T(8,128)S(1)} %get-tuple-element.26.refs_5_), channel_id=1, source_target_pairs={{0,16},{16,0},{1,17},{17,1},{2,18},{18,2},{3,19},{19,3},{4,20},{20... | collective-permute-start | bytes 12296 | tf_op jit(solution)/shard_map/ppermute | solution.py:202
  57.8 14.2 %copy-start.20 = (f32[8,128]{1,0:T(8,128)}, f32[8,128]{1,0:T(8,128)S(1)}, u32[]{:S(2)}) copy-start(f32[8,128]{1,0:T(8,128)S(1)} %collective-permute-done.3.refs_6_) | copy-start | bytes 12292
  57.8 5.8 %collective-permute-start.10 = (f32[2,2,16,512]{3,2,1,0:T(8,128)S(1)}, f32[2,2,16,512]{3,2,1,0:T(8,128)S(1)}, u32[]{:S(2)}, u32[]{:S(2)}) collective-permute-start(f32[2,2,16,512]{3,2,1,0:T(8,128)S(1)} %get-tuple-element.33), channel_id=1, source_target_pairs={{0,5},{1,4},{2,7},{3,6},{4,1},{5,0},{6,3},{7,2},{8,13},{9,12},{10,... | collective-permute-start | bytes 393224 | tf_op jit(solution)/shard_map/ppermute | solution.py:246
  58.4 13.6 %copy-start.6 = (f32[2,2,16,512]{3,2,1,0:T(8,128)}, f32[2,2,16,512]{3,2,1,0:T(8,128)S(1)}, u32[]{:S(2)}) copy-start(f32[2,2,16,512]{3,2,1,0:T(8,128)S(1)} %collective-permute-done.12.refs_0_) | copy-start | bytes 393220
  58.4 7.8 %collective-permute-start.8 = (f32[2,2,16,512]{3,2,1,0:T(8,128)S(1)}, f32[2,2,16,512]{3,2,1,0:T(8,128)S(1)}, u32[]{:S(2)}, u32[]{:S(2)}) collective-permute-start(f32[2,2,16,512]{3,2,1,0:T(8,128)S(1)} %get-tuple-element.31), channel_id=1, source_target_pairs={{0,4},{1,5},{2,6},{3,7},{4,0},{5,1},{6,2},{7,3},{8,12},{9,13},{10,... | collective-permute-start | bytes 393224 | tf_op jit(solution)/shard_map/ppermute | solution.py:246
  59.0 13.0 %copy-start.7 = (f32[2,2,16,512]{3,2,1,0:T(8,128)}, f32[2,2,16,512]{3,2,1,0:T(8,128)S(1)}, u32[]{:S(2)}) copy-start(f32[2,2,16,512]{3,2,1,0:T(8,128)S(1)} %collective-permute-done.14.refs_2_) | copy-start | bytes 393220
  59.0 10.2 %collective-permute-start.11 = (f32[2,2,16,512]{3,2,1,0:T(8,128)S(1)}, f32[2,2,16,512]{3,2,1,0:T(8,128)S(1)}, u32[]{:S(2)}, u32[]{:S(2)}) collective-permute-start(f32[2,2,16,512]{3,2,1,0:T(8,128)S(1)} %get-tuple-element.34), channel_id=1, source_target_pairs={{0,5},{1,4},{2,7},{3,6},{4,1},{5,0},{6,3},{7,2},{8,13},{9,12},{10,... | collective-permute-start | bytes 393224 | tf_op jit(solution)/shard_map/ppermute | solution.py:246
  60.4 11.6 %copy-start.8 = (f32[2,2,16,512]{3,2,1,0:T(8,128)}, f32[2,2,16,512]{3,2,1,0:T(8,128)S(1)}, u32[]{:S(2)}) copy-start(f32[2,2,16,512]{3,2,1,0:T(8,128)S(1)} %collective-permute-done.13.refs_1_) | copy-start | bytes 393220
  60.4 11.1 %collective-permute-start.9 = (f32[2,2,16,512]{3,2,1,0:T(8,128)S(1)}, f32[2,2,16,512]{3,2,1,0:T(8,128)S(1)}, u32[]{:S(2)}, u32[]{:S(2)}) collective-permute-start(f32[2,2,16,512]{3,2,1,0:T(8,128)S(1)} %get-tuple-element.32), channel_id=1, source_target_pairs={{0,4},{1,5},{2,6},{3,7},{4,0},{5,1},{6,2},{7,3},{8,12},{9,13},{10,... | collective-permute-start | bytes 393224 | tf_op jit(solution)/shard_map/ppermute | solution.py:246
  61.3 10.7 %copy-start.9 = (f32[2,2,16,512]{3,2,1,0:T(8,128)}, f32[2,2,16,512]{3,2,1,0:T(8,128)S(1)}, u32[]{:S(2)}) copy-start(f32[2,2,16,512]{3,2,1,0:T(8,128)S(1)} %collective-permute-done.15.refs_3_) | copy-start | bytes 393220
  61.3 10.5 %collective-permute-start.4 = (f32[2,2,16,512]{3,2,1,0:T(8,128)S(1)}, f32[2,2,16,512]{3,2,1,0:T(8,128)S(1)}, u32[]{:S(2)}, u32[]{:S(2)}) collective-permute-start(f32[2,2,16,512]{3,2,1,0:T(8,128)S(1)} %get-tuple-element.27), channel_id=1, source_target_pairs={{0,2},{1,3},{2,0},{3,1},{4,6},{5,7},{6,4},{7,5},{8,10},{9,11},{10,... | collective-permute-start | bytes 393224 | tf_op jit(solution)/shard_map/ppermute | solution.py:246
  63.6 10.7 %copy-start.10 = (f32[2,2,16,512]{3,2,1,0:T(8,128)}, f32[2,2,16,512]{3,2,1,0:T(8,128)S(1)}, u32[]{:S(2)}) copy-start(f32[2,2,16,512]{3,2,1,0:T(8,128)S(1)} %collective-permute-done.10.refs_2_) | copy-start | bytes 393220
  63.6 12.9 %collective-permute-start.6 = (f32[2,2,16,512]{3,2,1,0:T(8,128)}, f32[2,2,16,512]{3,2,1,0:T(8,128)S(1)}, u32[]{:S(2)}, u32[]{:S(2)}) collective-permute-start(f32[2,2,16,512]{3,2,1,0:T(8,128)} %get-tuple-element.29), channel_id=1, source_target_pairs={{0,3},{1,2},{2,1},{3,0},{4,7},{5,6},{6,5},{7,4},{8,11},{9,10},{10,... | collective-permute-start | bytes 393224 | tf_op jit(solution)/shard_map/ppermute | solution.py:246
  66.3 8.0 %copy-start.11 = (f32[2,2,16,512]{3,2,1,0:T(8,128)}, f32[2,2,16,512]{3,2,1,0:T(8,128)S(1)}, u32[]{:S(2)}) copy-start(f32[2,2,16,512]{3,2,1,0:T(8,128)S(1)} %collective-permute-done.8.refs_0_) | copy-start | bytes 393220
  66.3 10.2 %collective-permute-start.5 = (f32[2,2,16,512]{3,2,1,0:T(8,128)}, f32[2,2,16,512]{3,2,1,0:T(8,128)S(1)}, u32[]{:S(2)}, u32[]{:S(2)}) collective-permute-start(f32[2,2,16,512]{3,2,1,0:T(8,128)} %get-tuple-element.28), channel_id=1, source_target_pairs={{0,2},{1,3},{2,0},{3,1},{4,6},{5,7},{6,4},{7,5},{8,10},{9,11},{10,... | collective-permute-start | bytes 393224 | tf_op jit(solution)/shard_map/ppermute | solution.py:246
  69.2 5.1 %copy-start.13 = (f32[2,2,16,512]{3,2,1,0:T(8,128)}, f32[2,2,16,512]{3,2,1,0:T(8,128)S(1)}, u32[]{:S(2)}) copy-start(f32[2,2,16,512]{3,2,1,0:T(8,128)S(1)} %collective-permute-done.11.refs_3_) | copy-start | bytes 393220
  69.2 7.3 %collective-permute-start.7 = (f32[2,2,16,512]{3,2,1,0:T(8,128)}, f32[2,2,16,512]{3,2,1,0:T(8,128)S(1)}, u32[]{:S(2)}, u32[]{:S(2)}) collective-permute-start(f32[2,2,16,512]{3,2,1,0:T(8,128)} %get-tuple-element.30), channel_id=1, source_target_pairs={{0,3},{1,2},{2,1},{3,0},{4,7},{5,6},{6,5},{7,4},{8,11},{9,10},{10,... | collective-permute-start | bytes 393224 | tf_op jit(solution)/shard_map/ppermute | solution.py:246
  71.5 2.8 %copy-start.15 = (f32[2,2,16,512]{3,2,1,0:T(8,128)}, f32[2,2,16,512]{3,2,1,0:T(8,128)S(1)}, u32[]{:S(2)}) copy-start(f32[2,2,16,512]{3,2,1,0:T(8,128)S(1)} %collective-permute-done.9.refs_1_) | copy-start | bytes 393220
  71.5 8.6 %collective-permute-start.1 = (f32[2,2,16,512]{3,2,1,0:T(8,128)S(1)}, f32[2,2,16,512]{3,2,1,0:T(8,128)S(1)}, u32[]{:S(2)}, u32[]{:S(2)}) collective-permute-start(f32[2,2,16,512]{3,2,1,0:T(8,128)S(1)} %get-tuple-element.24), channel_id=1, source_target_pairs={{0,1},{1,0},{2,3},{3,2},{4,5},{5,4},{6,7},{7,6},{8,9},{9,8},{10,11... | collective-permute-start | bytes 393224 | tf_op jit(solution)/shard_map/ppermute | solution.py:246
  71.8 4.7 %copy-start.12 = (f32[2,2,16,512]{3,2,1,0:T(8,128)}, f32[2,2,16,512]{3,2,1,0:T(8,128)S(1)}, u32[]{:S(2)}) copy-start(f32[2,2,16,512]{3,2,1,0:T(8,128)S(1)} %collective-permute-done.4.refs_0_) | copy-start | bytes 393220
  71.8 8.2 %collective-permute-start.2 = (f32[2,2,16,512]{3,2,1,0:T(8,128)S(1)}, f32[2,2,16,512]{3,2,1,0:T(8,128)S(1)}, u32[]{:S(2)}, u32[]{:S(2)}) collective-permute-start(f32[2,2,16,512]{3,2,1,0:T(8,128)S(1)} %get-tuple-element.25), channel_id=1, source_target_pairs={{0,1},{1,0},{2,3},{3,2},{4,5},{5,4},{6,7},{7,6},{8,9},{9,8},{10,11... | collective-permute-start | bytes 393224 | tf_op jit(solution)/shard_map/ppermute | solution.py:246
  (7 other events, 4.5 us)

commit v3 on v2

--- a/solution.py
+++ b/solution.py
@@ -50,22 +50,18 @@
     return np.stack([high, low])
 
 
-def outer_tables(plan):
+def matmul_tables(plan):
     angle = np.arange(plan.n1)[:, None] * np.arange(plan.k1)[None, :] % plan.k1
     angle = angle * (2.0 * np.pi / plan.k1)
     cos, sin = np.cos(angle), np.sin(angle)
-    return split_bf16(np.block([[cos, -sin], [sin, cos]]))
-
-
-def inner_tables(plan):
+    parts = [cos, sin, -sin, cos]
     angle = np.arange(INNER)[:, None] * np.arange(INNER)[None, :] % INNER
     angle = angle * (2.0 * np.pi / INNER)
     cos, sin = np.cos(angle), np.sin(angle)
-    by_dest = []
     for q in range(plan.n_col):
         part = slice(q * plan.k2_dev, (q + 1) * plan.k2_dev)
-        by_dest.append(np.block([[cos[part], sin[part]], [-sin[part], cos[part]]]))
-    return split_bf16(np.stack(by_dest))
+        parts.append(np.block([[cos[part], sin[part]], [-sin[part], cos[part]]]))
+    return split_bf16(np.concatenate(parts))
 
 
 def twist_tables(plan):
@@ -127,7 +123,7 @@
             out_ref[g, dest, plan.chunk :, :] = open_ref[...]
 
 
-def transform_kernel(plan, first, rows, with_count, me_ref, x_ref, w1_ref, twist_ref, w2_ref, *refs):
+def transform_kernel(plan, first, rows, with_count, me_ref, x_ref, table_ref, twist_ref, *refs):
     chunk_row = plan.chunk // plan.rows
     me = me_ref[0]
 
@@ -139,7 +135,13 @@
 
     if with_count:
         refs[plan.group][...] = jnp.sum(x_ref[:, plan.chunk :, :], axis=0)
-    w2 = [jnp.concatenate([w2_ref[s, me ^ b] for b in range(plan.group)], axis=0) for s in range(2)]
+    side = 2 * plan.n1
+    size = 2 * plan.k2_dev
+    w1 = [jnp.concatenate([table_ref[s, :side], table_ref[s, side : 2 * side]], axis=1) for s in range(2)]
+    w2 = []
+    for s in range(2):
+        starts = [pl.multiple_of(2 * side + (me ^ b) * size, size) for b in range(plan.group)]
+        w2.append(jnp.concatenate([table_ref[s, pl.ds(start, size)] for start in starts], axis=0))
     tc, ts = twist_ref[0], twist_ref[1]
     for r in range(rows):
         halves = []
@@ -152,42 +154,53 @@
         x = jnp.concatenate(halves, axis=0)
         xh = x.astype(jnp.bfloat16)
         xl = (x - xh.astype(jnp.float32)).astype(jnp.bfloat16)
-        y = outer(xh, w1_ref[0]) + outer(xl, w1_ref[0]) + outer(xh, w1_ref[1])
+        y = outer(xh, w1[0]) + outer(xl, w1[0]) + outer(xh, w1[1])
         yr, yi = y[:, : plan.k1], y[:, plan.k1 :]
         f = jnp.concatenate([yr * tc + yi * ts, yi * tc - yr * ts], axis=0)
         fh = f.astype(jnp.bfloat16)
         fl = (f - fh.astype(jnp.float32)).astype(jnp.bfloat16)
         z = inner(w2[0], fh) + inner(w2[1], fh) + inner(w2[0], fl)
-        size = 2 * plan.k2_dev
         for b in range(plan.group):
             refs[b][r] = z[b * size : (b + 1) * size].reshape(2, plan.k2_dev, plan.k1)
 
 
-def merge_kernel(plan, splits, at_ref, *refs):
-    del at_ref
+def merge_kernel(plan, splits, me_ref, *refs):
     n = len(splits)
-    even, odd, parity_ref, counts = refs[:n], refs[n : 2 * n], refs[2 * n], refs[2 * n + 1 : 2 * n + 1 + plan.n_row]
-    out_ref, tile_ref = refs[-2], refs[-1]
+    chunks = [refs[i * plan.group : (i + 1) * plan.group] for i in range(n)]
+    counts = refs[n * plan.group : n * plan.group + plan.n_row]
+    out_ref, tile_ref, row_ref, sems = refs[n * plan.group + plan.n_row :]
     total = counts[0][...]
     for other in counts[1:]:
         total = total + other[...]
     total = jnp.sum(jnp.sum(total, axis=0, keepdims=True), axis=1, keepdims=True)
     scale = jnp.sqrt(float(plan.rows_all) / total)
-    swapped = parity_ref[0] == 1
+    inside = lax.rem(me_ref[0], plan.group)
+    swapped = lax.rem(inside, 2) == 1
     take = min(plan.k2_dev, SUBS)
-    for i, rows in enumerate(splits):
-        for r in range(rows):
-            for k2 in range(0, plan.k2_dev, take):
-                for j in range(plan.k1_tiles):
-                    lanes = slice(j * LANES, (j + 1) * LANES)
-                    a = even[i][r, 0, k2 : k2 + take, lanes] * scale
-                    b = odd[i][r, 0, k2 : k2 + take, lanes] * scale
-                    at = (k2 * plan.k1_tiles + j) * SUBS + sum(splits[:i]) + r
-                    stride = plan.k1_tiles * SUBS
-                    tile_ref[pl.ds(at, take, stride=stride), :] = jnp.where(swapped, b, a)
-                    tile_ref[pl.ds(at + plan.rows, take, stride=stride), :] = jnp.where(swapped, a, b)
-    for f in range(plan.freq_tiles):
-        out_ref[0, :, f * LANES : (f + 1) * LANES] = tile_ref[f * SUBS : (f + 1) * SUBS, :]
+    stride = plan.k1_tiles * SUBS
+    copies = []
+    for pair in range(plan.group // 2):
+        for part in range(2):
+            slot = pair * 2 + part
+            for i, rows in enumerate(splits):
+                for r in range(rows):
+                    for k2 in range(0, plan.k2_dev, take):
+                        for j in range(plan.k1_tiles):
+                            lanes = slice(j * LANES, (j + 1) * LANES)
+                            a = chunks[i][2 * pair][r, part, k2 : k2 + take, lanes] * scale
+                            b = chunks[i][2 * pair + 1][r, part, k2 : k2 + take, lanes] * scale
+                            at = (k2 * plan.k1_tiles + j) * SUBS + sum(splits[:i]) + r
+                            tile_ref[slot, pl.ds(at, take, stride=stride), :] = jnp.where(swapped, b, a)
+                            tile_ref[slot, pl.ds(at + plan.rows, take, stride=stride), :] = jnp.where(swapped, a, b)
+            for f in range(plan.freq_tiles):
+                row_ref[slot, :, f * LANES : (f + 1) * LANES] = tile_ref[slot, f * SUBS : (f + 1) * SUBS, :]
+            tile = lax.div(inside, 2) ^ pair
+            target = out_ref.at[part, pl.ds(pl.multiple_of(tile * SUBS, SUBS), SUBS), :]
+            copy = pltpu.make_async_copy(row_ref.at[slot], target, sems.at[slot])
+            copy.start()
+            copies.append(copy)
+    for copy in copies:
+        copy.wait()
 
 
 def per_device(phase_codes, aperture, tile_offsets):
@@ -224,7 +237,7 @@
     packed = packed.reshape(n_col, plan.chunk + SUBS, LANES)
     received = lax.all_to_all(packed, "col", split_axis=0, concat_axis=0, tiled=True)
 
-    w1, w2, twist = outer_tables(plan), inner_tables(plan), twist_tables(plan)
+    table, twist = matmul_tables(plan), twist_tables(plan)
     splits = SPLITS if sum(SPLITS) == plan.rows else (plan.rows,)
     chunks = []
     for i, rows in enumerate(splits):
@@ -234,11 +247,11 @@
         made = pl.pallas_call(
             partial(transform_kernel, plan, sum(splits[:i]), rows, i == 0),
             out_shape=shapes,
-            in_specs=[smem, vmem, vmem, vmem, vmem],
+            in_specs=[smem, vmem, vmem, vmem],
             out_specs=[vmem] * len(shapes),
             compiler_params=pltpu.CompilerParams(vmem_limit_bytes=24 * 2**20),
             name="transform",
-        )(me, received, w1, twist, w2)
+        )(me, received, table, twist)
         if i == 0:
             counts = [made[-1]] + along_rows(made[-1])
         chunks.append(
@@ -246,35 +259,20 @@
             + [lax.ppermute(made[b], "col", [(q, q ^ b) for q in range(n_col)]) for b in range(1, plan.group)]
         )
 
-    inside = col_index % plan.group
-    parity = inside % 2
-    out = None
-    for b in range(plan.group - 2, -1, -2):
-        tile = (inside // 2) ^ (b // 2)
-        pair = [c[b] for c in chunks] + [c[b + 1] for c in chunks]
-        in_specs = [pl.BlockSpec((rows, 1, plan.k2_dev, plan.k1), lambda c, t: (0, c, 0, 0)) for rows in splits] * 2
-        in_specs = in_specs + [smem] + [pl.BlockSpec((SUBS, LANES), lambda c, t: (0, 0))] * n_row
-        args = [tile, *pair, parity, *counts]
-        aliases = {}
-        kernel = partial(merge_kernel, plan, splits)
-        if out is not None:
-            in_specs = in_specs + [pl.BlockSpec(memory_space=pl.ANY)]
-            args = args + [out]
-            aliases = {len(args) - 1: 0}
-        out = pl.pallas_call(
-            kernel,
-            out_shape=jax.ShapeDtypeStruct((2, plan.row_dev, plan.freq_tiles * LANES), jnp.float32),
-            grid_spec=pltpu.PrefetchScalarGridSpec(
-                num_scalar_prefetch=1,
-                grid=(2,),
-                in_specs=in_specs,
-                out_specs=pl.BlockSpec((1, SUBS, plan.freq_tiles * LANES), lambda c, t: (c, t[0], 0)),
-                scratch_shapes=[pltpu.VMEM((plan.freq_tiles * SUBS, LANES), jnp.float32)],
-            ),
-            input_output_aliases=aliases,
-            name="merge",
-        )(*args)
-    return out
+    slots = plan.group
+    return pl.pallas_call(
+        partial(merge_kernel, plan, splits),
+        out_shape=jax.ShapeDtypeStruct((2, plan.row_dev, plan.freq_tiles * LANES), jnp.float32),
+        in_specs=[smem] + [vmem] * (len(splits) * plan.group + n_row),
+        out_specs=pl.BlockSpec(memory_space=pl.ANY),
+        scratch_shapes=[
+            pltpu.VMEM((slots, plan.freq_tiles * SUBS, LANES), jnp.float32),
+            pltpu.VMEM((slots, SUBS, plan.freq_tiles * LANES), jnp.float32),
+            pltpu.SemaphoreType.DMA((slots,)),
+        ],
+        compiler_params=pltpu.CompilerParams(vmem_limit_bytes=24 * 2**20),
+        name="merge",
+    )(me, *[chunk for part in chunks for chunk in part], *counts)
 
 
 def solution(mesh):

time: 83.4 us -> 79.7 us (0.956)
  waiting for transfers between devices: 33.2 us -> 42.8 us
  Pallas kernels: 17.7 us -> 9.89 us
  local copies, waits for them, and re-layouts: 4.46 us -> 1.77 us
  starting transfers between devices: 27.5 us -> 24.9 us
    ppermute x14, waiting for transfers between devices: 5.34 us -> 15 us  [per_device(): lax.ppermute(made[b], 'col', [(q, q ^ b) for q in range(n_col)])]
    pallas_call x4 -> x1, Pallas kernels: 8.79 us -> 2.4 us  [per_device(): pl.pallas_call(partial(merge_kernel, plan, splits), out_shape=jax.ShapeDt...]
    unnamed x44 -> x6, local copies, waits for them, and re-layouts: 4.46 us -> 1.77 us
    ppermute x14, starting transfers between devices: 16.5 us -> 14 us  [per_device(): lax.ppermute(made[b], 'col', [(q, q ^ b) for q in range(n_col)])]
    pallas_call x2, Pallas kernels: 5.91 us -> 4.54 us  [per_device(): pl.pallas_call(partial(transform_kernel, plan, sum(splits[:i]), rows, i =...]
  transfers between devices with their start and end apart: 17 -> 17, of which waited for: 7 -> 11; matrix products, arithmetic and copies ran while one was open for 0% -> 0% of each run, Pallas kernels for 12% -> 3%
where the time goes in v3:
time: 79.7 us; the launch traced here: 79.5 us
  waiting for transfers between devices  42.8 us (54%)
  starting transfers between devices  24.9 us (31%)
  Pallas kernels  9.89 us (12%)
  local copies, waits for them, and re-layouts  1.77 us (2%)
    all_to_all x1, waiting for transfers between devices, per_device(): lax.all_to_all(packed, 'col', split_axis=0, concat_axis=0, tiled=True)  24 us
    ppermute x14, waiting for transfers between devices, per_device(): lax.ppermute(made[b], 'col', [(q, q ^ b) for q in range(n_col)])  15 us
    ppermute x14, starting transfers between devices, per_device(): lax.ppermute(made[b], 'col', [(q, q ^ b) for q in range(n_col)])  14 us
    all_to_all x1, starting transfers between devices, per_device(): lax.all_to_all(packed, 'col', split_axis=0, concat_axis=0, tiled=True)  6.41 us
    ppermute x2, starting transfers between devices, along_rows(): lax.ppermute(value, 'row', [(i, (i + d) % n_row) for i in range(n_row)])  4.55 us
    pallas_call x2, Pallas kernels, per_device(): pl.pallas_call(partial(transform_kernel, plan, sum(splits[:i]), rows, i =...  4.54 us
    ppermute x2, waiting for transfers between devices, along_rows(): lax.ppermute(value, 'row', [(i, (i + d) % n_row) for i in range(n_row)])  3.84 us
    pallas_call x1, Pallas kernels, per_device(): pl.pallas_call(partial(field_kernel, plan), out_shape=jax.ShapeDtypeStruc...  2.96 us
  transfers between devices with their start and end apart: 17, of which 11 were waited for; matrix products, arithmetic and copies ran while one was open for 0% of the time, Pallas kernels for 3%

profile of v3, /device:TPU:0, one launch (start us, length us, event | category | flops | bytes accessed | tf_op | source)
XLA Modules:
  0.0 79.5 jit_solution(13831032484004592091)
XLA Ops:
  0.0 3.0 %collective-permute-start = (s32[2,4]{1,0:T(2,128)}, s32[2,4]{1,0:T(2,128)S(1)}, u32[]{:S(2)}, u32[]{:S(2)}) collective-permute-start(s32[2,4]{1,0:T(2,128)} %tiles_ref.1), channel_id=1, source_target_pairs={{0,16},{16,0},{1,17},{17,1},{2,18},{18,2},{3,19},{19,3},{4,20},{20... | collective-permute-start | bytes 104 | tf_op jit(solution)/shard_map/ppermute | solution.py:215
  3.0 1.8 %collective-permute-done.refs_0_ = s32[2,4]{1,0:T(2,128)S(1)} collective-permute-done((s32[2,4]{1,0:T(2,128)}, s32[2,4]{1,0:T(2,128)S(1)}, u32[]{:S(2)}, u32[]{:S(2)}) %collective-permute-start) | collective-permute-done | bytes 64 | tf_op jit(solution)/shard_map/ppermute | solution.py:215
  4.7 0.5 copy-done.2
  5.3 3.0 %field.1 = f32[2,8,136,128]{3,2,1,0:T(8,128)} custom-call(s32[1]{0:T(128)} %bitcast.1.row_ref, s32[2,4]{1,0:T(2,128)} %tiles_ref.1, s32[2,4]{1,0:T(2,128)} %copy-done.2, s32[32,2048]{1,0:T(8,128)} %refs_1_.1, s32[32,2048]{1,0:T(8,128)} %refs_3_.1, s32[32,2048]{1,0:T(8,128)} %refs_3_.1), custom_call_target="tpu_custom_call" | custom-call | tf_op jit(solution)/shard_map/field/pallas_call | solution.py:222
  8.2 6.4 %all-to-all-start = ((f32[16,136,128]{2,1,0:T(8,128)}), f32[16,136,128]{2,1,0:T(8,128)S(1)}, u32[]{:S(2)}, u32[]{:S(2)}) async-start(f32[16,136,128]{2,1,0:T(8,128)} %bitcast.3), calls=%async_computation | async-start | bytes 2228224 | tf_op jit(solution)/shard_map/all_to_all | solution.py:238
  14.7 24.0 %all-to-all-done.x_ref = f32[16,136,128]{2,1,0:T(8,128)S(1)} async-done(((f32[16,136,128]{2,1,0:T(8,128)}), f32[16,136,128]{2,1,0:T(8,128)S(1)}, u32[]{:S(2)}, u32[]{:S(2)}) %all-to-all-start) | async-done | bytes 1114144 | tf_op jit(solution)/shard_map/all_to_all | solution.py:238
  38.7 1.2 %copy-done.1 = f32[2,256,512]{2,1,0:T(8,128)S(1)} copy-done((f32[2,256,512]{2,1,0:T(8,128)S(1)}, f32[2,256,512]{2,1,0:T(8,128)}, u32[]{:S(2)}) %copy-start.1) | copy-done | bytes 1048600
  39.9 2.3 %transform.3 = (f32[2,2,16,512]{3,2,1,0:T(8,128)S(1)}, f32[2,2,16,512]{3,2,1,0:T(8,128)S(1)}, f32[2,2,16,512]{3,2,1,0:T(8,128)S(1)}, f32[2,2,16,512]{3,2,1,0:T(8...) custom-call(s32[1]{0:T(128)} %bitcast.me_ref, ...), custom_call_target="tpu_custom_call" | custom-call | tf_op jit(solution)/shard_map/transform/pallas_call | solution.py:247
  42.2 0.8 %collective-permute-start.8 = (f32[2,2,16,512]{3,2,1,0:T(8,128)S(1)}, f32[2,2,16,512]{3,2,1,0:T(8,128)S(1)}, u32[]{:S(2)}, u32[]{:S(2)}) collective-permute-start(f32[2,2,16,512]{3,2,1,0:T(8,128)S(1)} %get-tuple-element.31), channel_id=1, source_target_pairs={{0,1},{1,0},{2,3},{3,2},{4,5},{5,4},{6,7},{7,6},{8,9},{9,8},{10,11... | collective-permute-start | bytes 393224 | tf_op jit(solution)/shard_map/ppermute | solution.py:259
  43.0 2.1 %collective-permute-start.9 = (f32[2,2,16,512]{3,2,1,0:T(8,128)S(1)}, f32[2,2,16,512]{3,2,1,0:T(8,128)S(1)}, u32[]{:S(2)}, u32[]{:S(2)}) collective-permute-start(f32[2,2,16,512]{3,2,1,0:T(8,128)S(1)} %get-tuple-element.32), channel_id=1, source_target_pairs={{0,2},{1,3},{2,0},{3,1},{4,6},{5,7},{6,4},{7,5},{8,10},{9,11},{10,... | collective-permute-start | bytes 393224 | tf_op jit(solution)/shard_map/ppermute | solution.py:259
  45.0 3.1 %collective-permute-start.11 = (f32[2,2,16,512]{3,2,1,0:T(8,128)S(1)}, f32[2,2,16,512]{3,2,1,0:T(8,128)S(1)}, u32[]{:S(2)}, u32[]{:S(2)}) collective-permute-start(f32[2,2,16,512]{3,2,1,0:T(8,128)S(1)} %get-tuple-element.34), channel_id=1, source_target_pairs={{0,4},{1,5},{2,6},{3,7},{4,0},{5,1},{6,2},{7,3},{8,12},{9,13},{10,... | collective-permute-start | bytes 393224 | tf_op jit(solution)/shard_map/ppermute | solution.py:259
  48.1 2.3 %transform.2 = (f32[2,2,16,512]{3,2,1,0:T(8,128)S(1)}, f32[2,2,16,512]{3,2,1,0:T(8,128)S(1)}, f32[2,2,16,512]{3,2,1,0:T(8,128)S(1)}, f32[2,2,16,512]{3,2,1,0:T(8...) custom-call(s32[1]{0:T(128)} %bitcast.me_ref, ...), custom_call_target="tpu_custom_call" | custom-call | tf_op jit(solution)/shard_map/transform/pallas_call | solution.py:247
  50.4 1.6 %collective-permute-start.15 = (f32[8,128]{1,0:T(8,128)S(1)}, f32[8,128]{1,0:T(8,128)S(1)}, u32[]{:S(2)}, u32[]{:S(2)}) collective-permute-start(f32[8,128]{1,0:T(8,128)S(1)} %get-tuple-element.38.refs_16_), channel_id=1, source_target_pairs={{0,16},{16,0},{1,17},{17,1},{2,18},{18,2},{3,19},{19,3},{4,20},{20... | collective-permute-start | bytes 12296 | tf_op jit(solution)/shard_map/ppermute | solution.py:215
  52.0 2.1 %collective-permute-done.15.refs_17_ = f32[8,128]{1,0:T(8,128)S(1)} collective-permute-done((f32[8,128]{1,0:T(8,128)S(1)}, f32[8,128]{1,0:T(8,128)S(1)}, u32[]{:S(2)}, u32[]{:S(2)}) %collective-permute-start.15) | collective-permute-done | bytes 4128 | tf_op jit(solution)/shard_map/ppermute | solution.py:215
  54.1 1.8 %collective-permute-start.13 = (f32[2,2,16,512]{3,2,1,0:T(8,128)S(1)}, f32[2,2,16,512]{3,2,1,0:T(8,128)S(1)}, u32[]{:S(2)}, u32[]{:S(2)}) collective-permute-start(f32[2,2,16,512]{3,2,1,0:T(8,128)S(1)} %get-tuple-element.36), channel_id=1, source_target_pairs={{0,6},{1,7},{2,4},{3,5},{4,2},{5,3},{6,0},{7,1},{8,14},{9,15},{10,... | collective-permute-start | bytes 393224 | tf_op jit(solution)/shard_map/ppermute | solution.py:259
  55.9 1.0 %collective-permute-start.14 = (f32[2,2,16,512]{3,2,1,0:T(8,128)S(1)}, f32[2,2,16,512]{3,2,1,0:T(8,128)S(1)}, u32[]{:S(2)}, u32[]{:S(2)}) collective-permute-start(f32[2,2,16,512]{3,2,1,0:T(8,128)S(1)} %get-tuple-element.37), channel_id=1, source_target_pairs={{0,7},{1,6},{2,5},{3,4},{4,3},{5,2},{6,1},{7,0},{8,15},{9,14},{10,... | collective-permute-start | bytes 393224 | tf_op jit(solution)/shard_map/ppermute | solution.py:259
  56.9 0.2 collective-permute-start.1
  57.1 1.6 %collective-permute-start.2 = (f32[2,2,16,512]{3,2,1,0:T(8,128)S(1)}, f32[2,2,16,512]{3,2,1,0:T(8,128)S(1)}, u32[]{:S(2)}, u32[]{:S(2)}) collective-permute-start(f32[2,2,16,512]{3,2,1,0:T(8,128)S(1)} %get-tuple-element.24), channel_id=1, source_target_pairs={{0,2},{1,3},{2,0},{3,1},{4,6},{5,7},{6,4},{7,5},{8,10},{9,11},{10,... | collective-permute-start | bytes 393224 | tf_op jit(solution)/shard_map/ppermute | solution.py:259
  58.7 0.9 %collective-permute-done.12.refs_13_ = f32[2,2,16,512]{3,2,1,0:T(8,128)S(1)} collective-permute-done((f32[2,2,16,512]{3,2,1,0:T(8,128)S(1)}, f32[2,2,16,512]{3,2,1,0:T(8,128)S(1)}, u32[]{:S(2)}, u32[]{:S(2)}) %collective-permute-start.12) | collective-permute-done | bytes 131104 | tf_op jit(solution)/shard_map/ppermute | solution.py:259
  59.6 0.2 collective-permute-start.3
  59.9 2.6 %collective-permute-done.13.refs_14_ = f32[2,2,16,512]{3,2,1,0:T(8,128)S(1)} collective-permute-done((f32[2,2,16,512]{3,2,1,0:T(8,128)S(1)}, f32[2,2,16,512]{3,2,1,0:T(8,128)S(1)}, u32[]{:S(2)}, u32[]{:S(2)}) %collective-permute-start.13) | collective-permute-done | bytes 131104 | tf_op jit(solution)/shard_map/ppermute | solution.py:259
  62.5 1.8 %collective-permute-start.4 = (f32[2,2,16,512]{3,2,1,0:T(8,128)S(1)}, f32[2,2,16,512]{3,2,1,0:T(8,128)S(1)}, u32[]{:S(2)}, u32[]{:S(2)}) collective-permute-start(f32[2,2,16,512]{3,2,1,0:T(8,128)S(1)} %get-tuple-element.26), channel_id=1, source_target_pairs={{0,4},{1,5},{2,6},{3,7},{4,0},{5,1},{6,2},{7,3},{8,12},{9,13},{10,... | collective-permute-start | bytes 393224 | tf_op jit(solution)/shard_map/ppermute | solution.py:259
  64.3 1.6 %collective-permute-done.14.refs_15_ = f32[2,2,16,512]{3,2,1,0:T(8,128)S(1)} collective-permute-done((f32[2,2,16,512]{3,2,1,0:T(8,128)S(1)}, f32[2,2,16,512]{3,2,1,0:T(8,128)S(1)}, u32[]{:S(2)}, u32[]{:S(2)}) %collective-permute-start.14) | collective-permute-done | bytes 131104 | tf_op jit(solution)/shard_map/ppermute | solution.py:259
  65.9 0.2 collective-permute-start.5
  66.1 0.9 %collective-permute-start.6 = (f32[2,2,16,512]{3,2,1,0:T(8,128)S(1)}, f32[2,2,16,512]{3,2,1,0:T(8,128)S(1)}, u32[]{:S(2)}, u32[]{:S(2)}) collective-permute-start(f32[2,2,16,512]{3,2,1,0:T(8,128)S(1)} %get-tuple-element.28), channel_id=1, source_target_pairs={{0,6},{1,7},{2,4},{3,5},{4,2},{5,3},{6,0},{7,1},{8,14},{9,15},{10,... | collective-permute-start | bytes 393224 | tf_op jit(solution)/shard_map/ppermute | solution.py:259
  67.0 1.5 %collective-permute-done.2.refs_2_ = f32[2,2,16,512]{3,2,1,0:T(8,128)S(1)} collective-permute-done((f32[2,2,16,512]{3,2,1,0:T(8,128)S(1)}, f32[2,2,16,512]{3,2,1,0:T(8,128)S(1)}, u32[]{:S(2)}, u32[]{:S(2)}) %collective-permute-start.2) | collective-permute-done | bytes 131104 | tf_op jit(solution)/shard_map/ppermute | solution.py:259
  68.6 0.3 collective-permute-start.7
  68.9 1.8 %collective-permute-done.3.refs_3_ = f32[2,2,16,512]{3,2,1,0:T(8,128)S(1)} collective-permute-done((f32[2,2,16,512]{3,2,1,0:T(8,128)S(1)}, f32[2,2,16,512]{3,2,1,0:T(8,128)S(1)}, u32[]{:S(2)}, u32[]{:S(2)}) %collective-permute-start.3) | collective-permute-done | bytes 131104 | tf_op jit(solution)/shard_map/ppermute | solution.py:259
  70.7 1.1 %collective-permute-done.5.refs_5_ = f32[2,2,16,512]{3,2,1,0:T(8,128)S(1)} collective-permute-done((f32[2,2,16,512]{3,2,1,0:T(8,128)S(1)}, f32[2,2,16,512]{3,2,1,0:T(8,128)S(1)}, u32[]{:S(2)}, u32[]{:S(2)}) %collective-permute-start.5) | collective-permute-done | bytes 131104 | tf_op jit(solution)/shard_map/ppermute | solution.py:259
  71.8 2.4 %collective-permute-done.6.refs_6_ = f32[2,2,16,512]{3,2,1,0:T(8,128)S(1)} collective-permute-done((f32[2,2,16,512]{3,2,1,0:T(8,128)S(1)}, f32[2,2,16,512]{3,2,1,0:T(8,128)S(1)}, u32[]{:S(2)}, u32[]{:S(2)}) %collective-permute-start.6) | collective-permute-done | bytes 131104 | tf_op jit(solution)/shard_map/ppermute | solution.py:259
  74.1 3.0 %collective-permute-done.7.refs_7_ = f32[2,2,16,512]{3,2,1,0:T(8,128)S(1)} collective-permute-done((f32[2,2,16,512]{3,2,1,0:T(8,128)S(1)}, f32[2,2,16,512]{3,2,1,0:T(8,128)S(1)}, u32[]{:S(2)}, u32[]{:S(2)}) %collective-permute-start.7) | collective-permute-done | bytes 131104 | tf_op jit(solution)/shard_map/ppermute | solution.py:259
  77.1 2.4 %merge.1 = f32[2,32,8192]{2,1,0:T(8,128)} custom-call(s32[1]{0:T(128)} %bitcast.me_ref, f32[2,2,16,512]{3,2,1,0:T(8,128)S(1)} %get-tuple-element.22.refs_0_, f32[2,2,16,512]{3,2,1,0:T(8,128)S(1)} %collective-permute-done.1.refs_1_, f32[2,2,16,512]{3,2,1,0:T(8,128)S(1)} %collective-permute-done.2.refs_2_, ...), custom_call_target="tpu_custom_call" | custom-call | tf_op jit(solution)/shard_map/merge/pallas_call | solution.py:263
  (12 shorter events, 0.0 us)
Async XLA Ops:
  0.0 38.7 %copy-start = (bf16[2,1024,512]{2,1,0:T(8,128)(2,1)S(1)}, bf16[2,1024,512]{2,1,0:T(8,128)(2,1)}, u32[]{:S(2)}) copy-start(bf16[2,1024,512]{2,1,0:T(8,128)(2,1)} %constant.13.clone.table_ref) | copy-start | bytes 6291460
  0.0 4.7 %collective-permute-start = (s32[2,4]{1,0:T(2,128)}, s32[2,4]{1,0:T(2,128)S(1)}, u32[]{:S(2)}, u32[]{:S(2)}) collective-permute-start(s32[2,4]{1,0:T(2,128)} %tiles_ref.1), channel_id=1, source_target_pairs={{0,16},{16,0},{1,17},{17,1},{2,18},{18,2},{3,19},{19,3},{4,20},{20... | collective-permute-start | bytes 104 | tf_op jit(solution)/shard_map/ppermute | solution.py:215
  4.7 0.5 copy-start.2
  8.2 30.4 %all-to-all-start = ((f32[16,136,128]{2,1,0:T(8,128)}), f32[16,136,128]{2,1,0:T(8,128)S(1)}, u32[]{:S(2)}, u32[]{:S(2)}) async-start(f32[16,136,128]{2,1,0:T(8,128)} %bitcast.3), calls=%async_computation | async-start | bytes 2228224 | tf_op jit(solution)/shard_map/all_to_all | solution.py:238
  38.7 1.2 %copy-start.1 = (f32[2,256,512]{2,1,0:T(8,128)S(1)}, f32[2,256,512]{2,1,0:T(8,128)}, u32[]{:S(2)}) copy-start(f32[2,256,512]{2,1,0:T(8,128)} %constant.14.clone.twist_ref) | copy-start | bytes 3145732
  42.2 11.9 %collective-permute-start.8 = (f32[2,2,16,512]{3,2,1,0:T(8,128)S(1)}, f32[2,2,16,512]{3,2,1,0:T(8,128)S(1)}, u32[]{:S(2)}, u32[]{:S(2)}) collective-permute-start(f32[2,2,16,512]{3,2,1,0:T(8,128)S(1)} %get-tuple-element.31), channel_id=1, source_target_pairs={{0,1},{1,0},{2,3},{3,2},{4,5},{5,4},{6,7},{7,6},{8,9},{9,8},{10,11... | collective-permute-start | bytes 393224 | tf_op jit(solution)/shard_map/ppermute | solution.py:259
  43.0 12.9 %collective-permute-start.9 = (f32[2,2,16,512]{3,2,1,0:T(8,128)S(1)}, f32[2,2,16,512]{3,2,1,0:T(8,128)S(1)}, u32[]{:S(2)}, u32[]{:S(2)}) collective-permute-start(f32[2,2,16,512]{3,2,1,0:T(8,128)S(1)} %get-tuple-element.32), channel_id=1, source_target_pairs={{0,2},{1,3},{2,0},{3,1},{4,6},{5,7},{6,4},{7,5},{8,10},{9,11},{10,... | collective-permute-start | bytes 393224 | tf_op jit(solution)/shard_map/ppermute | solution.py:259
  45.0 11.9 %collective-permute-start.10 = (f32[2,2,16,512]{3,2,1,0:T(8,128)S(1)}, f32[2,2,16,512]{3,2,1,0:T(8,128)S(1)}, u32[]{:S(2)}, u32[]{:S(2)}) collective-permute-start(f32[2,2,16,512]{3,2,1,0:T(8,128)S(1)} %get-tuple-element.33), channel_id=1, source_target_pairs={{0,3},{1,2},{2,1},{3,0},{4,7},{5,6},{6,5},{7,4},{8,11},{9,10},{10,... | collective-permute-start | bytes 393224 | tf_op jit(solution)/shard_map/ppermute | solution.py:259
  45.0 12.1 %collective-permute-start.11 = (f32[2,2,16,512]{3,2,1,0:T(8,128)S(1)}, f32[2,2,16,512]{3,2,1,0:T(8,128)S(1)}, u32[]{:S(2)}, u32[]{:S(2)}) collective-permute-start(f32[2,2,16,512]{3,2,1,0:T(8,128)S(1)} %get-tuple-element.34), channel_id=1, source_target_pairs={{0,4},{1,5},{2,6},{3,7},{4,0},{5,1},{6,2},{7,3},{8,12},{9,13},{10,... | collective-permute-start | bytes 393224 | tf_op jit(solution)/shard_map/ppermute | solution.py:259
  50.4 3.7 %collective-permute-start.15 = (f32[8,128]{1,0:T(8,128)S(1)}, f32[8,128]{1,0:T(8,128)S(1)}, u32[]{:S(2)}, u32[]{:S(2)}) collective-permute-start(f32[8,128]{1,0:T(8,128)S(1)} %get-tuple-element.38.refs_16_), channel_id=1, source_target_pairs={{0,16},{16,0},{1,17},{17,1},{2,18},{18,2},{3,19},{19,3},{4,20},{20... | collective-permute-start | bytes 12296 | tf_op jit(solution)/shard_map/ppermute | solution.py:215
  54.1 5.6 %collective-permute-start.12 = (f32[2,2,16,512]{3,2,1,0:T(8,128)S(1)}, f32[2,2,16,512]{3,2,1,0:T(8,128)S(1)}, u32[]{:S(2)}, u32[]{:S(2)}) collective-permute-start(f32[2,2,16,512]{3,2,1,0:T(8,128)S(1)} %get-tuple-element.35), channel_id=1, source_target_pairs={{0,5},{1,4},{2,7},{3,6},{4,1},{5,0},{6,3},{7,2},{8,13},{9,12},{10,... | collective-permute-start | bytes 393224 | tf_op jit(solution)/shard_map/ppermute | solution.py:259
  54.1 8.4 %collective-permute-start.13 = (f32[2,2,16,512]{3,2,1,0:T(8,128)S(1)}, f32[2,2,16,512]{3,2,1,0:T(8,128)S(1)}, u32[]{:S(2)}, u32[]{:S(2)}) collective-permute-start(f32[2,2,16,512]{3,2,1,0:T(8,128)S(1)} %get-tuple-element.36), channel_id=1, source_target_pairs={{0,6},{1,7},{2,4},{3,5},{4,2},{5,3},{6,0},{7,1},{8,14},{9,15},{10,... | collective-permute-start | bytes 393224 | tf_op jit(solution)/shard_map/ppermute | solution.py:259
  55.9 10.1 %collective-permute-start.14 = (f32[2,2,16,512]{3,2,1,0:T(8,128)S(1)}, f32[2,2,16,512]{3,2,1,0:T(8,128)S(1)}, u32[]{:S(2)}, u32[]{:S(2)}) collective-permute-start(f32[2,2,16,512]{3,2,1,0:T(8,128)S(1)} %get-tuple-element.37), channel_id=1, source_target_pairs={{0,7},{1,6},{2,5},{3,4},{4,3},{5,2},{6,1},{7,0},{8,15},{9,14},{10,... | collective-permute-start | bytes 393224 | tf_op jit(solution)/shard_map/ppermute | solution.py:259
  56.9 9.2 %collective-permute-start.1 = (f32[2,2,16,512]{3,2,1,0:T(8,128)S(1)}, f32[2,2,16,512]{3,2,1,0:T(8,128)S(1)}, u32[]{:S(2)}, u32[]{:S(2)}) collective-permute-start(f32[2,2,16,512]{3,2,1,0:T(8,128)S(1)} %get-tuple-element.23), channel_id=1, source_target_pairs={{0,1},{1,0},{2,3},{3,2},{4,5},{5,4},{6,7},{7,6},{8,9},{9,8},{10,11... | collective-permute-start | bytes 393224 | tf_op jit(solution)/shard_map/ppermute | solution.py:259
  57.1 11.4 %collective-permute-start.2 = (f32[2,2,16,512]{3,2,1,0:T(8,128)S(1)}, f32[2,2,16,512]{3,2,1,0:T(8,128)S(1)}, u32[]{:S(2)}, u32[]{:S(2)}) collective-permute-start(f32[2,2,16,512]{3,2,1,0:T(8,128)S(1)} %get-tuple-element.24), channel_id=1, source_target_pairs={{0,2},{1,3},{2,0},{3,1},{4,6},{5,7},{6,4},{7,5},{8,10},{9,11},{10,... | collective-permute-start | bytes 393224 | tf_op jit(solution)/shard_map/ppermute | solution.py:259
  59.6 11.0 %collective-permute-start.3 = (f32[2,2,16,512]{3,2,1,0:T(8,128)S(1)}, f32[2,2,16,512]{3,2,1,0:T(8,128)S(1)}, u32[]{:S(2)}, u32[]{:S(2)}) collective-permute-start(f32[2,2,16,512]{3,2,1,0:T(8,128)S(1)} %get-tuple-element.25), channel_id=1, source_target_pairs={{0,3},{1,2},{2,1},{3,0},{4,7},{5,6},{6,5},{7,4},{8,11},{9,10},{10,... | collective-permute-start | bytes 393224 | tf_op jit(solution)/shard_map/ppermute | solution.py:259
  62.5 8.2 %collective-permute-start.4 = (f32[2,2,16,512]{3,2,1,0:T(8,128)S(1)}, f32[2,2,16,512]{3,2,1,0:T(8,128)S(1)}, u32[]{:S(2)}, u32[]{:S(2)}) collective-permute-start(f32[2,2,16,512]{3,2,1,0:T(8,128)S(1)} %get-tuple-element.26), channel_id=1, source_target_pairs={{0,4},{1,5},{2,6},{3,7},{4,0},{5,1},{6,2},{7,3},{8,12},{9,13},{10,... | collective-permute-start | bytes 393224 | tf_op jit(solution)/shard_map/ppermute | solution.py:259
  65.9 5.8 %collective-permute-start.5 = (f32[2,2,16,512]{3,2,1,0:T(8,128)S(1)}, f32[2,2,16,512]{3,2,1,0:T(8,128)S(1)}, u32[]{:S(2)}, u32[]{:S(2)}) collective-permute-start(f32[2,2,16,512]{3,2,1,0:T(8,128)S(1)} %get-tuple-element.27), channel_id=1, source_target_pairs={{0,5},{1,4},{2,7},{3,6},{4,1},{5,0},{6,3},{7,2},{8,13},{9,12},{10,... | collective-permute-start | bytes 393224 | tf_op jit(solution)/shard_map/ppermute | solution.py:259
  66.1 8.0 %collective-permute-start.6 = (f32[2,2,16,512]{3,2,1,0:T(8,128)S(1)}, f32[2,2,16,512]{3,2,1,0:T(8,128)S(1)}, u32[]{:S(2)}, u32[]{:S(2)}) collective-permute-start(f32[2,2,16,512]{3,2,1,0:T(8,128)S(1)} %get-tuple-element.28), channel_id=1, source_target_pairs={{0,6},{1,7},{2,4},{3,5},{4,2},{5,3},{6,0},{7,1},{8,14},{9,15},{10,... | collective-permute-start | bytes 393224 | tf_op jit(solution)/shard_map/ppermute | solution.py:259
  68.6 8.5 %collective-permute-start.7 = (f32[2,2,16,512]{3,2,1,0:T(8,128)S(1)}, f32[2,2,16,512]{3,2,1,0:T(8,128)S(1)}, u32[]{:S(2)}, u32[]{:S(2)}) collective-permute-start(f32[2,2,16,512]{3,2,1,0:T(8,128)S(1)} %get-tuple-element.29), channel_id=1, source_target_pairs={{0,7},{1,6},{2,5},{3,4},{4,3},{5,2},{6,1},{7,0},{8,15},{9,14},{10,... | collective-permute-start | bytes 393224 | tf_op jit(solution)/shard_map/ppermute | solution.py:259

commit v4 on v3

--- a/solution.py
+++ b/solution.py
@@ -17,7 +17,9 @@
 SUBS = 8
 INNER = 256
 PAD = 4
-SPLITS = (2, 2)
+FINE = 16
+ORDER = (7, 6, 5, 4, 3, 2, 1)
+SPLITS = (4,)
 GROUP = 8
 
 
@@ -50,23 +52,25 @@
     return np.stack([high, low])
 
 
-def matmul_tables(plan):
+def outer_tables(plan):
     angle = np.arange(plan.n1)[:, None] * np.arange(plan.k1)[None, :] % plan.k1
     angle = angle * (2.0 * np.pi / plan.k1)
-    cos, sin = np.cos(angle), np.sin(angle)
-    parts = [cos, sin, -sin, cos]
+    return split_bf16(np.concatenate([np.cos(angle), np.sin(angle)]))
+
+
+def inner_tables(plan):
     angle = np.arange(INNER)[:, None] * np.arange(INNER)[None, :] % INNER
     angle = angle * (2.0 * np.pi / INNER)
-    cos, sin = np.cos(angle), np.sin(angle)
-    for q in range(plan.n_col):
-        part = slice(q * plan.k2_dev, (q + 1) * plan.k2_dev)
-        parts.append(np.block([[cos[part], sin[part]], [-sin[part], cos[part]]]))
-    return split_bf16(np.concatenate(parts))
+    table = np.concatenate([np.cos(angle), np.sin(angle)], axis=1)
+    return split_bf16(table.reshape(plan.n_col, plan.k2_dev, 2 * INNER))
 
 
 def twist_tables(plan):
-    angle = np.arange(INNER)[:, None] * np.arange(plan.k1)[None, :] * (2.0 * np.pi / plan.n_pad)
-    return np.stack([np.cos(angle), np.sin(angle)]).astype(np.float32)
+    made = []
+    for cells in (np.arange(0, INNER, FINE), np.arange(FINE)):
+        angle = cells[:, None] * np.arange(plan.k1)[None, :] * (2.0 * np.pi / plan.n_pad)
+        made.extend([np.cos(angle), np.sin(angle)])
+    return np.concatenate(made).astype(np.float32)
 
 
 def field_kernel(plan, row_ref, tiles_ref, *refs):
@@ -123,7 +127,7 @@
             out_ref[g, dest, plan.chunk :, :] = open_ref[...]
 
 
-def transform_kernel(plan, first, rows, with_count, me_ref, x_ref, table_ref, twist_ref, *refs):
+def transform_kernel(plan, first, rows, with_count, me_ref, x_ref, outer_ref, inner_ref, twist_ref, *refs):
     chunk_row = plan.chunk // plan.rows
     me = me_ref[0]
 
@@ -135,14 +139,27 @@
 
     if with_count:
         refs[plan.group][...] = jnp.sum(x_ref[:, plan.chunk :, :], axis=0)
-    side = 2 * plan.n1
-    size = 2 * plan.k2_dev
-    w1 = [jnp.concatenate([table_ref[s, :side], table_ref[s, side : 2 * side]], axis=1) for s in range(2)]
-    w2 = []
+    n1, k2_dev = plan.n1, plan.k2_dev
+    w1, w2 = [], []
     for s in range(2):
-        starts = [pl.multiple_of(2 * side + (me ^ b) * size, size) for b in range(plan.group)]
-        w2.append(jnp.concatenate([table_ref[s, pl.ds(start, size)] for start in starts], axis=0))
-    tc, ts = twist_ref[0], twist_ref[1]
+        cos, sin = outer_ref[s, :n1], outer_ref[s, n1:]
+        w1.append(jnp.concatenate([jnp.concatenate([cos, sin]), jnp.concatenate([-sin, cos])], axis=1))
+        blocks = []
+        for b in range(plan.group):
+            both = inner_ref[s, me ^ b]
+            cos, sin = both[:, :INNER], both[:, INNER:]
+            blocks.append(both)
+            blocks.append(jnp.concatenate([-sin, cos], axis=1))
+        w2.append(jnp.concatenate(blocks))
+    size = 2 * k2_dev
+    count = INNER // FINE
+    fine_cos, fine_sin = twist_ref[2 * count : 2 * count + FINE], twist_ref[2 * count + FINE :]
+    tc, ts = [], []
+    for a in range(count):
+        cos, sin = twist_ref[a : a + 1], twist_ref[count + a : count + a + 1]
+        tc.append(cos * fine_cos - sin * fine_sin)
+        ts.append(sin * fine_cos + cos * fine_sin)
+    tc, ts = jnp.concatenate(tc), jnp.concatenate(ts)
     for r in range(rows):
         halves = []
         for part in range(2):
@@ -166,7 +183,10 @@
 
 def merge_kernel(plan, splits, me_ref, *refs):
     n = len(splits)
-    chunks = [refs[i * plan.group : (i + 1) * plan.group] for i in range(n)]
+    chunks = []
+    for i in range(n):
+        given = refs[i * plan.group : (i + 1) * plan.group]
+        chunks.append([given[(ORDER + (0,)).index(b)] for b in range(plan.group)])
     counts = refs[n * plan.group : n * plan.group + plan.n_row]
     out_ref, tile_ref, row_ref, sems = refs[n * plan.group + plan.n_row :]
     total = counts[0][...]
@@ -237,7 +257,7 @@
     packed = packed.reshape(n_col, plan.chunk + SUBS, LANES)
     received = lax.all_to_all(packed, "col", split_axis=0, concat_axis=0, tiled=True)
 
-    table, twist = matmul_tables(plan), twist_tables(plan)
+    tables = [outer_tables(plan), inner_tables(plan), twist_tables(plan)]
     splits = SPLITS if sum(SPLITS) == plan.rows else (plan.rows,)
     chunks = []
     for i, rows in enumerate(splits):
@@ -247,17 +267,15 @@
         made = pl.pallas_call(
             partial(transform_kernel, plan, sum(splits[:i]), rows, i == 0),
             out_shape=shapes,
-            in_specs=[smem, vmem, vmem, vmem],
+            in_specs=[smem, vmem, vmem, vmem, vmem],
             out_specs=[vmem] * len(shapes),
             compiler_params=pltpu.CompilerParams(vmem_limit_bytes=24 * 2**20),
             name="transform",
-        )(me, received, table, twist)
+        )(me, received, *tables)
+        sent = {b: lax.ppermute(made[b], "col", [(q, q ^ b) for q in range(n_col)]) for b in ORDER}
         if i == 0:
             counts = [made[-1]] + along_rows(made[-1])
-        chunks.append(
-            [made[0]]
-            + [lax.ppermute(made[b], "col", [(q, q ^ b) for q in range(n_col)]) for b in range(1, plan.group)]
-        )
+        chunks.append([sent[b] for b in ORDER] + [made[0]])
 
     slots = plan.group
     return pl.pallas_call(

time: 79.7 us -> 74.5 us (0.935)
  starting transfers between devices: 24.9 us -> 19.5 us
  waiting for transfers between devices: 42.8 us -> 44.5 us
  local copies, waits for them, and re-layouts: 1.77 us -> 0.59 us
    ppermute x14 -> x7, starting transfers between devices: 14 us -> 8.41 us  [per_device(): lax.ppermute(made[b], 'col', [(q, q ^ b) for q in range(n_col)])]
    ppermute x14 -> x7, waiting for transfers between devices: 15 us -> 18.4 us  [per_device(): lax.ppermute(made[b], 'col', [(q, q ^ b) for q in range(n_col)])]
    ppermute x2, waiting for transfers between devices: 3.84 us -> 2.07 us  [along_rows(): lax.ppermute(value, 'row', [(i, (i + d) % n_row) for i in range(n_row)])]
    unnamed x6 -> x8, local copies, waits for them, and re-layouts: 1.77 us -> 0.59 us
    pallas_call x2 -> x1, Pallas kernels: 4.54 us -> 4.29 us  [per_device(): pl.pallas_call(partial(transform_kernel, plan, sum(splits[:i]), rows, i =...]
  transfers between devices with their start and end apart: 17 -> 10, of which waited for: 11 -> 8; matrix products, arithmetic and copies ran while one was open for 0% -> 0% of each run, Pallas kernels for 3% -> 0%
where the time goes in v4:
time: 74.5 us; the launch traced here: 74.3 us
  waiting for transfers between devices  44.5 us (60%)
  starting transfers between devices  19.5 us (26%)
  Pallas kernels  9.65 us (13%)
    all_to_all x1, waiting for transfers between devices, per_device(): lax.all_to_all(packed, 'col', split_axis=0, concat_axis=0, tiled=True)  24 us
    ppermute x7, waiting for transfers between devices, per_device(): lax.ppermute(made[b], 'col', [(q, q ^ b) for q in range(n_col)])  18.4 us
    ppermute x7, starting transfers between devices, per_device(): lax.ppermute(made[b], 'col', [(q, q ^ b) for q in range(n_col)])  8.41 us
    all_to_all x1, starting transfers between devices, per_device(): lax.all_to_all(packed, 'col', split_axis=0, concat_axis=0, tiled=True)  6.56 us
    ppermute x2, starting transfers between devices, along_rows(): lax.ppermute(value, 'row', [(i, (i + d) % n_row) for i in range(n_row)])  4.48 us
    pallas_call x1, Pallas kernels, per_device(): pl.pallas_call(partial(transform_kernel, plan, sum(splits[:i]), rows, i =...  4.29 us
    pallas_call x1, Pallas kernels, per_device(): pl.pallas_call(partial(field_kernel, plan), out_shape=jax.ShapeDtypeStruc...  2.96 us
    pallas_call x1, Pallas kernels, per_device(): pl.pallas_call(partial(merge_kernel, plan, splits), out_shape=jax.ShapeDt...  2.4 us
  transfers between devices with their start and end apart: 10, of which 8 were waited for; matrix products, arithmetic and copies ran while one was open for 0% of the time, Pallas kernels for 0%

profile of v4, /device:TPU:0, one launch (start us, length us, event | category | flops | bytes accessed | tf_op | source)
XLA Modules:
  0.0 74.3 jit_solution(11978015715244315045)
XLA Ops:
  0.0 3.0 %collective-permute-start = (s32[2,4]{1,0:T(2,128)}, s32[2,4]{1,0:T(2,128)S(1)}, u32[]{:S(2)}, u32[]{:S(2)}) collective-permute-start(s32[2,4]{1,0:T(2,128)} %tiles_ref.1), channel_id=1, source_target_pairs={{0,16},{16,0},{1,17},{17,1},{2,18},{18,2},{3,19},{19,3},{4,20},{20... | collective-permute-start | bytes 104 | tf_op jit(solution)/shard_map/ppermute | solution.py:235
  3.0 1.8 %collective-permute-done.refs_0_ = s32[2,4]{1,0:T(2,128)S(1)} collective-permute-done((s32[2,4]{1,0:T(2,128)}, s32[2,4]{1,0:T(2,128)S(1)}, u32[]{:S(2)}, u32[]{:S(2)}) %collective-permute-start) | collective-permute-done | bytes 64 | tf_op jit(solution)/shard_map/ppermute | solution.py:235
  4.7 0.0 copy-start.3
  4.7 0.6 copy-done.3
  5.3 3.0 %field.1 = f32[2,8,136,128]{3,2,1,0:T(8,128)} custom-call(s32[1]{0:T(128)} %bitcast.1.row_ref, s32[2,4]{1,0:T(2,128)} %tiles_ref.1, s32[2,4]{1,0:T(2,128)} %copy-done.3, s32[32,2048]{1,0:T(8,128)} %refs_1_.1, s32[32,2048]{1,0:T(8,128)} %refs_3_.1, s32[32,2048]{1,0:T(8,128)} %refs_3_.1), custom_call_target="tpu_custom_call" | custom-call | tf_op jit(solution)/shard_map/field/pallas_call | solution.py:242
  8.3 0.0 copy-start
  8.3 0.0 copy-start.1
  8.3 0.0 copy-start.2
  8.3 6.6 %all-to-all-start = ((f32[16,136,128]{2,1,0:T(8,128)}), f32[16,136,128]{2,1,0:T(8,128)S(1)}, u32[]{:S(2)}, u32[]{:S(2)}) async-start(f32[16,136,128]{2,1,0:T(8,128)} %bitcast.3), calls=%async_computation | async-start | bytes 2228224 | tf_op jit(solution)/shard_map/all_to_all | solution.py:258
  14.8 24.0 %all-to-all-done.x_ref = f32[16,136,128]{2,1,0:T(8,128)S(1)} async-done(((f32[16,136,128]{2,1,0:T(8,128)}), f32[16,136,128]{2,1,0:T(8,128)S(1)}, u32[]{:S(2)}, u32[]{:S(2)}) %all-to-all-start) | async-done | bytes 1114144 | tf_op jit(solution)/shard_map/all_to_all | solution.py:258
  38.9 0.0 copy-done
  38.9 0.0 copy-done.1
  38.9 0.0 copy-done.2
  38.9 4.3 %transform.1 = (f32[4,2,16,512]{3,2,1,0:T(8,128)S(1)}, f32[4,2,16,512]{3,2,1,0:T(8,128)S(1)}, f32[4,2,16,512]{3,2,1,0:T(8,128)S(1)}, f32[4,2,16,512]{3,2,1,0:T(8...) custom-call(s32[1]{0:T(128)} %bitcast.me_ref, ...), custom_call_target="tpu_custom_call" | custom-call | tf_op jit(solution)/shard_map/transform/pallas_call | solution.py:267
  43.2 5.0 %collective-permute-start.1 = (f32[4,2,16,512]{3,2,1,0:T(8,128)S(1)}, f32[4,2,16,512]{3,2,1,0:T(8,128)S(1)}, u32[]{:S(2)}, u32[]{:S(2)}) collective-permute-start(f32[4,2,16,512]{3,2,1,0:T(8,128)S(1)} %get-tuple-element.14), channel_id=1, source_target_pairs={{0,7},{1,6},{2,5},{3,4},{4,3},{5,2},{6,1},{7,0},{8,15},{9,14},{10,... | collective-permute-start | bytes 786440 | tf_op jit(solution)/shard_map/ppermute | solution.py:275
  48.2 0.2 collective-permute-start.2
  48.3 1.5 %collective-permute-start.8 = (f32[8,128]{1,0:T(8,128)S(1)}, f32[8,128]{1,0:T(8,128)S(1)}, u32[]{:S(2)}, u32[]{:S(2)}) collective-permute-start(f32[8,128]{1,0:T(8,128)S(1)} %get-tuple-element.22.refs_8_), channel_id=1, source_target_pairs={{0,16},{16,0},{1,17},{17,1},{2,18},{18,2},{3,19},{19,3},{4,20},{20... | collective-permute-start | bytes 12296 | tf_op jit(solution)/shard_map/ppermute | solution.py:235
  49.8 0.5 collective-permute-start.3
  50.4 1.3 %collective-permute-start.4 = (f32[4,2,16,512]{3,2,1,0:T(8,128)S(1)}, f32[4,2,16,512]{3,2,1,0:T(8,128)S(1)}, u32[]{:S(2)}, u32[]{:S(2)}) collective-permute-start(f32[4,2,16,512]{3,2,1,0:T(8,128)S(1)} %get-tuple-element.17), channel_id=1, source_target_pairs={{0,4},{1,5},{2,6},{3,7},{4,0},{5,1},{6,2},{7,3},{8,12},{9,13},{10,... | collective-permute-start | bytes 786440 | tf_op jit(solution)/shard_map/ppermute | solution.py:275
  51.6 0.3 collective-permute-done.8.refs_9_
  51.9 1.0 %collective-permute-start.5 = (f32[4,2,16,512]{3,2,1,0:T(8,128)S(1)}, f32[4,2,16,512]{3,2,1,0:T(8,128)S(1)}, u32[]{:S(2)}, u32[]{:S(2)}) collective-permute-start(f32[4,2,16,512]{3,2,1,0:T(8,128)S(1)} %get-tuple-element.18), channel_id=1, source_target_pairs={{0,3},{1,2},{2,1},{3,0},{4,7},{5,6},{6,5},{7,4},{8,11},{9,10},{10,... | collective-permute-start | bytes 786440 | tf_op jit(solution)/shard_map/ppermute | solution.py:275
  52.9 1.9 %collective-permute-done.1.refs_0_ = f32[4,2,16,512]{3,2,1,0:T(8,128)S(1)} collective-permute-done((f32[4,2,16,512]{3,2,1,0:T(8,128)S(1)}, f32[4,2,16,512]{3,2,1,0:T(8,128)S(1)}, u32[]{:S(2)}, u32[]{:S(2)}) %collective-permute-start.1) | collective-permute-done | bytes 262176 | tf_op jit(solution)/shard_map/ppermute | solution.py:275
  54.8 0.5 collective-permute-start.6
  55.3 5.7 %collective-permute-done.2.refs_1_ = f32[4,2,16,512]{3,2,1,0:T(8,128)S(1)} collective-permute-done((f32[4,2,16,512]{3,2,1,0:T(8,128)S(1)}, f32[4,2,16,512]{3,2,1,0:T(8,128)S(1)}, u32[]{:S(2)}, u32[]{:S(2)}) %collective-permute-start.2) | collective-permute-done | bytes 262176 | tf_op jit(solution)/shard_map/ppermute | solution.py:275
  61.0 0.0 collective-permute-start.7
  61.0 5.1 %collective-permute-done.3.refs_2_ = f32[4,2,16,512]{3,2,1,0:T(8,128)S(1)} collective-permute-done((f32[4,2,16,512]{3,2,1,0:T(8,128)S(1)}, f32[4,2,16,512]{3,2,1,0:T(8,128)S(1)}, u32[]{:S(2)}, u32[]{:S(2)}) %collective-permute-start.3) | collective-permute-done | bytes 262176 | tf_op jit(solution)/shard_map/ppermute | solution.py:275
  66.1 5.2 %collective-permute-done.4.refs_3_ = f32[4,2,16,512]{3,2,1,0:T(8,128)S(1)} collective-permute-done((f32[4,2,16,512]{3,2,1,0:T(8,128)S(1)}, f32[4,2,16,512]{3,2,1,0:T(8,128)S(1)}, u32[]{:S(2)}, u32[]{:S(2)}) %collective-permute-start.4) | collective-permute-done | bytes 262176 | tf_op jit(solution)/shard_map/ppermute | solution.py:275
  71.3 0.0 collective-permute-done.5.refs_4_
  71.3 0.6 collective-permute-done.6.refs_5_
  71.9 0.0 collective-permute-done.7.refs_6_
  71.9 2.4 %merge.1 = f32[2,32,8192]{2,1,0:T(8,128)} custom-call(s32[1]{0:T(128)} %bitcast.me_ref, f32[4,2,16,512]{3,2,1,0:T(8,128)S(1)} %collective-permute-done.1.refs_0_, f32[4,2,16,512]{3,2,1,0:T(8,128)S(1)} %collective-permute-done.2.refs_1_, f32[4,2,16,512]{3,2,1,0:T(8,128)S(1)} %collective-permute-done.3.refs_2_, ...), custom_call_target="tpu_custom_call" | custom-call | tf_op jit(solution)/shard_map/merge/pallas_call | solution.py:281
Async XLA Ops:
  0.0 4.7 %collective-permute-start = (s32[2,4]{1,0:T(2,128)}, s32[2,4]{1,0:T(2,128)S(1)}, u32[]{:S(2)}, u32[]{:S(2)}) collective-permute-start(s32[2,4]{1,0:T(2,128)} %tiles_ref.1), channel_id=1, source_target_pairs={{0,16},{16,0},{1,17},{17,1},{2,18},{18,2},{3,19},{19,3},{4,20},{20... | collective-permute-start | bytes 104 | tf_op jit(solution)/shard_map/ppermute | solution.py:235
  4.7 0.6 copy-start.3
  8.3 30.6 %copy-start = (bf16[2,16,16,512]{3,2,1,0:T(8,128)(2,1)S(1)}, bf16[2,16,16,512]{3,2,1,0:T(8,128)(2,1)}, u32[]{:S(2)}) copy-start(bf16[2,16,16,512]{3,2,1,0:T(8,128)(2,1)} %constant.16.clone.inner_ref) | copy-start | bytes 1572868
  8.3 30.6 %copy-start.1 = (bf16[2,256,512]{2,1,0:T(8,128)(2,1)S(1)}, bf16[2,256,512]{2,1,0:T(8,128)(2,1)}, u32[]{:S(2)}) copy-start(bf16[2,256,512]{2,1,0:T(8,128)(2,1)} %constant.15.clone.outer_ref) | copy-start | bytes 1572868
  8.3 30.6 %copy-start.2 = (f32[64,512]{1,0:T(8,128)S(1)}, f32[64,512]{1,0:T(8,128)}, u32[]{:S(2)}) copy-start(f32[64,512]{1,0:T(8,128)} %constant.17.clone.twist_ref) | copy-start | bytes 393220
  8.3 30.6 %all-to-all-start = ((f32[16,136,128]{2,1,0:T(8,128)}), f32[16,136,128]{2,1,0:T(8,128)S(1)}, u32[]{:S(2)}, u32[]{:S(2)}) async-start(f32[16,136,128]{2,1,0:T(8,128)} %bitcast.3), calls=%async_computation | async-start | bytes 2228224 | tf_op jit(solution)/shard_map/all_to_all | solution.py:258
  43.2 11.6 %collective-permute-start.1 = (f32[4,2,16,512]{3,2,1,0:T(8,128)S(1)}, f32[4,2,16,512]{3,2,1,0:T(8,128)S(1)}, u32[]{:S(2)}, u32[]{:S(2)}) collective-permute-start(f32[4,2,16,512]{3,2,1,0:T(8,128)S(1)} %get-tuple-element.14), channel_id=1, source_target_pairs={{0,7},{1,6},{2,5},{3,4},{4,3},{5,2},{6,1},{7,0},{8,15},{9,14},{10,... | collective-permute-start | bytes 786440 | tf_op jit(solution)/shard_map/ppermute | solution.py:275
  48.2 12.8 %collective-permute-start.2 = (f32[4,2,16,512]{3,2,1,0:T(8,128)S(1)}, f32[4,2,16,512]{3,2,1,0:T(8,128)S(1)}, u32[]{:S(2)}, u32[]{:S(2)}) collective-permute-start(f32[4,2,16,512]{3,2,1,0:T(8,128)S(1)} %get-tuple-element.15), channel_id=1, source_target_pairs={{0,6},{1,7},{2,4},{3,5},{4,2},{5,3},{6,0},{7,1},{8,14},{9,15},{10,... | collective-permute-start | bytes 786440 | tf_op jit(solution)/shard_map/ppermute | solution.py:275
  48.3 3.6 %collective-permute-start.8 = (f32[8,128]{1,0:T(8,128)S(1)}, f32[8,128]{1,0:T(8,128)S(1)}, u32[]{:S(2)}, u32[]{:S(2)}) collective-permute-start(f32[8,128]{1,0:T(8,128)S(1)} %get-tuple-element.22.refs_8_), channel_id=1, source_target_pairs={{0,16},{16,0},{1,17},{17,1},{2,18},{18,2},{3,19},{19,3},{4,20},{20... | collective-permute-start | bytes 12296 | tf_op jit(solution)/shard_map/ppermute | solution.py:235
  49.8 16.2 %collective-permute-start.3 = (f32[4,2,16,512]{3,2,1,0:T(8,128)S(1)}, f32[4,2,16,512]{3,2,1,0:T(8,128)S(1)}, u32[]{:S(2)}, u32[]{:S(2)}) collective-permute-start(f32[4,2,16,512]{3,2,1,0:T(8,128)S(1)} %get-tuple-element.16), channel_id=1, source_target_pairs={{0,5},{1,4},{2,7},{3,6},{4,1},{5,0},{6,3},{7,2},{8,13},{9,12},{10,... | collective-permute-start | bytes 786440 | tf_op jit(solution)/shard_map/ppermute | solution.py:275
  50.4 20.9 %collective-permute-start.4 = (f32[4,2,16,512]{3,2,1,0:T(8,128)S(1)}, f32[4,2,16,512]{3,2,1,0:T(8,128)S(1)}, u32[]{:S(2)}, u32[]{:S(2)}) collective-permute-start(f32[4,2,16,512]{3,2,1,0:T(8,128)S(1)} %get-tuple-element.17), channel_id=1, source_target_pairs={{0,4},{1,5},{2,6},{3,7},{4,0},{5,1},{6,2},{7,3},{8,12},{9,13},{10,... | collective-permute-start | bytes 786440 | tf_op jit(solution)/shard_map/ppermute | solution.py:275
  51.9 19.4 %collective-permute-start.5 = (f32[4,2,16,512]{3,2,1,0:T(8,128)S(1)}, f32[4,2,16,512]{3,2,1,0:T(8,128)S(1)}, u32[]{:S(2)}, u32[]{:S(2)}) collective-permute-start(f32[4,2,16,512]{3,2,1,0:T(8,128)S(1)} %get-tuple-element.18), channel_id=1, source_target_pairs={{0,3},{1,2},{2,1},{3,0},{4,7},{5,6},{6,5},{7,4},{8,11},{9,10},{10,... | collective-permute-start | bytes 786440 | tf_op jit(solution)/shard_map/ppermute | solution.py:275
  54.8 17.1 %collective-permute-start.6 = (f32[4,2,16,512]{3,2,1,0:T(8,128)S(1)}, f32[4,2,16,512]{3,2,1,0:T(8,128)S(1)}, u32[]{:S(2)}, u32[]{:S(2)}) collective-permute-start(f32[4,2,16,512]{3,2,1,0:T(8,128)S(1)} %get-tuple-element.19), channel_id=1, source_target_pairs={{0,2},{1,3},{2,0},{3,1},{4,6},{5,7},{6,4},{7,5},{8,10},{9,11},{10,... | collective-permute-start | bytes 786440 | tf_op jit(solution)/shard_map/ppermute | solution.py:275
  61.0 10.9 %collective-permute-start.7 = (f32[4,2,16,512]{3,2,1,0:T(8,128)S(1)}, f32[4,2,16,512]{3,2,1,0:T(8,128)S(1)}, u32[]{:S(2)}, u32[]{:S(2)}) collective-permute-start(f32[4,2,16,512]{3,2,1,0:T(8,128)S(1)} %get-tuple-element.20), channel_id=1, source_target_pairs={{0,1},{1,0},{2,3},{3,2},{4,5},{5,4},{6,7},{7,6},{8,9},{9,8},{10,11... | collective-permute-start | bytes 786440 | tf_op jit(solution)/shard_map/ppermute | solution.py:275

commit v5 on v4

--- a/solution.py
+++ b/solution.py
@@ -73,61 +73,53 @@
     return np.concatenate(made).astype(np.float32)
 
 
-def field_kernel(plan, row_ref, tiles_ref, *refs):
-    others, (codes_ref, mask_ref, all_mask_ref, out_ref, open_ref) = refs[: plan.n_row - 1], refs[plan.n_row - 1 :]
+def unit_phase(code):
+    quadrant = (code + LEVELS // 8) >> 10
+    rest = (code - (quadrant << 10)).astype(jnp.float32) * (2.0 * math.pi / LEVELS)
+    sq = rest * rest
+    cos = 1.0 + sq * (-1.0 / 2 + sq * (1.0 / 24 + sq * (-1.0 / 720 + sq * (1.0 / 40320))))
+    sin = rest * (1.0 + sq * (-1.0 / 6 + sq * (1.0 / 120 + sq * (-1.0 / 5040 + sq * (1.0 / 362880)))))
+    swap = (quadrant & 1) == 1
+    minus_cos = ((quadrant + 1) & 2) == 2
+    minus_sin = (quadrant & 2) == 2
+    return jnp.where(swap, sin, cos), jnp.where(swap, cos, sin), minus_cos, minus_sin
+
+
+def field_kernel(plan, tiles_ref, codes_ref, mask_ref, out_ref, open_ref):
     step_id = pl.program_id(0)
-    tile_cols = plan.pupil_dev // TILE_C
-
-    @pl.when(step_id == 0)
-    def _():
-        total = jnp.zeros((SUBS, LANES), jnp.int32)
-        for t in range(plan.row_dev // SUBS):
-            for j in range(plan.pupil_dev // LANES):
-                total = total + all_mask_ref[t * SUBS : (t + 1) * SUBS, j * LANES : (j + 1) * LANES]
-        open_ref[...] = total.astype(jnp.float32)
-
     pistons = []
-    for i in range(tile_cols):
+    for i in range(plan.pupil_dev // TILE_C):
         piston = jnp.int32(0)
-        for d, other in enumerate(others):
-            column = other[0, i]
-            for k in range(1, plan.row_dev // TILE_R):
-                column = column + other[k, i]
-            piston = piston + jnp.where(row_ref[0] > d, column, 0)
         for k in range(plan.row_dev // TILE_R):
             piston = piston + jnp.where(step_id >= k, tiles_ref[k, i], 0)
         pistons.append(piston)
-    take = min(plan.rows, SUBS)
     stride = 2 * plan.lane_parts * plan.n1_dev
+    total = jnp.zeros((SUBS, LANES), jnp.float32)
     for t in range(TILE_R // SUBS):
         for j in range(plan.pupil_dev // LANES):
             rows = slice(t * SUBS, (t + 1) * SUBS)
             lanes = slice(j * LANES, (j + 1) * LANES)
             code = (codes_ref[rows, lanes] + pistons[j * LANES // TILE_C]) & (LEVELS - 1)
-            quadrant = (code + LEVELS // 8) >> 10
-            rest = (code - (quadrant << 10)).astype(jnp.float32) * (2.0 * math.pi / LEVELS)
-            sq = rest * rest
-            cos = 1.0 + sq * (-1.0 / 2 + sq * (1.0 / 24 + sq * (-1.0 / 720 + sq * (1.0 / 40320))))
-            sin = rest * (1.0 + sq * (-1.0 / 6 + sq * (1.0 / 120 + sq * (-1.0 / 5040 + sq * (1.0 / 362880)))))
+            cos, sin, minus_cos, minus_sin = unit_phase(code)
             amplitude = mask_ref[rows, lanes].astype(jnp.float32)
-            swap = (quadrant & 1) == 1
-            real = jnp.where(swap, sin, cos) * jnp.where(((quadrant + 1) & 2) == 2, -amplitude, amplitude)
-            imag = jnp.where(swap, cos, sin) * jnp.where((quadrant & 2) == 2, -amplitude, amplitude)
+            total = total + amplitude
+            real = cos * jnp.where(minus_cos, -amplitude, amplitude)
+            imag = sin * jnp.where(minus_sin, -amplitude, amplitude)
             for part, value in enumerate((real, imag)):
                 start = (part * plan.lane_parts + j % plan.lane_parts) * plan.n1_dev + j // plan.lane_parts
-                for d in range(SUBS // take):
-                    row = t * SUBS + d * take
-                    dest, first = row // plan.rows, row % plan.rows
-                    for g in range(plan.n_groups):
-                        out_ref[g, dest, pl.ds(first * stride + start, take, stride=stride), :] = value[
-                            d * take : (d + 1) * take
-                        ]
-    for g in range(plan.n_groups):
-        for dest in range(TILE_R // plan.rows):
-            out_ref[g, dest, plan.chunk :, :] = open_ref[...]
-
-
-def transform_kernel(plan, first, rows, with_count, me_ref, x_ref, outer_ref, inner_ref, twist_ref, *refs):
+                for g in range(plan.n_groups):
+                    out_ref[g, pl.ds(t * SUBS * stride + start, SUBS, stride=stride), :] = value
+
+    @pl.when(step_id == 0)
+    def _():
+        open_ref[...] = total
+
+    @pl.when(step_id > 0)
+    def _():
+        open_ref[...] = open_ref[...] + total
+
+
+def transform_kernel(plan, first, rows, me_ref, info_ref, x_ref, outer_ref, inner_ref, twist_ref, *refs):
     chunk_row = plan.chunk // plan.rows
     me = me_ref[0]
 
@@ -137,8 +129,14 @@
     def inner(a, b):
         return jnp.dot(a, b, preferred_element_type=jnp.float32)
 
-    if with_count:
-        refs[plan.group][...] = jnp.sum(x_ref[:, plan.chunk :, :], axis=0)
+    info = info_ref[: plan.n_col]
+    info = jnp.broadcast_to(info[:, None, :], (plan.n_col, plan.n1_dev, LANES)).reshape(plan.n1, LANES)
+    tile = lax.broadcasted_iota(jnp.int32, info.shape, 0) % plan.n1_dev * INNER // TILE_C
+    own = lax.broadcasted_iota(jnp.int32, info.shape, 1) == tile
+    before = jnp.sum(jnp.where(own, info, 0.0), axis=1, keepdims=True).astype(jnp.int32)
+    turn_cos, turn_sin, minus_cos, minus_sin = unit_phase(before)
+    turn_cos = jnp.where(minus_cos, -turn_cos, turn_cos)
+    turn_sin = jnp.where(minus_sin, -turn_sin, turn_sin)
     n1, k2_dev = plan.n1, plan.k2_dev
     w1, w2 = [], []
     for s in range(2):
@@ -168,7 +166,8 @@
                 at = (first + r) * chunk_row + (part * plan.lane_parts + lt) * plan.n1_dev
                 pieces.append(x_ref[:, at : at + plan.n1_dev, :].reshape(plan.n1, LANES))
             halves.append(jnp.concatenate(pieces, axis=1))
-        x = jnp.concatenate(halves, axis=0)
+        real, imag = halves
+        x = jnp.concatenate([real * turn_cos - imag * turn_sin, real * turn_sin + imag * turn_cos], axis=0)
         xh = x.astype(jnp.bfloat16)
         xl = (x - xh.astype(jnp.float32)).astype(jnp.bfloat16)
         y = outer(xh, w1[0]) + outer(xl, w1[0]) + outer(xh, w1[1])
@@ -227,54 +226,64 @@
     n_col = lax.axis_size("col")
     n_row = lax.axis_size("row")
     plan = Plan(*phase_codes.shape, n_col, n_row)
-    row_index = lax.axis_index("row").astype(jnp.int32).reshape(1)
-    col_index = lax.axis_index("col").astype(jnp.int32).reshape(1)
-    me = col_index
+    row_index = lax.axis_index("row")
+    col_index = lax.axis_index("col")
+    me = col_index.astype(jnp.int32).reshape(1)
 
     def along_rows(value):
         return [lax.ppermute(value, "row", [(i, (i + d) % n_row) for i in range(n_row)]) for d in range(1, n_row)]
 
     smem = pl.BlockSpec(memory_space=pltpu.SMEM)
     vmem = pl.BlockSpec(memory_space=pltpu.VMEM)
-    others = along_rows(tile_offsets)
+    before = jnp.zeros((1, plan.pupil_dev // TILE_C), jnp.int32)
+    for d, other in enumerate(along_rows(tile_offsets)):
+        before = before + jnp.where(row_index > d, jnp.sum(other, axis=0, keepdims=True), 0)
+    before = jnp.pad((before & (LEVELS - 1)).astype(jnp.float32), ((0, 0), (0, LANES - before.shape[1])))
+    mine = jnp.arange(n_col, dtype=jnp.int32)[:, None] == col_index
+
+    field_rows = plan.row_dev * 2 * plan.lane_parts * plan.n1_dev
     steps = plan.row_dev // TILE_R
-    block = (plan.n_groups, plan.group // steps, plan.chunk + SUBS, LANES)
-    packed = pl.pallas_call(
+    packed, opened = pl.pallas_call(
         partial(field_kernel, plan),
-        out_shape=jax.ShapeDtypeStruct((plan.n_groups, plan.group, plan.chunk + SUBS, LANES), jnp.float32),
+        out_shape=[
+            jax.ShapeDtypeStruct((plan.n_groups, field_rows, LANES), jnp.float32),
+            jax.ShapeDtypeStruct((SUBS, LANES), jnp.float32),
+        ],
         grid=(steps,),
-        in_specs=[smem, smem]
-        + [smem] * (n_row - 1)
-        + [
+        in_specs=[
+            smem,
             pl.BlockSpec((TILE_R, plan.pupil_dev), lambda t: (t, 0)),
             pl.BlockSpec((TILE_R, plan.pupil_dev), lambda t: (t, 0)),
-            pl.BlockSpec((plan.row_dev, plan.pupil_dev), lambda t: (0, 0)),
         ],
-        out_specs=pl.BlockSpec(block, lambda t: (0, t, 0, 0)),
-        scratch_shapes=[pltpu.VMEM((SUBS, LANES), jnp.float32)],
+        out_specs=[
+            pl.BlockSpec((plan.n_groups, field_rows // steps, LANES), lambda t: (0, t, 0)),
+            pl.BlockSpec((SUBS, LANES), lambda t: (0, 0)),
+        ],
         name="field",
-    )(row_index, tile_offsets, *others, phase_codes, aperture, aperture)
-    packed = packed.reshape(n_col, plan.chunk + SUBS, LANES)
+    )(tile_offsets, phase_codes, aperture)
+    packed = packed.reshape(n_col, plan.chunk, LANES)
     received = lax.all_to_all(packed, "col", split_axis=0, concat_axis=0, tiled=True)
+
+    info = jnp.concatenate([jnp.where(mine, before, 0.0), opened])
+    for bit in range(n_col.bit_length() - 1):
+        info = info + lax.ppermute(info, "col", [(q, q ^ 1 << bit) for q in range(n_col)])
+    opened = info[n_col:]
+    counts = [opened] + along_rows(opened)
 
     tables = [outer_tables(plan), inner_tables(plan), twist_tables(plan)]
     splits = SPLITS if sum(SPLITS) == plan.rows else (plan.rows,)
     chunks = []
     for i, rows in enumerate(splits):
         shapes = [jax.ShapeDtypeStruct((rows, 2, plan.k2_dev, plan.k1), jnp.float32)] * plan.group
-        if i == 0:
-            shapes = shapes + [jax.ShapeDtypeStruct((SUBS, LANES), jnp.float32)]
         made = pl.pallas_call(
-            partial(transform_kernel, plan, sum(splits[:i]), rows, i == 0),
+            partial(transform_kernel, plan, sum(splits[:i]), rows),
             out_shape=shapes,
-            in_specs=[smem, vmem, vmem, vmem, vmem],
+            in_specs=[smem] + [vmem] * 5,
             out_specs=[vmem] * len(shapes),
             compiler_params=pltpu.CompilerParams(vmem_limit_bytes=24 * 2**20),
             name="transform",
-        )(me, received, *tables)
+        )(me, info, received, *tables)
         sent = {b: lax.ppermute(made[b], "col", [(q, q ^ b) for q in range(n_col)]) for b in ORDER}
-        if i == 0:
-            counts = [made[-1]] + along_rows(made[-1])
         chunks.append([sent[b] for b in ORDER] + [made[0]])
 
     slots = plan.group

time: 74.5 us -> 70.8 us (0.950)
  waiting for transfers between devices: 44.5 us -> 34.2 us
  starting transfers between devices: 19.5 us -> 26.2 us
    all_to_all x1, waiting for transfers between devices: 24 us -> 0.01 us  [per_device(): lax.all_to_all(packed, 'col', split_axis=0, concat_axis=0, tiled=True)]
    ppermute x0 -> x4, waiting for transfers between devices: none -> 14.9 us  [per_device(): lax.ppermute(info, 'col', [(q, q ^ 1 << bit) for q in range(n_col)])]
    ppermute x0 -> x4, starting transfers between devices: none -> 8.36 us  [per_device(): lax.ppermute(info, 'col', [(q, q ^ 1 << bit) for q in range(n_col)])]
    ppermute x2, starting transfers between devices: 4.48 us -> 3.1 us  [along_rows(): lax.ppermute(value, 'row', [(i, (i + d) % n_row) for i in range(n_row)])]
    ppermute x7, waiting for transfers between devices: 18.4 us -> 17.2 us  [per_device(): lax.ppermute(made[b], 'col', [(q, q ^ b) for q in range(n_col)])]
    ppermute x7, starting transfers between devices: 8.41 us -> 7.2 us  [per_device(): lax.ppermute(made[b], 'col', [(q, q ^ b) for q in range(n_col)])]
    all_to_all x1, starting transfers between devices: 6.56 us -> 7.5 us  [per_device(): lax.all_to_all(packed, 'col', split_axis=0, concat_axis=0, tiled=True)]
  transfers between devices with their start and end apart: 10 -> 14, of which waited for: 8 -> 10; matrix products, arithmetic and copies ran while one was open for 0% -> 0% of each run, Pallas kernels for 0% -> 0%
where the time goes in v5:
time: 70.8 us; the launch traced here: 70.6 us
  waiting for transfers between devices  34.2 us (48%)
  starting transfers between devices  26.2 us (37%)
  Pallas kernels  10 us (14%)
    ppermute x7, waiting for transfers between devices, per_device(): lax.ppermute(made[b], 'col', [(q, q ^ b) for q in range(n_col)])  17.2 us
    ppermute x4, waiting for transfers between devices, per_device(): lax.ppermute(info, 'col', [(q, q ^ 1 << bit) for q in range(n_col)])  14.9 us
    ppermute x4, starting transfers between devices, per_device(): lax.ppermute(info, 'col', [(q, q ^ 1 << bit) for q in range(n_col)])  8.36 us
    all_to_all x1, starting transfers between devices, per_device(): lax.all_to_all(packed, 'col', split_axis=0, concat_axis=0, tiled=True)  7.5 us
    ppermute x7, starting transfers between devices, per_device(): lax.ppermute(made[b], 'col', [(q, q ^ b) for q in range(n_col)])  7.2 us
    pallas_call x1, Pallas kernels, per_device(): pl.pallas_call(partial(transform_kernel, plan, sum(splits[:i]), rows), ou...  4.56 us
    ppermute x2, starting transfers between devices, along_rows(): lax.ppermute(value, 'row', [(i, (i + d) % n_row) for i in range(n_row)])  3.1 us
    pallas_call x1, Pallas kernels, per_device(): pl.pallas_call(partial(field_kernel, plan), out_shape=[jax.ShapeDtypeStru...  3.06 us
  transfers between devices with their start and end apart: 14, of which 10 were waited for; matrix products, arithmetic and copies ran while one was open for 0% of the time, Pallas kernels for 0%

profile of v5, /device:TPU:0, one launch (start us, length us, event | category | flops | bytes accessed | tf_op | source)
XLA Modules:
  0.0 70.6 jit_solution(3131756449373410855)
XLA Ops:
  0.0 3.1 %field.1 = (f32[2,1024,128]{2,1,0:T(8,128)}, f32[8,128]{1,0:T(8,128)}) custom-call(s32[2,4]{1,0:T(2,128)} %tiles_ref.1, s32[32,2048]{1,0:T(8,128)} %codes_ref.1, s32[32,2048]{1,0:T(8,128)} %mask_ref.1), custom_call_target="tpu_custom_call" | custom-call | tf_op jit(solution)/shard_map/field/pallas_call | solution.py:246
  3.1 7.5 %all-to-all-start = ((f32[16,128,128]{2,1,0:T(8,128)}), f32[16,128,128]{2,1,0:T(8,128)S(1)}, u32[]{:S(2)}, u32[]{:S(2)}) async-start(f32[16,128,128]{2,1,0:T(8,128)} %bitcast.6), calls=%async_computation | async-start | bytes 2097152 | tf_op jit(solution)/shard_map/all_to_all | solution.py:265
  10.6 1.6 %collective-permute-start = (s32[2,4]{1,0:T(2,128)S(1)}, s32[2,4]{1,0:T(2,128)S(1)}, u32[]{:S(2)}, u32[]{:S(2)}) collective-permute-start(s32[2,4]{1,0:T(2,128)S(1)} %copy-done.4), channel_id=1, source_target_pairs={{0,16},{16,0},{1,17},{17,1},{2,18},{18,2},{3,19},{19,3},{4,20},{20... | collective-permute-start | bytes 104 | tf_op jit(solution)/shard_map/ppermute | solution.py:234
  12.2 2.0 %collective-permute-done = s32[2,4]{1,0:T(2,128)S(1)} collective-permute-done((s32[2,4]{1,0:T(2,128)S(1)}, s32[2,4]{1,0:T(2,128)S(1)}, u32[]{:S(2)}, u32[]{:S(2)}) %collective-permute-start) | collective-permute-done | bytes 64 | tf_op jit(solution)/shard_map/ppermute | solution.py:234
  14.3 0.1 broadcast_select_fusion
  14.3 0.1 collective-permute-start.1
  14.4 1.2 %collective-permute-done.1 = f32[24,128]{1,0:T(8,128)S(1)} collective-permute-done((f32[24,128]{1,0:T(8,128)S(1)}, f32[24,128]{1,0:T(8,128)S(1)}, u32[]{:S(2)}, u32[]{:S(2)}) %collective-permute-start.1) | collective-permute-done | bytes 12320 | tf_op jit(solution)/shard_map/ppermute | solution.py:269
  15.6 1.9 %collective-permute-start.2 = (f32[24,128]{1,0:T(8,128)S(1)}, f32[24,128]{1,0:T(8,128)S(1)}, u32[]{:S(2)}, u32[]{:S(2)}) collective-permute-start(f32[24,128]{1,0:T(8,128)S(1)} %fusion.3), channel_id=1, source_target_pairs={{0,2},{1,3},{2,0},{3,1},{4,6},{5,7},{6,4},{7,5},{8,10},{9,11},{10,... | collective-permute-start | bytes 36872 | tf_op jit(solution)/shard_map/ppermute | solution.py:269
  17.5 1.8 %collective-permute-done.2 = f32[24,128]{1,0:T(8,128)S(1)} collective-permute-done((f32[24,128]{1,0:T(8,128)S(1)}, f32[24,128]{1,0:T(8,128)S(1)}, u32[]{:S(2)}, u32[]{:S(2)}) %collective-permute-start.2) | collective-permute-done | bytes 12320 | tf_op jit(solution)/shard_map/ppermute | solution.py:269
  19.3 1.9 %collective-permute-start.3 = (f32[24,128]{1,0:T(8,128)S(1)}, f32[24,128]{1,0:T(8,128)S(1)}, u32[]{:S(2)}, u32[]{:S(2)}) collective-permute-start(f32[24,128]{1,0:T(8,128)S(1)} %add.15), channel_id=1, source_target_pairs={{0,4},{1,5},{2,6},{3,7},{4,0},{5,1},{6,2},{7,3},{8,12},{9,13},{10,... | collective-permute-start | bytes 36872 | tf_op jit(solution)/shard_map/ppermute | solution.py:269
  21.2 7.7 %collective-permute-done.3 = f32[24,128]{1,0:T(8,128)S(1)} collective-permute-done((f32[24,128]{1,0:T(8,128)S(1)}, f32[24,128]{1,0:T(8,128)S(1)}, u32[]{:S(2)}, u32[]{:S(2)}) %collective-permute-start.3) | collective-permute-done | bytes 12320 | tf_op jit(solution)/shard_map/ppermute | solution.py:269
  28.9 4.4 %collective-permute-start.4 = (f32[24,128]{1,0:T(8,128)S(1)}, f32[24,128]{1,0:T(8,128)S(1)}, u32[]{:S(2)}, u32[]{:S(2)}) collective-permute-start(f32[24,128]{1,0:T(8,128)S(1)} %add.16), channel_id=1, source_target_pairs={{0,8},{1,9},{2,10},{3,11},{4,12},{5,13},{6,14},{7,15},{8,0},{9,1},... | collective-permute-start | bytes 36872 | tf_op jit(solution)/shard_map/ppermute | solution.py:269
  33.3 4.3 %collective-permute-done.4 = f32[24,128]{1,0:T(8,128)S(1)} collective-permute-done((f32[24,128]{1,0:T(8,128)S(1)}, f32[24,128]{1,0:T(8,128)S(1)}, u32[]{:S(2)}, u32[]{:S(2)}) %collective-permute-start.4) | collective-permute-done | bytes 12320 | tf_op jit(solution)/shard_map/ppermute | solution.py:269
  37.7 0.0 all-to-all-done.x_ref
  37.7 4.6 %transform.1 = (f32[4,2,16,512]{3,2,1,0:T(8,128)S(1)}, f32[4,2,16,512]{3,2,1,0:T(8,128)S(1)}, f32[4,2,16,512]{3,2,1,0:T(8,128)S(1)}, f32[4,2,16,512]{3,2,1,0:T(8...) custom-call(s32[1]{0:T(128)} %bitcast.me_ref, ...), custom_call_target="tpu_custom_call" | custom-call | tf_op jit(solution)/shard_map/transform/pallas_call | solution.py:278
  42.3 0.8 %collective-permute-start.5 = (f32[4,2,16,512]{3,2,1,0:T(8,128)S(1)}, f32[4,2,16,512]{3,2,1,0:T(8,128)S(1)}, u32[]{:S(2)}, u32[]{:S(2)}) collective-permute-start(f32[4,2,16,512]{3,2,1,0:T(8,128)S(1)} %get-tuple-element.17), channel_id=1, source_target_pairs={{0,7},{1,6},{2,5},{3,4},{4,3},{5,2},{6,1},{7,0},{8,15},{9,14},{10,... | collective-permute-start | bytes 786440 | tf_op jit(solution)/shard_map/ppermute | solution.py:286
  43.1 1.1 %collective-permute-start.6 = (f32[4,2,16,512]{3,2,1,0:T(8,128)S(1)}, f32[4,2,16,512]{3,2,1,0:T(8,128)S(1)}, u32[]{:S(2)}, u32[]{:S(2)}) collective-permute-start(f32[4,2,16,512]{3,2,1,0:T(8,128)S(1)} %get-tuple-element.18), channel_id=1, source_target_pairs={{0,6},{1,7},{2,4},{3,5},{4,2},{5,3},{6,0},{7,1},{8,14},{9,15},{10,... | collective-permute-start | bytes 786440 | tf_op jit(solution)/shard_map/ppermute | solution.py:286
  44.2 1.5 %collective-permute-start.12 = (f32[8,128]{1,0:T(8,128)S(1)}, f32[8,128]{1,0:T(8,128)S(1)}, u32[]{:S(2)}, u32[]{:S(2)}) collective-permute-start(f32[8,128]{1,0:T(8,128)S(1)} %slice.4.refs_8_), channel_id=1, source_target_pairs={{0,16},{16,0},{1,17},{17,1},{2,18},{18,2},{3,19},{19,3},{4,20},{20... | collective-permute-start | bytes 12296 | tf_op jit(solution)/shard_map/ppermute | solution.py:234
  45.7 0.5 collective-permute-start.7
  46.2 1.7 %collective-permute-start.8 = (f32[4,2,16,512]{3,2,1,0:T(8,128)S(1)}, f32[4,2,16,512]{3,2,1,0:T(8,128)S(1)}, u32[]{:S(2)}, u32[]{:S(2)}) collective-permute-start(f32[4,2,16,512]{3,2,1,0:T(8,128)S(1)} %get-tuple-element.20), channel_id=1, source_target_pairs={{0,4},{1,5},{2,6},{3,7},{4,0},{5,1},{6,2},{7,3},{8,12},{9,13},{10,... | collective-permute-start | bytes 786440 | tf_op jit(solution)/shard_map/ppermute | solution.py:286
  48.0 0.0 collective-permute-done.12.refs_9_
  48.0 1.0 %collective-permute-start.9 = (f32[4,2,16,512]{3,2,1,0:T(8,128)S(1)}, f32[4,2,16,512]{3,2,1,0:T(8,128)S(1)}, u32[]{:S(2)}, u32[]{:S(2)}) collective-permute-start(f32[4,2,16,512]{3,2,1,0:T(8,128)S(1)} %get-tuple-element.21), channel_id=1, source_target_pairs={{0,3},{1,2},{2,1},{3,0},{4,7},{5,6},{6,5},{7,4},{8,11},{9,10},{10,... | collective-permute-start | bytes 786440 | tf_op jit(solution)/shard_map/ppermute | solution.py:286
  48.9 2.9 %collective-permute-done.5.refs_0_ = f32[4,2,16,512]{3,2,1,0:T(8,128)S(1)} collective-permute-done((f32[4,2,16,512]{3,2,1,0:T(8,128)S(1)}, f32[4,2,16,512]{3,2,1,0:T(8,128)S(1)}, u32[]{:S(2)}, u32[]{:S(2)}) %collective-permute-start.5) | collective-permute-done | bytes 262176 | tf_op jit(solution)/shard_map/ppermute | solution.py:286
  51.8 1.5 %collective-permute-start.10 = (f32[4,2,16,512]{3,2,1,0:T(8,128)S(1)}, f32[4,2,16,512]{3,2,1,0:T(8,128)S(1)}, u32[]{:S(2)}, u32[]{:S(2)}) collective-permute-start(f32[4,2,16,512]{3,2,1,0:T(8,128)S(1)} %get-tuple-element.22), channel_id=1, source_target_pairs={{0,2},{1,3},{2,0},{3,1},{4,6},{5,7},{6,4},{7,5},{8,10},{9,11},{10,... | collective-permute-start | bytes 786440 | tf_op jit(solution)/shard_map/ppermute | solution.py:286
  53.3 3.4 %collective-permute-done.6.refs_1_ = f32[4,2,16,512]{3,2,1,0:T(8,128)S(1)} collective-permute-done((f32[4,2,16,512]{3,2,1,0:T(8,128)S(1)}, f32[4,2,16,512]{3,2,1,0:T(8,128)S(1)}, u32[]{:S(2)}, u32[]{:S(2)}) %collective-permute-start.6) | collective-permute-done | bytes 262176 | tf_op jit(solution)/shard_map/ppermute | solution.py:286
  56.7 0.6 collective-permute-start.11
  57.2 5.8 %collective-permute-done.7.refs_2_ = f32[4,2,16,512]{3,2,1,0:T(8,128)S(1)} collective-permute-done((f32[4,2,16,512]{3,2,1,0:T(8,128)S(1)}, f32[4,2,16,512]{3,2,1,0:T(8,128)S(1)}, u32[]{:S(2)}, u32[]{:S(2)}) %collective-permute-start.7) | collective-permute-done | bytes 262176 | tf_op jit(solution)/shard_map/ppermute | solution.py:286
  63.1 4.8 %collective-permute-done.8.refs_3_ = f32[4,2,16,512]{3,2,1,0:T(8,128)S(1)} collective-permute-done((f32[4,2,16,512]{3,2,1,0:T(8,128)S(1)}, f32[4,2,16,512]{3,2,1,0:T(8,128)S(1)}, u32[]{:S(2)}, u32[]{:S(2)}) %collective-permute-start.8) | collective-permute-done | bytes 262176 | tf_op jit(solution)/shard_map/ppermute | solution.py:286
  67.9 0.0 collective-permute-done.9.refs_4_
  67.9 0.3 collective-permute-done.10.refs_5_
  68.2 0.0 collective-permute-done.11.refs_6_
  68.2 2.4 %merge.1 = f32[2,32,8192]{2,1,0:T(8,128)} custom-call(s32[1]{0:T(128)} %bitcast.me_ref, f32[4,2,16,512]{3,2,1,0:T(8,128)S(1)} %collective-permute-done.5.refs_0_, f32[4,2,16,512]{3,2,1,0:T(8,128)S(1)} %collective-permute-done.6.refs_1_, f32[4,2,16,512]{3,2,1,0:T(8,128)S(1)} %collective-permute-done.7.refs_2_, ...), custom_call_target="tpu_custom_call" | custom-call | tf_op jit(solution)/shard_map/merge/pallas_call | solution.py:290
  (20 shorter events, 0.1 us)
Async XLA Ops:
  0.0 37.7 %copy-start.2 = (f32[64,512]{1,0:T(8,128)S(1)}, f32[64,512]{1,0:T(8,128)}, u32[]{:S(2)}) copy-start(f32[64,512]{1,0:T(8,128)} %constant.24.clone.twist_ref) | copy-start | bytes 393220
  0.0 37.7 %copy-start = (bf16[2,16,16,512]{3,2,1,0:T(8,128)(2,1)S(1)}, bf16[2,16,16,512]{3,2,1,0:T(8,128)(2,1)}, u32[]{:S(2)}) copy-start(bf16[2,16,16,512]{3,2,1,0:T(8,128)(2,1)} %constant.23.clone.inner_ref) | copy-start | bytes 1572868
  0.0 37.7 %copy-start.1 = (bf16[2,256,512]{2,1,0:T(8,128)(2,1)S(1)}, bf16[2,256,512]{2,1,0:T(8,128)(2,1)}, u32[]{:S(2)}) copy-start(bf16[2,256,512]{2,1,0:T(8,128)(2,1)} %constant.22.clone.outer_ref) | copy-start | bytes 1572868
  0.0 10.6 %copy-start.4 = (s32[2,4]{1,0:T(2,128)S(1)}, s32[2,4]{1,0:T(2,128)}, u32[]{:S(2)}) copy-start(s32[2,4]{1,0:T(2,128)} %tiles_ref.1) | copy-start | bytes 100
  3.1 11.3 %copy-start.3 = (f32[8,128]{1,0:T(8,128)S(1)}, f32[8,128]{1,0:T(8,128)}, u32[]{:S(2)}) copy-start(f32[8,128]{1,0:T(8,128)} %get-tuple-element.15) | copy-start | bytes 12292
  3.1 34.6 %all-to-all-start = ((f32[16,128,128]{2,1,0:T(8,128)}), f32[16,128,128]{2,1,0:T(8,128)S(1)}, u32[]{:S(2)}, u32[]{:S(2)}) async-start(f32[16,128,128]{2,1,0:T(8,128)} %bitcast.6), calls=%async_computation | async-start | bytes 2097152 | tf_op jit(solution)/shard_map/all_to_all | solution.py:265
  10.6 3.6 %collective-permute-start = (s32[2,4]{1,0:T(2,128)S(1)}, s32[2,4]{1,0:T(2,128)S(1)}, u32[]{:S(2)}, u32[]{:S(2)}) collective-permute-start(s32[2,4]{1,0:T(2,128)S(1)} %copy-done.4), channel_id=1, source_target_pairs={{0,16},{16,0},{1,17},{17,1},{2,18},{18,2},{3,19},{19,3},{4,20},{20... | collective-permute-start | bytes 104 | tf_op jit(solution)/shard_map/ppermute | solution.py:234
  14.3 1.2 %collective-permute-start.1 = (f32[24,128]{1,0:T(8,128)S(1)}, f32[24,128]{1,0:T(8,128)S(1)}, u32[]{:S(2)}, u32[]{:S(2)}) collective-permute-start(f32[24,128]{1,0:T(8,128)S(1)} %pad_maximum_fusion), channel_id=1, source_target_pairs={{0,1},{1,0},{2,3},{3,2},{4,5},{5,4},{6,7},{7,6},{8,9},{9,8},{10,11... | collective-permute-start | bytes 36872 | tf_op jit(solution)/shard_map/ppermute | solution.py:269
  15.6 3.7 %collective-permute-start.2 = (f32[24,128]{1,0:T(8,128)S(1)}, f32[24,128]{1,0:T(8,128)S(1)}, u32[]{:S(2)}, u32[]{:S(2)}) collective-permute-start(f32[24,128]{1,0:T(8,128)S(1)} %fusion.3), channel_id=1, source_target_pairs={{0,2},{1,3},{2,0},{3,1},{4,6},{5,7},{6,4},{7,5},{8,10},{9,11},{10,... | collective-permute-start | bytes 36872 | tf_op jit(solution)/shard_map/ppermute | solution.py:269
  19.3 9.6 %collective-permute-start.3 = (f32[24,128]{1,0:T(8,128)S(1)}, f32[24,128]{1,0:T(8,128)S(1)}, u32[]{:S(2)}, u32[]{:S(2)}) collective-permute-start(f32[24,128]{1,0:T(8,128)S(1)} %add.15), channel_id=1, source_target_pairs={{0,4},{1,5},{2,6},{3,7},{4,0},{5,1},{6,2},{7,3},{8,12},{9,13},{10,... | collective-permute-start | bytes 36872 | tf_op jit(solution)/shard_map/ppermute | solution.py:269
  28.9 8.8 %collective-permute-start.4 = (f32[24,128]{1,0:T(8,128)S(1)}, f32[24,128]{1,0:T(8,128)S(1)}, u32[]{:S(2)}, u32[]{:S(2)}) collective-permute-start(f32[24,128]{1,0:T(8,128)S(1)} %add.16), channel_id=1, source_target_pairs={{0,8},{1,9},{2,10},{3,11},{4,12},{5,13},{6,14},{7,15},{8,0},{9,1},... | collective-permute-start | bytes 36872 | tf_op jit(solution)/shard_map/ppermute | solution.py:269
  42.3 9.6 %collective-permute-start.5 = (f32[4,2,16,512]{3,2,1,0:T(8,128)S(1)}, f32[4,2,16,512]{3,2,1,0:T(8,128)S(1)}, u32[]{:S(2)}, u32[]{:S(2)}) collective-permute-start(f32[4,2,16,512]{3,2,1,0:T(8,128)S(1)} %get-tuple-element.17), channel_id=1, source_target_pairs={{0,7},{1,6},{2,5},{3,4},{4,3},{5,2},{6,1},{7,0},{8,15},{9,14},{10,... | collective-permute-start | bytes 786440 | tf_op jit(solution)/shard_map/ppermute | solution.py:286
  43.1 13.6 %collective-permute-start.6 = (f32[4,2,16,512]{3,2,1,0:T(8,128)S(1)}, f32[4,2,16,512]{3,2,1,0:T(8,128)S(1)}, u32[]{:S(2)}, u32[]{:S(2)}) collective-permute-start(f32[4,2,16,512]{3,2,1,0:T(8,128)S(1)} %get-tuple-element.18), channel_id=1, source_target_pairs={{0,6},{1,7},{2,4},{3,5},{4,2},{5,3},{6,0},{7,1},{8,14},{9,15},{10,... | collective-permute-start | bytes 786440 | tf_op jit(solution)/shard_map/ppermute | solution.py:286
  44.2 3.8 %collective-permute-start.12 = (f32[8,128]{1,0:T(8,128)S(1)}, f32[8,128]{1,0:T(8,128)S(1)}, u32[]{:S(2)}, u32[]{:S(2)}) collective-permute-start(f32[8,128]{1,0:T(8,128)S(1)} %slice.4.refs_8_), channel_id=1, source_target_pairs={{0,16},{16,0},{1,17},{17,1},{2,18},{18,2},{3,19},{19,3},{4,20},{20... | collective-permute-start | bytes 12296 | tf_op jit(solution)/shard_map/ppermute | solution.py:234
  45.7 17.3 %collective-permute-start.7 = (f32[4,2,16,512]{3,2,1,0:T(8,128)S(1)}, f32[4,2,16,512]{3,2,1,0:T(8,128)S(1)}, u32[]{:S(2)}, u32[]{:S(2)}) collective-permute-start(f32[4,2,16,512]{3,2,1,0:T(8,128)S(1)} %get-tuple-element.19), channel_id=1, source_target_pairs={{0,5},{1,4},{2,7},{3,6},{4,1},{5,0},{6,3},{7,2},{8,13},{9,12},{10,... | collective-permute-start | bytes 786440 | tf_op jit(solution)/shard_map/ppermute | solution.py:286
  46.2 21.6 %collective-permute-start.8 = (f32[4,2,16,512]{3,2,1,0:T(8,128)S(1)}, f32[4,2,16,512]{3,2,1,0:T(8,128)S(1)}, u32[]{:S(2)}, u32[]{:S(2)}) collective-permute-start(f32[4,2,16,512]{3,2,1,0:T(8,128)S(1)} %get-tuple-element.20), channel_id=1, source_target_pairs={{0,4},{1,5},{2,6},{3,7},{4,0},{5,1},{6,2},{7,3},{8,12},{9,13},{10,... | collective-permute-start | bytes 786440 | tf_op jit(solution)/shard_map/ppermute | solution.py:286
  48.0 19.9 %collective-permute-start.9 = (f32[4,2,16,512]{3,2,1,0:T(8,128)S(1)}, f32[4,2,16,512]{3,2,1,0:T(8,128)S(1)}, u32[]{:S(2)}, u32[]{:S(2)}) collective-permute-start(f32[4,2,16,512]{3,2,1,0:T(8,128)S(1)} %get-tuple-element.21), channel_id=1, source_target_pairs={{0,3},{1,2},{2,1},{3,0},{4,7},{5,6},{6,5},{7,4},{8,11},{9,10},{10,... | collective-permute-start | bytes 786440 | tf_op jit(solution)/shard_map/ppermute | solution.py:286
  51.8 16.4 %collective-permute-start.10 = (f32[4,2,16,512]{3,2,1,0:T(8,128)S(1)}, f32[4,2,16,512]{3,2,1,0:T(8,128)S(1)}, u32[]{:S(2)}, u32[]{:S(2)}) collective-permute-start(f32[4,2,16,512]{3,2,1,0:T(8,128)S(1)} %get-tuple-element.22), channel_id=1, source_target_pairs={{0,2},{1,3},{2,0},{3,1},{4,6},{5,7},{6,4},{7,5},{8,10},{9,11},{10,... | collective-permute-start | bytes 786440 | tf_op jit(solution)/shard_map/ppermute | solution.py:286
  56.7 11.5 %collective-permute-start.11 = (f32[4,2,16,512]{3,2,1,0:T(8,128)S(1)}, f32[4,2,16,512]{3,2,1,0:T(8,128)S(1)}, u32[]{:S(2)}, u32[]{:S(2)}) collective-permute-start(f32[4,2,16,512]{3,2,1,0:T(8,128)S(1)} %get-tuple-element.23), channel_id=1, source_target_pairs={{0,1},{1,0},{2,3},{3,2},{4,5},{5,4},{6,7},{7,6},{8,9},{9,8},{10,11... | collective-permute-start | bytes 786440 | tf_op jit(solution)/shard_map/ppermute | solution.py:286

commit v6 on v5

--- a/solution.py
+++ b/solution.py
@@ -18,8 +18,8 @@
 INNER = 256
 PAD = 4
 FINE = 16
+CHIP_ORDER = (4, 1, 5, 2, 6, 3, 7)
 ORDER = (7, 6, 5, 4, 3, 2, 1)
-SPLITS = (4,)
 GROUP = 8
 
 
@@ -52,10 +52,11 @@
     return np.stack([high, low])
 
 
-def outer_tables(plan):
+def outer_tables(plan, blocks):
     angle = np.arange(plan.n1)[:, None] * np.arange(plan.k1)[None, :] % plan.k1
     angle = angle * (2.0 * np.pi / plan.k1)
-    return split_bf16(np.concatenate([np.cos(angle), np.sin(angle)]))
+    table = np.stack([np.cos(angle), np.sin(angle)]).reshape(2, blocks, plan.n1 // blocks, plan.k1)
+    return split_bf16(table.transpose(1, 0, 2, 3))
 
 
 def inner_tables(plan):
@@ -119,16 +120,92 @@
         open_ref[...] = open_ref[...] + total
 
 
-def transform_kernel(plan, first, rows, me_ref, info_ref, x_ref, outer_ref, inner_ref, twist_ref, *refs):
+def chip_field_kernel(plan, me_ref, *refs):
+    n_other = plan.n_row - 1
+    tiles, others, refs = refs[:2], (refs[2 : 2 + n_other], refs[2 + n_other : 2 + 2 * n_other]), refs[2 + 2 * n_other :]
+    codes_hbm, mask_hbm, near_codes_ref, near_mask_ref = refs[:4]
+    outs, (codes_ref, mask_ref, made_ref, sems) = refs[4:-4], refs[-4:]
+    core, chip, row = me_ref[0], me_ref[1], me_ref[2]
+    half = plan.row_dev // 2
+    first = pl.multiple_of(core * half, half)
+    copies = [
+        pltpu.make_async_copy(codes_hbm, codes_ref, sems.at[0]),
+        pltpu.make_async_copy(mask_hbm, mask_ref, sems.at[1]),
+    ]
+    for copy in copies:
+        copy.start()
+    total = jnp.zeros((SUBS, LANES), jnp.int32)
+    stride = 2 * plan.lane_parts * plan.n1_dev
+    for owner in (1, 0):
+        if owner == 0:
+            for copy in copies:
+                copy.wait()
+        codes, mask = ((codes_ref, mask_ref), (near_codes_ref, near_mask_ref))[owner]
+        before = jnp.zeros((1, plan.pupil_dev // TILE_C), jnp.int32)
+        for d, other in enumerate(others[owner]):
+            before = before + jnp.where(row > d, jnp.sum(other[...], axis=0, keepdims=True), 0)
+        for k in range(plan.row_dev // TILE_R):
+            before = before + jnp.where(first >= k * TILE_R, tiles[owner][k : k + 1], 0)
+        for t in range(plan.row_dev // SUBS):
+            for j in range(plan.pupil_dev // LANES):
+                total = total + mask[t * SUBS : (t + 1) * SUBS, j * LANES : (j + 1) * LANES]
+        for t in range(half // SUBS):
+            at = pl.multiple_of(first + t * SUBS, SUBS)
+            for j in range(plan.pupil_dev // LANES):
+                lanes = slice(j * LANES, (j + 1) * LANES)
+                column = j * LANES // TILE_C
+                piston = jnp.broadcast_to(before[:, column : column + 1], (SUBS, LANES))
+                code = (codes[pl.ds(at, SUBS), lanes] + piston) & (LEVELS - 1)
+                cos, sin, minus_cos, minus_sin = unit_phase(code)
+                amplitude = mask[pl.ds(at, SUBS), lanes].astype(jnp.float32)
+                real = cos * jnp.where(minus_cos, -amplitude, amplitude)
+                imag = sin * jnp.where(minus_sin, -amplitude, amplitude)
+                for part, value in enumerate((real, imag)):
+                    start = (part * plan.lane_parts + j % plan.lane_parts) * plan.n1_dev + j // plan.lane_parts
+                    made_ref[owner, pl.ds(t * SUBS * stride + start, SUBS, stride=stride), :] = value
+    own_rows = lax.rem(chip, len(outs))
+    for b, out in enumerate(outs):
+        source = pl.multiple_of((own_rows ^ b) * plan.chunk, plan.chunk)
+        for i in range(plan.chunk // plan.n1_dev):
+            for side in range(2):
+                block = made_ref[side ^ core, pl.ds(pl.multiple_of(source + i * plan.n1_dev, plan.n1_dev), plan.n1_dev), :]
+                out[(2 * i + side) * plan.n1_dev : (2 * i + side + 1) * plan.n1_dev, :] = block
+        out[2 * plan.chunk :, :] = total.astype(jnp.float32)
+
+
+def chip_transform_kernel(plan, order, me_ref, *refs):
+    n_chips = plan.n_col // 2
+    given = refs[:n_chips]
+    outer_ref, inner_ref, twist_ref = refs[n_chips : n_chips + 3]
+    outs, count_ref = refs[n_chips + 3 : -1], refs[-1]
+    chunks = [given[order.index(b)] for b in range(n_chips)]
+    me = me_ref[0]
+    chip = me >> 1
+    count = chunks[0][2 * plan.chunk :, :]
+    for chunk in chunks[1:]:
+        count = count + chunk[2 * plan.chunk :, :]
+    count_ref[...] = count
+    w1 = []
+    for s in range(2):
+        rows = [outer_ref[s, chip ^ b] for b in range(n_chips)]
+        w1.append([jnp.concatenate([both[i] for both in rows]) for i in range(2)])
+    n1_chip = 2 * plan.n1_dev
+
+    def part_of(r, part):
+        pieces = []
+        for lt in range(plan.lane_parts):
+            at = ((r * 2 + part) * plan.lane_parts + lt) * n1_chip
+            pieces.append(jnp.concatenate([chunk[at : at + n1_chip, :] for chunk in chunks]))
+        return jnp.concatenate(pieces, axis=1)
+
+    def field_of(r):
+        return jnp.concatenate([part_of(r, 0), part_of(r, 1)])
+
+    transform_rows(plan, me, plan.rows, field_of, w1, inner_ref, twist_ref, outs)
+
+
+def transform_kernel(plan, me_ref, info_ref, x_ref, outer_ref, inner_ref, twist_ref, *refs):
     chunk_row = plan.chunk // plan.rows
-    me = me_ref[0]
-
-    def outer(a, b):
-        return lax.dot_general(a, b, (((0,), (0,)), ((), ())), preferred_element_type=jnp.float32)
-
-    def inner(a, b):
-        return jnp.dot(a, b, preferred_element_type=jnp.float32)
-
     info = info_ref[: plan.n_col]
     info = jnp.broadcast_to(info[:, None, :], (plan.n_col, plan.n1_dev, LANES)).reshape(plan.n1, LANES)
     tile = lax.broadcasted_iota(jnp.int32, info.shape, 0) % plan.n1_dev * INNER // TILE_C
@@ -137,10 +214,33 @@
     turn_cos, turn_sin, minus_cos, minus_sin = unit_phase(before)
     turn_cos = jnp.where(minus_cos, -turn_cos, turn_cos)
     turn_sin = jnp.where(minus_sin, -turn_sin, turn_sin)
-    n1, k2_dev = plan.n1, plan.k2_dev
+    w1 = [[outer_ref[s, 0, i] for i in range(2)] for s in range(2)]
+
+    def field_of(r):
+        halves = []
+        for part in range(2):
+            pieces = []
+            for lt in range(plan.lane_parts):
+                at = r * chunk_row + (part * plan.lane_parts + lt) * plan.n1_dev
+                pieces.append(x_ref[:, at : at + plan.n1_dev, :].reshape(plan.n1, LANES))
+            halves.append(jnp.concatenate(pieces, axis=1))
+        real, imag = halves
+        return jnp.concatenate([real * turn_cos - imag * turn_sin, real * turn_sin + imag * turn_cos], axis=0)
+
+    transform_rows(plan, me_ref[0], plan.rows, field_of, w1, inner_ref, twist_ref, refs)
+
+
+def transform_rows(plan, me, rows, field_of, outer_parts, inner_ref, twist_ref, outs):
+    def outer(a, b):
+        return lax.dot_general(a, b, (((0,), (0,)), ((), ())), preferred_element_type=jnp.float32)
+
+    def inner(a, b):
+        return jnp.dot(a, b, preferred_element_type=jnp.float32)
+
+    k2_dev = plan.k2_dev
     w1, w2 = [], []
     for s in range(2):
-        cos, sin = outer_ref[s, :n1], outer_ref[s, n1:]
+        cos, sin = outer_parts[s]
         w1.append(jnp.concatenate([jnp.concatenate([cos, sin]), jnp.concatenate([-sin, cos])], axis=1))
         blocks = []
         for b in range(plan.group):
@@ -159,15 +259,7 @@
         ts.append(sin * fine_cos + cos * fine_sin)
     tc, ts = jnp.concatenate(tc), jnp.concatenate(ts)
     for r in range(rows):
-        halves = []
-        for part in range(2):
-            pieces = []
-            for lt in range(plan.lane_parts):
-                at = (first + r) * chunk_row + (part * plan.lane_parts + lt) * plan.n1_dev
-                pieces.append(x_ref[:, at : at + plan.n1_dev, :].reshape(plan.n1, LANES))
-            halves.append(jnp.concatenate(pieces, axis=1))
-        real, imag = halves
-        x = jnp.concatenate([real * turn_cos - imag * turn_sin, real * turn_sin + imag * turn_cos], axis=0)
+        x = field_of(r)
         xh = x.astype(jnp.bfloat16)
         xl = (x - xh.astype(jnp.float32)).astype(jnp.bfloat16)
         y = outer(xh, w1[0]) + outer(xl, w1[0]) + outer(xh, w1[1])
@@ -177,66 +269,117 @@
         fl = (f - fh.astype(jnp.float32)).astype(jnp.bfloat16)
         z = inner(w2[0], fh) + inner(w2[1], fh) + inner(w2[0], fl)
         for b in range(plan.group):
-            refs[b][r] = z[b * size : (b + 1) * size].reshape(2, plan.k2_dev, plan.k1)
-
-
-def merge_kernel(plan, splits, me_ref, *refs):
-    n = len(splits)
-    chunks = []
-    for i in range(n):
-        given = refs[i * plan.group : (i + 1) * plan.group]
-        chunks.append([given[(ORDER + (0,)).index(b)] for b in range(plan.group)])
-    counts = refs[n * plan.group : n * plan.group + plan.n_row]
-    out_ref, tile_ref, row_ref, sems = refs[n * plan.group + plan.n_row :]
+            outs[b][r] = z[b * size : (b + 1) * size].reshape(2, k2_dev, plan.k1)
+
+
+def merge_kernel(plan, swap_bit, me_ref, *refs):
+    chunks = [refs[(ORDER + (0,)).index(b)] for b in range(plan.group)]
+    counts = refs[plan.group : plan.group + plan.n_row]
+    out_ref, tile_ref, row_ref, sems = refs[plan.group + plan.n_row :]
     total = counts[0][...]
     for other in counts[1:]:
         total = total + other[...]
     total = jnp.sum(jnp.sum(total, axis=0, keepdims=True), axis=1, keepdims=True)
     scale = jnp.sqrt(float(plan.rows_all) / total)
     inside = lax.rem(me_ref[0], plan.group)
-    swapped = lax.rem(inside, 2) == 1
+    swapped = lax.rem(inside // swap_bit, 2) == 1
     take = min(plan.k2_dev, SUBS)
     stride = plan.k1_tiles * SUBS
     copies = []
-    for pair in range(plan.group // 2):
-        for part in range(2):
-            slot = pair * 2 + part
-            for i, rows in enumerate(splits):
-                for r in range(rows):
-                    for k2 in range(0, plan.k2_dev, take):
-                        for j in range(plan.k1_tiles):
-                            lanes = slice(j * LANES, (j + 1) * LANES)
-                            a = chunks[i][2 * pair][r, part, k2 : k2 + take, lanes] * scale
-                            b = chunks[i][2 * pair + 1][r, part, k2 : k2 + take, lanes] * scale
-                            at = (k2 * plan.k1_tiles + j) * SUBS + sum(splits[:i]) + r
-                            tile_ref[slot, pl.ds(at, take, stride=stride), :] = jnp.where(swapped, b, a)
-                            tile_ref[slot, pl.ds(at + plan.rows, take, stride=stride), :] = jnp.where(swapped, a, b)
-            for f in range(plan.freq_tiles):
-                row_ref[slot, :, f * LANES : (f + 1) * LANES] = tile_ref[slot, f * SUBS : (f + 1) * SUBS, :]
-            tile = lax.div(inside, 2) ^ pair
-            target = out_ref.at[part, pl.ds(pl.multiple_of(tile * SUBS, SUBS), SUBS), :]
-            copy = pltpu.make_async_copy(row_ref.at[slot], target, sems.at[slot])
-            copy.start()
-            copies.append(copy)
+    for slot in range(plan.group):
+        part = slot % 2
+        base = [b for b in range(plan.group) if b & swap_bit == 0][slot // 2]
+        for r in range(plan.rows):
+            for k2 in range(0, plan.k2_dev, take):
+                for j in range(plan.k1_tiles):
+                    lanes = slice(j * LANES, (j + 1) * LANES)
+                    a = chunks[base][r, part, k2 : k2 + take, lanes] * scale
+                    b = chunks[base + swap_bit][r, part, k2 : k2 + take, lanes] * scale
+                    at = (k2 * plan.k1_tiles + j) * SUBS + r
+                    tile_ref[slot, pl.ds(at, take, stride=stride), :] = jnp.where(swapped, b, a)
+                    tile_ref[slot, pl.ds(at + plan.rows, take, stride=stride), :] = jnp.where(swapped, a, b)
+        for f in range(plan.freq_tiles):
+            row_ref[slot, :, f * LANES : (f + 1) * LANES] = tile_ref[slot, f * SUBS : (f + 1) * SUBS, :]
+        source = inside ^ base
+        tile = source // 2 if swap_bit == 1 else source % 2 * 2 + source // 4
+        target = out_ref.at[part, pl.ds(pl.multiple_of(tile * SUBS, SUBS), SUBS), :]
+        copy = pltpu.make_async_copy(row_ref.at[slot], target, sems.at[slot])
+        copy.start()
+        copies.append(copy)
     for copy in copies:
         copy.wait()
 
 
-def per_device(phase_codes, aperture, tile_offsets):
-    n_col = lax.axis_size("col")
-    n_row = lax.axis_size("row")
-    plan = Plan(*phase_codes.shape, n_col, n_row)
+def along_rows(n_row, value):
+    return [lax.ppermute(value, "row", [(i, (i + d) % n_row) for i in range(n_row)]) for d in range(1, n_row)]
+
+
+def spectra_shapes(plan):
+    return [jax.ShapeDtypeStruct((plan.rows, 2, plan.k2_dev, plan.k1), jnp.float32)] * plan.group
+
+
+def spectra_by_chip(plan, phase_codes, aperture, tile_offsets):
+    n_col, n_row = plan.n_col, plan.n_row
+    n_chips = n_col // 2
+    row_index = lax.axis_index("row").astype(jnp.int32)
+    col_index = lax.axis_index("col").astype(jnp.int32)
+    smem, vmem, hbm = (pl.BlockSpec(memory_space=m) for m in (pltpu.SMEM, pltpu.VMEM, pl.ANY))
+    swap = [(q, q ^ 1) for q in range(n_col)]
+    others = along_rows(n_row, tile_offsets)
+    near_others = []
+    for d in range(1, n_row):
+        pairs = [(r * n_col + q, (r + d) % n_row * n_col + (q ^ 1)) for r in range(n_row) for q in range(n_col)]
+        near_others.append(lax.ppermute(tile_offsets, ("row", "col"), pairs))
+    near = [lax.ppermute(value, "col", swap) for value in (tile_offsets, phase_codes, aperture)]
+    alike = min(n_chips, plan.group // 2)
+    block = jax.ShapeDtypeStruct((2 * plan.chunk + SUBS, LANES), jnp.float32)
+    rows = pl.pallas_call(
+        partial(chip_field_kernel, plan),
+        out_shape=[block] * alike,
+        in_specs=[smem] + [vmem] * (2 * n_row) + [hbm, hbm, vmem, vmem],
+        out_specs=[vmem] * alike,
+        scratch_shapes=[
+            pltpu.VMEM(phase_codes.shape, jnp.int32),
+            pltpu.VMEM(aperture.shape, jnp.int32),
+            pltpu.VMEM((2, alike * plan.chunk, LANES), jnp.float32),
+            pltpu.SemaphoreType.DMA((2,)),
+        ],
+        compiler_params=pltpu.CompilerParams(vmem_limit_bytes=16 * 2**20),
+        name="field",
+    )(
+        jnp.stack([col_index % 2, col_index // 2, row_index]),
+        tile_offsets,
+        near[0],
+        *others,
+        *near_others,
+        phase_codes,
+        aperture,
+        near[1],
+        near[2],
+    )
+    order = CHIP_ORDER + (0,)
+    received = [rows[0] if b == 0 else lax.ppermute(rows[b % alike], "col", [(q, q ^ 2 * b) for q in range(n_col)]) for b in order]
+    tables = [outer_tables(plan, n_chips), inner_tables(plan), twist_tables(plan)]
+    *made, opened = pl.pallas_call(
+        partial(chip_transform_kernel, plan, order),
+        out_shape=spectra_shapes(plan) + [jax.ShapeDtypeStruct((SUBS, LANES), jnp.float32)],
+        in_specs=[smem] + [vmem] * (n_chips + 3),
+        out_specs=[vmem] * (plan.group + 1),
+        compiler_params=pltpu.CompilerParams(vmem_limit_bytes=24 * 2**20),
+        name="transform",
+    )(col_index.reshape(1), *received, *tables)
+    return made, opened
+
+
+def spectra_by_device(plan, phase_codes, aperture, tile_offsets):
+    n_col, n_row = plan.n_col, plan.n_row
     row_index = lax.axis_index("row")
     col_index = lax.axis_index("col")
     me = col_index.astype(jnp.int32).reshape(1)
-
-    def along_rows(value):
-        return [lax.ppermute(value, "row", [(i, (i + d) % n_row) for i in range(n_row)]) for d in range(1, n_row)]
-
     smem = pl.BlockSpec(memory_space=pltpu.SMEM)
     vmem = pl.BlockSpec(memory_space=pltpu.VMEM)
     before = jnp.zeros((1, plan.pupil_dev // TILE_C), jnp.int32)
-    for d, other in enumerate(along_rows(tile_offsets)):
+    for d, other in enumerate(along_rows(n_row, tile_offsets)):
         before = before + jnp.where(row_index > d, jnp.sum(other, axis=0, keepdims=True), 0)
     before = jnp.pad((before & (LEVELS - 1)).astype(jnp.float32), ((0, 0), (0, LANES - before.shape[1])))
     mine = jnp.arange(n_col, dtype=jnp.int32)[:, None] == col_index
@@ -267,39 +410,42 @@
     info = jnp.concatenate([jnp.where(mine, before, 0.0), opened])
     for bit in range(n_col.bit_length() - 1):
         info = info + lax.ppermute(info, "col", [(q, q ^ 1 << bit) for q in range(n_col)])
-    opened = info[n_col:]
-    counts = [opened] + along_rows(opened)
-
-    tables = [outer_tables(plan), inner_tables(plan), twist_tables(plan)]
-    splits = SPLITS if sum(SPLITS) == plan.rows else (plan.rows,)
-    chunks = []
-    for i, rows in enumerate(splits):
-        shapes = [jax.ShapeDtypeStruct((rows, 2, plan.k2_dev, plan.k1), jnp.float32)] * plan.group
-        made = pl.pallas_call(
-            partial(transform_kernel, plan, sum(splits[:i]), rows),
-            out_shape=shapes,
-            in_specs=[smem] + [vmem] * 5,
-            out_specs=[vmem] * len(shapes),
-            compiler_params=pltpu.CompilerParams(vmem_limit_bytes=24 * 2**20),
-            name="transform",
-        )(me, info, received, *tables)
-        sent = {b: lax.ppermute(made[b], "col", [(q, q ^ b) for q in range(n_col)]) for b in ORDER}
-        chunks.append([sent[b] for b in ORDER] + [made[0]])
-
-    slots = plan.group
+    tables = [outer_tables(plan, 1), inner_tables(plan), twist_tables(plan)]
+    made = pl.pallas_call(
+        partial(transform_kernel, plan),
+        out_shape=spectra_shapes(plan),
+        in_specs=[smem] + [vmem] * 5,
+        out_specs=[vmem] * plan.group,
+        compiler_params=pltpu.CompilerParams(vmem_limit_bytes=24 * 2**20),
+        name="transform",
+    )(me, info, received, *tables)
+    return made, info[n_col:]
+
+
+def per_device(phase_codes, aperture, tile_offsets):
+    n_col = lax.axis_size("col")
+    n_row = lax.axis_size("row")
+    plan = Plan(*phase_codes.shape, n_col, n_row)
+    by_chip = plan.n1_dev % SUBS == 0 and len(CHIP_ORDER) == n_col // 2 - 1
+    spectra = spectra_by_chip if by_chip else spectra_by_device
+    made, opened = spectra(plan, phase_codes, aperture, tile_offsets)
+    chunks = [lax.ppermute(made[b], "col", [(q, q ^ b) for q in range(n_col)]) for b in ORDER] + [made[0]]
+    counts = [opened] + along_rows(n_row, opened)
+    smem = pl.BlockSpec(memory_space=pltpu.SMEM)
+    vmem = pl.BlockSpec(memory_space=pltpu.VMEM)
     return pl.pallas_call(
-        partial(merge_kernel, plan, splits),
+        partial(merge_kernel, plan, 2 if by_chip else 1),
         out_shape=jax.ShapeDtypeStruct((2, plan.row_dev, plan.freq_tiles * LANES), jnp.float32),
-        in_specs=[smem] + [vmem] * (len(splits) * plan.group + n_row),
+        in_specs=[smem] + [vmem] * (plan.group + n_row),
         out_specs=pl.BlockSpec(memory_space=pl.ANY),
         scratch_shapes=[
-            pltpu.VMEM((slots, plan.freq_tiles * SUBS, LANES), jnp.float32),
-            pltpu.VMEM((slots, SUBS, plan.freq_tiles * LANES), jnp.float32),
-            pltpu.SemaphoreType.DMA((slots,)),
+            pltpu.VMEM((plan.group, plan.freq_tiles * SUBS, LANES), jnp.float32),
+            pltpu.VMEM((plan.group, SUBS, plan.freq_tiles * LANES), jnp.float32),
+            pltpu.SemaphoreType.DMA((plan.group,)),
         ],
         compiler_params=pltpu.CompilerParams(vmem_limit_bytes=24 * 2**20),
         name="merge",
-    )(me, *[chunk for part in chunks for chunk in part], *counts)
+    )(lax.axis_index("col").astype(jnp.int32).reshape(1), *chunks, *counts)
 
 
 def solution(mesh):

time: 70.8 us -> 74.8 us (1.056)
  local copies, waits for them, and re-layouts: 0.03 us -> 5.56 us
  waiting for transfers between devices: 34.2 us -> 37 us
  starting transfers between devices: 26.2 us -> 23.6 us
  Pallas kernels: 10 us -> 8.12 us
    all_to_all x1 -> x0, starting transfers between devices: 7.5 us -> none  [per_device(): lax.all_to_all(packed, 'col', split_axis=0, concat_axis=0, tiled=True)]
    unnamed x10 -> x12, local copies, waits for them, and re-layouts: 0.02 us -> 5.56 us
    ppermute x4 -> x11, starting transfers between devices: 8.36 us -> 12.7 us  [the longest x7 12.1 us: spectra_by_chip(): lax.ppermute(rows[b % alike], 'col', [(q, q ^ 2 * b) for q in range(n_col)])]
    ppermute x4 -> x11, waiting for transfers between devices: 14.9 us -> 16.9 us  [the longest x7 15.5 us: spectra_by_chip(): lax.ppermute(rows[b % alike], 'col', [(q, q ^ 2 * b) for q in range(n_col)])]
    pallas_call x3, Pallas kernels: 10 us -> 8.12 us  [the longest x1 4.38 us: spectra_by_chip(): pl.pallas_call(partial(chip_transform_kernel, plan, order), out_shape=spe...]
    ppermute x2, waiting for transfers between devices: 2.05 us -> 3.13 us  [along_rows(): lax.ppermute(value, 'row', [(i, (i + d) % n_row) for i in range(n_row)])]
  transfers between devices with their start and end apart: 14 -> 20, of which waited for: 10 -> 11; matrix products, arithmetic and copies ran while one was open for 0% -> 0% of each run, Pallas kernels for 0% -> 0%
where the time goes in v6:
time: 74.8 us; the launch traced here: 74.4 us
  waiting for transfers between devices  37 us (49%)
  starting transfers between devices  23.6 us (32%)
  Pallas kernels  8.12 us (11%)
  local copies, waits for them, and re-layouts  5.56 us (7%)
    ppermute x7, waiting for transfers between devices, per_device(): lax.ppermute(made[b], 'col', [(q, q ^ b) for q in range(n_col)])  17 us
    ppermute x7, waiting for transfers between devices, spectra_by_chip(): lax.ppermute(rows[b % alike], 'col', [(q, q ^ 2 * b) for q in range(n_col)])  15.5 us
    ppermute x7, starting transfers between devices, spectra_by_chip(): lax.ppermute(rows[b % alike], 'col', [(q, q ^ 2 * b) for q in range(n_col)])  12.1 us
    ppermute x7, starting transfers between devices, per_device(): lax.ppermute(made[b], 'col', [(q, q ^ b) for q in range(n_col)])  7.46 us
    unnamed x12, local copies, waits for them, and re-layouts  5.56 us
    pallas_call x1, Pallas kernels, spectra_by_chip(): pl.pallas_call(partial(chip_transform_kernel, plan, order), out_shape=spe...  4.38 us
    ppermute x2, starting transfers between devices, along_rows(): lax.ppermute(value, 'row', [(i, (i + d) % n_row) for i in range(n_row)])  3.37 us
    ppermute x2, waiting for transfers between devices, along_rows(): lax.ppermute(value, 'row', [(i, (i + d) % n_row) for i in range(n_row)])  3.13 us
  transfers between devices with their start and end apart: 20, of which 11 were waited for; matrix products, arithmetic and copies ran while one was open for 0% of the time, Pallas kernels for 0%

profile of v6, /device:TPU:0, one launch (start us, length us, event | category | flops | bytes accessed | tf_op | source)
XLA Modules:
  0.0 74.4 jit_solution(577804672538162986)
XLA Ops:
  0.0 0.5 collective-permute-start.3
  0.5 3.0 %collective-permute-start.1 = (s32[2,4]{1,0:T(2,128)}, s32[2,4]{1,0:T(2,128)S(1)}, u32[]{:S(2)}, u32[]{:S(2)}) collective-permute-start(s32[2,4]{1,0:T(2,128)} %refs_0_.1), channel_id=1, source_target_pairs={{0,16},{16,0},{1,17},{17,1},{2,18},{18,2},{3,19},{19,3},{4,20},{20... | collective-permute-start | bytes 104 | tf_op jit(solution)/shard_map/ppermute | solution.py:314
  3.7 1.6 %collective-permute-done.1.refs_2_ = s32[2,4]{1,0:T(2,128)S(1)} collective-permute-done((s32[2,4]{1,0:T(2,128)}, s32[2,4]{1,0:T(2,128)S(1)}, u32[]{:S(2)}, u32[]{:S(2)}) %collective-permute-start.1) | collective-permute-done | bytes 64 | tf_op jit(solution)/shard_map/ppermute | solution.py:314
  5.2 1.4 %collective-permute-done.2.refs_3_ = s32[2,4]{1,0:T(2,128)S(1)} collective-permute-done((s32[2,4]{1,0:T(2,128)}, s32[2,4]{1,0:T(2,128)S(1)}, u32[]{:S(2)}, u32[]{:S(2)}) %collective-permute-start.2) | collective-permute-done | bytes 64 | tf_op jit(solution)/shard_map/ppermute | solution.py:332
  6.7 0.9 %copy-done.2 = s32[32,2048]{1,0:T(8,128)S(1)} copy-done((s32[32,2048]{1,0:T(8,128)S(1)}, s32[32,2048]{1,0:T(8,128)}, u32[]{:S(2)}) %copy-start.2) | copy-done | bytes 262168
  7.6 0.9 %copy-done.3 = s32[32,2048]{1,0:T(8,128)S(1)} copy-done((s32[32,2048]{1,0:T(8,128)S(1)}, s32[32,2048]{1,0:T(8,128)}, u32[]{:S(2)}) %copy-start.3) | copy-done | bytes 262168
  8.6 0.7 copy-done.5
  9.3 1.3 %field.1 = (f32[264,128]{1,0:T(8,128)S(1)}, f32[264,128]{1,0:T(8,128)S(1)}, f32[264,128]{1,0:T(8,128)S(1)}, f32[264,128]{1,0:T(8,128)S(1)}) custom-call(s32[3]{0:T(128)S(1)} %pad_add_fusion.me_ref, s32[2,4]{1,0:T(2,128)S(1)} %copy-done.5, s32[2,4]{1,0:T(2,128)S(1)} %collective-permute-done.refs_1_, s32[2,4]{1,0:T(2,128)S(1)} %collective-permute-done.1.refs_2_, ...), custom_call_target="tpu_custom_call" | custom-call | tf_op jit(solution)/shard_map/field/pallas_call | solution.py:336
  10.6 2.7 %collective-permute-start.5 = (f32[264,128]{1,0:T(8,128)S(1)}, f32[264,128]{1,0:T(8,128)S(1)}, u32[]{:S(2)}, u32[]{:S(2)}) collective-permute-start(f32[264,128]{1,0:T(8,128)S(1)} %get-tuple-element.18.refs_7_), channel_id=1, source_target_pairs={{0,8},{1,9},{2,10},{3,11},{4,12},{5,13},{6,14},{7,15},{8,0},{9,1},... | collective-permute-start | bytes 405512 | tf_op jit(solution)/shard_map/ppermute | solution.py:361
  13.3 1.3 %collective-permute-start.7 = (f32[264,128]{1,0:T(8,128)S(1)}, f32[264,128]{1,0:T(8,128)S(1)}, u32[]{:S(2)}, u32[]{:S(2)}) collective-permute-start(f32[264,128]{1,0:T(8,128)S(1)} %get-tuple-element.19), channel_id=1, source_target_pairs={{0,10},{1,11},{2,8},{3,9},{4,14},{5,15},{6,12},{7,13},{8,2},{9,3},... | collective-permute-start | bytes 405512 | tf_op jit(solution)/shard_map/ppermute | solution.py:361
  14.5 0.5 collective-permute-start.6
  15.1 3.6 %collective-permute-start.9 = (f32[264,128]{1,0:T(8,128)S(1)}, f32[264,128]{1,0:T(8,128)S(1)}, u32[]{:S(2)}, u32[]{:S(2)}) collective-permute-start(f32[264,128]{1,0:T(8,128)S(1)} %get-tuple-element.20), channel_id=1, source_target_pairs={{0,12},{1,13},{2,14},{3,15},{4,8},{5,9},{6,10},{7,11},{8,4},{9,5},... | collective-permute-start | bytes 405512 | tf_op jit(solution)/shard_map/ppermute | solution.py:361
  18.7 8.1 %collective-permute-done.5.refs_0_ = f32[264,128]{1,0:T(8,128)S(1)} collective-permute-done((f32[264,128]{1,0:T(8,128)S(1)}, f32[264,128]{1,0:T(8,128)S(1)}, u32[]{:S(2)}, u32[]{:S(2)}) %collective-permute-start.5) | collective-permute-done | bytes 135200 | tf_op jit(solution)/shard_map/ppermute | solution.py:361
  26.8 4.0 %collective-permute-start.11 = (f32[264,128]{1,0:T(8,128)S(1)}, f32[264,128]{1,0:T(8,128)S(1)}, u32[]{:S(2)}, u32[]{:S(2)}) collective-permute-start(f32[264,128]{1,0:T(8,128)S(1)} %get-tuple-element.21), channel_id=1, source_target_pairs={{0,14},{1,15},{2,12},{3,13},{4,10},{5,11},{6,8},{7,9},{8,6},{9,7},... | collective-permute-start | bytes 405512 | tf_op jit(solution)/shard_map/ppermute | solution.py:361
  30.8 3.9 %collective-permute-done.11.refs_6_ = f32[264,128]{1,0:T(8,128)S(1)} collective-permute-done((f32[264,128]{1,0:T(8,128)S(1)}, f32[264,128]{1,0:T(8,128)S(1)}, u32[]{:S(2)}, u32[]{:S(2)}) %collective-permute-start.11) | collective-permute-done | bytes 135200 | tf_op jit(solution)/shard_map/ppermute | solution.py:361
  34.7 3.5 %collective-permute-done.10.refs_5_ = f32[264,128]{1,0:T(8,128)S(1)} collective-permute-done((f32[264,128]{1,0:T(8,128)S(1)}, f32[264,128]{1,0:T(8,128)S(1)}, u32[]{:S(2)}, u32[]{:S(2)}) %collective-permute-start.10) | collective-permute-done | bytes 135200 | tf_op jit(solution)/shard_map/ppermute | solution.py:361
  38.2 1.0 %copy-done = bf16[2,16,16,512]{3,2,1,0:T(8,128)(2,1)S(1)} copy-done((bf16[2,16,16,512]{3,2,1,0:T(8,128)(2,1)S(1)}, bf16[2,16,16,512]{3,2,1,0:T(8,128)(2,1)}, u32[]{:S(2)}) %copy-start) | copy-done | bytes 524312
  39.3 1.0 %copy-done.1 = bf16[2,8,2,16,512]{4,3,2,1,0:T(8,128)(2,1)S(1)} copy-done((bf16[2,8,2,16,512]{4,3,2,1,0:T(8,128)(2,1)S(1)}, bf16[2,8,2,16,512]{4,3,2,1,0:T(8,128)(2,1)}, u32[]{:S(2)}) %copy-start.1) | copy-done | bytes 524312
  40.3 0.9 %copy-done.4 = f32[64,512]{1,0:T(8,128)S(1)} copy-done((f32[64,512]{1,0:T(8,128)S(1)}, f32[64,512]{1,0:T(8,128)}, u32[]{:S(2)}) %copy-start.4) | copy-done | bytes 131096
  41.2 4.4 %transform.1 = (f32[4,2,16,512]{3,2,1,0:T(8,128)S(1)}, f32[4,2,16,512]{3,2,1,0:T(8,128)S(1)}, f32[4,2,16,512]{3,2,1,0:T(8,128)S(1)}, f32[4,2,16,512]{3,2,1,0:T(8...) custom-call(s32[1]{0:T(128)} %bitcast.me_ref, ...), custom_call_target="tpu_custom_call" | custom-call | tf_op jit(solution)/shard_map/transform/pallas_call | solution.py:363
  45.6 2.0 %collective-permute-start.12 = (f32[4,2,16,512]{3,2,1,0:T(8,128)S(1)}, f32[4,2,16,512]{3,2,1,0:T(8,128)S(1)}, u32[]{:S(2)}, u32[]{:S(2)}) collective-permute-start(f32[4,2,16,512]{3,2,1,0:T(8,128)S(1)} %get-tuple-element.22), channel_id=1, source_target_pairs={{0,7},{1,6},{2,5},{3,4},{4,3},{5,2},{6,1},{7,0},{8,15},{9,14},{10,... | collective-permute-start | bytes 786440 | tf_op jit(solution)/shard_map/ppermute | solution.py:432
  47.6 1.9 %collective-permute-start.13 = (f32[4,2,16,512]{3,2,1,0:T(8,128)S(1)}, f32[4,2,16,512]{3,2,1,0:T(8,128)S(1)}, u32[]{:S(2)}, u32[]{:S(2)}) collective-permute-start(f32[4,2,16,512]{3,2,1,0:T(8,128)S(1)} %get-tuple-element.23), channel_id=1, source_target_pairs={{0,6},{1,7},{2,4},{3,5},{4,2},{5,3},{6,0},{7,1},{8,14},{9,15},{10,... | collective-permute-start | bytes 786440 | tf_op jit(solution)/shard_map/ppermute | solution.py:432
  49.5 0.4 collective-permute-start.19
  49.9 1.6 %collective-permute-start.14 = (f32[4,2,16,512]{3,2,1,0:T(8,128)S(1)}, f32[4,2,16,512]{3,2,1,0:T(8,128)S(1)}, u32[]{:S(2)}, u32[]{:S(2)}) collective-permute-start(f32[4,2,16,512]{3,2,1,0:T(8,128)S(1)} %get-tuple-element.24), channel_id=1, source_target_pairs={{0,5},{1,4},{2,7},{3,6},{4,1},{5,0},{6,3},{7,2},{8,13},{9,12},{10,... | collective-permute-start | bytes 786440 | tf_op jit(solution)/shard_map/ppermute | solution.py:432
  51.5 1.6 %collective-permute-done.19.refs_9_ = f32[8,128]{1,0:T(8,128)S(1)} collective-permute-done((f32[8,128]{1,0:T(8,128)S(1)}, f32[8,128]{1,0:T(8,128)S(1)}, u32[]{:S(2)}, u32[]{:S(2)}) %collective-permute-start.19) | collective-permute-done | bytes 4128 | tf_op jit(solution)/shard_map/ppermute | solution.py:314
  53.1 0.6 collective-permute-done.12.refs_0_
  53.7 1.9 %collective-permute-start.17 = (f32[4,2,16,512]{3,2,1,0:T(8,128)S(1)}, f32[4,2,16,512]{3,2,1,0:T(8,128)S(1)}, u32[]{:S(2)}, u32[]{:S(2)}) collective-permute-start(f32[4,2,16,512]{3,2,1,0:T(8,128)S(1)} %get-tuple-element.27), channel_id=1, source_target_pairs={{0,2},{1,3},{2,0},{3,1},{4,6},{5,7},{6,4},{7,5},{8,10},{9,11},{10,... | collective-permute-start | bytes 786440 | tf_op jit(solution)/shard_map/ppermute | solution.py:432
  55.6 6.7 %collective-permute-done.13.refs_1_ = f32[4,2,16,512]{3,2,1,0:T(8,128)S(1)} collective-permute-done((f32[4,2,16,512]{3,2,1,0:T(8,128)S(1)}, f32[4,2,16,512]{3,2,1,0:T(8,128)S(1)}, u32[]{:S(2)}, u32[]{:S(2)}) %collective-permute-start.13) | collective-permute-done | bytes 262176 | tf_op jit(solution)/shard_map/ppermute | solution.py:432
  62.3 2.3 %collective-permute-done.14.refs_2_ = f32[4,2,16,512]{3,2,1,0:T(8,128)S(1)} collective-permute-done((f32[4,2,16,512]{3,2,1,0:T(8,128)S(1)}, f32[4,2,16,512]{3,2,1,0:T(8,128)S(1)}, u32[]{:S(2)}, u32[]{:S(2)}) %collective-permute-start.14) | collective-permute-done | bytes 262176 | tf_op jit(solution)/shard_map/ppermute | solution.py:432
  64.6 7.0 %collective-permute-done.15.refs_3_ = f32[4,2,16,512]{3,2,1,0:T(8,128)S(1)} collective-permute-done((f32[4,2,16,512]{3,2,1,0:T(8,128)S(1)}, f32[4,2,16,512]{3,2,1,0:T(8,128)S(1)}, u32[]{:S(2)}, u32[]{:S(2)}) %collective-permute-start.15) | collective-permute-done | bytes 262176 | tf_op jit(solution)/shard_map/ppermute | solution.py:432
  71.7 0.3 collective-permute-done.17.refs_5_
  72.0 2.4 %merge.1 = f32[2,32,8192]{2,1,0:T(8,128)} custom-call(s32[1]{0:T(128)} %bitcast.me_ref, f32[4,2,16,512]{3,2,1,0:T(8,128)S(1)} %collective-permute-done.12.refs_0_, f32[4,2,16,512]{3,2,1,0:T(8,128)S(1)} %collective-permute-done.13.refs_1_, f32[4,2,16,512]{3,2,1,0:T(8,128)S(1)} %collective-permute-done.14.refs_2_, ...), custom_call_target="tpu_custom_call" | custom-call | tf_op jit(solution)/shard_map/merge/pallas_call | solution.py:436
  (24 shorter events, 0.4 us)
Async XLA Ops:
  0.0 6.7 %collective-permute-start.3 = (s32[32,2048]{1,0:T(8,128)}, s32[32,2048]{1,0:T(8,128)S(1)}, u32[]{:S(2)}, u32[]{:S(2)}) collective-permute-start(s32[32,2048]{1,0:T(8,128)} %refs_4_.1), channel_id=1, source_target_pairs={{0,1},{1,0},{2,3},{3,2},{4,5},{5,4},{6,7},{7,6},{8,9},{9,8},{10,11... | collective-permute-start | bytes 786440 | tf_op jit(solution)/shard_map/ppermute | solution.py:333
  0.5 6.2 %collective-permute-start.4 = (s32[32,2048]{1,0:T(8,128)}, s32[32,2048]{1,0:T(8,128)S(1)}, u32[]{:S(2)}, u32[]{:S(2)}) collective-permute-start(s32[32,2048]{1,0:T(8,128)} %refs_5_.1), channel_id=1, source_target_pairs={{0,1},{1,0},{2,3},{3,2},{4,5},{5,4},{6,7},{7,6},{8,9},{9,8},{10,11... | collective-permute-start | bytes 786440 | tf_op jit(solution)/shard_map/ppermute | solution.py:333
  0.5 4.7 %collective-permute-start.1 = (s32[2,4]{1,0:T(2,128)}, s32[2,4]{1,0:T(2,128)S(1)}, u32[]{:S(2)}, u32[]{:S(2)}) collective-permute-start(s32[2,4]{1,0:T(2,128)} %refs_0_.1), channel_id=1, source_target_pairs={{0,16},{16,0},{1,17},{17,1},{2,18},{18,2},{3,19},{19,3},{4,20},{20... | collective-permute-start | bytes 104 | tf_op jit(solution)/shard_map/ppermute | solution.py:314
  3.5 1.8 %collective-permute-start = (s32[2,4]{1,0:T(2,128)}, s32[2,4]{1,0:T(2,128)S(1)}, u32[]{:S(2)}, u32[]{:S(2)}) collective-permute-start(s32[2,4]{1,0:T(2,128)} %refs_0_.1), channel_id=1, source_target_pairs={{0,1},{1,0},{2,3},{3,2},{4,5},{5,4},{6,7},{7,6},{8,9},{9,8},{10,11... | collective-permute-start | bytes 104 | tf_op jit(solution)/shard_map/ppermute | solution.py:333
  3.5 3.2 %collective-permute-start.2 = (s32[2,4]{1,0:T(2,128)}, s32[2,4]{1,0:T(2,128)S(1)}, u32[]{:S(2)}, u32[]{:S(2)}) collective-permute-start(s32[2,4]{1,0:T(2,128)} %refs_0_.1), channel_id=1, source_target_pairs={{0,17},{1,16},{2,19},{3,18},{4,21},{5,20},{6,23},{7,22},{8,25},{9,... | collective-permute-start | bytes 104 | tf_op jit(solution)/shard_map/ppermute | solution.py:332
  6.7 1.0 %copy-start.2 = (s32[32,2048]{1,0:T(8,128)S(1)}, s32[32,2048]{1,0:T(8,128)}, u32[]{:S(2)}) copy-start(s32[32,2048]{1,0:T(8,128)} %refs_4_.1) | copy-start | bytes 786436
  7.6 0.9 %copy-start.3 = (s32[32,2048]{1,0:T(8,128)S(1)}, s32[32,2048]{1,0:T(8,128)}, u32[]{:S(2)}) copy-start(s32[32,2048]{1,0:T(8,128)} %refs_5_.1) | copy-start | bytes 786436
  8.6 0.7 copy-start.5
  10.6 16.1 %collective-permute-start.5 = (f32[264,128]{1,0:T(8,128)S(1)}, f32[264,128]{1,0:T(8,128)S(1)}, u32[]{:S(2)}, u32[]{:S(2)}) collective-permute-start(f32[264,128]{1,0:T(8,128)S(1)} %get-tuple-element.18.refs_7_), channel_id=1, source_target_pairs={{0,8},{1,9},{2,10},{3,11},{4,12},{5,13},{6,14},{7,15},{8,0},{9,1},... | collective-permute-start | bytes 405512 | tf_op jit(solution)/shard_map/ppermute | solution.py:361
  13.3 17.5 %collective-permute-start.7 = (f32[264,128]{1,0:T(8,128)S(1)}, f32[264,128]{1,0:T(8,128)S(1)}, u32[]{:S(2)}, u32[]{:S(2)}) collective-permute-start(f32[264,128]{1,0:T(8,128)S(1)} %get-tuple-element.19), channel_id=1, source_target_pairs={{0,10},{1,11},{2,8},{3,9},{4,14},{5,15},{6,12},{7,13},{8,2},{9,3},... | collective-permute-start | bytes 405512 | tf_op jit(solution)/shard_map/ppermute | solution.py:361
  14.5 16.3 %collective-permute-start.6 = (f32[264,128]{1,0:T(8,128)S(1)}, f32[264,128]{1,0:T(8,128)S(1)}, u32[]{:S(2)}, u32[]{:S(2)}) collective-permute-start(f32[264,128]{1,0:T(8,128)S(1)} %get-tuple-element.19), channel_id=1, source_target_pairs={{0,2},{1,3},{2,0},{3,1},{4,6},{5,7},{6,4},{7,5},{8,10},{9,11},{10,... | collective-permute-start | bytes 405512 | tf_op jit(solution)/shard_map/ppermute | solution.py:361
  15.1 15.7 %collective-permute-start.9 = (f32[264,128]{1,0:T(8,128)S(1)}, f32[264,128]{1,0:T(8,128)S(1)}, u32[]{:S(2)}, u32[]{:S(2)}) collective-permute-start(f32[264,128]{1,0:T(8,128)S(1)} %get-tuple-element.20), channel_id=1, source_target_pairs={{0,12},{1,13},{2,14},{3,15},{4,8},{5,9},{6,10},{7,11},{8,4},{9,5},... | collective-permute-start | bytes 405512 | tf_op jit(solution)/shard_map/ppermute | solution.py:361
  18.7 12.2 %collective-permute-start.8 = (f32[264,128]{1,0:T(8,128)S(1)}, f32[264,128]{1,0:T(8,128)S(1)}, u32[]{:S(2)}, u32[]{:S(2)}) collective-permute-start(f32[264,128]{1,0:T(8,128)S(1)} %get-tuple-element.20), channel_id=1, source_target_pairs={{0,4},{1,5},{2,6},{3,7},{4,0},{5,1},{6,2},{7,3},{8,12},{9,13},{10,... | collective-permute-start | bytes 405512 | tf_op jit(solution)/shard_map/ppermute | solution.py:361
  26.8 8.0 %collective-permute-start.11 = (f32[264,128]{1,0:T(8,128)S(1)}, f32[264,128]{1,0:T(8,128)S(1)}, u32[]{:S(2)}, u32[]{:S(2)}) collective-permute-start(f32[264,128]{1,0:T(8,128)S(1)} %get-tuple-element.21), channel_id=1, source_target_pairs={{0,14},{1,15},{2,12},{3,13},{4,10},{5,11},{6,8},{7,9},{8,6},{9,7},... | collective-permute-start | bytes 405512 | tf_op jit(solution)/shard_map/ppermute | solution.py:361
  30.7 7.5 %collective-permute-start.10 = (f32[264,128]{1,0:T(8,128)S(1)}, f32[264,128]{1,0:T(8,128)S(1)}, u32[]{:S(2)}, u32[]{:S(2)}) collective-permute-start(f32[264,128]{1,0:T(8,128)S(1)} %get-tuple-element.21), channel_id=1, source_target_pairs={{0,6},{1,7},{2,4},{3,5},{4,2},{5,3},{6,0},{7,1},{8,14},{9,15},{10,... | collective-permute-start | bytes 405512 | tf_op jit(solution)/shard_map/ppermute | solution.py:361
  38.2 1.0 %copy-start = (bf16[2,16,16,512]{3,2,1,0:T(8,128)(2,1)S(1)}, bf16[2,16,16,512]{3,2,1,0:T(8,128)(2,1)}, u32[]{:S(2)}) copy-start(bf16[2,16,16,512]{3,2,1,0:T(8,128)(2,1)} %constant.40.clone.refs_9_) | copy-start | bytes 1572868
  39.3 1.0 %copy-start.1 = (bf16[2,8,2,16,512]{4,3,2,1,0:T(8,128)(2,1)S(1)}, bf16[2,8,2,16,512]{4,3,2,1,0:T(8,128)(2,1)}, u32[]{:S(2)}) copy-start(bf16[2,8,2,16,512]{4,3,2,1,0:T(8,128)(2,1)} %constant.39.clone.refs_8_) | copy-start | bytes 1572868
  40.3 0.9 %copy-start.4 = (f32[64,512]{1,0:T(8,128)S(1)}, f32[64,512]{1,0:T(8,128)}, u32[]{:S(2)}) copy-start(f32[64,512]{1,0:T(8,128)} %constant.41.clone.refs_10_) | copy-start | bytes 393220
  45.6 8.1 %collective-permute-start.12 = (f32[4,2,16,512]{3,2,1,0:T(8,128)S(1)}, f32[4,2,16,512]{3,2,1,0:T(8,128)S(1)}, u32[]{:S(2)}, u32[]{:S(2)}) collective-permute-start(f32[4,2,16,512]{3,2,1,0:T(8,128)S(1)} %get-tuple-element.22), channel_id=1, source_target_pairs={{0,7},{1,6},{2,5},{3,4},{4,3},{5,2},{6,1},{7,0},{8,15},{9,14},{10,... | collective-permute-start | bytes 786440 | tf_op jit(solution)/shard_map/ppermute | solution.py:432
  47.6 14.7 %collective-permute-start.13 = (f32[4,2,16,512]{3,2,1,0:T(8,128)S(1)}, f32[4,2,16,512]{3,2,1,0:T(8,128)S(1)}, u32[]{:S(2)}, u32[]{:S(2)}) collective-permute-start(f32[4,2,16,512]{3,2,1,0:T(8,128)S(1)} %get-tuple-element.23), channel_id=1, source_target_pairs={{0,6},{1,7},{2,4},{3,5},{4,2},{5,3},{6,0},{7,1},{8,14},{9,15},{10,... | collective-permute-start | bytes 786440 | tf_op jit(solution)/shard_map/ppermute | solution.py:432
  49.5 3.6 %collective-permute-start.19 = (f32[8,128]{1,0:T(8,128)S(1)}, f32[8,128]{1,0:T(8,128)S(1)}, u32[]{:S(2)}, u32[]{:S(2)}) collective-permute-start(f32[8,128]{1,0:T(8,128)S(1)} %get-tuple-element.30.refs_8_), channel_id=1, source_target_pairs={{0,16},{16,0},{1,17},{17,1},{2,18},{18,2},{3,19},{19,3},{4,20},{20... | collective-permute-start | bytes 12296 | tf_op jit(solution)/shard_map/ppermute | solution.py:314
  49.9 14.7 %collective-permute-start.14 = (f32[4,2,16,512]{3,2,1,0:T(8,128)S(1)}, f32[4,2,16,512]{3,2,1,0:T(8,128)S(1)}, u32[]{:S(2)}, u32[]{:S(2)}) collective-permute-start(f32[4,2,16,512]{3,2,1,0:T(8,128)S(1)} %get-tuple-element.24), channel_id=1, source_target_pairs={{0,5},{1,4},{2,7},{3,6},{4,1},{5,0},{6,3},{7,2},{8,13},{9,12},{10,... | collective-permute-start | bytes 786440 | tf_op jit(solution)/shard_map/ppermute | solution.py:432
  51.5 20.1 %collective-permute-start.15 = (f32[4,2,16,512]{3,2,1,0:T(8,128)S(1)}, f32[4,2,16,512]{3,2,1,0:T(8,128)S(1)}, u32[]{:S(2)}, u32[]{:S(2)}) collective-permute-start(f32[4,2,16,512]{3,2,1,0:T(8,128)S(1)} %get-tuple-element.25), channel_id=1, source_target_pairs={{0,4},{1,5},{2,6},{3,7},{4,0},{5,1},{6,2},{7,3},{8,12},{9,13},{10,... | collective-permute-start | bytes 786440 | tf_op jit(solution)/shard_map/ppermute | solution.py:432
  53.1 18.6 %collective-permute-start.16 = (f32[4,2,16,512]{3,2,1,0:T(8,128)S(1)}, f32[4,2,16,512]{3,2,1,0:T(8,128)S(1)}, u32[]{:S(2)}, u32[]{:S(2)}) collective-permute-start(f32[4,2,16,512]{3,2,1,0:T(8,128)S(1)} %get-tuple-element.26), channel_id=1, source_target_pairs={{0,3},{1,2},{2,1},{3,0},{4,7},{5,6},{6,5},{7,4},{8,11},{9,10},{10,... | collective-permute-start | bytes 786440 | tf_op jit(solution)/shard_map/ppermute | solution.py:432
  53.7 18.3 %collective-permute-start.17 = (f32[4,2,16,512]{3,2,1,0:T(8,128)S(1)}, f32[4,2,16,512]{3,2,1,0:T(8,128)S(1)}, u32[]{:S(2)}, u32[]{:S(2)}) collective-permute-start(f32[4,2,16,512]{3,2,1,0:T(8,128)S(1)} %get-tuple-element.27), channel_id=1, source_target_pairs={{0,2},{1,3},{2,0},{3,1},{4,6},{5,7},{6,4},{7,5},{8,10},{9,11},{10,... | collective-permute-start | bytes 786440 | tf_op jit(solution)/shard_map/ppermute | solution.py:432
  62.3 9.7 %collective-permute-start.18 = (f32[4,2,16,512]{3,2,1,0:T(8,128)S(1)}, f32[4,2,16,512]{3,2,1,0:T(8,128)S(1)}, u32[]{:S(2)}, u32[]{:S(2)}) collective-permute-start(f32[4,2,16,512]{3,2,1,0:T(8,128)S(1)} %get-tuple-element.28), channel_id=1, source_target_pairs={{0,1},{1,0},{2,3},{3,2},{4,5},{5,4},{6,7},{7,6},{8,9},{9,8},{10,11... | collective-permute-start | bytes 786440 | tf_op jit(solution)/shard_map/ppermute | solution.py:432

commit v7 on v5

--- a/solution.py
+++ b/solution.py
@@ -18,7 +18,7 @@
 INNER = 256
 PAD = 4
 FINE = 16
-ORDER = (7, 6, 5, 4, 3, 2, 1)
+ORDER = (6, 4, 2, 7, 5, 3, 1)
 SPLITS = (4,)
 GROUP = 8
 
@@ -158,6 +158,7 @@
         tc.append(cos * fine_cos - sin * fine_sin)
         ts.append(sin * fine_cos + cos * fine_sin)
     tc, ts = jnp.concatenate(tc), jnp.concatenate(ts)
+    xs = []
     for r in range(rows):
         halves = []
         for part in range(2):
@@ -167,17 +168,22 @@
                 pieces.append(x_ref[:, at : at + plan.n1_dev, :].reshape(plan.n1, LANES))
             halves.append(jnp.concatenate(pieces, axis=1))
         real, imag = halves
-        x = jnp.concatenate([real * turn_cos - imag * turn_sin, real * turn_sin + imag * turn_cos], axis=0)
-        xh = x.astype(jnp.bfloat16)
-        xl = (x - xh.astype(jnp.float32)).astype(jnp.bfloat16)
-        y = outer(xh, w1[0]) + outer(xl, w1[0]) + outer(xh, w1[1])
-        yr, yi = y[:, : plan.k1], y[:, plan.k1 :]
-        f = jnp.concatenate([yr * tc + yi * ts, yi * tc - yr * ts], axis=0)
-        fh = f.astype(jnp.bfloat16)
-        fl = (f - fh.astype(jnp.float32)).astype(jnp.bfloat16)
-        z = inner(w2[0], fh) + inner(w2[1], fh) + inner(w2[0], fl)
+        xs.append(jnp.concatenate([real * turn_cos - imag * turn_sin, real * turn_sin + imag * turn_cos], axis=0))
+    x = jnp.concatenate(xs, axis=1)
+    xh = x.astype(jnp.bfloat16)
+    xl = (x - xh.astype(jnp.float32)).astype(jnp.bfloat16)
+    y = outer(jnp.concatenate([xh, xl, xh]), jnp.concatenate([w1[0], w1[0], w1[1]]))
+    fs = []
+    for r in range(rows):
+        yr, yi = y[r * INNER : (r + 1) * INNER, : plan.k1], y[r * INNER : (r + 1) * INNER, plan.k1 :]
+        fs.append(jnp.concatenate([yr * tc + yi * ts, yi * tc - yr * ts], axis=0))
+    f = jnp.concatenate(fs, axis=1)
+    fh = f.astype(jnp.bfloat16)
+    fl = (f - fh.astype(jnp.float32)).astype(jnp.bfloat16)
+    z = inner(jnp.concatenate([w2[0], w2[1], w2[0]], axis=1), jnp.concatenate([fh, fh, fl]))
+    for r in range(rows):
         for b in range(plan.group):
-            refs[b][r] = z[b * size : (b + 1) * size].reshape(2, plan.k2_dev, plan.k1)
+            refs[b][r] = z[b * size : (b + 1) * size, r * plan.k1 : (r + 1) * plan.k1].reshape(2, plan.k2_dev, plan.k1)
 
 
 def merge_kernel(plan, splits, me_ref, *refs):

time: 70.8 us -> 69.4 us (0.980)
  starting transfers between devices: 26.2 us -> 23.7 us
  waiting for transfers between devices: 34.2 us -> 35.4 us
    ppermute x7, starting transfers between devices: 7.2 us -> 4.69 us  [per_device(): lax.ppermute(made[b], 'col', [(q, q ^ b) for q in range(n_col)])]
    ppermute x2, waiting for transfers between devices: 2.05 us -> 3.59 us  [along_rows(): lax.ppermute(value, 'row', [(i, (i + d) % n_row) for i in range(n_row)])]
  transfers between devices with their start and end apart: 14 -> 14, of which waited for: 10 -> 11; matrix products, arithmetic and copies ran while one was open for 0% -> 0% of each run, Pallas kernels for 0% -> 0%
where the time goes in v7:
time: 69.4 us; the launch traced here: 68.9 us
  waiting for transfers between devices  35.4 us (51%)
  starting transfers between devices  23.7 us (34%)
  Pallas kernels  9.64 us (14%)
    ppermute x7, waiting for transfers between devices, per_device(): lax.ppermute(made[b], 'col', [(q, q ^ b) for q in range(n_col)])  16.9 us
    ppermute x4, waiting for transfers between devices, per_device(): lax.ppermute(info, 'col', [(q, q ^ 1 << bit) for q in range(n_col)])  14.9 us
    ppermute x4, starting transfers between devices, per_device(): lax.ppermute(info, 'col', [(q, q ^ 1 << bit) for q in range(n_col)])  8.36 us
    all_to_all x1, starting transfers between devices, per_device(): lax.all_to_all(packed, 'col', split_axis=0, concat_axis=0, tiled=True)  7.5 us
    ppermute x7, starting transfers between devices, per_device(): lax.ppermute(made[b], 'col', [(q, q ^ b) for q in range(n_col)])  4.69 us
    pallas_call x1, Pallas kernels, per_device(): pl.pallas_call(partial(transform_kernel, plan, sum(splits[:i]), rows), ou...  4.19 us
    ppermute x2, waiting for transfers between devices, along_rows(): lax.ppermute(value, 'row', [(i, (i + d) % n_row) for i in range(n_row)])  3.59 us
    ppermute x2, starting transfers between devices, along_rows(): lax.ppermute(value, 'row', [(i, (i + d) % n_row) for i in range(n_row)])  3.11 us
  transfers between devices with their start and end apart: 14, of which 11 were waited for; matrix products, arithmetic and copies ran while one was open for 0% of the time, Pallas kernels for 0%

profile of v7, /device:TPU:0, one launch (start us, length us, event | category | flops | bytes accessed | tf_op | source)
XLA Modules:
  0.0 68.9 jit_solution(15492231862519966172)
XLA Ops:
  0.0 3.1 %field.1 = (f32[2,1024,128]{2,1,0:T(8,128)}, f32[8,128]{1,0:T(8,128)}) custom-call(s32[2,4]{1,0:T(2,128)} %tiles_ref.1, s32[32,2048]{1,0:T(8,128)} %codes_ref.1, s32[32,2048]{1,0:T(8,128)} %mask_ref.1), custom_call_target="tpu_custom_call" | custom-call | tf_op jit(solution)/shard_map/field/pallas_call | solution.py:252
  3.1 7.5 %all-to-all-start = ((f32[16,128,128]{2,1,0:T(8,128)}), f32[16,128,128]{2,1,0:T(8,128)S(1)}, u32[]{:S(2)}, u32[]{:S(2)}) async-start(f32[16,128,128]{2,1,0:T(8,128)} %bitcast.6), calls=%async_computation | async-start | bytes 2097152 | tf_op jit(solution)/shard_map/all_to_all | solution.py:271
  10.6 1.6 %collective-permute-start = (s32[2,4]{1,0:T(2,128)S(1)}, s32[2,4]{1,0:T(2,128)S(1)}, u32[]{:S(2)}, u32[]{:S(2)}) collective-permute-start(s32[2,4]{1,0:T(2,128)S(1)} %copy-done.4), channel_id=1, source_target_pairs={{0,16},{16,0},{1,17},{17,1},{2,18},{18,2},{3,19},{19,3},{4,20},{20... | collective-permute-start | bytes 104 | tf_op jit(solution)/shard_map/ppermute | solution.py:240
  12.2 2.0 %collective-permute-done = s32[2,4]{1,0:T(2,128)S(1)} collective-permute-done((s32[2,4]{1,0:T(2,128)S(1)}, s32[2,4]{1,0:T(2,128)S(1)}, u32[]{:S(2)}, u32[]{:S(2)}) %collective-permute-start) | collective-permute-done | bytes 64 | tf_op jit(solution)/shard_map/ppermute | solution.py:240
  14.3 0.1 broadcast_select_fusion
  14.3 0.1 collective-permute-start.1
  14.4 1.2 %collective-permute-done.1 = f32[24,128]{1,0:T(8,128)S(1)} collective-permute-done((f32[24,128]{1,0:T(8,128)S(1)}, f32[24,128]{1,0:T(8,128)S(1)}, u32[]{:S(2)}, u32[]{:S(2)}) %collective-permute-start.1) | collective-permute-done | bytes 12320 | tf_op jit(solution)/shard_map/ppermute | solution.py:275
  15.6 1.9 %collective-permute-start.2 = (f32[24,128]{1,0:T(8,128)S(1)}, f32[24,128]{1,0:T(8,128)S(1)}, u32[]{:S(2)}, u32[]{:S(2)}) collective-permute-start(f32[24,128]{1,0:T(8,128)S(1)} %fusion.3), channel_id=1, source_target_pairs={{0,2},{1,3},{2,0},{3,1},{4,6},{5,7},{6,4},{7,5},{8,10},{9,11},{10,... | collective-permute-start | bytes 36872 | tf_op jit(solution)/shard_map/ppermute | solution.py:275
  17.5 1.8 %collective-permute-done.2 = f32[24,128]{1,0:T(8,128)S(1)} collective-permute-done((f32[24,128]{1,0:T(8,128)S(1)}, f32[24,128]{1,0:T(8,128)S(1)}, u32[]{:S(2)}, u32[]{:S(2)}) %collective-permute-start.2) | collective-permute-done | bytes 12320 | tf_op jit(solution)/shard_map/ppermute | solution.py:275
  19.3 1.9 %collective-permute-start.3 = (f32[24,128]{1,0:T(8,128)S(1)}, f32[24,128]{1,0:T(8,128)S(1)}, u32[]{:S(2)}, u32[]{:S(2)}) collective-permute-start(f32[24,128]{1,0:T(8,128)S(1)} %add.15), channel_id=1, source_target_pairs={{0,4},{1,5},{2,6},{3,7},{4,0},{5,1},{6,2},{7,3},{8,12},{9,13},{10,... | collective-permute-start | bytes 36872 | tf_op jit(solution)/shard_map/ppermute | solution.py:275
  21.2 7.7 %collective-permute-done.3 = f32[24,128]{1,0:T(8,128)S(1)} collective-permute-done((f32[24,128]{1,0:T(8,128)S(1)}, f32[24,128]{1,0:T(8,128)S(1)}, u32[]{:S(2)}, u32[]{:S(2)}) %collective-permute-start.3) | collective-permute-done | bytes 12320 | tf_op jit(solution)/shard_map/ppermute | solution.py:275
  28.9 4.4 %collective-permute-start.4 = (f32[24,128]{1,0:T(8,128)S(1)}, f32[24,128]{1,0:T(8,128)S(1)}, u32[]{:S(2)}, u32[]{:S(2)}) collective-permute-start(f32[24,128]{1,0:T(8,128)S(1)} %add.16), channel_id=1, source_target_pairs={{0,8},{1,9},{2,10},{3,11},{4,12},{5,13},{6,14},{7,15},{8,0},{9,1},... | collective-permute-start | bytes 36872 | tf_op jit(solution)/shard_map/ppermute | solution.py:275
  33.3 4.3 %collective-permute-done.4 = f32[24,128]{1,0:T(8,128)S(1)} collective-permute-done((f32[24,128]{1,0:T(8,128)S(1)}, f32[24,128]{1,0:T(8,128)S(1)}, u32[]{:S(2)}, u32[]{:S(2)}) %collective-permute-start.4) | collective-permute-done | bytes 12320 | tf_op jit(solution)/shard_map/ppermute | solution.py:275
  37.7 0.0 all-to-all-done.x_ref
  37.7 4.2 %transform.1 = (f32[4,2,16,512]{3,2,1,0:T(8,128)S(1)}, f32[4,2,16,512]{3,2,1,0:T(8,128)S(1)}, f32[4,2,16,512]{3,2,1,0:T(8,128)S(1)}, f32[4,2,16,512]{3,2,1,0:T(8...) custom-call(s32[1]{0:T(128)} %bitcast.me_ref, ...), custom_call_target="tpu_custom_call" | custom-call | tf_op jit(solution)/shard_map/transform/pallas_call | solution.py:284
  41.9 0.8 %collective-permute-start.5 = (f32[4,2,16,512]{3,2,1,0:T(8,128)S(1)}, f32[4,2,16,512]{3,2,1,0:T(8,128)S(1)}, u32[]{:S(2)}, u32[]{:S(2)}) collective-permute-start(f32[4,2,16,512]{3,2,1,0:T(8,128)S(1)} %get-tuple-element.17), channel_id=1, source_target_pairs={{0,6},{1,7},{2,4},{3,5},{4,2},{5,3},{6,0},{7,1},{8,14},{9,15},{10,... | collective-permute-start | bytes 786440 | tf_op jit(solution)/shard_map/ppermute | solution.py:292
  42.7 2.2 %collective-permute-start.6 = (f32[4,2,16,512]{3,2,1,0:T(8,128)S(1)}, f32[4,2,16,512]{3,2,1,0:T(8,128)S(1)}, u32[]{:S(2)}, u32[]{:S(2)}) collective-permute-start(f32[4,2,16,512]{3,2,1,0:T(8,128)S(1)} %get-tuple-element.18), channel_id=1, source_target_pairs={{0,4},{1,5},{2,6},{3,7},{4,0},{5,1},{6,2},{7,3},{8,12},{9,13},{10,... | collective-permute-start | bytes 786440 | tf_op jit(solution)/shard_map/ppermute | solution.py:292
  44.9 1.5 %collective-permute-start.12 = (f32[8,128]{1,0:T(8,128)S(1)}, f32[8,128]{1,0:T(8,128)S(1)}, u32[]{:S(2)}, u32[]{:S(2)}) collective-permute-start(f32[8,128]{1,0:T(8,128)S(1)} %slice.4.refs_8_), channel_id=1, source_target_pairs={{0,16},{16,0},{1,17},{17,1},{2,18},{18,2},{3,19},{19,3},{4,20},{20... | collective-permute-start | bytes 12296 | tf_op jit(solution)/shard_map/ppermute | solution.py:240
  46.4 0.5 collective-permute-start.7
  47.0 0.0 collective-permute-start.8
  47.0 1.5 %collective-permute-done.12.refs_9_ = f32[8,128]{1,0:T(8,128)S(1)} collective-permute-done((f32[8,128]{1,0:T(8,128)S(1)}, f32[8,128]{1,0:T(8,128)S(1)}, u32[]{:S(2)}, u32[]{:S(2)}) %collective-permute-start.12) | collective-permute-done | bytes 4128 | tf_op jit(solution)/shard_map/ppermute | solution.py:240
  48.5 1.1 %collective-permute-start.9 = (f32[4,2,16,512]{3,2,1,0:T(8,128)S(1)}, f32[4,2,16,512]{3,2,1,0:T(8,128)S(1)}, u32[]{:S(2)}, u32[]{:S(2)}) collective-permute-start(f32[4,2,16,512]{3,2,1,0:T(8,128)S(1)} %get-tuple-element.21), channel_id=1, source_target_pairs={{0,5},{1,4},{2,7},{3,6},{4,1},{5,0},{6,3},{7,2},{8,13},{9,12},{10,... | collective-permute-start | bytes 786440 | tf_op jit(solution)/shard_map/ppermute | solution.py:292
  49.6 2.4 %collective-permute-done.5.refs_0_ = f32[4,2,16,512]{3,2,1,0:T(8,128)S(1)} collective-permute-done((f32[4,2,16,512]{3,2,1,0:T(8,128)S(1)}, f32[4,2,16,512]{3,2,1,0:T(8,128)S(1)}, u32[]{:S(2)}, u32[]{:S(2)}) %collective-permute-start.5) | collective-permute-done | bytes 262176 | tf_op jit(solution)/shard_map/ppermute | solution.py:292
  52.1 0.0 collective-permute-start.10
  52.1 5.7 %collective-permute-done.6.refs_1_ = f32[4,2,16,512]{3,2,1,0:T(8,128)S(1)} collective-permute-done((f32[4,2,16,512]{3,2,1,0:T(8,128)S(1)}, f32[4,2,16,512]{3,2,1,0:T(8,128)S(1)}, u32[]{:S(2)}, u32[]{:S(2)}) %collective-permute-start.6) | collective-permute-done | bytes 262176 | tf_op jit(solution)/shard_map/ppermute | solution.py:292
  57.8 0.0 collective-permute-start.11
  57.8 3.5 %collective-permute-done.7.refs_2_ = f32[4,2,16,512]{3,2,1,0:T(8,128)S(1)} collective-permute-done((f32[4,2,16,512]{3,2,1,0:T(8,128)S(1)}, f32[4,2,16,512]{3,2,1,0:T(8,128)S(1)}, u32[]{:S(2)}, u32[]{:S(2)}) %collective-permute-start.7) | collective-permute-done | bytes 262176 | tf_op jit(solution)/shard_map/ppermute | solution.py:292
  61.3 0.0 collective-permute-done.8.refs_3_
  61.3 4.5 %collective-permute-done.9.refs_4_ = f32[4,2,16,512]{3,2,1,0:T(8,128)S(1)} collective-permute-done((f32[4,2,16,512]{3,2,1,0:T(8,128)S(1)}, f32[4,2,16,512]{3,2,1,0:T(8,128)S(1)}, u32[]{:S(2)}, u32[]{:S(2)}) %collective-permute-start.9) | collective-permute-done | bytes 262176 | tf_op jit(solution)/shard_map/ppermute | solution.py:292
  65.8 0.8 %collective-permute-done.10.refs_5_ = f32[4,2,16,512]{3,2,1,0:T(8,128)S(1)} collective-permute-done((f32[4,2,16,512]{3,2,1,0:T(8,128)S(1)}, f32[4,2,16,512]{3,2,1,0:T(8,128)S(1)}, u32[]{:S(2)}, u32[]{:S(2)}) %collective-permute-start.10) | collective-permute-done | bytes 262176 | tf_op jit(solution)/shard_map/ppermute | solution.py:292
  66.5 0.0 collective-permute-done.11.refs_6_
  66.6 2.4 %merge.1 = f32[2,32,8192]{2,1,0:T(8,128)} custom-call(s32[1]{0:T(128)} %bitcast.me_ref, f32[4,2,16,512]{3,2,1,0:T(8,128)S(1)} %collective-permute-done.5.refs_0_, f32[4,2,16,512]{3,2,1,0:T(8,128)S(1)} %collective-permute-done.6.refs_1_, f32[4,2,16,512]{3,2,1,0:T(8,128)S(1)} %collective-permute-done.7.refs_2_, ...), custom_call_target="tpu_custom_call" | custom-call | tf_op jit(solution)/shard_map/merge/pallas_call | solution.py:296
  (20 shorter events, 0.1 us)
Async XLA Ops:
  0.0 37.7 %copy-start.2 = (f32[64,512]{1,0:T(8,128)S(1)}, f32[64,512]{1,0:T(8,128)}, u32[]{:S(2)}) copy-start(f32[64,512]{1,0:T(8,128)} %constant.24.clone.twist_ref) | copy-start | bytes 393220
  0.0 37.7 %copy-start = (bf16[2,16,16,512]{3,2,1,0:T(8,128)(2,1)S(1)}, bf16[2,16,16,512]{3,2,1,0:T(8,128)(2,1)}, u32[]{:S(2)}) copy-start(bf16[2,16,16,512]{3,2,1,0:T(8,128)(2,1)} %constant.23.clone.inner_ref) | copy-start | bytes 1572868
  0.0 37.7 %copy-start.1 = (bf16[2,256,512]{2,1,0:T(8,128)(2,1)S(1)}, bf16[2,256,512]{2,1,0:T(8,128)(2,1)}, u32[]{:S(2)}) copy-start(bf16[2,256,512]{2,1,0:T(8,128)(2,1)} %constant.22.clone.outer_ref) | copy-start | bytes 1572868
  0.0 10.6 %copy-start.4 = (s32[2,4]{1,0:T(2,128)S(1)}, s32[2,4]{1,0:T(2,128)}, u32[]{:S(2)}) copy-start(s32[2,4]{1,0:T(2,128)} %tiles_ref.1) | copy-start | bytes 100
  3.1 11.3 %copy-start.3 = (f32[8,128]{1,0:T(8,128)S(1)}, f32[8,128]{1,0:T(8,128)}, u32[]{:S(2)}) copy-start(f32[8,128]{1,0:T(8,128)} %get-tuple-element.15) | copy-start | bytes 12292
  3.1 34.6 %all-to-all-start = ((f32[16,128,128]{2,1,0:T(8,128)}), f32[16,128,128]{2,1,0:T(8,128)S(1)}, u32[]{:S(2)}, u32[]{:S(2)}) async-start(f32[16,128,128]{2,1,0:T(8,128)} %bitcast.6), calls=%async_computation | async-start | bytes 2097152 | tf_op jit(solution)/shard_map/all_to_all | solution.py:271
  10.6 3.6 %collective-permute-start = (s32[2,4]{1,0:T(2,128)S(1)}, s32[2,4]{1,0:T(2,128)S(1)}, u32[]{:S(2)}, u32[]{:S(2)}) collective-permute-start(s32[2,4]{1,0:T(2,128)S(1)} %copy-done.4), channel_id=1, source_target_pairs={{0,16},{16,0},{1,17},{17,1},{2,18},{18,2},{3,19},{19,3},{4,20},{20... | collective-permute-start | bytes 104 | tf_op jit(solution)/shard_map/ppermute | solution.py:240
  14.3 1.2 %collective-permute-start.1 = (f32[24,128]{1,0:T(8,128)S(1)}, f32[24,128]{1,0:T(8,128)S(1)}, u32[]{:S(2)}, u32[]{:S(2)}) collective-permute-start(f32[24,128]{1,0:T(8,128)S(1)} %pad_maximum_fusion), channel_id=1, source_target_pairs={{0,1},{1,0},{2,3},{3,2},{4,5},{5,4},{6,7},{7,6},{8,9},{9,8},{10,11... | collective-permute-start | bytes 36872 | tf_op jit(solution)/shard_map/ppermute | solution.py:275
  15.6 3.7 %collective-permute-start.2 = (f32[24,128]{1,0:T(8,128)S(1)}, f32[24,128]{1,0:T(8,128)S(1)}, u32[]{:S(2)}, u32[]{:S(2)}) collective-permute-start(f32[24,128]{1,0:T(8,128)S(1)} %fusion.3), channel_id=1, source_target_pairs={{0,2},{1,3},{2,0},{3,1},{4,6},{5,7},{6,4},{7,5},{8,10},{9,11},{10,... | collective-permute-start | bytes 36872 | tf_op jit(solution)/shard_map/ppermute | solution.py:275
  19.3 9.6 %collective-permute-start.3 = (f32[24,128]{1,0:T(8,128)S(1)}, f32[24,128]{1,0:T(8,128)S(1)}, u32[]{:S(2)}, u32[]{:S(2)}) collective-permute-start(f32[24,128]{1,0:T(8,128)S(1)} %add.15), channel_id=1, source_target_pairs={{0,4},{1,5},{2,6},{3,7},{4,0},{5,1},{6,2},{7,3},{8,12},{9,13},{10,... | collective-permute-start | bytes 36872 | tf_op jit(solution)/shard_map/ppermute | solution.py:275
  28.9 8.8 %collective-permute-start.4 = (f32[24,128]{1,0:T(8,128)S(1)}, f32[24,128]{1,0:T(8,128)S(1)}, u32[]{:S(2)}, u32[]{:S(2)}) collective-permute-start(f32[24,128]{1,0:T(8,128)S(1)} %add.16), channel_id=1, source_target_pairs={{0,8},{1,9},{2,10},{3,11},{4,12},{5,13},{6,14},{7,15},{8,0},{9,1},... | collective-permute-start | bytes 36872 | tf_op jit(solution)/shard_map/ppermute | solution.py:275
  41.9 10.2 %collective-permute-start.5 = (f32[4,2,16,512]{3,2,1,0:T(8,128)S(1)}, f32[4,2,16,512]{3,2,1,0:T(8,128)S(1)}, u32[]{:S(2)}, u32[]{:S(2)}) collective-permute-start(f32[4,2,16,512]{3,2,1,0:T(8,128)S(1)} %get-tuple-element.17), channel_id=1, source_target_pairs={{0,6},{1,7},{2,4},{3,5},{4,2},{5,3},{6,0},{7,1},{8,14},{9,15},{10,... | collective-permute-start | bytes 786440 | tf_op jit(solution)/shard_map/ppermute | solution.py:292
  42.7 15.1 %collective-permute-start.6 = (f32[4,2,16,512]{3,2,1,0:T(8,128)S(1)}, f32[4,2,16,512]{3,2,1,0:T(8,128)S(1)}, u32[]{:S(2)}, u32[]{:S(2)}) collective-permute-start(f32[4,2,16,512]{3,2,1,0:T(8,128)S(1)} %get-tuple-element.18), channel_id=1, source_target_pairs={{0,4},{1,5},{2,6},{3,7},{4,0},{5,1},{6,2},{7,3},{8,12},{9,13},{10,... | collective-permute-start | bytes 786440 | tf_op jit(solution)/shard_map/ppermute | solution.py:292
  44.9 3.6 %collective-permute-start.12 = (f32[8,128]{1,0:T(8,128)S(1)}, f32[8,128]{1,0:T(8,128)S(1)}, u32[]{:S(2)}, u32[]{:S(2)}) collective-permute-start(f32[8,128]{1,0:T(8,128)S(1)} %slice.4.refs_8_), channel_id=1, source_target_pairs={{0,16},{16,0},{1,17},{17,1},{2,18},{18,2},{3,19},{19,3},{4,20},{20... | collective-permute-start | bytes 12296 | tf_op jit(solution)/shard_map/ppermute | solution.py:240
  46.4 14.9 %collective-permute-start.7 = (f32[4,2,16,512]{3,2,1,0:T(8,128)S(1)}, f32[4,2,16,512]{3,2,1,0:T(8,128)S(1)}, u32[]{:S(2)}, u32[]{:S(2)}) collective-permute-start(f32[4,2,16,512]{3,2,1,0:T(8,128)S(1)} %get-tuple-element.19), channel_id=1, source_target_pairs={{0,2},{1,3},{2,0},{3,1},{4,6},{5,7},{6,4},{7,5},{8,10},{9,11},{10,... | collective-permute-start | bytes 786440 | tf_op jit(solution)/shard_map/ppermute | solution.py:292
  47.0 14.4 %collective-permute-start.8 = (f32[4,2,16,512]{3,2,1,0:T(8,128)S(1)}, f32[4,2,16,512]{3,2,1,0:T(8,128)S(1)}, u32[]{:S(2)}, u32[]{:S(2)}) collective-permute-start(f32[4,2,16,512]{3,2,1,0:T(8,128)S(1)} %get-tuple-element.20), channel_id=1, source_target_pairs={{0,7},{1,6},{2,5},{3,4},{4,3},{5,2},{6,1},{7,0},{8,15},{9,14},{10,... | collective-permute-start | bytes 786440 | tf_op jit(solution)/shard_map/ppermute | solution.py:292
  48.5 17.3 %collective-permute-start.9 = (f32[4,2,16,512]{3,2,1,0:T(8,128)S(1)}, f32[4,2,16,512]{3,2,1,0:T(8,128)S(1)}, u32[]{:S(2)}, u32[]{:S(2)}) collective-permute-start(f32[4,2,16,512]{3,2,1,0:T(8,128)S(1)} %get-tuple-element.21), channel_id=1, source_target_pairs={{0,5},{1,4},{2,7},{3,6},{4,1},{5,0},{6,3},{7,2},{8,13},{9,12},{10,... | collective-permute-start | bytes 786440 | tf_op jit(solution)/shard_map/ppermute | solution.py:292
  52.1 14.5 %collective-permute-start.10 = (f32[4,2,16,512]{3,2,1,0:T(8,128)S(1)}, f32[4,2,16,512]{3,2,1,0:T(8,128)S(1)}, u32[]{:S(2)}, u32[]{:S(2)}) collective-permute-start(f32[4,2,16,512]{3,2,1,0:T(8,128)S(1)} %get-tuple-element.22), channel_id=1, source_target_pairs={{0,3},{1,2},{2,1},{3,0},{4,7},{5,6},{6,5},{7,4},{8,11},{9,10},{10,... | collective-permute-start | bytes 786440 | tf_op jit(solution)/shard_map/ppermute | solution.py:292
  57.8 8.8 %collective-permute-start.11 = (f32[4,2,16,512]{3,2,1,0:T(8,128)S(1)}, f32[4,2,16,512]{3,2,1,0:T(8,128)S(1)}, u32[]{:S(2)}, u32[]{:S(2)}) collective-permute-start(f32[4,2,16,512]{3,2,1,0:T(8,128)S(1)} %get-tuple-element.23), channel_id=1, source_target_pairs={{0,1},{1,0},{2,3},{3,2},{4,5},{5,4},{6,7},{7,6},{8,9},{9,8},{10,11... | collective-permute-start | bytes 786440 | tf_op jit(solution)/shard_map/ppermute | solution.py:292

commit v8 on v6

--- a/solution.py
+++ b/solution.py
@@ -19,7 +19,7 @@
 PAD = 4
 FINE = 16
 CHIP_ORDER = (4, 1, 5, 2, 6, 3, 7)
-ORDER = (7, 6, 5, 4, 3, 2, 1)
+ORDER = (6, 4, 2, 7, 5, 3, 1)
 GROUP = 8
 
 
@@ -120,75 +120,94 @@
         open_ref[...] = open_ref[...] + total
 
 
+def own_kernel(plan, me_ref, tiles_ref, codes_ref, mask_ref, code_ref, kept_ref, open_ref):
+    half = plan.row_dev // 2
+    first = pl.multiple_of(me_ref[0] * half, half)
+    total = jnp.zeros((SUBS, LANES), jnp.int32)
+    for t in range(plan.row_dev // SUBS):
+        for j in range(plan.pupil_dev // LANES):
+            total = total + mask_ref[t * SUBS : (t + 1) * SUBS, j * LANES : (j + 1) * LANES]
+    open_ref[...] = total
+    for i in range(plan.pupil_dev // TILE_C):
+        lanes = slice(i * TILE_C, (i + 1) * TILE_C)
+        piston = jnp.int32(0)
+        for k in range(plan.row_dev // TILE_R):
+            piston = piston + jnp.where(first >= k * TILE_R, tiles_ref[k, i], 0)
+        code_ref[:, lanes] = codes_ref[:, lanes] + piston
+    kept_ref[...] = mask_ref[pl.ds(first, half), :]
+
+
 def chip_field_kernel(plan, me_ref, *refs):
     n_other = plan.n_row - 1
-    tiles, others, refs = refs[:2], (refs[2 : 2 + n_other], refs[2 + n_other : 2 + 2 * n_other]), refs[2 + 2 * n_other :]
-    codes_hbm, mask_hbm, near_codes_ref, near_mask_ref = refs[:4]
-    outs, (codes_ref, mask_ref, made_ref, sems) = refs[4:-4], refs[-4:]
+    others, refs = (refs[:n_other], refs[n_other : 2 * n_other]), refs[2 * n_other :]
+    near_tiles_ref, own_codes_ref, own_mask_ref, open_ref, near_codes_ref, near_mask_ref = refs[:6]
+    outs, made_ref = refs[6:-1], refs[-1]
     core, chip, row = me_ref[0], me_ref[1], me_ref[2]
     half = plan.row_dev // 2
     first = pl.multiple_of(core * half, half)
-    copies = [
-        pltpu.make_async_copy(codes_hbm, codes_ref, sems.at[0]),
-        pltpu.make_async_copy(mask_hbm, mask_ref, sems.at[1]),
-    ]
-    for copy in copies:
-        copy.start()
-    total = jnp.zeros((SUBS, LANES), jnp.int32)
+    total = open_ref[...]
+    for t in range(plan.row_dev // SUBS):
+        for j in range(plan.pupil_dev // LANES):
+            total = total + near_mask_ref[t * SUBS : (t + 1) * SUBS, j * LANES : (j + 1) * LANES]
+    total = total.astype(jnp.float32)
     stride = 2 * plan.lane_parts * plan.n1_dev
-    for owner in (1, 0):
-        if owner == 0:
-            for copy in copies:
-                copy.wait()
-        codes, mask = ((codes_ref, mask_ref), (near_codes_ref, near_mask_ref))[owner]
+    for owner in range(2):
         before = jnp.zeros((1, plan.pupil_dev // TILE_C), jnp.int32)
         for d, other in enumerate(others[owner]):
             before = before + jnp.where(row > d, jnp.sum(other[...], axis=0, keepdims=True), 0)
-        for k in range(plan.row_dev // TILE_R):
-            before = before + jnp.where(first >= k * TILE_R, tiles[owner][k : k + 1], 0)
-        for t in range(plan.row_dev // SUBS):
-            for j in range(plan.pupil_dev // LANES):
-                total = total + mask[t * SUBS : (t + 1) * SUBS, j * LANES : (j + 1) * LANES]
+        if owner == 1:
+            for k in range(plan.row_dev // TILE_R):
+                before = before + jnp.where(first >= k * TILE_R, near_tiles_ref[k : k + 1], 0)
+        codes, mask = ((own_codes_ref, own_mask_ref), (near_codes_ref, near_mask_ref))[owner]
         for t in range(half // SUBS):
-            at = pl.multiple_of(first + t * SUBS, SUBS)
+            rows = pl.ds(t * SUBS, SUBS) if owner == 0 else pl.ds(pl.multiple_of(first + t * SUBS, SUBS), SUBS)
             for j in range(plan.pupil_dev // LANES):
                 lanes = slice(j * LANES, (j + 1) * LANES)
                 column = j * LANES // TILE_C
                 piston = jnp.broadcast_to(before[:, column : column + 1], (SUBS, LANES))
-                code = (codes[pl.ds(at, SUBS), lanes] + piston) & (LEVELS - 1)
-                cos, sin, minus_cos, minus_sin = unit_phase(code)
-                amplitude = mask[pl.ds(at, SUBS), lanes].astype(jnp.float32)
+                cos, sin, minus_cos, minus_sin = unit_phase((codes[rows, lanes] + piston) & (LEVELS - 1))
+                amplitude = mask[rows, lanes].astype(jnp.float32)
                 real = cos * jnp.where(minus_cos, -amplitude, amplitude)
                 imag = sin * jnp.where(minus_sin, -amplitude, amplitude)
                 for part, value in enumerate((real, imag)):
                     start = (part * plan.lane_parts + j % plan.lane_parts) * plan.n1_dev + j // plan.lane_parts
                     made_ref[owner, pl.ds(t * SUBS * stride + start, SUBS, stride=stride), :] = value
-    own_rows = lax.rem(chip, len(outs))
+    own_rows = lax.rem(chip, plan.group // 2)
     for b, out in enumerate(outs):
-        source = pl.multiple_of((own_rows ^ b) * plan.chunk, plan.chunk)
+        source = pl.multiple_of((own_rows ^ b % (plan.group // 2)) * plan.chunk, plan.chunk)
         for i in range(plan.chunk // plan.n1_dev):
             for side in range(2):
                 block = made_ref[side ^ core, pl.ds(pl.multiple_of(source + i * plan.n1_dev, plan.n1_dev), plan.n1_dev), :]
                 out[(2 * i + side) * plan.n1_dev : (2 * i + side + 1) * plan.n1_dev, :] = block
-        out[2 * plan.chunk :, :] = total.astype(jnp.float32)
-
-
-def chip_transform_kernel(plan, order, me_ref, *refs):
+        out[2 * plan.chunk :, :] = total
+
+
+def tables_kernel(plan, blocks, me_ref, outer_ref, inner_ref, twist_ref, w1_ref, w2_ref, turn_ref):
+    me = me_ref[0]
+    w1, w2 = [], []
+    for s in range(2):
+        rows = [outer_ref[s, (me >> 1) ^ b if blocks > 1 else 0] for b in range(blocks)]
+        cos, sin = (jnp.concatenate([both[i] for both in rows]) for i in range(2))
+        w1.append(jnp.concatenate([jnp.concatenate([cos, sin]), jnp.concatenate([-sin, cos])], axis=1))
+        parts = []
+        for b in range(plan.group):
+            both = inner_ref[s, me ^ b]
+            parts.append(both)
+            parts.append(jnp.concatenate([-both[:, INNER:], both[:, :INNER]], axis=1))
+        w2.append(jnp.concatenate(parts))
+    w1_ref[...] = jnp.concatenate([w1[0], w1[0], w1[1]])
+    w2_ref[...] = jnp.concatenate([w2[0], w2[1], w2[0]], axis=1)
+    turn_ref[...] = twist_ref[...]
+
+
+def chip_transform_kernel(plan, order, *refs):
     n_chips = plan.n_col // 2
-    given = refs[:n_chips]
-    outer_ref, inner_ref, twist_ref = refs[n_chips : n_chips + 3]
-    outs, count_ref = refs[n_chips + 3 : -1], refs[-1]
-    chunks = [given[order.index(b)] for b in range(n_chips)]
-    me = me_ref[0]
-    chip = me >> 1
+    chunks = [refs[order.index(b)] for b in range(n_chips)]
+    tables, outs, count_ref = refs[n_chips : n_chips + 3], refs[n_chips + 3 : -1], refs[-1]
     count = chunks[0][2 * plan.chunk :, :]
     for chunk in chunks[1:]:
         count = count + chunk[2 * plan.chunk :, :]
     count_ref[...] = count
-    w1 = []
-    for s in range(2):
-        rows = [outer_ref[s, chip ^ b] for b in range(n_chips)]
-        w1.append([jnp.concatenate([both[i] for both in rows]) for i in range(2)])
     n1_chip = 2 * plan.n1_dev
 
     def part_of(r, part):
@@ -198,13 +217,11 @@
             pieces.append(jnp.concatenate([chunk[at : at + n1_chip, :] for chunk in chunks]))
         return jnp.concatenate(pieces, axis=1)
 
-    def field_of(r):
-        return jnp.concatenate([part_of(r, 0), part_of(r, 1)])
-
-    transform_rows(plan, me, plan.rows, field_of, w1, inner_ref, twist_ref, outs)
-
-
-def transform_kernel(plan, me_ref, info_ref, x_ref, outer_ref, inner_ref, twist_ref, *refs):
+    fields = [jnp.concatenate([part_of(r, 0), part_of(r, 1)]) for r in range(plan.rows)]
+    transform_rows(plan, fields, tables, outs)
+
+
+def transform_kernel(plan, info_ref, x_ref, *refs):
     chunk_row = plan.chunk // plan.rows
     info = info_ref[: plan.n_col]
     info = jnp.broadcast_to(info[:, None, :], (plan.n_col, plan.n1_dev, LANES)).reshape(plan.n1, LANES)
@@ -214,7 +231,6 @@
     turn_cos, turn_sin, minus_cos, minus_sin = unit_phase(before)
     turn_cos = jnp.where(minus_cos, -turn_cos, turn_cos)
     turn_sin = jnp.where(minus_sin, -turn_sin, turn_sin)
-    w1 = [[outer_ref[s, 0, i] for i in range(2)] for s in range(2)]
 
     def field_of(r):
         halves = []
@@ -227,55 +243,43 @@
         real, imag = halves
         return jnp.concatenate([real * turn_cos - imag * turn_sin, real * turn_sin + imag * turn_cos], axis=0)
 
-    transform_rows(plan, me_ref[0], plan.rows, field_of, w1, inner_ref, twist_ref, refs)
-
-
-def transform_rows(plan, me, rows, field_of, outer_parts, inner_ref, twist_ref, outs):
-    def outer(a, b):
-        return lax.dot_general(a, b, (((0,), (0,)), ((), ())), preferred_element_type=jnp.float32)
-
-    def inner(a, b):
-        return jnp.dot(a, b, preferred_element_type=jnp.float32)
-
-    k2_dev = plan.k2_dev
-    w1, w2 = [], []
-    for s in range(2):
-        cos, sin = outer_parts[s]
-        w1.append(jnp.concatenate([jnp.concatenate([cos, sin]), jnp.concatenate([-sin, cos])], axis=1))
-        blocks = []
-        for b in range(plan.group):
-            both = inner_ref[s, me ^ b]
-            cos, sin = both[:, :INNER], both[:, INNER:]
-            blocks.append(both)
-            blocks.append(jnp.concatenate([-sin, cos], axis=1))
-        w2.append(jnp.concatenate(blocks))
-    size = 2 * k2_dev
+    transform_rows(plan, [field_of(r) for r in range(plan.rows)], refs[:3], refs[3:])
+
+
+def transform_rows(plan, fields, tables, outs):
+    w1_ref, w2_ref, turn_ref = tables
+    size = 2 * plan.k2_dev
+    x = jnp.concatenate(fields, axis=1)
+    xh = x.astype(jnp.bfloat16)
+    xl = (x - xh.astype(jnp.float32)).astype(jnp.bfloat16)
+    y = lax.dot_general(
+        jnp.concatenate([xh, xl, xh]), w1_ref[...], (((0,), (0,)), ((), ())), preferred_element_type=jnp.float32
+    )
+    tc, ts = [], []
     count = INNER // FINE
-    fine_cos, fine_sin = twist_ref[2 * count : 2 * count + FINE], twist_ref[2 * count + FINE :]
-    tc, ts = [], []
+    fine_cos, fine_sin = turn_ref[2 * count : 2 * count + FINE], turn_ref[2 * count + FINE :]
     for a in range(count):
-        cos, sin = twist_ref[a : a + 1], twist_ref[count + a : count + a + 1]
+        cos, sin = turn_ref[a : a + 1], turn_ref[count + a : count + a + 1]
         tc.append(cos * fine_cos - sin * fine_sin)
         ts.append(sin * fine_cos + cos * fine_sin)
     tc, ts = jnp.concatenate(tc), jnp.concatenate(ts)
-    for r in range(rows):
-        x = field_of(r)
-        xh = x.astype(jnp.bfloat16)
-        xl = (x - xh.astype(jnp.float32)).astype(jnp.bfloat16)
-        y = outer(xh, w1[0]) + outer(xl, w1[0]) + outer(xh, w1[1])
-        yr, yi = y[:, : plan.k1], y[:, plan.k1 :]
-        f = jnp.concatenate([yr * tc + yi * ts, yi * tc - yr * ts], axis=0)
-        fh = f.astype(jnp.bfloat16)
-        fl = (f - fh.astype(jnp.float32)).astype(jnp.bfloat16)
-        z = inner(w2[0], fh) + inner(w2[1], fh) + inner(w2[0], fl)
+    fs = []
+    for r in range(plan.rows):
+        yr, yi = y[r * INNER : (r + 1) * INNER, : plan.k1], y[r * INNER : (r + 1) * INNER, plan.k1 :]
+        fs.append(jnp.concatenate([yr * tc + yi * ts, yi * tc - yr * ts], axis=0))
+    f = jnp.concatenate(fs, axis=1)
+    fh = f.astype(jnp.bfloat16)
+    fl = (f - fh.astype(jnp.float32)).astype(jnp.bfloat16)
+    z = jnp.dot(w2_ref[...], jnp.concatenate([fh, fh, fl]), preferred_element_type=jnp.float32)
+    for r in range(plan.rows):
         for b in range(plan.group):
-            outs[b][r] = z[b * size : (b + 1) * size].reshape(2, k2_dev, plan.k1)
+            outs[b][r] = z[b * size : (b + 1) * size, r * plan.k1 : (r + 1) * plan.k1].reshape(2, plan.k2_dev, plan.k1)
 
 
 def merge_kernel(plan, swap_bit, me_ref, *refs):
     chunks = [refs[(ORDER + (0,)).index(b)] for b in range(plan.group)]
     counts = refs[plan.group : plan.group + plan.n_row]
-    out_ref, tile_ref, row_ref, sems = refs[plan.group + plan.n_row :]
+    out_ref, tile_ref, sems = refs[plan.group + plan.n_row :]
     total = counts[0][...]
     for other in counts[1:]:
         total = total + other[...]
@@ -298,12 +302,9 @@
                     at = (k2 * plan.k1_tiles + j) * SUBS + r
                     tile_ref[slot, pl.ds(at, take, stride=stride), :] = jnp.where(swapped, b, a)
                     tile_ref[slot, pl.ds(at + plan.rows, take, stride=stride), :] = jnp.where(swapped, a, b)
-        for f in range(plan.freq_tiles):
-            row_ref[slot, :, f * LANES : (f + 1) * LANES] = tile_ref[slot, f * SUBS : (f + 1) * SUBS, :]
         source = inside ^ base
         tile = source // 2 if swap_bit == 1 else source % 2 * 2 + source // 4
-        target = out_ref.at[part, pl.ds(pl.multiple_of(tile * SUBS, SUBS), SUBS), :]
-        copy = pltpu.make_async_copy(row_ref.at[slot], target, sems.at[slot])
+        copy = pltpu.make_async_copy(tile_ref.at[slot], out_ref.at[part, tile], sems.at[slot])
         copy.start()
         copies.append(copy)
     for copy in copies:
@@ -318,12 +319,29 @@
     return [jax.ShapeDtypeStruct((plan.rows, 2, plan.k2_dev, plan.k1), jnp.float32)] * plan.group
 
 
+def ready_tables(plan, me, blocks):
+    smem, vmem = pl.BlockSpec(memory_space=pltpu.SMEM), pl.BlockSpec(memory_space=pltpu.VMEM)
+    return pl.pallas_call(
+        partial(tables_kernel, plan, blocks),
+        out_shape=[
+            jax.ShapeDtypeStruct((6 * plan.n1, 2 * plan.k1), jnp.bfloat16),
+            jax.ShapeDtypeStruct((2 * plan.group * plan.k2_dev, 6 * INNER), jnp.bfloat16),
+            jax.ShapeDtypeStruct((2 * (INNER // FINE + FINE), plan.k1), jnp.float32),
+        ],
+        in_specs=[smem] + [vmem] * 3,
+        out_specs=[vmem] * 3,
+        compiler_params=pltpu.CompilerParams(vmem_limit_bytes=24 * 2**20),
+        name="tables",
+    )(me, outer_tables(plan, blocks), inner_tables(plan), twist_tables(plan))
+
+
 def spectra_by_chip(plan, phase_codes, aperture, tile_offsets):
     n_col, n_row = plan.n_col, plan.n_row
     n_chips = n_col // 2
+    half = plan.row_dev // 2
     row_index = lax.axis_index("row").astype(jnp.int32)
     col_index = lax.axis_index("col").astype(jnp.int32)
-    smem, vmem, hbm = (pl.BlockSpec(memory_space=m) for m in (pltpu.SMEM, pltpu.VMEM, pl.ANY))
+    smem, vmem = pl.BlockSpec(memory_space=pltpu.SMEM), pl.BlockSpec(memory_space=pltpu.VMEM)
     swap = [(q, q ^ 1) for q in range(n_col)]
     others = along_rows(n_row, tile_offsets)
     near_others = []
@@ -331,43 +349,44 @@
         pairs = [(r * n_col + q, (r + d) % n_row * n_col + (q ^ 1)) for r in range(n_row) for q in range(n_col)]
         near_others.append(lax.ppermute(tile_offsets, ("row", "col"), pairs))
     near = [lax.ppermute(value, "col", swap) for value in (tile_offsets, phase_codes, aperture)]
-    alike = min(n_chips, plan.group // 2)
+    place = jnp.stack([col_index % 2, col_index // 2, row_index])
+    own = pl.pallas_call(
+        partial(own_kernel, plan),
+        out_shape=[jax.ShapeDtypeStruct((half, plan.pupil_dev), jnp.int32)] * 2
+        + [jax.ShapeDtypeStruct((SUBS, LANES), jnp.int32)],
+        grid_spec=pltpu.PrefetchScalarGridSpec(
+            num_scalar_prefetch=1,
+            grid=(1,),
+            in_specs=[
+                smem,
+                pl.BlockSpec((half, plan.pupil_dev), lambda i, p: (p[0], 0)),
+                pl.BlockSpec((plan.row_dev, plan.pupil_dev), lambda i, p: (0, 0)),
+            ],
+            out_specs=[vmem] * 3,
+        ),
+        compiler_params=pltpu.CompilerParams(vmem_limit_bytes=16 * 2**20),
+        name="own",
+    )(place, tile_offsets, phase_codes, aperture)
     block = jax.ShapeDtypeStruct((2 * plan.chunk + SUBS, LANES), jnp.float32)
     rows = pl.pallas_call(
         partial(chip_field_kernel, plan),
-        out_shape=[block] * alike,
-        in_specs=[smem] + [vmem] * (2 * n_row) + [hbm, hbm, vmem, vmem],
-        out_specs=[vmem] * alike,
-        scratch_shapes=[
-            pltpu.VMEM(phase_codes.shape, jnp.int32),
-            pltpu.VMEM(aperture.shape, jnp.int32),
-            pltpu.VMEM((2, alike * plan.chunk, LANES), jnp.float32),
-            pltpu.SemaphoreType.DMA((2,)),
-        ],
+        out_shape=[block] * n_chips,
+        in_specs=[smem] + [vmem] * (2 * n_row + 4),
+        out_specs=[vmem] * n_chips,
+        scratch_shapes=[pltpu.VMEM((2, half * plan.chunk // plan.rows, LANES), jnp.float32)],
         compiler_params=pltpu.CompilerParams(vmem_limit_bytes=16 * 2**20),
         name="field",
-    )(
-        jnp.stack([col_index % 2, col_index // 2, row_index]),
-        tile_offsets,
-        near[0],
-        *others,
-        *near_others,
-        phase_codes,
-        aperture,
-        near[1],
-        near[2],
-    )
+    )(place, *others, *near_others, near[0], *own, near[1], near[2])
     order = CHIP_ORDER + (0,)
-    received = [rows[0] if b == 0 else lax.ppermute(rows[b % alike], "col", [(q, q ^ 2 * b) for q in range(n_col)]) for b in order]
-    tables = [outer_tables(plan, n_chips), inner_tables(plan), twist_tables(plan)]
+    received = [rows[0] if b == 0 else lax.ppermute(rows[b], "col", [(q, q ^ 2 * b) for q in range(n_col)]) for b in order]
     *made, opened = pl.pallas_call(
         partial(chip_transform_kernel, plan, order),
         out_shape=spectra_shapes(plan) + [jax.ShapeDtypeStruct((SUBS, LANES), jnp.float32)],
-        in_specs=[smem] + [vmem] * (n_chips + 3),
+        in_specs=[vmem] * (n_chips + 3),
         out_specs=[vmem] * (plan.group + 1),
         compiler_params=pltpu.CompilerParams(vmem_limit_bytes=24 * 2**20),
         name="transform",
-    )(col_index.reshape(1), *received, *tables)
+    )(*received, *ready_tables(plan, col_index.reshape(1), n_chips))
     return made, opened
 
 
@@ -410,15 +429,14 @@
     info = jnp.concatenate([jnp.where(mine, before, 0.0), opened])
     for bit in range(n_col.bit_length() - 1):
         info = info + lax.ppermute(info, "col", [(q, q ^ 1 << bit) for q in range(n_col)])
-    tables = [outer_tables(plan, 1), inner_tables(plan), twist_tables(plan)]
     made = pl.pallas_call(
         partial(transform_kernel, plan),
         out_shape=spectra_shapes(plan),
-        in_specs=[smem] + [vmem] * 5,
+        in_specs=[vmem] * 5,
         out_specs=[vmem] * plan.group,
         compiler_params=pltpu.CompilerParams(vmem_limit_bytes=24 * 2**20),
         name="transform",
-    )(me, info, received, *tables)
+    )(info, received, *ready_tables(plan, me, 1))
     return made, info[n_col:]
 
 
@@ -430,22 +448,25 @@
     spectra = spectra_by_chip if by_chip else spectra_by_device
     made, opened = spectra(plan, phase_codes, aperture, tile_offsets)
     chunks = [lax.ppermute(made[b], "col", [(q, q ^ b) for q in range(n_col)]) for b in ORDER] + [made[0]]
+    opened, chunks[2] = lax.optimization_barrier((opened, chunks[2]))
     counts = [opened] + along_rows(n_row, opened)
     smem = pl.BlockSpec(memory_space=pltpu.SMEM)
     vmem = pl.BlockSpec(memory_space=pltpu.VMEM)
-    return pl.pallas_call(
+    tiles = plan.row_dev // SUBS
+    out = pl.pallas_call(
         partial(merge_kernel, plan, 2 if by_chip else 1),
-        out_shape=jax.ShapeDtypeStruct((2, plan.row_dev, plan.freq_tiles * LANES), jnp.float32),
+        out_shape=jax.ShapeDtypeStruct((2, tiles, plan.freq_tiles * SUBS, LANES), jnp.float32),
         in_specs=[smem] + [vmem] * (plan.group + n_row),
         out_specs=pl.BlockSpec(memory_space=pl.ANY),
         scratch_shapes=[
             pltpu.VMEM((plan.group, plan.freq_tiles * SUBS, LANES), jnp.float32),
-            pltpu.VMEM((plan.group, SUBS, plan.freq_tiles * LANES), jnp.float32),
             pltpu.SemaphoreType.DMA((plan.group,)),
         ],
         compiler_params=pltpu.CompilerParams(vmem_limit_bytes=24 * 2**20),
         name="merge",
     )(lax.axis_index("col").astype(jnp.int32).reshape(1), *chunks, *counts)
+    out = out.reshape(2, tiles, plan.freq_tiles, SUBS, LANES).transpose(0, 1, 3, 2, 4)
+    return out.reshape(2, plan.row_dev, plan.freq_tiles * LANES)
 
 
 def solution(mesh):

time: 74.8 us -> 67.7 us (0.905)
  waiting for transfers between devices: 37 us -> 27.2 us
  starting transfers between devices: 23.6 us -> 25.5 us
  Pallas kernels: 8.12 us -> 8.99 us
    ppermute x7, waiting for transfers between devices: 15.5 us -> 8.62 us  [spectra_by_chip(): lax.ppermute(rows[b], 'col', [(q, q ^ 2 * b) for q in range(n_col)])]
    ppermute x2, waiting for transfers between devices: 3.13 us -> 0.01 us  [along_rows(): lax.ppermute(value, 'row', [(i, (i + d) % n_row) for i in range(n_row)])]
    ppermute x1, starting transfers between devices: 0.11 us -> 2.57 us  [spectra_by_chip(): near_others.append(lax.ppermute(tile_offsets, ('row', 'col'), pairs))]
    ppermute x7, waiting for transfers between devices: 17 us -> 18.5 us  [per_device(): lax.ppermute(made[b], 'col', [(q, q ^ b) for q in range(n_col)])]
    ppermute x1, waiting for transfers between devices: 1.45 us -> 0.01 us  [spectra_by_chip(): near_others.append(lax.ppermute(tile_offsets, ('row', 'col'), pairs))]
    ppermute x2, starting transfers between devices: 3.37 us -> 1.95 us  [along_rows(): lax.ppermute(value, 'row', [(i, (i + d) % n_row) for i in range(n_row)])]
    ppermute x7, starting transfers between devices: 12.1 us -> 13.5 us  [spectra_by_chip(): lax.ppermute(rows[b], 'col', [(q, q ^ 2 * b) for q in range(n_col)])]
    pallas_call x1 -> x3, Pallas kernels: 1.34 us -> 2.61 us  [the longest x1 1.29 us: spectra_by_chip(): pl.pallas_call(partial(chip_field_kernel, plan), out_shape=[block] * n_ch...]
  transfers between devices with their start and end apart: 20 -> 20, of which waited for: 11 -> 7; matrix products, arithmetic and copies ran while one was open for 0% -> 0% of each run, Pallas kernels for 0% -> 2%
where the time goes in v8:
time: 67.7 us; the launch traced here: 67.4 us
  waiting for transfers between devices  27.2 us (40%)
  starting transfers between devices  25.5 us (38%)
  Pallas kernels  8.99 us (13%)
  local copies, waits for them, and re-layouts  5.56 us (8%)
    ppermute x7, waiting for transfers between devices, per_device(): lax.ppermute(made[b], 'col', [(q, q ^ b) for q in range(n_col)])  18.5 us
    ppermute x7, starting transfers between devices, spectra_by_chip(): lax.ppermute(rows[b], 'col', [(q, q ^ 2 * b) for q in range(n_col)])  13.5 us
    ppermute x7, waiting for transfers between devices, spectra_by_chip(): lax.ppermute(rows[b], 'col', [(q, q ^ 2 * b) for q in range(n_col)])  8.62 us
    ppermute x7, starting transfers between devices, per_device(): lax.ppermute(made[b], 'col', [(q, q ^ b) for q in range(n_col)])  6.9 us
    unnamed x12, local copies, waits for them, and re-layouts  5.56 us
    pallas_call x1, Pallas kernels, spectra_by_chip(): pl.pallas_call(partial(chip_transform_kernel, plan, order), out_shape=spe...  4.26 us
    ppermute x1, starting transfers between devices, spectra_by_chip(): near_others.append(lax.ppermute(tile_offsets, ('row', 'col'), pairs))  2.57 us
    pallas_call x1, Pallas kernels, per_device(): pl.pallas_call(partial(merge_kernel, plan, 2 if by_chip else 1), out_shap...  2.12 us
  transfers between devices with their start and end apart: 20, of which 7 were waited for; matrix products, arithmetic and copies ran while one was open for 0% of the time, Pallas kernels for 2%

profile of v8, /device:TPU:0, one launch (start us, length us, event | category | flops | bytes accessed | tf_op | source)
XLA Modules:
  0.0 67.4 jit_solution(6058493146926010687)
XLA Ops:
  0.0 0.5 collective-permute-start.3
  0.5 2.6 %collective-permute-start.1 = (s32[2,4]{1,0:T(2,128)}, s32[2,4]{1,0:T(2,128)S(1)}, u32[]{:S(2)}, u32[]{:S(2)}) collective-permute-start(s32[2,4]{1,0:T(2,128)} %tiles_ref.1), channel_id=1, source_target_pairs={{0,17},{1,16},{2,19},{3,18},{4,21},{5,20},{6,23},{7,22},{8,25},{9,... | collective-permute-start | bytes 104 | tf_op jit(solution)/shard_map/ppermute | solution.py:350
  3.1 0.4 collective-permute-start
  3.7 0.9 %copy-done.2 = s32[32,2048]{1,0:T(8,128)S(1)} copy-done((s32[32,2048]{1,0:T(8,128)S(1)}, s32[32,2048]{1,0:T(8,128)}, u32[]{:S(2)}) %copy-start.2) | copy-done | bytes 262168
  4.6 0.9 %copy-done.3 = s32[32,2048]{1,0:T(8,128)S(1)} copy-done((s32[32,2048]{1,0:T(8,128)S(1)}, s32[32,2048]{1,0:T(8,128)}, u32[]{:S(2)}) %copy-start.3) | copy-done | bytes 262168
  5.6 0.7 %copy-done.5 = s32[2,4]{1,0:T(2,128)S(1)} copy-done((s32[2,4]{1,0:T(2,128)S(1)}, s32[2,4]{1,0:T(2,128)}, u32[]{:S(2)}) %copy-start.5) | copy-done | bytes 56
  6.3 1.2 %own.1 = (s32[16,2048]{1,0:T(8,128)S(1)}, s32[16,2048]{1,0:T(8,128)S(1)}, s32[8,128]{1,0:T(8,128)S(1)}) custom-call(s32[3]{0:T(128)S(1)} %pad_add_fusion.me_ref, s32[2,4]{1,0:T(2,128)S(1)} %copy-done.5, s32[32,2048]{1,0:T(8,128)S(1)} %copy-done.2, s32[32,2048]{1,0:T(8,128)S(1)} %copy-done.3), custom_call_target="tpu_custom_call" | custom-call | tf_op jit(solution)/shard_map/own/pallas_call | solution.py:353
  7.5 1.3 %field.1 = (f32[264,128]{1,0:T(8,128)S(1)}, f32[264,128]{1,0:T(8,128)S(1)}, f32[264,128]{1,0:T(8,128)S(1)}, f32[264,128]{1,0:T(8,128)S(1)}, f32[264,128]{1,0:T(8...) custom-call(s32[3]{0:T(128)S(1)} %pad_add_fusion.me_ref, ...), custom_call_target="tpu_custom_call" | custom-call | tf_op jit(solution)/shard_map/field/pallas_call | solution.py:371
  8.8 2.9 %collective-permute-start.5 = (f32[264,128]{1,0:T(8,128)S(1)}, f32[264,128]{1,0:T(8,128)S(1)}, u32[]{:S(2)}, u32[]{:S(2)}) collective-permute-start(f32[264,128]{1,0:T(8,128)S(1)} %get-tuple-element.33), channel_id=1, source_target_pairs={{0,8},{1,9},{2,10},{3,11},{4,12},{5,13},{6,14},{7,15},{8,0},{9,1},... | collective-permute-start | bytes 405512 | tf_op jit(solution)/shard_map/ppermute | solution.py:381
  11.6 1.5 %collective-permute-start.6 = (f32[264,128]{1,0:T(8,128)S(1)}, f32[264,128]{1,0:T(8,128)S(1)}, u32[]{:S(2)}, u32[]{:S(2)}) collective-permute-start(f32[264,128]{1,0:T(8,128)S(1)} %get-tuple-element.34), channel_id=1, source_target_pairs={{0,2},{1,3},{2,0},{3,1},{4,6},{5,7},{6,4},{7,5},{8,10},{9,11},{10,... | collective-permute-start | bytes 405512 | tf_op jit(solution)/shard_map/ppermute | solution.py:381
  13.2 1.8 %collective-permute-start.8 = (f32[264,128]{1,0:T(8,128)S(1)}, f32[264,128]{1,0:T(8,128)S(1)}, u32[]{:S(2)}, u32[]{:S(2)}) collective-permute-start(f32[264,128]{1,0:T(8,128)S(1)} %get-tuple-element.36), channel_id=1, source_target_pairs={{0,4},{1,5},{2,6},{3,7},{4,0},{5,1},{6,2},{7,3},{8,12},{9,13},{10,... | collective-permute-start | bytes 405512 | tf_op jit(solution)/shard_map/ppermute | solution.py:381
  15.0 2.5 %collective-permute-start.9 = (f32[264,128]{1,0:T(8,128)S(1)}, f32[264,128]{1,0:T(8,128)S(1)}, u32[]{:S(2)}, u32[]{:S(2)}) collective-permute-start(f32[264,128]{1,0:T(8,128)S(1)} %get-tuple-element.37), channel_id=1, source_target_pairs={{0,12},{1,13},{2,14},{3,15},{4,8},{5,9},{6,10},{7,11},{8,4},{9,5},... | collective-permute-start | bytes 405512 | tf_op jit(solution)/shard_map/ppermute | solution.py:381
  17.5 4.4 %collective-permute-done.5.refs_0_ = f32[264,128]{1,0:T(8,128)S(1)} collective-permute-done((f32[264,128]{1,0:T(8,128)S(1)}, f32[264,128]{1,0:T(8,128)S(1)}, u32[]{:S(2)}, u32[]{:S(2)}) %collective-permute-start.5) | collective-permute-done | bytes 135200 | tf_op jit(solution)/shard_map/ppermute | solution.py:381
  21.9 1.7 %collective-permute-start.10 = (f32[264,128]{1,0:T(8,128)S(1)}, f32[264,128]{1,0:T(8,128)S(1)}, u32[]{:S(2)}, u32[]{:S(2)}) collective-permute-start(f32[264,128]{1,0:T(8,128)S(1)} %get-tuple-element.38), channel_id=1, source_target_pairs={{0,6},{1,7},{2,4},{3,5},{4,2},{5,3},{6,0},{7,1},{8,14},{9,15},{10,... | collective-permute-start | bytes 405512 | tf_op jit(solution)/shard_map/ppermute | solution.py:381
  23.6 3.1 %collective-permute-start.11 = (f32[264,128]{1,0:T(8,128)S(1)}, f32[264,128]{1,0:T(8,128)S(1)}, u32[]{:S(2)}, u32[]{:S(2)}) collective-permute-start(f32[264,128]{1,0:T(8,128)S(1)} %get-tuple-element.39), channel_id=1, source_target_pairs={{0,14},{1,15},{2,12},{3,13},{4,10},{5,11},{6,8},{7,9},{8,6},{9,7},... | collective-permute-start | bytes 405512 | tf_op jit(solution)/shard_map/ppermute | solution.py:381
  26.6 1.0 %copy-done = bf16[2,16,16,512]{3,2,1,0:T(8,128)(2,1)S(1)} copy-done((bf16[2,16,16,512]{3,2,1,0:T(8,128)(2,1)S(1)}, bf16[2,16,16,512]{3,2,1,0:T(8,128)(2,1)}, u32[]{:S(2)}) %copy-start) | copy-done | bytes 524312
  27.7 1.0 %copy-done.1 = bf16[2,8,2,16,512]{4,3,2,1,0:T(8,128)(2,1)S(1)} copy-done((bf16[2,8,2,16,512]{4,3,2,1,0:T(8,128)(2,1)S(1)}, bf16[2,8,2,16,512]{4,3,2,1,0:T(8,128)(2,1)}, u32[]{:S(2)}) %copy-start.1) | copy-done | bytes 524312
  28.7 0.9 %copy-done.4 = f32[64,512]{1,0:T(8,128)S(1)} copy-done((f32[64,512]{1,0:T(8,128)S(1)}, f32[64,512]{1,0:T(8,128)}, u32[]{:S(2)}) %copy-start.4) | copy-done | bytes 131096
  29.6 0.2 tables.1
  29.8 4.2 %collective-permute-done.10.refs_5_ = f32[264,128]{1,0:T(8,128)S(1)} collective-permute-done((f32[264,128]{1,0:T(8,128)S(1)}, f32[264,128]{1,0:T(8,128)S(1)}, u32[]{:S(2)}, u32[]{:S(2)}) %collective-permute-start.10) | collective-permute-done | bytes 135200 | tf_op jit(solution)/shard_map/ppermute | solution.py:381
  34.0 4.3 %transform.1 = (f32[4,2,16,512]{3,2,1,0:T(8,128)S(1)}, f32[4,2,16,512]{3,2,1,0:T(8,128)S(1)}, f32[4,2,16,512]{3,2,1,0:T(8,128)S(1)}, f32[4,2,16,512]{3,2,1,0:T(8...) custom-call(f32[264,128]{1,0:T(8,128)S(1)} %collective-permute-done., ...), custom_call_target="tpu_custom_call" | custom-call | tf_op jit(solution)/shard_map/transform/pallas_call | solution.py:382
  38.3 3.7 %collective-permute-start.12 = (f32[4,2,16,512]{3,2,1,0:T(8,128)S(1)}, f32[4,2,16,512]{3,2,1,0:T(8,128)S(1)}, u32[]{:S(2)}, u32[]{:S(2)}) collective-permute-start(f32[4,2,16,512]{3,2,1,0:T(8,128)S(1)} %get-tuple-element.44), channel_id=1, source_target_pairs={{0,6},{1,7},{2,4},{3,5},{4,2},{5,3},{6,0},{7,1},{8,14},{9,15},{10,... | collective-permute-start | bytes 786440 | tf_op jit(solution)/shard_map/ppermute | solution.py:450
  42.0 1.3 %collective-permute-start.14 = (f32[4,2,16,512]{3,2,1,0:T(8,128)S(1)}, f32[4,2,16,512]{3,2,1,0:T(8,128)S(1)}, u32[]{:S(2)}, u32[]{:S(2)}) collective-permute-start(f32[4,2,16,512]{3,2,1,0:T(8,128)S(1)} %get-tuple-element.47), channel_id=1, source_target_pairs={{0,2},{1,3},{2,0},{3,1},{4,6},{5,7},{6,4},{7,5},{8,10},{9,11},{10,... | collective-permute-start | bytes 786440 | tf_op jit(solution)/shard_map/ppermute | solution.py:450
  43.3 0.9 %collective-permute-start.15 = (f32[4,2,16,512]{3,2,1,0:T(8,128)S(1)}, f32[4,2,16,512]{3,2,1,0:T(8,128)S(1)}, u32[]{:S(2)}, u32[]{:S(2)}) collective-permute-start(f32[4,2,16,512]{3,2,1,0:T(8,128)S(1)} %get-tuple-element.49), channel_id=1, source_target_pairs={{0,7},{1,6},{2,5},{3,4},{4,3},{5,2},{6,1},{7,0},{8,15},{9,14},{10,... | collective-permute-start | bytes 786440 | tf_op jit(solution)/shard_map/ppermute | solution.py:450
  44.3 0.9 %collective-permute-start.16 = (f32[4,2,16,512]{3,2,1,0:T(8,128)S(1)}, f32[4,2,16,512]{3,2,1,0:T(8,128)S(1)}, u32[]{:S(2)}, u32[]{:S(2)}) collective-permute-start(f32[4,2,16,512]{3,2,1,0:T(8,128)S(1)} %get-tuple-element.50), channel_id=1, source_target_pairs={{0,5},{1,4},{2,7},{3,6},{4,1},{5,0},{6,3},{7,2},{8,13},{9,12},{10,... | collective-permute-start | bytes 786440 | tf_op jit(solution)/shard_map/ppermute | solution.py:450
  45.2 3.9 %collective-permute-done.12.refs_0_ = f32[4,2,16,512]{3,2,1,0:T(8,128)S(1)} collective-permute-done((f32[4,2,16,512]{3,2,1,0:T(8,128)S(1)}, f32[4,2,16,512]{3,2,1,0:T(8,128)S(1)}, u32[]{:S(2)}, u32[]{:S(2)}) %collective-permute-start.12) | collective-permute-done | bytes 262176 | tf_op jit(solution)/shard_map/ppermute | solution.py:450
  49.1 5.7 %collective-permute-done.14.refs_2_ = f32[4,2,16,512]{3,2,1,0:T(8,128)S(1)} collective-permute-done((f32[4,2,16,512]{3,2,1,0:T(8,128)S(1)}, f32[4,2,16,512]{3,2,1,0:T(8,128)S(1)}, u32[]{:S(2)}, u32[]{:S(2)}) %collective-permute-start.14) | collective-permute-done | bytes 262176 | tf_op jit(solution)/shard_map/ppermute | solution.py:450
  54.8 1.5 %collective-permute-start.19 = (f32[8,128]{1,0:T(8,128)S(1)}, f32[8,128]{1,0:T(8,128)S(1)}, u32[]{:S(2)}, u32[]{:S(2)}) collective-permute-start(f32[8,128]{1,0:T(8,128)S(1)} %get-tuple-element.54.refs_8_), channel_id=1, source_target_pairs={{0,16},{16,0},{1,17},{17,1},{2,18},{18,2},{3,19},{19,3},{4,20},{20... | collective-permute-start | bytes 12296 | tf_op jit(solution)/shard_map/ppermute | solution.py:315
  56.3 3.7 %collective-permute-done.15.refs_3_ = f32[4,2,16,512]{3,2,1,0:T(8,128)S(1)} collective-permute-done((f32[4,2,16,512]{3,2,1,0:T(8,128)S(1)}, f32[4,2,16,512]{3,2,1,0:T(8,128)S(1)}, u32[]{:S(2)}, u32[]{:S(2)}) %collective-permute-start.15) | collective-permute-done | bytes 262176 | tf_op jit(solution)/shard_map/ppermute | solution.py:450
  60.0 4.7 %collective-permute-done.16.refs_4_ = f32[4,2,16,512]{3,2,1,0:T(8,128)S(1)} collective-permute-done((f32[4,2,16,512]{3,2,1,0:T(8,128)S(1)}, f32[4,2,16,512]{3,2,1,0:T(8,128)S(1)}, u32[]{:S(2)}, u32[]{:S(2)}) %collective-permute-start.16) | collective-permute-done | bytes 262176 | tf_op jit(solution)/shard_map/ppermute | solution.py:450
  64.7 0.6 collective-permute-done.17.refs_5_
  65.2 2.1 %merge.1 = f32[2,4,512,128]{3,2,1,0:T(8,128)} custom-call(s32[1]{0:T(128)} %bitcast.me_ref, f32[4,2,16,512]{3,2,1,0:T(8,128)S(1)} %collective-permute-done.12.refs_0_, f32[4,2,16,512]{3,2,1,0:T(8,128)S(1)} %collective-permute-done.13.refs_1_, f32[4,2,16,512]{3,2,1,0:T(8,128)S(1)} %collective-permute-done.14.refs_2_, ...), custom_call_target="tpu_custom_call" | custom-call | tf_op jit(solution)/shard_map/merge/pallas_call | solution.py:456
  (26 shorter events, 0.4 us)
Async XLA Ops:
  0.0 7.4 %collective-permute-start.3 = (s32[32,2048]{1,0:T(8,128)}, s32[32,2048]{1,0:T(8,128)S(1)}, u32[]{:S(2)}, u32[]{:S(2)}) collective-permute-start(s32[32,2048]{1,0:T(8,128)} %codes_ref.1), channel_id=1, source_target_pairs={{0,1},{1,0},{2,3},{3,2},{4,5},{5,4},{6,7},{7,6},{8,9},{9,8},{10,11... | collective-permute-start | bytes 786440 | tf_op jit(solution)/shard_map/ppermute | solution.py:351
  0.5 7.0 %collective-permute-start.4 = (s32[32,2048]{1,0:T(8,128)}, s32[32,2048]{1,0:T(8,128)S(1)}, u32[]{:S(2)}, u32[]{:S(2)}) collective-permute-start(s32[32,2048]{1,0:T(8,128)} %mask_ref.1), channel_id=1, source_target_pairs={{0,1},{1,0},{2,3},{3,2},{4,5},{5,4},{6,7},{7,6},{8,9},{9,8},{10,11... | collective-permute-start | bytes 786440 | tf_op jit(solution)/shard_map/ppermute | solution.py:351
  0.5 6.9 %collective-permute-start.1 = (s32[2,4]{1,0:T(2,128)}, s32[2,4]{1,0:T(2,128)S(1)}, u32[]{:S(2)}, u32[]{:S(2)}) collective-permute-start(s32[2,4]{1,0:T(2,128)} %tiles_ref.1), channel_id=1, source_target_pairs={{0,17},{1,16},{2,19},{3,18},{4,21},{5,20},{6,23},{7,22},{8,25},{9,... | collective-permute-start | bytes 104 | tf_op jit(solution)/shard_map/ppermute | solution.py:350
  3.1 4.3 %collective-permute-start = (s32[2,4]{1,0:T(2,128)}, s32[2,4]{1,0:T(2,128)S(1)}, u32[]{:S(2)}, u32[]{:S(2)}) collective-permute-start(s32[2,4]{1,0:T(2,128)} %tiles_ref.1), channel_id=1, source_target_pairs={{0,16},{16,0},{1,17},{17,1},{2,18},{18,2},{3,19},{19,3},{4,20},{20... | collective-permute-start | bytes 104 | tf_op jit(solution)/shard_map/ppermute | solution.py:315
  3.5 3.9 %collective-permute-start.2 = (s32[2,4]{1,0:T(2,128)}, s32[2,4]{1,0:T(2,128)S(1)}, u32[]{:S(2)}, u32[]{:S(2)}) collective-permute-start(s32[2,4]{1,0:T(2,128)} %tiles_ref.1), channel_id=1, source_target_pairs={{0,1},{1,0},{2,3},{3,2},{4,5},{5,4},{6,7},{7,6},{8,9},{9,8},{10,11... | collective-permute-start | bytes 104 | tf_op jit(solution)/shard_map/ppermute | solution.py:351
  3.7 1.0 %copy-start.2 = (s32[32,2048]{1,0:T(8,128)S(1)}, s32[32,2048]{1,0:T(8,128)}, u32[]{:S(2)}) copy-start(s32[32,2048]{1,0:T(8,128)} %codes_ref.1) | copy-start | bytes 786436
  4.6 0.9 %copy-start.3 = (s32[32,2048]{1,0:T(8,128)S(1)}, s32[32,2048]{1,0:T(8,128)}, u32[]{:S(2)}) copy-start(s32[32,2048]{1,0:T(8,128)} %mask_ref.1) | copy-start | bytes 786436
  5.6 0.7 %copy-start.5 = (s32[2,4]{1,0:T(2,128)S(1)}, s32[2,4]{1,0:T(2,128)}, u32[]{:S(2)}) copy-start(s32[2,4]{1,0:T(2,128)} %tiles_ref.1) | copy-start | bytes 100
  8.8 13.1 %collective-permute-start.5 = (f32[264,128]{1,0:T(8,128)S(1)}, f32[264,128]{1,0:T(8,128)S(1)}, u32[]{:S(2)}, u32[]{:S(2)}) collective-permute-start(f32[264,128]{1,0:T(8,128)S(1)} %get-tuple-element.33), channel_id=1, source_target_pairs={{0,8},{1,9},{2,10},{3,11},{4,12},{5,13},{6,14},{7,15},{8,0},{9,1},... | collective-permute-start | bytes 405512 | tf_op jit(solution)/shard_map/ppermute | solution.py:381
  11.6 11.9 %collective-permute-start.6 = (f32[264,128]{1,0:T(8,128)S(1)}, f32[264,128]{1,0:T(8,128)S(1)}, u32[]{:S(2)}, u32[]{:S(2)}) collective-permute-start(f32[264,128]{1,0:T(8,128)S(1)} %get-tuple-element.34), channel_id=1, source_target_pairs={{0,2},{1,3},{2,0},{3,1},{4,6},{5,7},{6,4},{7,5},{8,10},{9,11},{10,... | collective-permute-start | bytes 405512 | tf_op jit(solution)/shard_map/ppermute | solution.py:381
  13.1 16.7 %collective-permute-start.7 = (f32[264,128]{1,0:T(8,128)S(1)}, f32[264,128]{1,0:T(8,128)S(1)}, u32[]{:S(2)}, u32[]{:S(2)}) collective-permute-start(f32[264,128]{1,0:T(8,128)S(1)} %get-tuple-element.35), channel_id=1, source_target_pairs={{0,10},{1,11},{2,8},{3,9},{4,14},{5,15},{6,12},{7,13},{8,2},{9,3},... | collective-permute-start | bytes 405512 | tf_op jit(solution)/shard_map/ppermute | solution.py:381
  13.2 16.6 %collective-permute-start.8 = (f32[264,128]{1,0:T(8,128)S(1)}, f32[264,128]{1,0:T(8,128)S(1)}, u32[]{:S(2)}, u32[]{:S(2)}) collective-permute-start(f32[264,128]{1,0:T(8,128)S(1)} %get-tuple-element.36), channel_id=1, source_target_pairs={{0,4},{1,5},{2,6},{3,7},{4,0},{5,1},{6,2},{7,3},{8,12},{9,13},{10,... | collective-permute-start | bytes 405512 | tf_op jit(solution)/shard_map/ppermute | solution.py:381
  15.0 14.8 %collective-permute-start.9 = (f32[264,128]{1,0:T(8,128)S(1)}, f32[264,128]{1,0:T(8,128)S(1)}, u32[]{:S(2)}, u32[]{:S(2)}) collective-permute-start(f32[264,128]{1,0:T(8,128)S(1)} %get-tuple-element.37), channel_id=1, source_target_pairs={{0,12},{1,13},{2,14},{3,15},{4,8},{5,9},{6,10},{7,11},{8,4},{9,5},... | collective-permute-start | bytes 405512 | tf_op jit(solution)/shard_map/ppermute | solution.py:381
  21.9 12.1 %collective-permute-start.10 = (f32[264,128]{1,0:T(8,128)S(1)}, f32[264,128]{1,0:T(8,128)S(1)}, u32[]{:S(2)}, u32[]{:S(2)}) collective-permute-start(f32[264,128]{1,0:T(8,128)S(1)} %get-tuple-element.38), channel_id=1, source_target_pairs={{0,6},{1,7},{2,4},{3,5},{4,2},{5,3},{6,0},{7,1},{8,14},{9,15},{10,... | collective-permute-start | bytes 405512 | tf_op jit(solution)/shard_map/ppermute | solution.py:381
  23.6 10.5 %collective-permute-start.11 = (f32[264,128]{1,0:T(8,128)S(1)}, f32[264,128]{1,0:T(8,128)S(1)}, u32[]{:S(2)}, u32[]{:S(2)}) collective-permute-start(f32[264,128]{1,0:T(8,128)S(1)} %get-tuple-element.39), channel_id=1, source_target_pairs={{0,14},{1,15},{2,12},{3,13},{4,10},{5,11},{6,8},{7,9},{8,6},{9,7},... | collective-permute-start | bytes 405512 | tf_op jit(solution)/shard_map/ppermute | solution.py:381
  26.6 1.0 %copy-start = (bf16[2,16,16,512]{3,2,1,0:T(8,128)(2,1)S(1)}, bf16[2,16,16,512]{3,2,1,0:T(8,128)(2,1)}, u32[]{:S(2)}) copy-start(bf16[2,16,16,512]{3,2,1,0:T(8,128)(2,1)} %constant.40.clone.inner_ref) | copy-start | bytes 1572868
  27.7 1.0 %copy-start.1 = (bf16[2,8,2,16,512]{4,3,2,1,0:T(8,128)(2,1)S(1)}, bf16[2,8,2,16,512]{4,3,2,1,0:T(8,128)(2,1)}, u32[]{:S(2)}) copy-start(bf16[2,8,2,16,512]{4,3,2,1,0:T(8,128)(2,1)} %constant.39.clone.outer_ref) | copy-start | bytes 1572868
  28.7 0.9 %copy-start.4 = (f32[64,512]{1,0:T(8,128)S(1)}, f32[64,512]{1,0:T(8,128)}, u32[]{:S(2)}) copy-start(f32[64,512]{1,0:T(8,128)} %constant.41.clone.twist_ref) | copy-start | bytes 393220
  38.3 10.8 %collective-permute-start.12 = (f32[4,2,16,512]{3,2,1,0:T(8,128)S(1)}, f32[4,2,16,512]{3,2,1,0:T(8,128)S(1)}, u32[]{:S(2)}, u32[]{:S(2)}) collective-permute-start(f32[4,2,16,512]{3,2,1,0:T(8,128)S(1)} %get-tuple-element.44), channel_id=1, source_target_pairs={{0,6},{1,7},{2,4},{3,5},{4,2},{5,3},{6,0},{7,1},{8,14},{9,15},{10,... | collective-permute-start | bytes 786440 | tf_op jit(solution)/shard_map/ppermute | solution.py:450
  42.0 12.8 %collective-permute-start.14 = (f32[4,2,16,512]{3,2,1,0:T(8,128)S(1)}, f32[4,2,16,512]{3,2,1,0:T(8,128)S(1)}, u32[]{:S(2)}, u32[]{:S(2)}) collective-permute-start(f32[4,2,16,512]{3,2,1,0:T(8,128)S(1)} %get-tuple-element.47), channel_id=1, source_target_pairs={{0,2},{1,3},{2,0},{3,1},{4,6},{5,7},{6,4},{7,5},{8,10},{9,11},{10,... | collective-permute-start | bytes 786440 | tf_op jit(solution)/shard_map/ppermute | solution.py:450
  43.3 11.5 %collective-permute-start.13 = (f32[4,2,16,512]{3,2,1,0:T(8,128)S(1)}, f32[4,2,16,512]{3,2,1,0:T(8,128)S(1)}, u32[]{:S(2)}, u32[]{:S(2)}) collective-permute-start(f32[4,2,16,512]{3,2,1,0:T(8,128)S(1)} %get-tuple-element.45), channel_id=1, source_target_pairs={{0,4},{1,5},{2,6},{3,7},{4,0},{5,1},{6,2},{7,3},{8,12},{9,13},{10,... | collective-permute-start | bytes 786440 | tf_op jit(solution)/shard_map/ppermute | solution.py:450
  43.3 16.7 %collective-permute-start.15 = (f32[4,2,16,512]{3,2,1,0:T(8,128)S(1)}, f32[4,2,16,512]{3,2,1,0:T(8,128)S(1)}, u32[]{:S(2)}, u32[]{:S(2)}) collective-permute-start(f32[4,2,16,512]{3,2,1,0:T(8,128)S(1)} %get-tuple-element.49), channel_id=1, source_target_pairs={{0,7},{1,6},{2,5},{3,4},{4,3},{5,2},{6,1},{7,0},{8,15},{9,14},{10,... | collective-permute-start | bytes 786440 | tf_op jit(solution)/shard_map/ppermute | solution.py:450
  44.3 20.4 %collective-permute-start.16 = (f32[4,2,16,512]{3,2,1,0:T(8,128)S(1)}, f32[4,2,16,512]{3,2,1,0:T(8,128)S(1)}, u32[]{:S(2)}, u32[]{:S(2)}) collective-permute-start(f32[4,2,16,512]{3,2,1,0:T(8,128)S(1)} %get-tuple-element.50), channel_id=1, source_target_pairs={{0,5},{1,4},{2,7},{3,6},{4,1},{5,0},{6,3},{7,2},{8,13},{9,12},{10,... | collective-permute-start | bytes 786440 | tf_op jit(solution)/shard_map/ppermute | solution.py:450
  49.1 16.1 %collective-permute-start.17 = (f32[4,2,16,512]{3,2,1,0:T(8,128)S(1)}, f32[4,2,16,512]{3,2,1,0:T(8,128)S(1)}, u32[]{:S(2)}, u32[]{:S(2)}) collective-permute-start(f32[4,2,16,512]{3,2,1,0:T(8,128)S(1)} %get-tuple-element.51), channel_id=1, source_target_pairs={{0,3},{1,2},{2,1},{3,0},{4,7},{5,6},{6,5},{7,4},{8,11},{9,10},{10,... | collective-permute-start | bytes 786440 | tf_op jit(solution)/shard_map/ppermute | solution.py:450
  54.8 10.4 %collective-permute-start.18 = (f32[4,2,16,512]{3,2,1,0:T(8,128)S(1)}, f32[4,2,16,512]{3,2,1,0:T(8,128)S(1)}, u32[]{:S(2)}, u32[]{:S(2)}) collective-permute-start(f32[4,2,16,512]{3,2,1,0:T(8,128)S(1)} %get-tuple-element.52), channel_id=1, source_target_pairs={{0,1},{1,0},{2,3},{3,2},{4,5},{5,4},{6,7},{7,6},{8,9},{9,8},{10,11... | collective-permute-start | bytes 786440 | tf_op jit(solution)/shard_map/ppermute | solution.py:450
  54.8 10.4 %collective-permute-start.19 = (f32[8,128]{1,0:T(8,128)S(1)}, f32[8,128]{1,0:T(8,128)S(1)}, u32[]{:S(2)}, u32[]{:S(2)}) collective-permute-start(f32[8,128]{1,0:T(8,128)S(1)} %get-tuple-element.54.refs_8_), channel_id=1, source_target_pairs={{0,16},{16,0},{1,17},{17,1},{2,18},{18,2},{3,19},{19,3},{4,20},{20... | collective-permute-start | bytes 12296 | tf_op jit(solution)/shard_map/ppermute | solution.py:315

commit v9 on v8

--- a/solution.py
+++ b/solution.py
@@ -366,7 +366,7 @@
         ),
         compiler_params=pltpu.CompilerParams(vmem_limit_bytes=16 * 2**20),
         name="own",
-    )(place, tile_offsets, phase_codes, aperture)
+    )(place, *(pltpu.with_memory_space_constraint(a, pltpu.HBM) for a in (tile_offsets, phase_codes, aperture)))
     block = jax.ShapeDtypeStruct((2 * plan.chunk + SUBS, LANES), jnp.float32)
     rows = pl.pallas_call(
         partial(chip_field_kernel, plan),

time: 67.7 us -> 65.9 us (0.973)
  local copies, waits for them, and re-layouts: 5.56 us -> 2.99 us
  waiting for transfers between devices: 27.2 us -> 28.2 us
  starting transfers between devices: 25.5 us -> 24.8 us
    unnamed x12 -> x6, local copies, waits for them, and re-layouts: 5.56 us -> 2.99 us
    ppermute x2, waiting for transfers between devices: 0.01 us -> 1.55 us  [along_rows(): lax.ppermute(value, 'row', [(i, (i + d) % n_row) for i in range(n_row)])]
    ppermute x7, waiting for transfers between devices: 8.62 us -> 7.79 us  [spectra_by_chip(): lax.ppermute(rows[b], 'col', [(q, q ^ 2 * b) for q in range(n_col)])]
  transfers between devices with their start and end apart: 20 -> 20, of which waited for: 7 -> 9; matrix products, arithmetic and copies ran while one was open for 0% -> 0% of each run, Pallas kernels for 2% -> 3%
where the time goes in v9:
time: 65.9 us; the launch traced here: 65.6 us
  waiting for transfers between devices  28.2 us (43%)
  starting transfers between devices  24.8 us (38%)
  Pallas kernels  9.47 us (14%)
  local copies, waits for them, and re-layouts  2.99 us (5%)
    ppermute x7, waiting for transfers between devices, per_device(): lax.ppermute(made[b], 'col', [(q, q ^ b) for q in range(n_col)])  18.9 us
    ppermute x7, starting transfers between devices, spectra_by_chip(): lax.ppermute(rows[b], 'col', [(q, q ^ 2 * b) for q in range(n_col)])  13.3 us
    ppermute x7, waiting for transfers between devices, spectra_by_chip(): lax.ppermute(rows[b], 'col', [(q, q ^ 2 * b) for q in range(n_col)])  7.79 us
    ppermute x7, starting transfers between devices, per_device(): lax.ppermute(made[b], 'col', [(q, q ^ b) for q in range(n_col)])  6.74 us
    pallas_call x1, Pallas kernels, spectra_by_chip(): pl.pallas_call(partial(chip_transform_kernel, plan, order), out_shape=spe...  4.25 us
    unnamed x6, local copies, waits for them, and re-layouts  2.99 us
    ppermute x1, starting transfers between devices, spectra_by_chip(): near_others.append(lax.ppermute(tile_offsets, ('row', 'col'), pairs))  2.57 us
    pallas_call x1, Pallas kernels, per_device(): pl.pallas_call(partial(merge_kernel, plan, 2 if by_chip else 1), out_shap...  2.12 us
  transfers between devices with their start and end apart: 20, of which 9 were waited for; matrix products, arithmetic and copies ran while one was open for 0% of the time, Pallas kernels for 3%

profile of v9, /device:TPU:0, one launch (start us, length us, event | category | flops | bytes accessed | tf_op | source)
XLA Modules:
  0.0 65.6 jit_solution(13287195299470454683)
XLA Ops:
  0.0 0.5 collective-permute-start.3
  0.5 2.6 %collective-permute-start.1 = (s32[2,4]{1,0:T(2,128)}, s32[2,4]{1,0:T(2,128)S(1)}, u32[]{:S(2)}, u32[]{:S(2)}) collective-permute-start(s32[2,4]{1,0:T(2,128)} %tiles_ref.1), channel_id=1, source_target_pairs={{0,17},{1,16},{2,19},{3,18},{4,21},{5,20},{6,23},{7,22},{8,25},{9,... | collective-permute-start | bytes 104 | tf_op jit(solution)/shard_map/ppermute | solution.py:350
  3.1 0.4 collective-permute-start
  3.7 1.6 %own.1 = (s32[16,2048]{1,0:T(8,128)S(1)}, s32[16,2048]{1,0:T(8,128)S(1)}, s32[8,128]{1,0:T(8,128)S(1)}) custom-call(s32[3]{0:T(128)S(1)} %pad_add_fusion.me_ref, s32[2,4]{1,0:T(2,128)} %tiles_ref.1, s32[32,2048]{1,0:T(8,128)} %codes_ref.1, s32[32,2048]{1,0:T(8,128)} %mask_ref.1), custom_call_target="tpu_custom_call" | custom-call | tf_op jit(solution)/shard_map/own/pallas_call | solution.py:353
  5.3 1.5 %collective-permute-done.refs_0_ = s32[2,4]{1,0:T(2,128)S(1)} collective-permute-done((s32[2,4]{1,0:T(2,128)}, s32[2,4]{1,0:T(2,128)S(1)}, u32[]{:S(2)}, u32[]{:S(2)}) %collective-permute-start) | collective-permute-done | bytes 64 | tf_op jit(solution)/shard_map/ppermute | solution.py:315
  6.9 1.3 %field.1 = (f32[264,128]{1,0:T(8,128)S(1)}, f32[264,128]{1,0:T(8,128)S(1)}, f32[264,128]{1,0:T(8,128)S(1)}, f32[264,128]{1,0:T(8,128)S(1)}, f32[264,128]{1,0:T(8...) custom-call(s32[3]{0:T(128)S(1)} %pad_add_fusion.me_ref, ...), custom_call_target="tpu_custom_call" | custom-call | tf_op jit(solution)/shard_map/field/pallas_call | solution.py:371
  8.2 2.7 %collective-permute-start.5 = (f32[264,128]{1,0:T(8,128)S(1)}, f32[264,128]{1,0:T(8,128)S(1)}, u32[]{:S(2)}, u32[]{:S(2)}) collective-permute-start(f32[264,128]{1,0:T(8,128)S(1)} %get-tuple-element.33), channel_id=1, source_target_pairs={{0,8},{1,9},{2,10},{3,11},{4,12},{5,13},{6,14},{7,15},{8,0},{9,1},... | collective-permute-start | bytes 405512 | tf_op jit(solution)/shard_map/ppermute | solution.py:381
  10.8 1.5 %collective-permute-start.6 = (f32[264,128]{1,0:T(8,128)S(1)}, f32[264,128]{1,0:T(8,128)S(1)}, u32[]{:S(2)}, u32[]{:S(2)}) collective-permute-start(f32[264,128]{1,0:T(8,128)S(1)} %get-tuple-element.34), channel_id=1, source_target_pairs={{0,2},{1,3},{2,0},{3,1},{4,6},{5,7},{6,4},{7,5},{8,10},{9,11},{10,... | collective-permute-start | bytes 405512 | tf_op jit(solution)/shard_map/ppermute | solution.py:381
  12.3 0.3 collective-permute-start.7
  12.6 1.6 %collective-permute-start.8 = (f32[264,128]{1,0:T(8,128)S(1)}, f32[264,128]{1,0:T(8,128)S(1)}, u32[]{:S(2)}, u32[]{:S(2)}) collective-permute-start(f32[264,128]{1,0:T(8,128)S(1)} %get-tuple-element.36), channel_id=1, source_target_pairs={{0,4},{1,5},{2,6},{3,7},{4,0},{5,1},{6,2},{7,3},{8,12},{9,13},{10,... | collective-permute-start | bytes 405512 | tf_op jit(solution)/shard_map/ppermute | solution.py:381
  14.2 2.5 %collective-permute-start.9 = (f32[264,128]{1,0:T(8,128)S(1)}, f32[264,128]{1,0:T(8,128)S(1)}, u32[]{:S(2)}, u32[]{:S(2)}) collective-permute-start(f32[264,128]{1,0:T(8,128)S(1)} %get-tuple-element.37), channel_id=1, source_target_pairs={{0,12},{1,13},{2,14},{3,15},{4,8},{5,9},{6,10},{7,11},{8,4},{9,5},... | collective-permute-start | bytes 405512 | tf_op jit(solution)/shard_map/ppermute | solution.py:381
  16.7 5.7 %collective-permute-done.5.refs_0_ = f32[264,128]{1,0:T(8,128)S(1)} collective-permute-done((f32[264,128]{1,0:T(8,128)S(1)}, f32[264,128]{1,0:T(8,128)S(1)}, u32[]{:S(2)}, u32[]{:S(2)}) %collective-permute-start.5) | collective-permute-done | bytes 135200 | tf_op jit(solution)/shard_map/ppermute | solution.py:381
  22.4 0.5 collective-permute-start.10
  22.9 4.3 %collective-permute-start.11 = (f32[264,128]{1,0:T(8,128)S(1)}, f32[264,128]{1,0:T(8,128)S(1)}, u32[]{:S(2)}, u32[]{:S(2)}) collective-permute-start(f32[264,128]{1,0:T(8,128)S(1)} %get-tuple-element.39), channel_id=1, source_target_pairs={{0,14},{1,15},{2,12},{3,13},{4,10},{5,11},{6,8},{7,9},{8,6},{9,7},... | collective-permute-start | bytes 405512 | tf_op jit(solution)/shard_map/ppermute | solution.py:381
  27.2 1.0 %copy-done = bf16[2,16,16,512]{3,2,1,0:T(8,128)(2,1)S(1)} copy-done((bf16[2,16,16,512]{3,2,1,0:T(8,128)(2,1)S(1)}, bf16[2,16,16,512]{3,2,1,0:T(8,128)(2,1)}, u32[]{:S(2)}) %copy-start) | copy-done | bytes 524312
  28.3 1.0 %copy-done.1 = bf16[2,8,2,16,512]{4,3,2,1,0:T(8,128)(2,1)S(1)} copy-done((bf16[2,8,2,16,512]{4,3,2,1,0:T(8,128)(2,1)S(1)}, bf16[2,8,2,16,512]{4,3,2,1,0:T(8,128)(2,1)}, u32[]{:S(2)}) %copy-start.1) | copy-done | bytes 524312
  29.3 0.9 %copy-done.2 = f32[64,512]{1,0:T(8,128)S(1)} copy-done((f32[64,512]{1,0:T(8,128)S(1)}, f32[64,512]{1,0:T(8,128)}, u32[]{:S(2)}) %copy-start.2) | copy-done | bytes 131096
  30.2 0.2 tables.1
  30.4 0.5 collective-permute-done.10.refs_5_
  30.8 1.6 %collective-permute-done.11.refs_6_ = f32[264,128]{1,0:T(8,128)S(1)} collective-permute-done((f32[264,128]{1,0:T(8,128)S(1)}, f32[264,128]{1,0:T(8,128)S(1)}, u32[]{:S(2)}, u32[]{:S(2)}) %collective-permute-start.11) | collective-permute-done | bytes 135200 | tf_op jit(solution)/shard_map/ppermute | solution.py:381
  32.5 4.3 %transform.1 = (f32[4,2,16,512]{3,2,1,0:T(8,128)S(1)}, f32[4,2,16,512]{3,2,1,0:T(8,128)S(1)}, f32[4,2,16,512]{3,2,1,0:T(8,128)S(1)}, f32[4,2,16,512]{3,2,1,0:T(8...) custom-call(f32[264,128]{1,0:T(8,128)S(1)} %collective-permute-done., ...), custom_call_target="tpu_custom_call" | custom-call | tf_op jit(solution)/shard_map/transform/pallas_call | solution.py:382
  36.7 3.5 %collective-permute-start.12 = (f32[4,2,16,512]{3,2,1,0:T(8,128)S(1)}, f32[4,2,16,512]{3,2,1,0:T(8,128)S(1)}, u32[]{:S(2)}, u32[]{:S(2)}) collective-permute-start(f32[4,2,16,512]{3,2,1,0:T(8,128)S(1)} %get-tuple-element.44), channel_id=1, source_target_pairs={{0,6},{1,7},{2,4},{3,5},{4,2},{5,3},{6,0},{7,1},{8,14},{9,15},{10,... | collective-permute-start | bytes 786440 | tf_op jit(solution)/shard_map/ppermute | solution.py:450
  40.2 1.3 %collective-permute-start.14 = (f32[4,2,16,512]{3,2,1,0:T(8,128)S(1)}, f32[4,2,16,512]{3,2,1,0:T(8,128)S(1)}, u32[]{:S(2)}, u32[]{:S(2)}) collective-permute-start(f32[4,2,16,512]{3,2,1,0:T(8,128)S(1)} %get-tuple-element.47), channel_id=1, source_target_pairs={{0,2},{1,3},{2,0},{3,1},{4,6},{5,7},{6,4},{7,5},{8,10},{9,11},{10,... | collective-permute-start | bytes 786440 | tf_op jit(solution)/shard_map/ppermute | solution.py:450
  41.6 1.0 %collective-permute-start.15 = (f32[4,2,16,512]{3,2,1,0:T(8,128)S(1)}, f32[4,2,16,512]{3,2,1,0:T(8,128)S(1)}, u32[]{:S(2)}, u32[]{:S(2)}) collective-permute-start(f32[4,2,16,512]{3,2,1,0:T(8,128)S(1)} %get-tuple-element.49), channel_id=1, source_target_pairs={{0,7},{1,6},{2,5},{3,4},{4,3},{5,2},{6,1},{7,0},{8,15},{9,14},{10,... | collective-permute-start | bytes 786440 | tf_op jit(solution)/shard_map/ppermute | solution.py:450
  42.5 0.9 %collective-permute-start.16 = (f32[4,2,16,512]{3,2,1,0:T(8,128)S(1)}, f32[4,2,16,512]{3,2,1,0:T(8,128)S(1)}, u32[]{:S(2)}, u32[]{:S(2)}) collective-permute-start(f32[4,2,16,512]{3,2,1,0:T(8,128)S(1)} %get-tuple-element.50), channel_id=1, source_target_pairs={{0,5},{1,4},{2,7},{3,6},{4,1},{5,0},{6,3},{7,2},{8,13},{9,12},{10,... | collective-permute-start | bytes 786440 | tf_op jit(solution)/shard_map/ppermute | solution.py:450
  43.5 3.9 %collective-permute-done.12.refs_0_ = f32[4,2,16,512]{3,2,1,0:T(8,128)S(1)} collective-permute-done((f32[4,2,16,512]{3,2,1,0:T(8,128)S(1)}, f32[4,2,16,512]{3,2,1,0:T(8,128)S(1)}, u32[]{:S(2)}, u32[]{:S(2)}) %collective-permute-start.12) | collective-permute-done | bytes 262176 | tf_op jit(solution)/shard_map/ppermute | solution.py:450
  47.4 5.7 %collective-permute-done.14.refs_2_ = f32[4,2,16,512]{3,2,1,0:T(8,128)S(1)} collective-permute-done((f32[4,2,16,512]{3,2,1,0:T(8,128)S(1)}, f32[4,2,16,512]{3,2,1,0:T(8,128)S(1)}, u32[]{:S(2)}, u32[]{:S(2)}) %collective-permute-start.14) | collective-permute-done | bytes 262176 | tf_op jit(solution)/shard_map/ppermute | solution.py:450
  53.1 1.2 %collective-permute-start.19 = (f32[8,128]{1,0:T(8,128)S(1)}, f32[8,128]{1,0:T(8,128)S(1)}, u32[]{:S(2)}, u32[]{:S(2)}) collective-permute-start(f32[8,128]{1,0:T(8,128)S(1)} %get-tuple-element.54.refs_8_), channel_id=1, source_target_pairs={{0,16},{16,0},{1,17},{17,1},{2,18},{18,2},{3,19},{19,3},{4,20},{20... | collective-permute-start | bytes 12296 | tf_op jit(solution)/shard_map/ppermute | solution.py:315
  54.2 4.0 %collective-permute-done.15.refs_3_ = f32[4,2,16,512]{3,2,1,0:T(8,128)S(1)} collective-permute-done((f32[4,2,16,512]{3,2,1,0:T(8,128)S(1)}, f32[4,2,16,512]{3,2,1,0:T(8,128)S(1)}, u32[]{:S(2)}, u32[]{:S(2)}) %collective-permute-start.15) | collective-permute-done | bytes 262176 | tf_op jit(solution)/shard_map/ppermute | solution.py:450
  58.2 4.7 %collective-permute-done.16.refs_4_ = f32[4,2,16,512]{3,2,1,0:T(8,128)S(1)} collective-permute-done((f32[4,2,16,512]{3,2,1,0:T(8,128)S(1)}, f32[4,2,16,512]{3,2,1,0:T(8,128)S(1)}, u32[]{:S(2)}, u32[]{:S(2)}) %collective-permute-start.16) | collective-permute-done | bytes 262176 | tf_op jit(solution)/shard_map/ppermute | solution.py:450
  62.9 0.6 collective-permute-done.17.refs_5_
  63.5 2.1 %merge.1 = f32[2,4,512,128]{3,2,1,0:T(8,128)} custom-call(s32[1]{0:T(128)} %bitcast.me_ref, f32[4,2,16,512]{3,2,1,0:T(8,128)S(1)} %collective-permute-done.12.refs_0_, f32[4,2,16,512]{3,2,1,0:T(8,128)S(1)} %collective-permute-done.13.refs_1_, f32[4,2,16,512]{3,2,1,0:T(8,128)S(1)} %collective-permute-done.14.refs_2_, ...), custom_call_target="tpu_custom_call" | custom-call | tf_op jit(solution)/shard_map/merge/pallas_call | solution.py:456
  (20 shorter events, 0.3 us)
Async XLA Ops:
  0.0 6.9 %collective-permute-start.3 = (s32[32,2048]{1,0:T(8,128)}, s32[32,2048]{1,0:T(8,128)S(1)}, u32[]{:S(2)}, u32[]{:S(2)}) collective-permute-start(s32[32,2048]{1,0:T(8,128)} %codes_ref.1), channel_id=1, source_target_pairs={{0,1},{1,0},{2,3},{3,2},{4,5},{5,4},{6,7},{7,6},{8,9},{9,8},{10,11... | collective-permute-start | bytes 786440 | tf_op jit(solution)/shard_map/ppermute | solution.py:351
  0.5 6.4 %collective-permute-start.4 = (s32[32,2048]{1,0:T(8,128)}, s32[32,2048]{1,0:T(8,128)S(1)}, u32[]{:S(2)}, u32[]{:S(2)}) collective-permute-start(s32[32,2048]{1,0:T(8,128)} %mask_ref.1), channel_id=1, source_target_pairs={{0,1},{1,0},{2,3},{3,2},{4,5},{5,4},{6,7},{7,6},{8,9},{9,8},{10,11... | collective-permute-start | bytes 786440 | tf_op jit(solution)/shard_map/ppermute | solution.py:351
  0.5 4.8 %collective-permute-start.1 = (s32[2,4]{1,0:T(2,128)}, s32[2,4]{1,0:T(2,128)S(1)}, u32[]{:S(2)}, u32[]{:S(2)}) collective-permute-start(s32[2,4]{1,0:T(2,128)} %tiles_ref.1), channel_id=1, source_target_pairs={{0,17},{1,16},{2,19},{3,18},{4,21},{5,20},{6,23},{7,22},{8,25},{9,... | collective-permute-start | bytes 104 | tf_op jit(solution)/shard_map/ppermute | solution.py:350
  3.1 3.8 %collective-permute-start = (s32[2,4]{1,0:T(2,128)}, s32[2,4]{1,0:T(2,128)S(1)}, u32[]{:S(2)}, u32[]{:S(2)}) collective-permute-start(s32[2,4]{1,0:T(2,128)} %tiles_ref.1), channel_id=1, source_target_pairs={{0,16},{16,0},{1,17},{17,1},{2,18},{18,2},{3,19},{19,3},{4,20},{20... | collective-permute-start | bytes 104 | tf_op jit(solution)/shard_map/ppermute | solution.py:315
  3.5 3.4 %collective-permute-start.2 = (s32[2,4]{1,0:T(2,128)}, s32[2,4]{1,0:T(2,128)S(1)}, u32[]{:S(2)}, u32[]{:S(2)}) collective-permute-start(s32[2,4]{1,0:T(2,128)} %tiles_ref.1), channel_id=1, source_target_pairs={{0,1},{1,0},{2,3},{3,2},{4,5},{5,4},{6,7},{7,6},{8,9},{9,8},{10,11... | collective-permute-start | bytes 104 | tf_op jit(solution)/shard_map/ppermute | solution.py:351
  8.2 14.2 %collective-permute-start.5 = (f32[264,128]{1,0:T(8,128)S(1)}, f32[264,128]{1,0:T(8,128)S(1)}, u32[]{:S(2)}, u32[]{:S(2)}) collective-permute-start(f32[264,128]{1,0:T(8,128)S(1)} %get-tuple-element.33), channel_id=1, source_target_pairs={{0,8},{1,9},{2,10},{3,11},{4,12},{5,13},{6,14},{7,15},{8,0},{9,1},... | collective-permute-start | bytes 405512 | tf_op jit(solution)/shard_map/ppermute | solution.py:381
  10.8 12.1 %collective-permute-start.6 = (f32[264,128]{1,0:T(8,128)S(1)}, f32[264,128]{1,0:T(8,128)S(1)}, u32[]{:S(2)}, u32[]{:S(2)}) collective-permute-start(f32[264,128]{1,0:T(8,128)S(1)} %get-tuple-element.34), channel_id=1, source_target_pairs={{0,2},{1,3},{2,0},{3,1},{4,6},{5,7},{6,4},{7,5},{8,10},{9,11},{10,... | collective-permute-start | bytes 405512 | tf_op jit(solution)/shard_map/ppermute | solution.py:381
  12.3 18.0 %collective-permute-start.7 = (f32[264,128]{1,0:T(8,128)S(1)}, f32[264,128]{1,0:T(8,128)S(1)}, u32[]{:S(2)}, u32[]{:S(2)}) collective-permute-start(f32[264,128]{1,0:T(8,128)S(1)} %get-tuple-element.35), channel_id=1, source_target_pairs={{0,10},{1,11},{2,8},{3,9},{4,14},{5,15},{6,12},{7,13},{8,2},{9,3},... | collective-permute-start | bytes 405512 | tf_op jit(solution)/shard_map/ppermute | solution.py:381
  12.6 17.7 %collective-permute-start.8 = (f32[264,128]{1,0:T(8,128)S(1)}, f32[264,128]{1,0:T(8,128)S(1)}, u32[]{:S(2)}, u32[]{:S(2)}) collective-permute-start(f32[264,128]{1,0:T(8,128)S(1)} %get-tuple-element.36), channel_id=1, source_target_pairs={{0,4},{1,5},{2,6},{3,7},{4,0},{5,1},{6,2},{7,3},{8,12},{9,13},{10,... | collective-permute-start | bytes 405512 | tf_op jit(solution)/shard_map/ppermute | solution.py:381
  14.2 16.2 %collective-permute-start.9 = (f32[264,128]{1,0:T(8,128)S(1)}, f32[264,128]{1,0:T(8,128)S(1)}, u32[]{:S(2)}, u32[]{:S(2)}) collective-permute-start(f32[264,128]{1,0:T(8,128)S(1)} %get-tuple-element.37), channel_id=1, source_target_pairs={{0,12},{1,13},{2,14},{3,15},{4,8},{5,9},{6,10},{7,11},{8,4},{9,5},... | collective-permute-start | bytes 405512 | tf_op jit(solution)/shard_map/ppermute | solution.py:381
  22.4 8.4 %collective-permute-start.10 = (f32[264,128]{1,0:T(8,128)S(1)}, f32[264,128]{1,0:T(8,128)S(1)}, u32[]{:S(2)}, u32[]{:S(2)}) collective-permute-start(f32[264,128]{1,0:T(8,128)S(1)} %get-tuple-element.38), channel_id=1, source_target_pairs={{0,6},{1,7},{2,4},{3,5},{4,2},{5,3},{6,0},{7,1},{8,14},{9,15},{10,... | collective-permute-start | bytes 405512 | tf_op jit(solution)/shard_map/ppermute | solution.py:381
  22.9 9.5 %collective-permute-start.11 = (f32[264,128]{1,0:T(8,128)S(1)}, f32[264,128]{1,0:T(8,128)S(1)}, u32[]{:S(2)}, u32[]{:S(2)}) collective-permute-start(f32[264,128]{1,0:T(8,128)S(1)} %get-tuple-element.39), channel_id=1, source_target_pairs={{0,14},{1,15},{2,12},{3,13},{4,10},{5,11},{6,8},{7,9},{8,6},{9,7},... | collective-permute-start | bytes 405512 | tf_op jit(solution)/shard_map/ppermute | solution.py:381
  27.2 1.0 %copy-start = (bf16[2,16,16,512]{3,2,1,0:T(8,128)(2,1)S(1)}, bf16[2,16,16,512]{3,2,1,0:T(8,128)(2,1)}, u32[]{:S(2)}) copy-start(bf16[2,16,16,512]{3,2,1,0:T(8,128)(2,1)} %constant.40.clone.inner_ref) | copy-start | bytes 1572868
  28.2 1.0 %copy-start.1 = (bf16[2,8,2,16,512]{4,3,2,1,0:T(8,128)(2,1)S(1)}, bf16[2,8,2,16,512]{4,3,2,1,0:T(8,128)(2,1)}, u32[]{:S(2)}) copy-start(bf16[2,8,2,16,512]{4,3,2,1,0:T(8,128)(2,1)} %constant.39.clone.outer_ref) | copy-start | bytes 1572868
  29.3 0.9 %copy-start.2 = (f32[64,512]{1,0:T(8,128)S(1)}, f32[64,512]{1,0:T(8,128)}, u32[]{:S(2)}) copy-start(f32[64,512]{1,0:T(8,128)} %constant.41.clone.twist_ref) | copy-start | bytes 393220
  36.7 10.7 %collective-permute-start.12 = (f32[4,2,16,512]{3,2,1,0:T(8,128)S(1)}, f32[4,2,16,512]{3,2,1,0:T(8,128)S(1)}, u32[]{:S(2)}, u32[]{:S(2)}) collective-permute-start(f32[4,2,16,512]{3,2,1,0:T(8,128)S(1)} %get-tuple-element.44), channel_id=1, source_target_pairs={{0,6},{1,7},{2,4},{3,5},{4,2},{5,3},{6,0},{7,1},{8,14},{9,15},{10,... | collective-permute-start | bytes 786440 | tf_op jit(solution)/shard_map/ppermute | solution.py:450
  40.2 12.8 %collective-permute-start.14 = (f32[4,2,16,512]{3,2,1,0:T(8,128)S(1)}, f32[4,2,16,512]{3,2,1,0:T(8,128)S(1)}, u32[]{:S(2)}, u32[]{:S(2)}) collective-permute-start(f32[4,2,16,512]{3,2,1,0:T(8,128)S(1)} %get-tuple-element.47), channel_id=1, source_target_pairs={{0,2},{1,3},{2,0},{3,1},{4,6},{5,7},{6,4},{7,5},{8,10},{9,11},{10,... | collective-permute-start | bytes 786440 | tf_op jit(solution)/shard_map/ppermute | solution.py:450
  41.5 11.5 %collective-permute-start.13 = (f32[4,2,16,512]{3,2,1,0:T(8,128)S(1)}, f32[4,2,16,512]{3,2,1,0:T(8,128)S(1)}, u32[]{:S(2)}, u32[]{:S(2)}) collective-permute-start(f32[4,2,16,512]{3,2,1,0:T(8,128)S(1)} %get-tuple-element.45), channel_id=1, source_target_pairs={{0,4},{1,5},{2,6},{3,7},{4,0},{5,1},{6,2},{7,3},{8,12},{9,13},{10,... | collective-permute-start | bytes 786440 | tf_op jit(solution)/shard_map/ppermute | solution.py:450
  41.6 16.7 %collective-permute-start.15 = (f32[4,2,16,512]{3,2,1,0:T(8,128)S(1)}, f32[4,2,16,512]{3,2,1,0:T(8,128)S(1)}, u32[]{:S(2)}, u32[]{:S(2)}) collective-permute-start(f32[4,2,16,512]{3,2,1,0:T(8,128)S(1)} %get-tuple-element.49), channel_id=1, source_target_pairs={{0,7},{1,6},{2,5},{3,4},{4,3},{5,2},{6,1},{7,0},{8,15},{9,14},{10,... | collective-permute-start | bytes 786440 | tf_op jit(solution)/shard_map/ppermute | solution.py:450
  42.5 20.4 %collective-permute-start.16 = (f32[4,2,16,512]{3,2,1,0:T(8,128)S(1)}, f32[4,2,16,512]{3,2,1,0:T(8,128)S(1)}, u32[]{:S(2)}, u32[]{:S(2)}) collective-permute-start(f32[4,2,16,512]{3,2,1,0:T(8,128)S(1)} %get-tuple-element.50), channel_id=1, source_target_pairs={{0,5},{1,4},{2,7},{3,6},{4,1},{5,0},{6,3},{7,2},{8,13},{9,12},{10,... | collective-permute-start | bytes 786440 | tf_op jit(solution)/shard_map/ppermute | solution.py:450
  47.4 16.1 %collective-permute-start.17 = (f32[4,2,16,512]{3,2,1,0:T(8,128)S(1)}, f32[4,2,16,512]{3,2,1,0:T(8,128)S(1)}, u32[]{:S(2)}, u32[]{:S(2)}) collective-permute-start(f32[4,2,16,512]{3,2,1,0:T(8,128)S(1)} %get-tuple-element.51), channel_id=1, source_target_pairs={{0,3},{1,2},{2,1},{3,0},{4,7},{5,6},{6,5},{7,4},{8,11},{9,10},{10,... | collective-permute-start | bytes 786440 | tf_op jit(solution)/shard_map/ppermute | solution.py:450
  53.1 10.4 %collective-permute-start.18 = (f32[4,2,16,512]{3,2,1,0:T(8,128)S(1)}, f32[4,2,16,512]{3,2,1,0:T(8,128)S(1)}, u32[]{:S(2)}, u32[]{:S(2)}) collective-permute-start(f32[4,2,16,512]{3,2,1,0:T(8,128)S(1)} %get-tuple-element.52), channel_id=1, source_target_pairs={{0,1},{1,0},{2,3},{3,2},{4,5},{5,4},{6,7},{7,6},{8,9},{9,8},{10,11... | collective-permute-start | bytes 786440 | tf_op jit(solution)/shard_map/ppermute | solution.py:450
  53.1 10.4 %collective-permute-start.19 = (f32[8,128]{1,0:T(8,128)S(1)}, f32[8,128]{1,0:T(8,128)S(1)}, u32[]{:S(2)}, u32[]{:S(2)}) collective-permute-start(f32[8,128]{1,0:T(8,128)S(1)} %get-tuple-element.54.refs_8_), channel_id=1, source_target_pairs={{0,16},{16,0},{1,17},{17,1},{2,18},{18,2},{3,19},{19,3},{4,20},{20... | collective-permute-start | bytes 12296 | tf_op jit(solution)/shard_map/ppermute | solution.py:315

commit v10 on v9

--- a/solution.py
+++ b/solution.py
@@ -60,10 +60,10 @@
 
 
 def inner_tables(plan):
-    angle = np.arange(INNER)[:, None] * np.arange(INNER)[None, :] % INNER
+    angle = np.arange(INNER)[:, None] * np.arange(INNER // 2)[None, :] % INNER
     angle = angle * (2.0 * np.pi / INNER)
     table = np.concatenate([np.cos(angle), np.sin(angle)], axis=1)
-    return split_bf16(table.reshape(plan.n_col, plan.k2_dev, 2 * INNER))
+    return split_bf16(table.reshape(plan.n_col, plan.k2_dev // 2, 2, INNER).transpose(0, 2, 1, 3))
 
 
 def twist_tables(plan):
@@ -184,19 +184,21 @@
 
 def tables_kernel(plan, blocks, me_ref, outer_ref, inner_ref, twist_ref, w1_ref, w2_ref, turn_ref):
     me = me_ref[0]
-    w1, w2 = [], []
+    w1, w2 = [], ([], [])
     for s in range(2):
         rows = [outer_ref[s, (me >> 1) ^ b if blocks > 1 else 0] for b in range(blocks)]
         cos, sin = (jnp.concatenate([both[i] for both in rows]) for i in range(2))
         w1.append(jnp.concatenate([jnp.concatenate([cos, sin]), jnp.concatenate([-sin, cos])], axis=1))
-        parts = []
-        for b in range(plan.group):
-            both = inner_ref[s, me ^ b]
-            parts.append(both)
-            parts.append(jnp.concatenate([-both[:, INNER:], both[:, :INNER]], axis=1))
-        w2.append(jnp.concatenate(parts))
+        for p in range(2):
+            parts = []
+            for b in range(plan.group):
+                both = inner_ref[s, me ^ b, p].astype(jnp.float32)
+                parts.append(both)
+                parts.append(jnp.concatenate([-both[:, INNER // 2 :], both[:, : INNER // 2]], axis=1))
+            w2[p].append(jnp.concatenate(parts).astype(jnp.bfloat16))
     w1_ref[...] = jnp.concatenate([w1[0], w1[0], w1[1]])
-    w2_ref[...] = jnp.concatenate([w2[0], w2[1], w2[0]], axis=1)
+    for p in range(2):
+        w2_ref[p] = jnp.concatenate([w2[p][0], w2[p][1]])
     turn_ref[...] = twist_ref[...]
 
 
@@ -248,7 +250,6 @@
 
 def transform_rows(plan, fields, tables, outs):
     w1_ref, w2_ref, turn_ref = tables
-    size = 2 * plan.k2_dev
     x = jnp.concatenate(fields, axis=1)
     xh = x.astype(jnp.bfloat16)
     xl = (x - xh.astype(jnp.float32)).astype(jnp.bfloat16)
@@ -263,17 +264,25 @@
         tc.append(cos * fine_cos - sin * fine_sin)
         ts.append(sin * fine_cos + cos * fine_sin)
     tc, ts = jnp.concatenate(tc), jnp.concatenate(ts)
-    fs = []
+    fs = ([], [])
     for r in range(plan.rows):
         yr, yi = y[r * INNER : (r + 1) * INNER, : plan.k1], y[r * INNER : (r + 1) * INNER, plan.k1 :]
-        fs.append(jnp.concatenate([yr * tc + yi * ts, yi * tc - yr * ts], axis=0))
-    f = jnp.concatenate(fs, axis=1)
-    fh = f.astype(jnp.bfloat16)
-    fl = (f - fh.astype(jnp.float32)).astype(jnp.bfloat16)
-    z = jnp.dot(w2_ref[...], jnp.concatenate([fh, fh, fl]), preferred_element_type=jnp.float32)
-    for r in range(plan.rows):
-        for b in range(plan.group):
-            outs[b][r] = z[b * size : (b + 1) * size, r * plan.k1 : (r + 1) * plan.k1].reshape(2, plan.k2_dev, plan.k1)
+        fr, fi = yr * tc + yi * ts, yi * tc - yr * ts
+        for p in range(2):
+            pair = [f[: INNER // 2] + f[INNER // 2 :] if p == 0 else f[: INNER // 2] - f[INNER // 2 :] for f in (fr, fi)]
+            fs[p].append(jnp.concatenate(pair))
+    half = plan.k2_dev // 2
+    for p in range(2):
+        f = jnp.concatenate(fs[p], axis=1)
+        fh = f.astype(jnp.bfloat16)
+        fl = (f - fh.astype(jnp.float32)).astype(jnp.bfloat16)
+        size = plan.group * plan.k2_dev
+        z = jnp.dot(w2_ref[p], fh, preferred_element_type=jnp.float32)
+        z = z[:size] + z[size:] + jnp.dot(w2_ref[p, :size], fl, preferred_element_type=jnp.float32)
+        for r in range(plan.rows):
+            for b in range(plan.group):
+                part = z[b * plan.k2_dev : (b + 1) * plan.k2_dev, r * plan.k1 : (r + 1) * plan.k1]
+                outs[b][r, :, p * half : (p + 1) * half, :] = part.reshape(2, half, plan.k1)
 
 
 def merge_kernel(plan, swap_bit, me_ref, *refs):
@@ -287,21 +296,21 @@
     scale = jnp.sqrt(float(plan.rows_all) / total)
     inside = lax.rem(me_ref[0], plan.group)
     swapped = lax.rem(inside // swap_bit, 2) == 1
-    take = min(plan.k2_dev, SUBS)
-    stride = plan.k1_tiles * SUBS
+    half = plan.k2_dev // 2
+    stride = 2 * plan.k1_tiles * SUBS
     copies = []
     for slot in range(plan.group):
         part = slot % 2
         base = [b for b in range(plan.group) if b & swap_bit == 0][slot // 2]
         for r in range(plan.rows):
-            for k2 in range(0, plan.k2_dev, take):
+            for p in range(2):
                 for j in range(plan.k1_tiles):
-                    lanes = slice(j * LANES, (j + 1) * LANES)
-                    a = chunks[base][r, part, k2 : k2 + take, lanes] * scale
-                    b = chunks[base + swap_bit][r, part, k2 : k2 + take, lanes] * scale
-                    at = (k2 * plan.k1_tiles + j) * SUBS + r
-                    tile_ref[slot, pl.ds(at, take, stride=stride), :] = jnp.where(swapped, b, a)
-                    tile_ref[slot, pl.ds(at + plan.rows, take, stride=stride), :] = jnp.where(swapped, a, b)
+                    rows, lanes = slice(p * half, (p + 1) * half), slice(j * LANES, (j + 1) * LANES)
+                    a = chunks[base][r, part, rows, lanes] * scale
+                    b = chunks[base + swap_bit][r, part, rows, lanes] * scale
+                    at = (p * plan.k1_tiles + j) * SUBS + r
+                    tile_ref[slot, pl.ds(at, half, stride=stride), :] = jnp.where(swapped, b, a)
+                    tile_ref[slot, pl.ds(at + plan.rows, half, stride=stride), :] = jnp.where(swapped, a, b)
         source = inside ^ base
         tile = source // 2 if swap_bit == 1 else source % 2 * 2 + source // 4
         copy = pltpu.make_async_copy(tile_ref.at[slot], out_ref.at[part, tile], sems.at[slot])
@@ -325,7 +334,7 @@
         partial(tables_kernel, plan, blocks),
         out_shape=[
             jax.ShapeDtypeStruct((6 * plan.n1, 2 * plan.k1), jnp.bfloat16),
-            jax.ShapeDtypeStruct((2 * plan.group * plan.k2_dev, 6 * INNER), jnp.bfloat16),
+            jax.ShapeDtypeStruct((2, 2 * plan.group * plan.k2_dev, INNER), jnp.bfloat16),
             jax.ShapeDtypeStruct((2 * (INNER // FINE + FINE), plan.k1), jnp.float32),
         ],
         in_specs=[smem] + [vmem] * 3,

time: 65.9 us -> 65 us (0.986)
  Pallas kernels: 9.47 us -> 8.62 us
    pallas_call x1, Pallas kernels: 4.25 us -> 3.44 us  [spectra_by_chip(): pl.pallas_call(partial(chip_transform_kernel, plan, order), out_shape=spe...]
where the time goes in v10:
time: 65 us; the launch traced here: 64.8 us
  waiting for transfers between devices  28.3 us (44%)
  starting transfers between devices  24.8 us (38%)
  Pallas kernels  8.62 us (13%)
  local copies, waits for them, and re-layouts  2.89 us (4%)
    ppermute x7, waiting for transfers between devices, per_device(): lax.ppermute(made[b], 'col', [(q, q ^ b) for q in range(n_col)])  18.9 us
    ppermute x7, starting transfers between devices, spectra_by_chip(): lax.ppermute(rows[b], 'col', [(q, q ^ 2 * b) for q in range(n_col)])  13.3 us
    ppermute x7, waiting for transfers between devices, spectra_by_chip(): lax.ppermute(rows[b], 'col', [(q, q ^ 2 * b) for q in range(n_col)])  7.91 us
    ppermute x7, starting transfers between devices, per_device(): lax.ppermute(made[b], 'col', [(q, q ^ b) for q in range(n_col)])  6.74 us
    pallas_call x1, Pallas kernels, spectra_by_chip(): pl.pallas_call(partial(chip_transform_kernel, plan, order), out_shape=spe...  3.44 us
    unnamed x6, local copies, waits for them, and re-layouts  2.89 us
    ppermute x1, starting transfers between devices, spectra_by_chip(): near_others.append(lax.ppermute(tile_offsets, ('row', 'col'), pairs))  2.57 us
    pallas_call x1, Pallas kernels, per_device(): pl.pallas_call(partial(merge_kernel, plan, 2 if by_chip else 1), out_shap...  2.12 us
  transfers between devices with their start and end apart: 20, of which 9 were waited for; matrix products, arithmetic and copies ran while one was open for 0% of the time, Pallas kernels for 3%

profile of v10, /device:TPU:0, one launch (start us, length us, event | category | flops | bytes accessed | tf_op | source)
XLA Modules:
  0.0 64.8 jit_solution(18082485246283578667)
XLA Ops:
  0.0 0.5 collective-permute-start.3
  0.5 2.6 %collective-permute-start.1 = (s32[2,4]{1,0:T(2,128)}, s32[2,4]{1,0:T(2,128)S(1)}, u32[]{:S(2)}, u32[]{:S(2)}) collective-permute-start(s32[2,4]{1,0:T(2,128)} %tiles_ref.1), channel_id=1, source_target_pairs={{0,17},{1,16},{2,19},{3,18},{4,21},{5,20},{6,23},{7,22},{8,25},{9,... | collective-permute-start | bytes 104 | tf_op jit(solution)/shard_map/ppermute | solution.py:359
  3.1 0.4 collective-permute-start
  3.7 1.6 %own.1 = (s32[16,2048]{1,0:T(8,128)S(1)}, s32[16,2048]{1,0:T(8,128)S(1)}, s32[8,128]{1,0:T(8,128)S(1)}) custom-call(s32[3]{0:T(128)S(1)} %pad_add_fusion.me_ref, s32[2,4]{1,0:T(2,128)} %tiles_ref.1, s32[32,2048]{1,0:T(8,128)} %codes_ref.1, s32[32,2048]{1,0:T(8,128)} %mask_ref.1), custom_call_target="tpu_custom_call" | custom-call | tf_op jit(solution)/shard_map/own/pallas_call | solution.py:362
  5.3 1.5 %collective-permute-done.refs_0_ = s32[2,4]{1,0:T(2,128)S(1)} collective-permute-done((s32[2,4]{1,0:T(2,128)}, s32[2,4]{1,0:T(2,128)S(1)}, u32[]{:S(2)}, u32[]{:S(2)}) %collective-permute-start) | collective-permute-done | bytes 64 | tf_op jit(solution)/shard_map/ppermute | solution.py:324
  6.9 1.3 %field.1 = (f32[264,128]{1,0:T(8,128)S(1)}, f32[264,128]{1,0:T(8,128)S(1)}, f32[264,128]{1,0:T(8,128)S(1)}, f32[264,128]{1,0:T(8,128)S(1)}, f32[264,128]{1,0:T(8...) custom-call(s32[3]{0:T(128)S(1)} %pad_add_fusion.me_ref, ...), custom_call_target="tpu_custom_call" | custom-call | tf_op jit(solution)/shard_map/field/pallas_call | solution.py:380
  8.2 2.7 %collective-permute-start.5 = (f32[264,128]{1,0:T(8,128)S(1)}, f32[264,128]{1,0:T(8,128)S(1)}, u32[]{:S(2)}, u32[]{:S(2)}) collective-permute-start(f32[264,128]{1,0:T(8,128)S(1)} %get-tuple-element.33), channel_id=1, source_target_pairs={{0,8},{1,9},{2,10},{3,11},{4,12},{5,13},{6,14},{7,15},{8,0},{9,1},... | collective-permute-start | bytes 405512 | tf_op jit(solution)/shard_map/ppermute | solution.py:390
  10.8 1.5 %collective-permute-start.6 = (f32[264,128]{1,0:T(8,128)S(1)}, f32[264,128]{1,0:T(8,128)S(1)}, u32[]{:S(2)}, u32[]{:S(2)}) collective-permute-start(f32[264,128]{1,0:T(8,128)S(1)} %get-tuple-element.34), channel_id=1, source_target_pairs={{0,2},{1,3},{2,0},{3,1},{4,6},{5,7},{6,4},{7,5},{8,10},{9,11},{10,... | collective-permute-start | bytes 405512 | tf_op jit(solution)/shard_map/ppermute | solution.py:390
  12.3 0.3 collective-permute-start.7
  12.6 1.6 %collective-permute-start.8 = (f32[264,128]{1,0:T(8,128)S(1)}, f32[264,128]{1,0:T(8,128)S(1)}, u32[]{:S(2)}, u32[]{:S(2)}) collective-permute-start(f32[264,128]{1,0:T(8,128)S(1)} %get-tuple-element.36), channel_id=1, source_target_pairs={{0,4},{1,5},{2,6},{3,7},{4,0},{5,1},{6,2},{7,3},{8,12},{9,13},{10,... | collective-permute-start | bytes 405512 | tf_op jit(solution)/shard_map/ppermute | solution.py:390
  14.2 2.5 %collective-permute-start.9 = (f32[264,128]{1,0:T(8,128)S(1)}, f32[264,128]{1,0:T(8,128)S(1)}, u32[]{:S(2)}, u32[]{:S(2)}) collective-permute-start(f32[264,128]{1,0:T(8,128)S(1)} %get-tuple-element.37), channel_id=1, source_target_pairs={{0,12},{1,13},{2,14},{3,15},{4,8},{5,9},{6,10},{7,11},{8,4},{9,5},... | collective-permute-start | bytes 405512 | tf_op jit(solution)/shard_map/ppermute | solution.py:390
  16.7 5.7 %collective-permute-done.5.refs_0_ = f32[264,128]{1,0:T(8,128)S(1)} collective-permute-done((f32[264,128]{1,0:T(8,128)S(1)}, f32[264,128]{1,0:T(8,128)S(1)}, u32[]{:S(2)}, u32[]{:S(2)}) %collective-permute-start.5) | collective-permute-done | bytes 135200 | tf_op jit(solution)/shard_map/ppermute | solution.py:390
  22.4 0.5 collective-permute-start.10
  22.9 4.3 %collective-permute-start.11 = (f32[264,128]{1,0:T(8,128)S(1)}, f32[264,128]{1,0:T(8,128)S(1)}, u32[]{:S(2)}, u32[]{:S(2)}) collective-permute-start(f32[264,128]{1,0:T(8,128)S(1)} %get-tuple-element.39), channel_id=1, source_target_pairs={{0,14},{1,15},{2,12},{3,13},{4,10},{5,11},{6,8},{7,9},{8,6},{9,7},... | collective-permute-start | bytes 405512 | tf_op jit(solution)/shard_map/ppermute | solution.py:390
  27.2 1.0 %copy-done = bf16[2,8,2,16,512]{4,3,2,1,0:T(8,128)(2,1)S(1)} copy-done((bf16[2,8,2,16,512]{4,3,2,1,0:T(8,128)(2,1)S(1)}, bf16[2,8,2,16,512]{4,3,2,1,0:T(8,128)(2,1)}, u32[]{:S(2)}) %copy-start) | copy-done | bytes 524312
  28.3 0.9 %copy-done.1 = bf16[2,16,2,8,256]{4,3,2,1,0:T(8,128)(2,1)S(1)} copy-done((bf16[2,16,2,8,256]{4,3,2,1,0:T(8,128)(2,1)S(1)}, bf16[2,16,2,8,256]{4,3,2,1,0:T(8,128)(2,1)}, u32[]{:S(2)}) %copy-start.1) | copy-done | bytes 262168
  29.2 0.9 %copy-done.2 = f32[64,512]{1,0:T(8,128)S(1)} copy-done((f32[64,512]{1,0:T(8,128)S(1)}, f32[64,512]{1,0:T(8,128)}, u32[]{:S(2)}) %copy-start.2) | copy-done | bytes 131096
  30.1 0.1 tables.1
  30.3 0.6 collective-permute-done.10.refs_5_
  30.8 1.6 %collective-permute-done.11.refs_6_ = f32[264,128]{1,0:T(8,128)S(1)} collective-permute-done((f32[264,128]{1,0:T(8,128)S(1)}, f32[264,128]{1,0:T(8,128)S(1)}, u32[]{:S(2)}, u32[]{:S(2)}) %collective-permute-start.11) | collective-permute-done | bytes 135200 | tf_op jit(solution)/shard_map/ppermute | solution.py:390
  32.5 3.4 %transform.1 = (f32[4,2,16,512]{3,2,1,0:T(8,128)S(1)}, f32[4,2,16,512]{3,2,1,0:T(8,128)S(1)}, f32[4,2,16,512]{3,2,1,0:T(8,128)S(1)}, f32[4,2,16,512]{3,2,1,0:T(8...) custom-call(f32[264,128]{1,0:T(8,128)S(1)} %collective-permute-done., ...), custom_call_target="tpu_custom_call" | custom-call | tf_op jit(solution)/shard_map/transform/pallas_call | solution.py:391
  35.9 3.5 %collective-permute-start.12 = (f32[4,2,16,512]{3,2,1,0:T(8,128)S(1)}, f32[4,2,16,512]{3,2,1,0:T(8,128)S(1)}, u32[]{:S(2)}, u32[]{:S(2)}) collective-permute-start(f32[4,2,16,512]{3,2,1,0:T(8,128)S(1)} %get-tuple-element.44), channel_id=1, source_target_pairs={{0,6},{1,7},{2,4},{3,5},{4,2},{5,3},{6,0},{7,1},{8,14},{9,15},{10,... | collective-permute-start | bytes 786440 | tf_op jit(solution)/shard_map/ppermute | solution.py:459
  39.4 1.3 %collective-permute-start.14 = (f32[4,2,16,512]{3,2,1,0:T(8,128)S(1)}, f32[4,2,16,512]{3,2,1,0:T(8,128)S(1)}, u32[]{:S(2)}, u32[]{:S(2)}) collective-permute-start(f32[4,2,16,512]{3,2,1,0:T(8,128)S(1)} %get-tuple-element.47), channel_id=1, source_target_pairs={{0,2},{1,3},{2,0},{3,1},{4,6},{5,7},{6,4},{7,5},{8,10},{9,11},{10,... | collective-permute-start | bytes 786440 | tf_op jit(solution)/shard_map/ppermute | solution.py:459
  40.7 0.9 %collective-permute-start.15 = (f32[4,2,16,512]{3,2,1,0:T(8,128)S(1)}, f32[4,2,16,512]{3,2,1,0:T(8,128)S(1)}, u32[]{:S(2)}, u32[]{:S(2)}) collective-permute-start(f32[4,2,16,512]{3,2,1,0:T(8,128)S(1)} %get-tuple-element.49), channel_id=1, source_target_pairs={{0,7},{1,6},{2,5},{3,4},{4,3},{5,2},{6,1},{7,0},{8,15},{9,14},{10,... | collective-permute-start | bytes 786440 | tf_op jit(solution)/shard_map/ppermute | solution.py:459
  41.7 0.9 %collective-permute-start.16 = (f32[4,2,16,512]{3,2,1,0:T(8,128)S(1)}, f32[4,2,16,512]{3,2,1,0:T(8,128)S(1)}, u32[]{:S(2)}, u32[]{:S(2)}) collective-permute-start(f32[4,2,16,512]{3,2,1,0:T(8,128)S(1)} %get-tuple-element.50), channel_id=1, source_target_pairs={{0,5},{1,4},{2,7},{3,6},{4,1},{5,0},{6,3},{7,2},{8,13},{9,12},{10,... | collective-permute-start | bytes 786440 | tf_op jit(solution)/shard_map/ppermute | solution.py:459
  42.6 3.9 %collective-permute-done.12.refs_0_ = f32[4,2,16,512]{3,2,1,0:T(8,128)S(1)} collective-permute-done((f32[4,2,16,512]{3,2,1,0:T(8,128)S(1)}, f32[4,2,16,512]{3,2,1,0:T(8,128)S(1)}, u32[]{:S(2)}, u32[]{:S(2)}) %collective-permute-start.12) | collective-permute-done | bytes 262176 | tf_op jit(solution)/shard_map/ppermute | solution.py:459
  46.6 5.7 %collective-permute-done.14.refs_2_ = f32[4,2,16,512]{3,2,1,0:T(8,128)S(1)} collective-permute-done((f32[4,2,16,512]{3,2,1,0:T(8,128)S(1)}, f32[4,2,16,512]{3,2,1,0:T(8,128)S(1)}, u32[]{:S(2)}, u32[]{:S(2)}) %collective-permute-start.14) | collective-permute-done | bytes 262176 | tf_op jit(solution)/shard_map/ppermute | solution.py:459
  52.3 1.1 %collective-permute-start.19 = (f32[8,128]{1,0:T(8,128)S(1)}, f32[8,128]{1,0:T(8,128)S(1)}, u32[]{:S(2)}, u32[]{:S(2)}) collective-permute-start(f32[8,128]{1,0:T(8,128)S(1)} %get-tuple-element.54.refs_8_), channel_id=1, source_target_pairs={{0,16},{16,0},{1,17},{17,1},{2,18},{18,2},{3,19},{19,3},{4,20},{20... | collective-permute-start | bytes 12296 | tf_op jit(solution)/shard_map/ppermute | solution.py:324
  53.4 4.0 %collective-permute-done.15.refs_3_ = f32[4,2,16,512]{3,2,1,0:T(8,128)S(1)} collective-permute-done((f32[4,2,16,512]{3,2,1,0:T(8,128)S(1)}, f32[4,2,16,512]{3,2,1,0:T(8,128)S(1)}, u32[]{:S(2)}, u32[]{:S(2)}) %collective-permute-start.15) | collective-permute-done | bytes 262176 | tf_op jit(solution)/shard_map/ppermute | solution.py:459
  57.4 4.7 %collective-permute-done.16.refs_4_ = f32[4,2,16,512]{3,2,1,0:T(8,128)S(1)} collective-permute-done((f32[4,2,16,512]{3,2,1,0:T(8,128)S(1)}, f32[4,2,16,512]{3,2,1,0:T(8,128)S(1)}, u32[]{:S(2)}, u32[]{:S(2)}) %collective-permute-start.16) | collective-permute-done | bytes 262176 | tf_op jit(solution)/shard_map/ppermute | solution.py:459
  62.1 0.6 collective-permute-done.17.refs_5_
  62.7 2.1 %merge.1 = f32[2,4,512,128]{3,2,1,0:T(8,128)} custom-call(s32[1]{0:T(128)} %bitcast.me_ref, f32[4,2,16,512]{3,2,1,0:T(8,128)S(1)} %collective-permute-done.12.refs_0_, f32[4,2,16,512]{3,2,1,0:T(8,128)S(1)} %collective-permute-done.13.refs_1_, f32[4,2,16,512]{3,2,1,0:T(8,128)S(1)} %collective-permute-done.14.refs_2_, ...), custom_call_target="tpu_custom_call" | custom-call | tf_op jit(solution)/shard_map/merge/pallas_call | solution.py:465
  (20 shorter events, 0.3 us)
Async XLA Ops:
  0.0 6.9 %collective-permute-start.3 = (s32[32,2048]{1,0:T(8,128)}, s32[32,2048]{1,0:T(8,128)S(1)}, u32[]{:S(2)}, u32[]{:S(2)}) collective-permute-start(s32[32,2048]{1,0:T(8,128)} %codes_ref.1), channel_id=1, source_target_pairs={{0,1},{1,0},{2,3},{3,2},{4,5},{5,4},{6,7},{7,6},{8,9},{9,8},{10,11... | collective-permute-start | bytes 786440 | tf_op jit(solution)/shard_map/ppermute | solution.py:360
  0.5 6.4 %collective-permute-start.4 = (s32[32,2048]{1,0:T(8,128)}, s32[32,2048]{1,0:T(8,128)S(1)}, u32[]{:S(2)}, u32[]{:S(2)}) collective-permute-start(s32[32,2048]{1,0:T(8,128)} %mask_ref.1), channel_id=1, source_target_pairs={{0,1},{1,0},{2,3},{3,2},{4,5},{5,4},{6,7},{7,6},{8,9},{9,8},{10,11... | collective-permute-start | bytes 786440 | tf_op jit(solution)/shard_map/ppermute | solution.py:360
  0.5 4.8 %collective-permute-start.1 = (s32[2,4]{1,0:T(2,128)}, s32[2,4]{1,0:T(2,128)S(1)}, u32[]{:S(2)}, u32[]{:S(2)}) collective-permute-start(s32[2,4]{1,0:T(2,128)} %tiles_ref.1), channel_id=1, source_target_pairs={{0,17},{1,16},{2,19},{3,18},{4,21},{5,20},{6,23},{7,22},{8,25},{9,... | collective-permute-start | bytes 104 | tf_op jit(solution)/shard_map/ppermute | solution.py:359
  3.1 3.8 %collective-permute-start = (s32[2,4]{1,0:T(2,128)}, s32[2,4]{1,0:T(2,128)S(1)}, u32[]{:S(2)}, u32[]{:S(2)}) collective-permute-start(s32[2,4]{1,0:T(2,128)} %tiles_ref.1), channel_id=1, source_target_pairs={{0,16},{16,0},{1,17},{17,1},{2,18},{18,2},{3,19},{19,3},{4,20},{20... | collective-permute-start | bytes 104 | tf_op jit(solution)/shard_map/ppermute | solution.py:324
  3.5 3.4 %collective-permute-start.2 = (s32[2,4]{1,0:T(2,128)}, s32[2,4]{1,0:T(2,128)S(1)}, u32[]{:S(2)}, u32[]{:S(2)}) collective-permute-start(s32[2,4]{1,0:T(2,128)} %tiles_ref.1), channel_id=1, source_target_pairs={{0,1},{1,0},{2,3},{3,2},{4,5},{5,4},{6,7},{7,6},{8,9},{9,8},{10,11... | collective-permute-start | bytes 104 | tf_op jit(solution)/shard_map/ppermute | solution.py:360
  8.2 14.2 %collective-permute-start.5 = (f32[264,128]{1,0:T(8,128)S(1)}, f32[264,128]{1,0:T(8,128)S(1)}, u32[]{:S(2)}, u32[]{:S(2)}) collective-permute-start(f32[264,128]{1,0:T(8,128)S(1)} %get-tuple-element.33), channel_id=1, source_target_pairs={{0,8},{1,9},{2,10},{3,11},{4,12},{5,13},{6,14},{7,15},{8,0},{9,1},... | collective-permute-start | bytes 405512 | tf_op jit(solution)/shard_map/ppermute | solution.py:390
  10.8 12.1 %collective-permute-start.6 = (f32[264,128]{1,0:T(8,128)S(1)}, f32[264,128]{1,0:T(8,128)S(1)}, u32[]{:S(2)}, u32[]{:S(2)}) collective-permute-start(f32[264,128]{1,0:T(8,128)S(1)} %get-tuple-element.34), channel_id=1, source_target_pairs={{0,2},{1,3},{2,0},{3,1},{4,6},{5,7},{6,4},{7,5},{8,10},{9,11},{10,... | collective-permute-start | bytes 405512 | tf_op jit(solution)/shard_map/ppermute | solution.py:390
  12.3 17.9 %collective-permute-start.7 = (f32[264,128]{1,0:T(8,128)S(1)}, f32[264,128]{1,0:T(8,128)S(1)}, u32[]{:S(2)}, u32[]{:S(2)}) collective-permute-start(f32[264,128]{1,0:T(8,128)S(1)} %get-tuple-element.35), channel_id=1, source_target_pairs={{0,10},{1,11},{2,8},{3,9},{4,14},{5,15},{6,12},{7,13},{8,2},{9,3},... | collective-permute-start | bytes 405512 | tf_op jit(solution)/shard_map/ppermute | solution.py:390
  12.6 17.6 %collective-permute-start.8 = (f32[264,128]{1,0:T(8,128)S(1)}, f32[264,128]{1,0:T(8,128)S(1)}, u32[]{:S(2)}, u32[]{:S(2)}) collective-permute-start(f32[264,128]{1,0:T(8,128)S(1)} %get-tuple-element.36), channel_id=1, source_target_pairs={{0,4},{1,5},{2,6},{3,7},{4,0},{5,1},{6,2},{7,3},{8,12},{9,13},{10,... | collective-permute-start | bytes 405512 | tf_op jit(solution)/shard_map/ppermute | solution.py:390
  14.2 16.1 %collective-permute-start.9 = (f32[264,128]{1,0:T(8,128)S(1)}, f32[264,128]{1,0:T(8,128)S(1)}, u32[]{:S(2)}, u32[]{:S(2)}) collective-permute-start(f32[264,128]{1,0:T(8,128)S(1)} %get-tuple-element.37), channel_id=1, source_target_pairs={{0,12},{1,13},{2,14},{3,15},{4,8},{5,9},{6,10},{7,11},{8,4},{9,5},... | collective-permute-start | bytes 405512 | tf_op jit(solution)/shard_map/ppermute | solution.py:390
  22.4 8.4 %collective-permute-start.10 = (f32[264,128]{1,0:T(8,128)S(1)}, f32[264,128]{1,0:T(8,128)S(1)}, u32[]{:S(2)}, u32[]{:S(2)}) collective-permute-start(f32[264,128]{1,0:T(8,128)S(1)} %get-tuple-element.38), channel_id=1, source_target_pairs={{0,6},{1,7},{2,4},{3,5},{4,2},{5,3},{6,0},{7,1},{8,14},{9,15},{10,... | collective-permute-start | bytes 405512 | tf_op jit(solution)/shard_map/ppermute | solution.py:390
  22.9 9.5 %collective-permute-start.11 = (f32[264,128]{1,0:T(8,128)S(1)}, f32[264,128]{1,0:T(8,128)S(1)}, u32[]{:S(2)}, u32[]{:S(2)}) collective-permute-start(f32[264,128]{1,0:T(8,128)S(1)} %get-tuple-element.39), channel_id=1, source_target_pairs={{0,14},{1,15},{2,12},{3,13},{4,10},{5,11},{6,8},{7,9},{8,6},{9,7},... | collective-permute-start | bytes 405512 | tf_op jit(solution)/shard_map/ppermute | solution.py:390
  27.2 1.0 %copy-start = (bf16[2,8,2,16,512]{4,3,2,1,0:T(8,128)(2,1)S(1)}, bf16[2,8,2,16,512]{4,3,2,1,0:T(8,128)(2,1)}, u32[]{:S(2)}) copy-start(bf16[2,8,2,16,512]{4,3,2,1,0:T(8,128)(2,1)} %constant.39.clone.outer_ref) | copy-start | bytes 1572868
  28.2 0.9 %copy-start.1 = (bf16[2,16,2,8,256]{4,3,2,1,0:T(8,128)(2,1)S(1)}, bf16[2,16,2,8,256]{4,3,2,1,0:T(8,128)(2,1)}, u32[]{:S(2)}) copy-start(bf16[2,16,2,8,256]{4,3,2,1,0:T(8,128)(2,1)} %constant.40.clone.inner_ref) | copy-start | bytes 786436
  29.2 0.9 %copy-start.2 = (f32[64,512]{1,0:T(8,128)S(1)}, f32[64,512]{1,0:T(8,128)}, u32[]{:S(2)}) copy-start(f32[64,512]{1,0:T(8,128)} %constant.41.clone.twist_ref) | copy-start | bytes 393220
  35.9 10.7 %collective-permute-start.12 = (f32[4,2,16,512]{3,2,1,0:T(8,128)S(1)}, f32[4,2,16,512]{3,2,1,0:T(8,128)S(1)}, u32[]{:S(2)}, u32[]{:S(2)}) collective-permute-start(f32[4,2,16,512]{3,2,1,0:T(8,128)S(1)} %get-tuple-element.44), channel_id=1, source_target_pairs={{0,6},{1,7},{2,4},{3,5},{4,2},{5,3},{6,0},{7,1},{8,14},{9,15},{10,... | collective-permute-start | bytes 786440 | tf_op jit(solution)/shard_map/ppermute | solution.py:459
  39.4 12.8 %collective-permute-start.14 = (f32[4,2,16,512]{3,2,1,0:T(8,128)S(1)}, f32[4,2,16,512]{3,2,1,0:T(8,128)S(1)}, u32[]{:S(2)}, u32[]{:S(2)}) collective-permute-start(f32[4,2,16,512]{3,2,1,0:T(8,128)S(1)} %get-tuple-element.47), channel_id=1, source_target_pairs={{0,2},{1,3},{2,0},{3,1},{4,6},{5,7},{6,4},{7,5},{8,10},{9,11},{10,... | collective-permute-start | bytes 786440 | tf_op jit(solution)/shard_map/ppermute | solution.py:459
  40.7 11.5 %collective-permute-start.13 = (f32[4,2,16,512]{3,2,1,0:T(8,128)S(1)}, f32[4,2,16,512]{3,2,1,0:T(8,128)S(1)}, u32[]{:S(2)}, u32[]{:S(2)}) collective-permute-start(f32[4,2,16,512]{3,2,1,0:T(8,128)S(1)} %get-tuple-element.45), channel_id=1, source_target_pairs={{0,4},{1,5},{2,6},{3,7},{4,0},{5,1},{6,2},{7,3},{8,12},{9,13},{10,... | collective-permute-start | bytes 786440 | tf_op jit(solution)/shard_map/ppermute | solution.py:459
  40.7 16.7 %collective-permute-start.15 = (f32[4,2,16,512]{3,2,1,0:T(8,128)S(1)}, f32[4,2,16,512]{3,2,1,0:T(8,128)S(1)}, u32[]{:S(2)}, u32[]{:S(2)}) collective-permute-start(f32[4,2,16,512]{3,2,1,0:T(8,128)S(1)} %get-tuple-element.49), channel_id=1, source_target_pairs={{0,7},{1,6},{2,5},{3,4},{4,3},{5,2},{6,1},{7,0},{8,15},{9,14},{10,... | collective-permute-start | bytes 786440 | tf_op jit(solution)/shard_map/ppermute | solution.py:459
  41.7 20.4 %collective-permute-start.16 = (f32[4,2,16,512]{3,2,1,0:T(8,128)S(1)}, f32[4,2,16,512]{3,2,1,0:T(8,128)S(1)}, u32[]{:S(2)}, u32[]{:S(2)}) collective-permute-start(f32[4,2,16,512]{3,2,1,0:T(8,128)S(1)} %get-tuple-element.50), channel_id=1, source_target_pairs={{0,5},{1,4},{2,7},{3,6},{4,1},{5,0},{6,3},{7,2},{8,13},{9,12},{10,... | collective-permute-start | bytes 786440 | tf_op jit(solution)/shard_map/ppermute | solution.py:459
  46.6 16.1 %collective-permute-start.17 = (f32[4,2,16,512]{3,2,1,0:T(8,128)S(1)}, f32[4,2,16,512]{3,2,1,0:T(8,128)S(1)}, u32[]{:S(2)}, u32[]{:S(2)}) collective-permute-start(f32[4,2,16,512]{3,2,1,0:T(8,128)S(1)} %get-tuple-element.51), channel_id=1, source_target_pairs={{0,3},{1,2},{2,1},{3,0},{4,7},{5,6},{6,5},{7,4},{8,11},{9,10},{10,... | collective-permute-start | bytes 786440 | tf_op jit(solution)/shard_map/ppermute | solution.py:459
  52.3 10.4 %collective-permute-start.18 = (f32[4,2,16,512]{3,2,1,0:T(8,128)S(1)}, f32[4,2,16,512]{3,2,1,0:T(8,128)S(1)}, u32[]{:S(2)}, u32[]{:S(2)}) collective-permute-start(f32[4,2,16,512]{3,2,1,0:T(8,128)S(1)} %get-tuple-element.52), channel_id=1, source_target_pairs={{0,1},{1,0},{2,3},{3,2},{4,5},{5,4},{6,7},{7,6},{8,9},{9,8},{10,11... | collective-permute-start | bytes 786440 | tf_op jit(solution)/shard_map/ppermute | solution.py:459
  52.3 10.4 %collective-permute-start.19 = (f32[8,128]{1,0:T(8,128)S(1)}, f32[8,128]{1,0:T(8,128)S(1)}, u32[]{:S(2)}, u32[]{:S(2)}) collective-permute-start(f32[8,128]{1,0:T(8,128)S(1)} %get-tuple-element.54.refs_8_), channel_id=1, source_target_pairs={{0,16},{16,0},{1,17},{17,1},{2,18},{18,2},{3,19},{19,3},{4,20},{20... | collective-permute-start | bytes 12296 | tf_op jit(solution)/shard_map/ppermute | solution.py:324

commit v11 on v10

--- a/solution.py
+++ b/solution.py
@@ -53,10 +53,11 @@
 
 
 def outer_tables(plan, blocks):
-    angle = np.arange(plan.n1)[:, None] * np.arange(plan.k1)[None, :] % plan.k1
+    k1 = plan.k1 // 2
+    angle = np.arange(plan.n1)[:, None] * np.arange(k1)[None, :] % plan.k1
     angle = angle * (2.0 * np.pi / plan.k1)
-    table = np.stack([np.cos(angle), np.sin(angle)]).reshape(2, blocks, plan.n1 // blocks, plan.k1)
-    return split_bf16(table.transpose(1, 0, 2, 3))
+    table = np.stack([np.cos(angle), np.sin(angle)]).reshape(2, blocks, plan.n1 // blocks // 2, 2, k1)
+    return split_bf16(table.transpose(1, 3, 0, 2, 4))
 
 
 def inner_tables(plan):
@@ -184,11 +185,13 @@
 
 def tables_kernel(plan, blocks, me_ref, outer_ref, inner_ref, twist_ref, w1_ref, w2_ref, turn_ref):
     me = me_ref[0]
-    w1, w2 = [], ([], [])
+    w1, w2 = ([], []), ([], [])
     for s in range(2):
-        rows = [outer_ref[s, (me >> 1) ^ b if blocks > 1 else 0] for b in range(blocks)]
-        cos, sin = (jnp.concatenate([both[i] for both in rows]) for i in range(2))
-        w1.append(jnp.concatenate([jnp.concatenate([cos, sin]), jnp.concatenate([-sin, cos])], axis=1))
+        rows = [outer_ref[s, (me >> 1) ^ b if blocks > 1 else 0].astype(jnp.float32) for b in range(blocks)]
+        for p in range(2):
+            cos, sin = (jnp.concatenate([both[p, i] for both in rows]) for i in range(2))
+            both = jnp.concatenate([jnp.concatenate([cos, sin]), jnp.concatenate([-sin, cos])], axis=1)
+            w1[p].append(both.astype(jnp.bfloat16))
         for p in range(2):
             parts = []
             for b in range(plan.group):
@@ -196,8 +199,8 @@
                 parts.append(both)
                 parts.append(jnp.concatenate([-both[:, INNER // 2 :], both[:, : INNER // 2]], axis=1))
             w2[p].append(jnp.concatenate(parts).astype(jnp.bfloat16))
-    w1_ref[...] = jnp.concatenate([w1[0], w1[0], w1[1]])
     for p in range(2):
+        w1_ref[p] = jnp.concatenate([w1[p][0], w1[p][0], w1[p][1]])
         w2_ref[p] = jnp.concatenate([w2[p][0], w2[p][1]])
     turn_ref[...] = twist_ref[...]
 
@@ -212,50 +215,59 @@
     count_ref[...] = count
     n1_chip = 2 * plan.n1_dev
 
-    def part_of(r, part):
+    def part_of(r, part, p):
         pieces = []
         for lt in range(plan.lane_parts):
-            at = ((r * 2 + part) * plan.lane_parts + lt) * n1_chip
-            pieces.append(jnp.concatenate([chunk[at : at + n1_chip, :] for chunk in chunks]))
+            at = ((r * 2 + part) * plan.lane_parts + lt) * n1_chip + p
+            pieces.append(jnp.concatenate([chunk[pl.ds(at, n1_chip // 2, stride=2), :] for chunk in chunks]))
         return jnp.concatenate(pieces, axis=1)
 
-    fields = [jnp.concatenate([part_of(r, 0), part_of(r, 1)]) for r in range(plan.rows)]
+    fields = []
+    for p in range(2):
+        fields.append([jnp.concatenate([part_of(r, 0, p), part_of(r, 1, p)]) for r in range(plan.rows)])
     transform_rows(plan, fields, tables, outs)
 
 
 def transform_kernel(plan, info_ref, x_ref, *refs):
     chunk_row = plan.chunk // plan.rows
+    n1_half, n1_dev = plan.n1 // 2, plan.n1_dev // 2
     info = info_ref[: plan.n_col]
-    info = jnp.broadcast_to(info[:, None, :], (plan.n_col, plan.n1_dev, LANES)).reshape(plan.n1, LANES)
-    tile = lax.broadcasted_iota(jnp.int32, info.shape, 0) % plan.n1_dev * INNER // TILE_C
+    info = jnp.broadcast_to(info[:, None, :], (plan.n_col, n1_dev, LANES)).reshape(n1_half, LANES)
+    tile = lax.broadcasted_iota(jnp.int32, info.shape, 0) % n1_dev * 2 * INNER // TILE_C
     own = lax.broadcasted_iota(jnp.int32, info.shape, 1) == tile
     before = jnp.sum(jnp.where(own, info, 0.0), axis=1, keepdims=True).astype(jnp.int32)
     turn_cos, turn_sin, minus_cos, minus_sin = unit_phase(before)
     turn_cos = jnp.where(minus_cos, -turn_cos, turn_cos)
     turn_sin = jnp.where(minus_sin, -turn_sin, turn_sin)
 
-    def field_of(r):
+    def field_of(r, p):
         halves = []
         for part in range(2):
             pieces = []
             for lt in range(plan.lane_parts):
-                at = r * chunk_row + (part * plan.lane_parts + lt) * plan.n1_dev
-                pieces.append(x_ref[:, at : at + plan.n1_dev, :].reshape(plan.n1, LANES))
+                at = r * chunk_row + (part * plan.lane_parts + lt) * plan.n1_dev + p
+                cells = [x_ref[:, at + 2 * i : at + 2 * i + 1, :] for i in range(n1_dev)]
+                pieces.append(jnp.concatenate(cells, axis=1).reshape(n1_half, LANES))
             halves.append(jnp.concatenate(pieces, axis=1))
         real, imag = halves
         return jnp.concatenate([real * turn_cos - imag * turn_sin, real * turn_sin + imag * turn_cos], axis=0)
 
-    transform_rows(plan, [field_of(r) for r in range(plan.rows)], refs[:3], refs[3:])
+    fields = [[field_of(r, p) for r in range(plan.rows)] for p in range(2)]
+    transform_rows(plan, fields, refs[:3], refs[3:])
 
 
 def transform_rows(plan, fields, tables, outs):
     w1_ref, w2_ref, turn_ref = tables
-    x = jnp.concatenate(fields, axis=1)
-    xh = x.astype(jnp.bfloat16)
-    xl = (x - xh.astype(jnp.float32)).astype(jnp.bfloat16)
-    y = lax.dot_general(
-        jnp.concatenate([xh, xl, xh]), w1_ref[...], (((0,), (0,)), ((), ())), preferred_element_type=jnp.float32
-    )
+    ys = []
+    for p in range(2):
+        x = jnp.concatenate(fields[p], axis=1)
+        xh = x.astype(jnp.bfloat16)
+        xl = (x - xh.astype(jnp.float32)).astype(jnp.bfloat16)
+        ys.append(
+            lax.dot_general(
+                jnp.concatenate([xh, xl, xh]), w1_ref[p], (((0,), (0,)), ((), ())), preferred_element_type=jnp.float32
+            )
+        )
     tc, ts = [], []
     count = INNER // FINE
     fine_cos, fine_sin = turn_ref[2 * count : 2 * count + FINE], turn_ref[2 * count + FINE :]
@@ -266,7 +278,9 @@
     tc, ts = jnp.concatenate(tc), jnp.concatenate(ts)
     fs = ([], [])
     for r in range(plan.rows):
-        yr, yi = y[r * INNER : (r + 1) * INNER, : plan.k1], y[r * INNER : (r + 1) * INNER, plan.k1 :]
+        even, odd = (y[r * INNER : (r + 1) * INNER] for y in ys)
+        y = [even + odd, even - odd]
+        yr, yi = (jnp.concatenate([one[:, i * plan.k1 // 2 : (i + 1) * plan.k1 // 2] for one in y], axis=1) for i in range(2))
         fr, fi = yr * tc + yi * ts, yi * tc - yr * ts
         for p in range(2):
             pair = [f[: INNER // 2] + f[INNER // 2 :] if p == 0 else f[: INNER // 2] - f[INNER // 2 :] for f in (fr, fi)]
@@ -333,7 +347,7 @@
     return pl.pallas_call(
         partial(tables_kernel, plan, blocks),
         out_shape=[
-            jax.ShapeDtypeStruct((6 * plan.n1, 2 * plan.k1), jnp.bfloat16),
+            jax.ShapeDtypeStruct((2, 3 * plan.n1, plan.k1), jnp.bfloat16),
             jax.ShapeDtypeStruct((2, 2 * plan.group * plan.k2_dev, INNER), jnp.bfloat16),
             jax.ShapeDtypeStruct((2 * (INNER // FINE + FINE), plan.k1), jnp.float32),
         ],

time: 65 us -> 64.8 us (level)
  no operation moved by 1% of the time
where the time goes in v11:
time: 64.8 us; the launch traced here: 64.5 us
  waiting for transfers between devices  28.5 us (44%)
  starting transfers between devices  24.8 us (38%)
  Pallas kernels  8.32 us (13%)
  local copies, waits for them, and re-layouts  2.8 us (4%)
    ppermute x7, waiting for transfers between devices, per_device(): lax.ppermute(made[b], 'col', [(q, q ^ b) for q in range(n_col)])  18.9 us
    ppermute x7, starting transfers between devices, spectra_by_chip(): lax.ppermute(rows[b], 'col', [(q, q ^ 2 * b) for q in range(n_col)])  13.3 us
    ppermute x7, waiting for transfers between devices, spectra_by_chip(): lax.ppermute(rows[b], 'col', [(q, q ^ 2 * b) for q in range(n_col)])  8.05 us
    ppermute x7, starting transfers between devices, per_device(): lax.ppermute(made[b], 'col', [(q, q ^ b) for q in range(n_col)])  6.74 us
    pallas_call x1, Pallas kernels, spectra_by_chip(): pl.pallas_call(partial(chip_transform_kernel, plan, order), out_shape=spe...  3.19 us
    unnamed x6, local copies, waits for them, and re-layouts  2.8 us
    ppermute x1, starting transfers between devices, spectra_by_chip(): near_others.append(lax.ppermute(tile_offsets, ('row', 'col'), pairs))  2.57 us
    pallas_call x1, Pallas kernels, per_device(): pl.pallas_call(partial(merge_kernel, plan, 2 if by_chip else 1), out_shap...  2.12 us
  transfers between devices with their start and end apart: 20, of which 9 were waited for; matrix products, arithmetic and copies ran while one was open for 0% of the time, Pallas kernels for 3%

profile of v11, /device:TPU:0, one launch (start us, length us, event | category | flops | bytes accessed | tf_op | source)
XLA Modules:
  0.0 64.5 jit_solution(1015119209887134660)
XLA Ops:
  0.0 0.5 collective-permute-start.3
  0.5 2.6 %collective-permute-start.1 = (s32[2,4]{1,0:T(2,128)}, s32[2,4]{1,0:T(2,128)S(1)}, u32[]{:S(2)}, u32[]{:S(2)}) collective-permute-start(s32[2,4]{1,0:T(2,128)} %tiles_ref.1), channel_id=1, source_target_pairs={{0,17},{1,16},{2,19},{3,18},{4,21},{5,20},{6,23},{7,22},{8,25},{9,... | collective-permute-start | bytes 104 | tf_op jit(solution)/shard_map/ppermute | solution.py:373
  3.1 0.4 collective-permute-start
  3.5 0.1 collective-permute-start.2
  3.7 1.6 %own.1 = (s32[16,2048]{1,0:T(8,128)S(1)}, s32[16,2048]{1,0:T(8,128)S(1)}, s32[8,128]{1,0:T(8,128)S(1)}) custom-call(s32[3]{0:T(128)S(1)} %pad_add_fusion.me_ref, s32[2,4]{1,0:T(2,128)} %tiles_ref.1, s32[32,2048]{1,0:T(8,128)} %codes_ref.1, s32[32,2048]{1,0:T(8,128)} %mask_ref.1), custom_call_target="tpu_custom_call" | custom-call | tf_op jit(solution)/shard_map/own/pallas_call | solution.py:376
  5.3 1.5 %collective-permute-done.refs_0_ = s32[2,4]{1,0:T(2,128)S(1)} collective-permute-done((s32[2,4]{1,0:T(2,128)}, s32[2,4]{1,0:T(2,128)S(1)}, u32[]{:S(2)}, u32[]{:S(2)}) %collective-permute-start) | collective-permute-done | bytes 64 | tf_op jit(solution)/shard_map/ppermute | solution.py:338
  6.9 1.3 %field.1 = (f32[264,128]{1,0:T(8,128)S(1)}, f32[264,128]{1,0:T(8,128)S(1)}, f32[264,128]{1,0:T(8,128)S(1)}, f32[264,128]{1,0:T(8,128)S(1)}, f32[264,128]{1,0:T(8...) custom-call(s32[3]{0:T(128)S(1)} %pad_add_fusion.me_ref, ...), custom_call_target="tpu_custom_call" | custom-call | tf_op jit(solution)/shard_map/field/pallas_call | solution.py:394
  8.2 2.7 %collective-permute-start.5 = (f32[264,128]{1,0:T(8,128)S(1)}, f32[264,128]{1,0:T(8,128)S(1)}, u32[]{:S(2)}, u32[]{:S(2)}) collective-permute-start(f32[264,128]{1,0:T(8,128)S(1)} %get-tuple-element.33), channel_id=1, source_target_pairs={{0,8},{1,9},{2,10},{3,11},{4,12},{5,13},{6,14},{7,15},{8,0},{9,1},... | collective-permute-start | bytes 405512 | tf_op jit(solution)/shard_map/ppermute | solution.py:404
  10.8 1.5 %collective-permute-start.6 = (f32[264,128]{1,0:T(8,128)S(1)}, f32[264,128]{1,0:T(8,128)S(1)}, u32[]{:S(2)}, u32[]{:S(2)}) collective-permute-start(f32[264,128]{1,0:T(8,128)S(1)} %get-tuple-element.34), channel_id=1, source_target_pairs={{0,2},{1,3},{2,0},{3,1},{4,6},{5,7},{6,4},{7,5},{8,10},{9,11},{10,... | collective-permute-start | bytes 405512 | tf_op jit(solution)/shard_map/ppermute | solution.py:404
  12.3 0.3 collective-permute-start.7
  12.6 1.6 %collective-permute-start.8 = (f32[264,128]{1,0:T(8,128)S(1)}, f32[264,128]{1,0:T(8,128)S(1)}, u32[]{:S(2)}, u32[]{:S(2)}) collective-permute-start(f32[264,128]{1,0:T(8,128)S(1)} %get-tuple-element.36), channel_id=1, source_target_pairs={{0,4},{1,5},{2,6},{3,7},{4,0},{5,1},{6,2},{7,3},{8,12},{9,13},{10,... | collective-permute-start | bytes 405512 | tf_op jit(solution)/shard_map/ppermute | solution.py:404
  14.2 2.5 %collective-permute-start.9 = (f32[264,128]{1,0:T(8,128)S(1)}, f32[264,128]{1,0:T(8,128)S(1)}, u32[]{:S(2)}, u32[]{:S(2)}) collective-permute-start(f32[264,128]{1,0:T(8,128)S(1)} %get-tuple-element.37), channel_id=1, source_target_pairs={{0,12},{1,13},{2,14},{3,15},{4,8},{5,9},{6,10},{7,11},{8,4},{9,5},... | collective-permute-start | bytes 405512 | tf_op jit(solution)/shard_map/ppermute | solution.py:404
  16.7 5.7 %collective-permute-done.5.refs_0_ = f32[264,128]{1,0:T(8,128)S(1)} collective-permute-done((f32[264,128]{1,0:T(8,128)S(1)}, f32[264,128]{1,0:T(8,128)S(1)}, u32[]{:S(2)}, u32[]{:S(2)}) %collective-permute-start.5) | collective-permute-done | bytes 135200 | tf_op jit(solution)/shard_map/ppermute | solution.py:404
  22.4 0.5 collective-permute-start.10
  22.9 4.3 %collective-permute-start.11 = (f32[264,128]{1,0:T(8,128)S(1)}, f32[264,128]{1,0:T(8,128)S(1)}, u32[]{:S(2)}, u32[]{:S(2)}) collective-permute-start(f32[264,128]{1,0:T(8,128)S(1)} %get-tuple-element.39), channel_id=1, source_target_pairs={{0,14},{1,15},{2,12},{3,13},{4,10},{5,11},{6,8},{7,9},{8,6},{9,7},... | collective-permute-start | bytes 405512 | tf_op jit(solution)/shard_map/ppermute | solution.py:404
  27.2 0.9 %copy-done = bf16[2,16,2,8,256]{4,3,2,1,0:T(8,128)(2,1)S(1)} copy-done((bf16[2,16,2,8,256]{4,3,2,1,0:T(8,128)(2,1)S(1)}, bf16[2,16,2,8,256]{4,3,2,1,0:T(8,128)(2,1)}, u32[]{:S(2)}) %copy-start) | copy-done | bytes 262168
  28.2 0.9 %copy-done.1 = bf16[2,8,2,2,8,256]{5,4,3,2,1,0:T(8,128)(2,1)S(1)} copy-done((bf16[2,8,2,2,8,256]{5,4,3,2,1,0:T(8,128)(2,1)S(1)}, bf16[2,8,2,2,8,256]{5,4,3,2,1,0:T(8,128)(2,1)}, u32[]{:S(2)}) %copy-start.1) | copy-done | bytes 262168
  29.1 0.9 %copy-done.2 = f32[64,512]{1,0:T(8,128)S(1)} copy-done((f32[64,512]{1,0:T(8,128)S(1)}, f32[64,512]{1,0:T(8,128)}, u32[]{:S(2)}) %copy-start.2) | copy-done | bytes 131096
  30.1 0.7 %collective-permute-done.10.refs_5_ = f32[264,128]{1,0:T(8,128)S(1)} collective-permute-done((f32[264,128]{1,0:T(8,128)S(1)}, f32[264,128]{1,0:T(8,128)S(1)}, u32[]{:S(2)}, u32[]{:S(2)}) %collective-permute-start.10) | collective-permute-done | bytes 135200 | tf_op jit(solution)/shard_map/ppermute | solution.py:404
  30.8 1.6 %collective-permute-done.11.refs_6_ = f32[264,128]{1,0:T(8,128)S(1)} collective-permute-done((f32[264,128]{1,0:T(8,128)S(1)}, f32[264,128]{1,0:T(8,128)S(1)}, u32[]{:S(2)}, u32[]{:S(2)}) %collective-permute-start.11) | collective-permute-done | bytes 135200 | tf_op jit(solution)/shard_map/ppermute | solution.py:404
  32.5 3.2 %transform.1 = (f32[4,2,16,512]{3,2,1,0:T(8,128)S(1)}, f32[4,2,16,512]{3,2,1,0:T(8,128)S(1)}, f32[4,2,16,512]{3,2,1,0:T(8,128)S(1)}, f32[4,2,16,512]{3,2,1,0:T(8...) custom-call(f32[264,128]{1,0:T(8,128)S(1)} %collective-permute-done., ...), custom_call_target="tpu_custom_call" | custom-call | tf_op jit(solution)/shard_map/transform/pallas_call | solution.py:405
  35.6 3.5 %collective-permute-start.12 = (f32[4,2,16,512]{3,2,1,0:T(8,128)S(1)}, f32[4,2,16,512]{3,2,1,0:T(8,128)S(1)}, u32[]{:S(2)}, u32[]{:S(2)}) collective-permute-start(f32[4,2,16,512]{3,2,1,0:T(8,128)S(1)} %get-tuple-element.44), channel_id=1, source_target_pairs={{0,6},{1,7},{2,4},{3,5},{4,2},{5,3},{6,0},{7,1},{8,14},{9,15},{10,... | collective-permute-start | bytes 786440 | tf_op jit(solution)/shard_map/ppermute | solution.py:473
  39.2 1.3 %collective-permute-start.14 = (f32[4,2,16,512]{3,2,1,0:T(8,128)S(1)}, f32[4,2,16,512]{3,2,1,0:T(8,128)S(1)}, u32[]{:S(2)}, u32[]{:S(2)}) collective-permute-start(f32[4,2,16,512]{3,2,1,0:T(8,128)S(1)} %get-tuple-element.47), channel_id=1, source_target_pairs={{0,2},{1,3},{2,0},{3,1},{4,6},{5,7},{6,4},{7,5},{8,10},{9,11},{10,... | collective-permute-start | bytes 786440 | tf_op jit(solution)/shard_map/ppermute | solution.py:473
  40.5 1.0 %collective-permute-start.15 = (f32[4,2,16,512]{3,2,1,0:T(8,128)S(1)}, f32[4,2,16,512]{3,2,1,0:T(8,128)S(1)}, u32[]{:S(2)}, u32[]{:S(2)}) collective-permute-start(f32[4,2,16,512]{3,2,1,0:T(8,128)S(1)} %get-tuple-element.49), channel_id=1, source_target_pairs={{0,7},{1,6},{2,5},{3,4},{4,3},{5,2},{6,1},{7,0},{8,15},{9,14},{10,... | collective-permute-start | bytes 786440 | tf_op jit(solution)/shard_map/ppermute | solution.py:473
  41.4 0.9 %collective-permute-start.16 = (f32[4,2,16,512]{3,2,1,0:T(8,128)S(1)}, f32[4,2,16,512]{3,2,1,0:T(8,128)S(1)}, u32[]{:S(2)}, u32[]{:S(2)}) collective-permute-start(f32[4,2,16,512]{3,2,1,0:T(8,128)S(1)} %get-tuple-element.50), channel_id=1, source_target_pairs={{0,5},{1,4},{2,7},{3,6},{4,1},{5,0},{6,3},{7,2},{8,13},{9,12},{10,... | collective-permute-start | bytes 786440 | tf_op jit(solution)/shard_map/ppermute | solution.py:473
  42.4 3.9 %collective-permute-done.12.refs_0_ = f32[4,2,16,512]{3,2,1,0:T(8,128)S(1)} collective-permute-done((f32[4,2,16,512]{3,2,1,0:T(8,128)S(1)}, f32[4,2,16,512]{3,2,1,0:T(8,128)S(1)}, u32[]{:S(2)}, u32[]{:S(2)}) %collective-permute-start.12) | collective-permute-done | bytes 262176 | tf_op jit(solution)/shard_map/ppermute | solution.py:473
  46.3 5.7 %collective-permute-done.14.refs_2_ = f32[4,2,16,512]{3,2,1,0:T(8,128)S(1)} collective-permute-done((f32[4,2,16,512]{3,2,1,0:T(8,128)S(1)}, f32[4,2,16,512]{3,2,1,0:T(8,128)S(1)}, u32[]{:S(2)}, u32[]{:S(2)}) %collective-permute-start.14) | collective-permute-done | bytes 262176 | tf_op jit(solution)/shard_map/ppermute | solution.py:473
  52.0 1.2 %collective-permute-start.19 = (f32[8,128]{1,0:T(8,128)S(1)}, f32[8,128]{1,0:T(8,128)S(1)}, u32[]{:S(2)}, u32[]{:S(2)}) collective-permute-start(f32[8,128]{1,0:T(8,128)S(1)} %get-tuple-element.54.refs_8_), channel_id=1, source_target_pairs={{0,16},{16,0},{1,17},{17,1},{2,18},{18,2},{3,19},{19,3},{4,20},{20... | collective-permute-start | bytes 12296 | tf_op jit(solution)/shard_map/ppermute | solution.py:338
  53.2 4.0 %collective-permute-done.15.refs_3_ = f32[4,2,16,512]{3,2,1,0:T(8,128)S(1)} collective-permute-done((f32[4,2,16,512]{3,2,1,0:T(8,128)S(1)}, f32[4,2,16,512]{3,2,1,0:T(8,128)S(1)}, u32[]{:S(2)}, u32[]{:S(2)}) %collective-permute-start.15) | collective-permute-done | bytes 262176 | tf_op jit(solution)/shard_map/ppermute | solution.py:473
  57.2 4.7 %collective-permute-done.16.refs_4_ = f32[4,2,16,512]{3,2,1,0:T(8,128)S(1)} collective-permute-done((f32[4,2,16,512]{3,2,1,0:T(8,128)S(1)}, f32[4,2,16,512]{3,2,1,0:T(8,128)S(1)}, u32[]{:S(2)}, u32[]{:S(2)}) %collective-permute-start.16) | collective-permute-done | bytes 262176 | tf_op jit(solution)/shard_map/ppermute | solution.py:473
  61.9 0.6 collective-permute-done.17.refs_5_
  62.4 2.1 %merge.1 = f32[2,4,512,128]{3,2,1,0:T(8,128)} custom-call(s32[1]{0:T(128)} %bitcast.me_ref, f32[4,2,16,512]{3,2,1,0:T(8,128)S(1)} %collective-permute-done.12.refs_0_, f32[4,2,16,512]{3,2,1,0:T(8,128)S(1)} %collective-permute-done.13.refs_1_, f32[4,2,16,512]{3,2,1,0:T(8,128)S(1)} %collective-permute-done.14.refs_2_, ...), custom_call_target="tpu_custom_call" | custom-call | tf_op jit(solution)/shard_map/merge/pallas_call | solution.py:479
  (20 shorter events, 0.3 us)
Async XLA Ops:
  0.0 6.9 %collective-permute-start.3 = (s32[32,2048]{1,0:T(8,128)}, s32[32,2048]{1,0:T(8,128)S(1)}, u32[]{:S(2)}, u32[]{:S(2)}) collective-permute-start(s32[32,2048]{1,0:T(8,128)} %codes_ref.1), channel_id=1, source_target_pairs={{0,1},{1,0},{2,3},{3,2},{4,5},{5,4},{6,7},{7,6},{8,9},{9,8},{10,11... | collective-permute-start | bytes 786440 | tf_op jit(solution)/shard_map/ppermute | solution.py:374
  0.5 6.4 %collective-permute-start.4 = (s32[32,2048]{1,0:T(8,128)}, s32[32,2048]{1,0:T(8,128)S(1)}, u32[]{:S(2)}, u32[]{:S(2)}) collective-permute-start(s32[32,2048]{1,0:T(8,128)} %mask_ref.1), channel_id=1, source_target_pairs={{0,1},{1,0},{2,3},{3,2},{4,5},{5,4},{6,7},{7,6},{8,9},{9,8},{10,11... | collective-permute-start | bytes 786440 | tf_op jit(solution)/shard_map/ppermute | solution.py:374
  0.5 4.8 %collective-permute-start.1 = (s32[2,4]{1,0:T(2,128)}, s32[2,4]{1,0:T(2,128)S(1)}, u32[]{:S(2)}, u32[]{:S(2)}) collective-permute-start(s32[2,4]{1,0:T(2,128)} %tiles_ref.1), channel_id=1, source_target_pairs={{0,17},{1,16},{2,19},{3,18},{4,21},{5,20},{6,23},{7,22},{8,25},{9,... | collective-permute-start | bytes 104 | tf_op jit(solution)/shard_map/ppermute | solution.py:373
  3.1 3.8 %collective-permute-start = (s32[2,4]{1,0:T(2,128)}, s32[2,4]{1,0:T(2,128)S(1)}, u32[]{:S(2)}, u32[]{:S(2)}) collective-permute-start(s32[2,4]{1,0:T(2,128)} %tiles_ref.1), channel_id=1, source_target_pairs={{0,16},{16,0},{1,17},{17,1},{2,18},{18,2},{3,19},{19,3},{4,20},{20... | collective-permute-start | bytes 104 | tf_op jit(solution)/shard_map/ppermute | solution.py:338
  3.5 3.4 %collective-permute-start.2 = (s32[2,4]{1,0:T(2,128)}, s32[2,4]{1,0:T(2,128)S(1)}, u32[]{:S(2)}, u32[]{:S(2)}) collective-permute-start(s32[2,4]{1,0:T(2,128)} %tiles_ref.1), channel_id=1, source_target_pairs={{0,1},{1,0},{2,3},{3,2},{4,5},{5,4},{6,7},{7,6},{8,9},{9,8},{10,11... | collective-permute-start | bytes 104 | tf_op jit(solution)/shard_map/ppermute | solution.py:374
  8.2 14.2 %collective-permute-start.5 = (f32[264,128]{1,0:T(8,128)S(1)}, f32[264,128]{1,0:T(8,128)S(1)}, u32[]{:S(2)}, u32[]{:S(2)}) collective-permute-start(f32[264,128]{1,0:T(8,128)S(1)} %get-tuple-element.33), channel_id=1, source_target_pairs={{0,8},{1,9},{2,10},{3,11},{4,12},{5,13},{6,14},{7,15},{8,0},{9,1},... | collective-permute-start | bytes 405512 | tf_op jit(solution)/shard_map/ppermute | solution.py:404
  10.8 12.1 %collective-permute-start.6 = (f32[264,128]{1,0:T(8,128)S(1)}, f32[264,128]{1,0:T(8,128)S(1)}, u32[]{:S(2)}, u32[]{:S(2)}) collective-permute-start(f32[264,128]{1,0:T(8,128)S(1)} %get-tuple-element.34), channel_id=1, source_target_pairs={{0,2},{1,3},{2,0},{3,1},{4,6},{5,7},{6,4},{7,5},{8,10},{9,11},{10,... | collective-permute-start | bytes 405512 | tf_op jit(solution)/shard_map/ppermute | solution.py:404
  12.3 17.8 %collective-permute-start.7 = (f32[264,128]{1,0:T(8,128)S(1)}, f32[264,128]{1,0:T(8,128)S(1)}, u32[]{:S(2)}, u32[]{:S(2)}) collective-permute-start(f32[264,128]{1,0:T(8,128)S(1)} %get-tuple-element.35), channel_id=1, source_target_pairs={{0,10},{1,11},{2,8},{3,9},{4,14},{5,15},{6,12},{7,13},{8,2},{9,3},... | collective-permute-start | bytes 405512 | tf_op jit(solution)/shard_map/ppermute | solution.py:404
  12.6 17.5 %collective-permute-start.8 = (f32[264,128]{1,0:T(8,128)S(1)}, f32[264,128]{1,0:T(8,128)S(1)}, u32[]{:S(2)}, u32[]{:S(2)}) collective-permute-start(f32[264,128]{1,0:T(8,128)S(1)} %get-tuple-element.36), channel_id=1, source_target_pairs={{0,4},{1,5},{2,6},{3,7},{4,0},{5,1},{6,2},{7,3},{8,12},{9,13},{10,... | collective-permute-start | bytes 405512 | tf_op jit(solution)/shard_map/ppermute | solution.py:404
  14.2 15.9 %collective-permute-start.9 = (f32[264,128]{1,0:T(8,128)S(1)}, f32[264,128]{1,0:T(8,128)S(1)}, u32[]{:S(2)}, u32[]{:S(2)}) collective-permute-start(f32[264,128]{1,0:T(8,128)S(1)} %get-tuple-element.37), channel_id=1, source_target_pairs={{0,12},{1,13},{2,14},{3,15},{4,8},{5,9},{6,10},{7,11},{8,4},{9,5},... | collective-permute-start | bytes 405512 | tf_op jit(solution)/shard_map/ppermute | solution.py:404
  22.4 8.4 %collective-permute-start.10 = (f32[264,128]{1,0:T(8,128)S(1)}, f32[264,128]{1,0:T(8,128)S(1)}, u32[]{:S(2)}, u32[]{:S(2)}) collective-permute-start(f32[264,128]{1,0:T(8,128)S(1)} %get-tuple-element.38), channel_id=1, source_target_pairs={{0,6},{1,7},{2,4},{3,5},{4,2},{5,3},{6,0},{7,1},{8,14},{9,15},{10,... | collective-permute-start | bytes 405512 | tf_op jit(solution)/shard_map/ppermute | solution.py:404
  22.9 9.5 %collective-permute-start.11 = (f32[264,128]{1,0:T(8,128)S(1)}, f32[264,128]{1,0:T(8,128)S(1)}, u32[]{:S(2)}, u32[]{:S(2)}) collective-permute-start(f32[264,128]{1,0:T(8,128)S(1)} %get-tuple-element.39), channel_id=1, source_target_pairs={{0,14},{1,15},{2,12},{3,13},{4,10},{5,11},{6,8},{7,9},{8,6},{9,7},... | collective-permute-start | bytes 405512 | tf_op jit(solution)/shard_map/ppermute | solution.py:404
  27.2 0.9 %copy-start = (bf16[2,16,2,8,256]{4,3,2,1,0:T(8,128)(2,1)S(1)}, bf16[2,16,2,8,256]{4,3,2,1,0:T(8,128)(2,1)}, u32[]{:S(2)}) copy-start(bf16[2,16,2,8,256]{4,3,2,1,0:T(8,128)(2,1)} %constant.40.clone.inner_ref) | copy-start | bytes 786436
  28.2 0.9 %copy-start.1 = (bf16[2,8,2,2,8,256]{5,4,3,2,1,0:T(8,128)(2,1)S(1)}, bf16[2,8,2,2,8,256]{5,4,3,2,1,0:T(8,128)(2,1)}, u32[]{:S(2)}) copy-start(bf16[2,8,2,2,8,256]{5,4,3,2,1,0:T(8,128)(2,1)} %constant.39.clone.outer_ref) | copy-start | bytes 786436
  29.1 0.9 %copy-start.2 = (f32[64,512]{1,0:T(8,128)S(1)}, f32[64,512]{1,0:T(8,128)}, u32[]{:S(2)}) copy-start(f32[64,512]{1,0:T(8,128)} %constant.41.clone.twist_ref) | copy-start | bytes 393220
  35.6 10.7 %collective-permute-start.12 = (f32[4,2,16,512]{3,2,1,0:T(8,128)S(1)}, f32[4,2,16,512]{3,2,1,0:T(8,128)S(1)}, u32[]{:S(2)}, u32[]{:S(2)}) collective-permute-start(f32[4,2,16,512]{3,2,1,0:T(8,128)S(1)} %get-tuple-element.44), channel_id=1, source_target_pairs={{0,6},{1,7},{2,4},{3,5},{4,2},{5,3},{6,0},{7,1},{8,14},{9,15},{10,... | collective-permute-start | bytes 786440 | tf_op jit(solution)/shard_map/ppermute | solution.py:473
  39.2 12.8 %collective-permute-start.14 = (f32[4,2,16,512]{3,2,1,0:T(8,128)S(1)}, f32[4,2,16,512]{3,2,1,0:T(8,128)S(1)}, u32[]{:S(2)}, u32[]{:S(2)}) collective-permute-start(f32[4,2,16,512]{3,2,1,0:T(8,128)S(1)} %get-tuple-element.47), channel_id=1, source_target_pairs={{0,2},{1,3},{2,0},{3,1},{4,6},{5,7},{6,4},{7,5},{8,10},{9,11},{10,... | collective-permute-start | bytes 786440 | tf_op jit(solution)/shard_map/ppermute | solution.py:473
  40.5 11.5 %collective-permute-start.13 = (f32[4,2,16,512]{3,2,1,0:T(8,128)S(1)}, f32[4,2,16,512]{3,2,1,0:T(8,128)S(1)}, u32[]{:S(2)}, u32[]{:S(2)}) collective-permute-start(f32[4,2,16,512]{3,2,1,0:T(8,128)S(1)} %get-tuple-element.45), channel_id=1, source_target_pairs={{0,4},{1,5},{2,6},{3,7},{4,0},{5,1},{6,2},{7,3},{8,12},{9,13},{10,... | collective-permute-start | bytes 786440 | tf_op jit(solution)/shard_map/ppermute | solution.py:473
  40.5 16.7 %collective-permute-start.15 = (f32[4,2,16,512]{3,2,1,0:T(8,128)S(1)}, f32[4,2,16,512]{3,2,1,0:T(8,128)S(1)}, u32[]{:S(2)}, u32[]{:S(2)}) collective-permute-start(f32[4,2,16,512]{3,2,1,0:T(8,128)S(1)} %get-tuple-element.49), channel_id=1, source_target_pairs={{0,7},{1,6},{2,5},{3,4},{4,3},{5,2},{6,1},{7,0},{8,15},{9,14},{10,... | collective-permute-start | bytes 786440 | tf_op jit(solution)/shard_map/ppermute | solution.py:473
  41.4 20.4 %collective-permute-start.16 = (f32[4,2,16,512]{3,2,1,0:T(8,128)S(1)}, f32[4,2,16,512]{3,2,1,0:T(8,128)S(1)}, u32[]{:S(2)}, u32[]{:S(2)}) collective-permute-start(f32[4,2,16,512]{3,2,1,0:T(8,128)S(1)} %get-tuple-element.50), channel_id=1, source_target_pairs={{0,5},{1,4},{2,7},{3,6},{4,1},{5,0},{6,3},{7,2},{8,13},{9,12},{10,... | collective-permute-start | bytes 786440 | tf_op jit(solution)/shard_map/ppermute | solution.py:473
  46.3 16.1 %collective-permute-start.17 = (f32[4,2,16,512]{3,2,1,0:T(8,128)S(1)}, f32[4,2,16,512]{3,2,1,0:T(8,128)S(1)}, u32[]{:S(2)}, u32[]{:S(2)}) collective-permute-start(f32[4,2,16,512]{3,2,1,0:T(8,128)S(1)} %get-tuple-element.51), channel_id=1, source_target_pairs={{0,3},{1,2},{2,1},{3,0},{4,7},{5,6},{6,5},{7,4},{8,11},{9,10},{10,... | collective-permute-start | bytes 786440 | tf_op jit(solution)/shard_map/ppermute | solution.py:473
  52.0 10.4 %collective-permute-start.18 = (f32[4,2,16,512]{3,2,1,0:T(8,128)S(1)}, f32[4,2,16,512]{3,2,1,0:T(8,128)S(1)}, u32[]{:S(2)}, u32[]{:S(2)}) collective-permute-start(f32[4,2,16,512]{3,2,1,0:T(8,128)S(1)} %get-tuple-element.52), channel_id=1, source_target_pairs={{0,1},{1,0},{2,3},{3,2},{4,5},{5,4},{6,7},{7,6},{8,9},{9,8},{10,11... | collective-permute-start | bytes 786440 | tf_op jit(solution)/shard_map/ppermute | solution.py:473
  52.0 10.4 %collective-permute-start.19 = (f32[8,128]{1,0:T(8,128)S(1)}, f32[8,128]{1,0:T(8,128)S(1)}, u32[]{:S(2)}, u32[]{:S(2)}) collective-permute-start(f32[8,128]{1,0:T(8,128)S(1)} %get-tuple-element.54.refs_8_), channel_id=1, source_target_pairs={{0,16},{16,0},{1,17},{17,1},{2,18},{18,2},{3,19},{19,3},{4,20},{20... | collective-permute-start | bytes 12296 | tf_op jit(solution)/shard_map/ppermute | solution.py:338

commit v12 on v11

--- a/solution.py
+++ b/solution.py
@@ -18,7 +18,7 @@
 INNER = 256
 PAD = 4
 FINE = 16
-CHIP_ORDER = (4, 1, 5, 2, 6, 3, 7)
+CHIP_ORDER = (4, 1, 5, 3, 6, 2, 7)
 ORDER = (6, 4, 2, 7, 5, 3, 1)
 GROUP = 8
 
@@ -327,7 +327,8 @@
                     tile_ref[slot, pl.ds(at + plan.rows, half, stride=stride), :] = jnp.where(swapped, a, b)
         source = inside ^ base
         tile = source // 2 if swap_bit == 1 else source % 2 * 2 + source // 4
-        copy = pltpu.make_async_copy(tile_ref.at[slot], out_ref.at[part, tile], sems.at[slot])
+        whole = tile_ref.at[slot, pl.ds(0, plan.freq_tiles * SUBS), :]
+        copy = pltpu.make_async_copy(whole, out_ref.at[part, tile], sems.at[slot])
         copy.start()
         copies.append(copy)
     for copy in copies:
@@ -396,7 +397,7 @@
         out_shape=[block] * n_chips,
         in_specs=[smem] + [vmem] * (2 * n_row + 4),
         out_specs=[vmem] * n_chips,
-        scratch_shapes=[pltpu.VMEM((2, half * plan.chunk // plan.rows, LANES), jnp.float32)],
+        scratch_shapes=[pltpu.VMEM((2, (half + 1) * plan.chunk // plan.rows, LANES), jnp.float32)],
         compiler_params=pltpu.CompilerParams(vmem_limit_bytes=16 * 2**20),
         name="field",
     )(place, *others, *near_others, near[0], *own, near[1], near[2])
@@ -482,7 +483,7 @@
         in_specs=[smem] + [vmem] * (plan.group + n_row),
         out_specs=pl.BlockSpec(memory_space=pl.ANY),
         scratch_shapes=[
-            pltpu.VMEM((plan.group, plan.freq_tiles * SUBS, LANES), jnp.float32),
+            pltpu.VMEM((plan.group, (plan.freq_tiles + 2 * plan.k1_tiles) * SUBS, LANES), jnp.float32),
             pltpu.SemaphoreType.DMA((plan.group,)),
         ],
         compiler_params=pltpu.CompilerParams(vmem_limit_bytes=24 * 2**20),

time: 64.8 us -> 64.8 us (level)
  waiting for transfers between devices: 28.5 us -> 27.5 us
  starting transfers between devices: 24.8 us -> 25.7 us
    ppermute x7, waiting for transfers between devices: 8.05 us -> 7.09 us  [spectra_by_chip(): lax.ppermute(rows[b], 'col', [(q, q ^ 2 * b) for q in range(n_col)])]
    ppermute x7, starting transfers between devices: 13.3 us -> 14.3 us  [spectra_by_chip(): lax.ppermute(rows[b], 'col', [(q, q ^ 2 * b) for q in range(n_col)])]
  transfers between devices with their start and end apart: 20 -> 20, of which waited for: 9 -> 8; matrix products, arithmetic and copies ran while one was open for 0% -> 0% of each run, Pallas kernels for 3% -> 3%
where the time goes in v12:
time: 64.8 us; the launch traced here: 64.5 us
  waiting for transfers between devices  27.5 us (42%)
  starting transfers between devices  25.7 us (40%)
  Pallas kernels  8.33 us (13%)
  local copies, waits for them, and re-layouts  2.8 us (4%)
    ppermute x7, waiting for transfers between devices, per_device(): lax.ppermute(made[b], 'col', [(q, q ^ b) for q in range(n_col)])  18.9 us
    ppermute x7, starting transfers between devices, spectra_by_chip(): lax.ppermute(rows[b], 'col', [(q, q ^ 2 * b) for q in range(n_col)])  14.3 us
    ppermute x7, waiting for transfers between devices, spectra_by_chip(): lax.ppermute(rows[b], 'col', [(q, q ^ 2 * b) for q in range(n_col)])  7.09 us
    ppermute x7, starting transfers between devices, per_device(): lax.ppermute(made[b], 'col', [(q, q ^ b) for q in range(n_col)])  6.74 us
    pallas_call x1, Pallas kernels, spectra_by_chip(): pl.pallas_call(partial(chip_transform_kernel, plan, order), out_shape=spe...  3.19 us
    unnamed x6, local copies, waits for them, and re-layouts  2.8 us
    ppermute x1, starting transfers between devices, spectra_by_chip(): near_others.append(lax.ppermute(tile_offsets, ('row', 'col'), pairs))  2.57 us
    pallas_call x1, Pallas kernels, per_device(): pl.pallas_call(partial(merge_kernel, plan, 2 if by_chip else 1), out_shap...  2.12 us
  transfers between devices with their start and end apart: 20, of which 8 were waited for; matrix products, arithmetic and copies ran while one was open for 0% of the time, Pallas kernels for 3%

profile of v12, /device:TPU:0, one launch (start us, length us, event | category | flops | bytes accessed | tf_op | source)
XLA Modules:
  0.0 64.5 jit_solution(14498108791684771480)
XLA Ops:
  0.0 0.5 collective-permute-start.3
  0.5 2.6 %collective-permute-start.1 = (s32[2,4]{1,0:T(2,128)}, s32[2,4]{1,0:T(2,128)S(1)}, u32[]{:S(2)}, u32[]{:S(2)}) collective-permute-start(s32[2,4]{1,0:T(2,128)} %tiles_ref.1), channel_id=1, source_target_pairs={{0,17},{1,16},{2,19},{3,18},{4,21},{5,20},{6,23},{7,22},{8,25},{9,... | collective-permute-start | bytes 104 | tf_op jit(solution)/shard_map/ppermute | solution.py:374
  3.1 0.4 collective-permute-start
  3.5 0.1 collective-permute-start.2
  3.6 0.1 pad_add_fusion.me_ref
  3.7 1.6 %own.1 = (s32[16,2048]{1,0:T(8,128)S(1)}, s32[16,2048]{1,0:T(8,128)S(1)}, s32[8,128]{1,0:T(8,128)S(1)}) custom-call(s32[3]{0:T(128)S(1)} %pad_add_fusion.me_ref, s32[2,4]{1,0:T(2,128)} %tiles_ref.1, s32[32,2048]{1,0:T(8,128)} %codes_ref.1, s32[32,2048]{1,0:T(8,128)} %mask_ref.1), custom_call_target="tpu_custom_call" | custom-call | tf_op jit(solution)/shard_map/own/pallas_call | solution.py:377
  5.3 1.5 %collective-permute-done.refs_0_ = s32[2,4]{1,0:T(2,128)S(1)} collective-permute-done((s32[2,4]{1,0:T(2,128)}, s32[2,4]{1,0:T(2,128)S(1)}, u32[]{:S(2)}, u32[]{:S(2)}) %collective-permute-start) | collective-permute-done | bytes 64 | tf_op jit(solution)/shard_map/ppermute | solution.py:339
  6.9 1.3 %field.1 = (f32[264,128]{1,0:T(8,128)S(1)}, f32[264,128]{1,0:T(8,128)S(1)}, f32[264,128]{1,0:T(8,128)S(1)}, f32[264,128]{1,0:T(8,128)S(1)}, f32[264,128]{1,0:T(8...) custom-call(s32[3]{0:T(128)S(1)} %pad_add_fusion.me_ref, ...), custom_call_target="tpu_custom_call" | custom-call | tf_op jit(solution)/shard_map/field/pallas_call | solution.py:395
  8.2 2.7 %collective-permute-start.5 = (f32[264,128]{1,0:T(8,128)S(1)}, f32[264,128]{1,0:T(8,128)S(1)}, u32[]{:S(2)}, u32[]{:S(2)}) collective-permute-start(f32[264,128]{1,0:T(8,128)S(1)} %get-tuple-element.33), channel_id=1, source_target_pairs={{0,8},{1,9},{2,10},{3,11},{4,12},{5,13},{6,14},{7,15},{8,0},{9,1},... | collective-permute-start | bytes 405512 | tf_op jit(solution)/shard_map/ppermute | solution.py:405
  10.8 1.5 %collective-permute-start.6 = (f32[264,128]{1,0:T(8,128)S(1)}, f32[264,128]{1,0:T(8,128)S(1)}, u32[]{:S(2)}, u32[]{:S(2)}) collective-permute-start(f32[264,128]{1,0:T(8,128)S(1)} %get-tuple-element.34), channel_id=1, source_target_pairs={{0,2},{1,3},{2,0},{3,1},{4,6},{5,7},{6,4},{7,5},{8,10},{9,11},{10,... | collective-permute-start | bytes 405512 | tf_op jit(solution)/shard_map/ppermute | solution.py:405
  12.3 0.3 collective-permute-start.7
  12.6 2.5 %collective-permute-start.8 = (f32[264,128]{1,0:T(8,128)S(1)}, f32[264,128]{1,0:T(8,128)S(1)}, u32[]{:S(2)}, u32[]{:S(2)}) collective-permute-start(f32[264,128]{1,0:T(8,128)S(1)} %get-tuple-element.36), channel_id=1, source_target_pairs={{0,6},{1,7},{2,4},{3,5},{4,2},{5,3},{6,0},{7,1},{8,14},{9,15},{10,... | collective-permute-start | bytes 405512 | tf_op jit(solution)/shard_map/ppermute | solution.py:405
  15.1 2.5 %collective-permute-start.9 = (f32[264,128]{1,0:T(8,128)S(1)}, f32[264,128]{1,0:T(8,128)S(1)}, u32[]{:S(2)}, u32[]{:S(2)}) collective-permute-start(f32[264,128]{1,0:T(8,128)S(1)} %get-tuple-element.37), channel_id=1, source_target_pairs={{0,12},{1,13},{2,14},{3,15},{4,8},{5,9},{6,10},{7,11},{8,4},{9,5},... | collective-permute-start | bytes 405512 | tf_op jit(solution)/shard_map/ppermute | solution.py:405
  17.6 4.8 %collective-permute-done.5.refs_0_ = f32[264,128]{1,0:T(8,128)S(1)} collective-permute-done((f32[264,128]{1,0:T(8,128)S(1)}, f32[264,128]{1,0:T(8,128)S(1)}, u32[]{:S(2)}, u32[]{:S(2)}) %collective-permute-start.5) | collective-permute-done | bytes 135200 | tf_op jit(solution)/shard_map/ppermute | solution.py:405
  22.4 4.8 %collective-permute-start.11 = (f32[264,128]{1,0:T(8,128)S(1)}, f32[264,128]{1,0:T(8,128)S(1)}, u32[]{:S(2)}, u32[]{:S(2)}) collective-permute-start(f32[264,128]{1,0:T(8,128)S(1)} %get-tuple-element.39), channel_id=1, source_target_pairs={{0,14},{1,15},{2,12},{3,13},{4,10},{5,11},{6,8},{7,9},{8,6},{9,7},... | collective-permute-start | bytes 405512 | tf_op jit(solution)/shard_map/ppermute | solution.py:405
  27.2 0.9 %copy-done = bf16[2,16,2,8,256]{4,3,2,1,0:T(8,128)(2,1)S(1)} copy-done((bf16[2,16,2,8,256]{4,3,2,1,0:T(8,128)(2,1)S(1)}, bf16[2,16,2,8,256]{4,3,2,1,0:T(8,128)(2,1)}, u32[]{:S(2)}) %copy-start) | copy-done | bytes 262168
  28.2 0.9 %copy-done.1 = bf16[2,8,2,2,8,256]{5,4,3,2,1,0:T(8,128)(2,1)S(1)} copy-done((bf16[2,8,2,2,8,256]{5,4,3,2,1,0:T(8,128)(2,1)S(1)}, bf16[2,8,2,2,8,256]{5,4,3,2,1,0:T(8,128)(2,1)}, u32[]{:S(2)}) %copy-start.1) | copy-done | bytes 262168
  29.1 0.9 %copy-done.2 = f32[64,512]{1,0:T(8,128)S(1)} copy-done((f32[64,512]{1,0:T(8,128)S(1)}, f32[64,512]{1,0:T(8,128)}, u32[]{:S(2)}) %copy-start.2) | copy-done | bytes 131096
  30.0 0.1 tables.1
  30.2 2.3 %collective-permute-done.11.refs_6_ = f32[264,128]{1,0:T(8,128)S(1)} collective-permute-done((f32[264,128]{1,0:T(8,128)S(1)}, f32[264,128]{1,0:T(8,128)S(1)}, u32[]{:S(2)}, u32[]{:S(2)}) %collective-permute-start.11) | collective-permute-done | bytes 135200 | tf_op jit(solution)/shard_map/ppermute | solution.py:405
  32.5 3.2 %transform.1 = (f32[4,2,16,512]{3,2,1,0:T(8,128)S(1)}, f32[4,2,16,512]{3,2,1,0:T(8,128)S(1)}, f32[4,2,16,512]{3,2,1,0:T(8,128)S(1)}, f32[4,2,16,512]{3,2,1,0:T(8...) custom-call(f32[264,128]{1,0:T(8,128)S(1)} %collective-permute-done., ...), custom_call_target="tpu_custom_call" | custom-call | tf_op jit(solution)/shard_map/transform/pallas_call | solution.py:406
  35.7 3.5 %collective-permute-start.12 = (f32[4,2,16,512]{3,2,1,0:T(8,128)S(1)}, f32[4,2,16,512]{3,2,1,0:T(8,128)S(1)}, u32[]{:S(2)}, u32[]{:S(2)}) collective-permute-start(f32[4,2,16,512]{3,2,1,0:T(8,128)S(1)} %get-tuple-element.44), channel_id=1, source_target_pairs={{0,6},{1,7},{2,4},{3,5},{4,2},{5,3},{6,0},{7,1},{8,14},{9,15},{10,... | collective-permute-start | bytes 786440 | tf_op jit(solution)/shard_map/ppermute | solution.py:474
  39.2 1.3 %collective-permute-start.14 = (f32[4,2,16,512]{3,2,1,0:T(8,128)S(1)}, f32[4,2,16,512]{3,2,1,0:T(8,128)S(1)}, u32[]{:S(2)}, u32[]{:S(2)}) collective-permute-start(f32[4,2,16,512]{3,2,1,0:T(8,128)S(1)} %get-tuple-element.47), channel_id=1, source_target_pairs={{0,2},{1,3},{2,0},{3,1},{4,6},{5,7},{6,4},{7,5},{8,10},{9,11},{10,... | collective-permute-start | bytes 786440 | tf_op jit(solution)/shard_map/ppermute | solution.py:474
  40.5 0.9 %collective-permute-start.15 = (f32[4,2,16,512]{3,2,1,0:T(8,128)S(1)}, f32[4,2,16,512]{3,2,1,0:T(8,128)S(1)}, u32[]{:S(2)}, u32[]{:S(2)}) collective-permute-start(f32[4,2,16,512]{3,2,1,0:T(8,128)S(1)} %get-tuple-element.49), channel_id=1, source_target_pairs={{0,7},{1,6},{2,5},{3,4},{4,3},{5,2},{6,1},{7,0},{8,15},{9,14},{10,... | collective-permute-start | bytes 786440 | tf_op jit(solution)/shard_map/ppermute | solution.py:474
  41.4 0.9 %collective-permute-start.16 = (f32[4,2,16,512]{3,2,1,0:T(8,128)S(1)}, f32[4,2,16,512]{3,2,1,0:T(8,128)S(1)}, u32[]{:S(2)}, u32[]{:S(2)}) collective-permute-start(f32[4,2,16,512]{3,2,1,0:T(8,128)S(1)} %get-tuple-element.50), channel_id=1, source_target_pairs={{0,5},{1,4},{2,7},{3,6},{4,1},{5,0},{6,3},{7,2},{8,13},{9,12},{10,... | collective-permute-start | bytes 786440 | tf_op jit(solution)/shard_map/ppermute | solution.py:474
  42.4 3.9 %collective-permute-done.12.refs_0_ = f32[4,2,16,512]{3,2,1,0:T(8,128)S(1)} collective-permute-done((f32[4,2,16,512]{3,2,1,0:T(8,128)S(1)}, f32[4,2,16,512]{3,2,1,0:T(8,128)S(1)}, u32[]{:S(2)}, u32[]{:S(2)}) %collective-permute-start.12) | collective-permute-done | bytes 262176 | tf_op jit(solution)/shard_map/ppermute | solution.py:474
  46.3 5.7 %collective-permute-done.14.refs_2_ = f32[4,2,16,512]{3,2,1,0:T(8,128)S(1)} collective-permute-done((f32[4,2,16,512]{3,2,1,0:T(8,128)S(1)}, f32[4,2,16,512]{3,2,1,0:T(8,128)S(1)}, u32[]{:S(2)}, u32[]{:S(2)}) %collective-permute-start.14) | collective-permute-done | bytes 262176 | tf_op jit(solution)/shard_map/ppermute | solution.py:474
  52.0 1.1 %collective-permute-start.19 = (f32[8,128]{1,0:T(8,128)S(1)}, f32[8,128]{1,0:T(8,128)S(1)}, u32[]{:S(2)}, u32[]{:S(2)}) collective-permute-start(f32[8,128]{1,0:T(8,128)S(1)} %get-tuple-element.54.refs_8_), channel_id=1, source_target_pairs={{0,16},{16,0},{1,17},{17,1},{2,18},{18,2},{3,19},{19,3},{4,20},{20... | collective-permute-start | bytes 12296 | tf_op jit(solution)/shard_map/ppermute | solution.py:339
  53.2 4.0 %collective-permute-done.15.refs_3_ = f32[4,2,16,512]{3,2,1,0:T(8,128)S(1)} collective-permute-done((f32[4,2,16,512]{3,2,1,0:T(8,128)S(1)}, f32[4,2,16,512]{3,2,1,0:T(8,128)S(1)}, u32[]{:S(2)}, u32[]{:S(2)}) %collective-permute-start.15) | collective-permute-done | bytes 262176 | tf_op jit(solution)/shard_map/ppermute | solution.py:474
  57.2 4.7 %collective-permute-done.16.refs_4_ = f32[4,2,16,512]{3,2,1,0:T(8,128)S(1)} collective-permute-done((f32[4,2,16,512]{3,2,1,0:T(8,128)S(1)}, f32[4,2,16,512]{3,2,1,0:T(8,128)S(1)}, u32[]{:S(2)}, u32[]{:S(2)}) %collective-permute-start.16) | collective-permute-done | bytes 262176 | tf_op jit(solution)/shard_map/ppermute | solution.py:474
  61.9 0.6 collective-permute-done.17.refs_5_
  62.4 2.1 %merge.1 = f32[2,4,512,128]{3,2,1,0:T(8,128)} custom-call(s32[1]{0:T(128)} %bitcast.me_ref, f32[4,2,16,512]{3,2,1,0:T(8,128)S(1)} %collective-permute-done.12.refs_0_, f32[4,2,16,512]{3,2,1,0:T(8,128)S(1)} %collective-permute-done.13.refs_1_, f32[4,2,16,512]{3,2,1,0:T(8,128)S(1)} %collective-permute-done.14.refs_2_, ...), custom_call_target="tpu_custom_call" | custom-call | tf_op jit(solution)/shard_map/merge/pallas_call | solution.py:480
  (20 shorter events, 0.1 us)
Async XLA Ops:
  0.0 6.9 %collective-permute-start.3 = (s32[32,2048]{1,0:T(8,128)}, s32[32,2048]{1,0:T(8,128)S(1)}, u32[]{:S(2)}, u32[]{:S(2)}) collective-permute-start(s32[32,2048]{1,0:T(8,128)} %codes_ref.1), channel_id=1, source_target_pairs={{0,1},{1,0},{2,3},{3,2},{4,5},{5,4},{6,7},{7,6},{8,9},{9,8},{10,11... | collective-permute-start | bytes 786440 | tf_op jit(solution)/shard_map/ppermute | solution.py:375
  0.5 6.4 %collective-permute-start.4 = (s32[32,2048]{1,0:T(8,128)}, s32[32,2048]{1,0:T(8,128)S(1)}, u32[]{:S(2)}, u32[]{:S(2)}) collective-permute-start(s32[32,2048]{1,0:T(8,128)} %mask_ref.1), channel_id=1, source_target_pairs={{0,1},{1,0},{2,3},{3,2},{4,5},{5,4},{6,7},{7,6},{8,9},{9,8},{10,11... | collective-permute-start | bytes 786440 | tf_op jit(solution)/shard_map/ppermute | solution.py:375
  0.5 4.8 %collective-permute-start.1 = (s32[2,4]{1,0:T(2,128)}, s32[2,4]{1,0:T(2,128)S(1)}, u32[]{:S(2)}, u32[]{:S(2)}) collective-permute-start(s32[2,4]{1,0:T(2,128)} %tiles_ref.1), channel_id=1, source_target_pairs={{0,17},{1,16},{2,19},{3,18},{4,21},{5,20},{6,23},{7,22},{8,25},{9,... | collective-permute-start | bytes 104 | tf_op jit(solution)/shard_map/ppermute | solution.py:374
  3.1 3.8 %collective-permute-start = (s32[2,4]{1,0:T(2,128)}, s32[2,4]{1,0:T(2,128)S(1)}, u32[]{:S(2)}, u32[]{:S(2)}) collective-permute-start(s32[2,4]{1,0:T(2,128)} %tiles_ref.1), channel_id=1, source_target_pairs={{0,16},{16,0},{1,17},{17,1},{2,18},{18,2},{3,19},{19,3},{4,20},{20... | collective-permute-start | bytes 104 | tf_op jit(solution)/shard_map/ppermute | solution.py:339
  3.5 3.4 %collective-permute-start.2 = (s32[2,4]{1,0:T(2,128)}, s32[2,4]{1,0:T(2,128)S(1)}, u32[]{:S(2)}, u32[]{:S(2)}) collective-permute-start(s32[2,4]{1,0:T(2,128)} %tiles_ref.1), channel_id=1, source_target_pairs={{0,1},{1,0},{2,3},{3,2},{4,5},{5,4},{6,7},{7,6},{8,9},{9,8},{10,11... | collective-permute-start | bytes 104 | tf_op jit(solution)/shard_map/ppermute | solution.py:375
  8.2 14.2 %collective-permute-start.5 = (f32[264,128]{1,0:T(8,128)S(1)}, f32[264,128]{1,0:T(8,128)S(1)}, u32[]{:S(2)}, u32[]{:S(2)}) collective-permute-start(f32[264,128]{1,0:T(8,128)S(1)} %get-tuple-element.33), channel_id=1, source_target_pairs={{0,8},{1,9},{2,10},{3,11},{4,12},{5,13},{6,14},{7,15},{8,0},{9,1},... | collective-permute-start | bytes 405512 | tf_op jit(solution)/shard_map/ppermute | solution.py:405
  10.8 11.6 %collective-permute-start.6 = (f32[264,128]{1,0:T(8,128)S(1)}, f32[264,128]{1,0:T(8,128)S(1)}, u32[]{:S(2)}, u32[]{:S(2)}) collective-permute-start(f32[264,128]{1,0:T(8,128)S(1)} %get-tuple-element.34), channel_id=1, source_target_pairs={{0,2},{1,3},{2,0},{3,1},{4,6},{5,7},{6,4},{7,5},{8,10},{9,11},{10,... | collective-permute-start | bytes 405512 | tf_op jit(solution)/shard_map/ppermute | solution.py:405
  12.3 17.8 %collective-permute-start.7 = (f32[264,128]{1,0:T(8,128)S(1)}, f32[264,128]{1,0:T(8,128)S(1)}, u32[]{:S(2)}, u32[]{:S(2)}) collective-permute-start(f32[264,128]{1,0:T(8,128)S(1)} %get-tuple-element.35), channel_id=1, source_target_pairs={{0,10},{1,11},{2,8},{3,9},{4,14},{5,15},{6,12},{7,13},{8,2},{9,3},... | collective-permute-start | bytes 405512 | tf_op jit(solution)/shard_map/ppermute | solution.py:405
  12.6 17.5 %collective-permute-start.8 = (f32[264,128]{1,0:T(8,128)S(1)}, f32[264,128]{1,0:T(8,128)S(1)}, u32[]{:S(2)}, u32[]{:S(2)}) collective-permute-start(f32[264,128]{1,0:T(8,128)S(1)} %get-tuple-element.36), channel_id=1, source_target_pairs={{0,6},{1,7},{2,4},{3,5},{4,2},{5,3},{6,0},{7,1},{8,14},{9,15},{10,... | collective-permute-start | bytes 405512 | tf_op jit(solution)/shard_map/ppermute | solution.py:405
  15.1 15.0 %collective-permute-start.9 = (f32[264,128]{1,0:T(8,128)S(1)}, f32[264,128]{1,0:T(8,128)S(1)}, u32[]{:S(2)}, u32[]{:S(2)}) collective-permute-start(f32[264,128]{1,0:T(8,128)S(1)} %get-tuple-element.37), channel_id=1, source_target_pairs={{0,12},{1,13},{2,14},{3,15},{4,8},{5,9},{6,10},{7,11},{8,4},{9,5},... | collective-permute-start | bytes 405512 | tf_op jit(solution)/shard_map/ppermute | solution.py:405
  22.4 7.8 %collective-permute-start.10 = (f32[264,128]{1,0:T(8,128)S(1)}, f32[264,128]{1,0:T(8,128)S(1)}, u32[]{:S(2)}, u32[]{:S(2)}) collective-permute-start(f32[264,128]{1,0:T(8,128)S(1)} %get-tuple-element.38), channel_id=1, source_target_pairs={{0,4},{1,5},{2,6},{3,7},{4,0},{5,1},{6,2},{7,3},{8,12},{9,13},{10,... | collective-permute-start | bytes 405512 | tf_op jit(solution)/shard_map/ppermute | solution.py:405
  22.4 10.0 %collective-permute-start.11 = (f32[264,128]{1,0:T(8,128)S(1)}, f32[264,128]{1,0:T(8,128)S(1)}, u32[]{:S(2)}, u32[]{:S(2)}) collective-permute-start(f32[264,128]{1,0:T(8,128)S(1)} %get-tuple-element.39), channel_id=1, source_target_pairs={{0,14},{1,15},{2,12},{3,13},{4,10},{5,11},{6,8},{7,9},{8,6},{9,7},... | collective-permute-start | bytes 405512 | tf_op jit(solution)/shard_map/ppermute | solution.py:405
  27.2 0.9 %copy-start = (bf16[2,16,2,8,256]{4,3,2,1,0:T(8,128)(2,1)S(1)}, bf16[2,16,2,8,256]{4,3,2,1,0:T(8,128)(2,1)}, u32[]{:S(2)}) copy-start(bf16[2,16,2,8,256]{4,3,2,1,0:T(8,128)(2,1)} %constant.40.clone.inner_ref) | copy-start | bytes 786436
  28.2 0.9 %copy-start.1 = (bf16[2,8,2,2,8,256]{5,4,3,2,1,0:T(8,128)(2,1)S(1)}, bf16[2,8,2,2,8,256]{5,4,3,2,1,0:T(8,128)(2,1)}, u32[]{:S(2)}) copy-start(bf16[2,8,2,2,8,256]{5,4,3,2,1,0:T(8,128)(2,1)} %constant.39.clone.outer_ref) | copy-start | bytes 786436
  29.1 0.9 %copy-start.2 = (f32[64,512]{1,0:T(8,128)S(1)}, f32[64,512]{1,0:T(8,128)}, u32[]{:S(2)}) copy-start(f32[64,512]{1,0:T(8,128)} %constant.41.clone.twist_ref) | copy-start | bytes 393220
  35.7 10.7 %collective-permute-start.12 = (f32[4,2,16,512]{3,2,1,0:T(8,128)S(1)}, f32[4,2,16,512]{3,2,1,0:T(8,128)S(1)}, u32[]{:S(2)}, u32[]{:S(2)}) collective-permute-start(f32[4,2,16,512]{3,2,1,0:T(8,128)S(1)} %get-tuple-element.44), channel_id=1, source_target_pairs={{0,6},{1,7},{2,4},{3,5},{4,2},{5,3},{6,0},{7,1},{8,14},{9,15},{10,... | collective-permute-start | bytes 786440 | tf_op jit(solution)/shard_map/ppermute | solution.py:474
  39.2 12.8 %collective-permute-start.14 = (f32[4,2,16,512]{3,2,1,0:T(8,128)S(1)}, f32[4,2,16,512]{3,2,1,0:T(8,128)S(1)}, u32[]{:S(2)}, u32[]{:S(2)}) collective-permute-start(f32[4,2,16,512]{3,2,1,0:T(8,128)S(1)} %get-tuple-element.47), channel_id=1, source_target_pairs={{0,2},{1,3},{2,0},{3,1},{4,6},{5,7},{6,4},{7,5},{8,10},{9,11},{10,... | collective-permute-start | bytes 786440 | tf_op jit(solution)/shard_map/ppermute | solution.py:474
  40.5 11.5 %collective-permute-start.13 = (f32[4,2,16,512]{3,2,1,0:T(8,128)S(1)}, f32[4,2,16,512]{3,2,1,0:T(8,128)S(1)}, u32[]{:S(2)}, u32[]{:S(2)}) collective-permute-start(f32[4,2,16,512]{3,2,1,0:T(8,128)S(1)} %get-tuple-element.45), channel_id=1, source_target_pairs={{0,4},{1,5},{2,6},{3,7},{4,0},{5,1},{6,2},{7,3},{8,12},{9,13},{10,... | collective-permute-start | bytes 786440 | tf_op jit(solution)/shard_map/ppermute | solution.py:474
  40.5 16.7 %collective-permute-start.15 = (f32[4,2,16,512]{3,2,1,0:T(8,128)S(1)}, f32[4,2,16,512]{3,2,1,0:T(8,128)S(1)}, u32[]{:S(2)}, u32[]{:S(2)}) collective-permute-start(f32[4,2,16,512]{3,2,1,0:T(8,128)S(1)} %get-tuple-element.49), channel_id=1, source_target_pairs={{0,7},{1,6},{2,5},{3,4},{4,3},{5,2},{6,1},{7,0},{8,15},{9,14},{10,... | collective-permute-start | bytes 786440 | tf_op jit(solution)/shard_map/ppermute | solution.py:474
  41.4 20.4 %collective-permute-start.16 = (f32[4,2,16,512]{3,2,1,0:T(8,128)S(1)}, f32[4,2,16,512]{3,2,1,0:T(8,128)S(1)}, u32[]{:S(2)}, u32[]{:S(2)}) collective-permute-start(f32[4,2,16,512]{3,2,1,0:T(8,128)S(1)} %get-tuple-element.50), channel_id=1, source_target_pairs={{0,5},{1,4},{2,7},{3,6},{4,1},{5,0},{6,3},{7,2},{8,13},{9,12},{10,... | collective-permute-start | bytes 786440 | tf_op jit(solution)/shard_map/ppermute | solution.py:474
  46.3 16.1 %collective-permute-start.17 = (f32[4,2,16,512]{3,2,1,0:T(8,128)S(1)}, f32[4,2,16,512]{3,2,1,0:T(8,128)S(1)}, u32[]{:S(2)}, u32[]{:S(2)}) collective-permute-start(f32[4,2,16,512]{3,2,1,0:T(8,128)S(1)} %get-tuple-element.51), channel_id=1, source_target_pairs={{0,3},{1,2},{2,1},{3,0},{4,7},{5,6},{6,5},{7,4},{8,11},{9,10},{10,... | collective-permute-start | bytes 786440 | tf_op jit(solution)/shard_map/ppermute | solution.py:474
  52.0 10.4 %collective-permute-start.18 = (f32[4,2,16,512]{3,2,1,0:T(8,128)S(1)}, f32[4,2,16,512]{3,2,1,0:T(8,128)S(1)}, u32[]{:S(2)}, u32[]{:S(2)}) collective-permute-start(f32[4,2,16,512]{3,2,1,0:T(8,128)S(1)} %get-tuple-element.52), channel_id=1, source_target_pairs={{0,1},{1,0},{2,3},{3,2},{4,5},{5,4},{6,7},{7,6},{8,9},{9,8},{10,11... | collective-permute-start | bytes 786440 | tf_op jit(solution)/shard_map/ppermute | solution.py:474
  52.0 10.4 %collective-permute-start.19 = (f32[8,128]{1,0:T(8,128)S(1)}, f32[8,128]{1,0:T(8,128)S(1)}, u32[]{:S(2)}, u32[]{:S(2)}) collective-permute-start(f32[8,128]{1,0:T(8,128)S(1)} %get-tuple-element.54.refs_8_), channel_id=1, source_target_pairs={{0,16},{16,0},{1,17},{17,1},{2,18},{18,2},{3,19},{19,3},{4,20},{20... | collective-permute-start | bytes 12296 | tf_op jit(solution)/shard_map/ppermute | solution.py:339

commit v13 on v12

--- a/solution.py
+++ b/solution.py
@@ -121,7 +121,7 @@
         open_ref[...] = open_ref[...] + total
 
 
-def own_kernel(plan, me_ref, tiles_ref, codes_ref, mask_ref, code_ref, kept_ref, open_ref):
+def own_kernel(plan, me_ref, tiles_ref, codes_ref, mask_ref, real_ref, imag_ref, open_ref):
     half = plan.row_dev // 2
     first = pl.multiple_of(me_ref[0] * half, half)
     total = jnp.zeros((SUBS, LANES), jnp.int32)
@@ -134,14 +134,18 @@
         piston = jnp.int32(0)
         for k in range(plan.row_dev // TILE_R):
             piston = piston + jnp.where(first >= k * TILE_R, tiles_ref[k, i], 0)
-        code_ref[:, lanes] = codes_ref[:, lanes] + piston
-    kept_ref[...] = mask_ref[pl.ds(first, half), :]
+        for t in range(half // SUBS):
+            rows = slice(t * SUBS, (t + 1) * SUBS)
+            cos, sin, minus_cos, minus_sin = unit_phase((codes_ref[rows, lanes] + piston) & (LEVELS - 1))
+            amplitude = mask_ref[pl.ds(pl.multiple_of(first + t * SUBS, SUBS), SUBS), lanes].astype(jnp.float32)
+            real_ref[rows, lanes] = cos * jnp.where(minus_cos, -amplitude, amplitude)
+            imag_ref[rows, lanes] = sin * jnp.where(minus_sin, -amplitude, amplitude)
 
 
 def chip_field_kernel(plan, me_ref, *refs):
     n_other = plan.n_row - 1
     others, refs = (refs[:n_other], refs[n_other : 2 * n_other]), refs[2 * n_other :]
-    near_tiles_ref, own_codes_ref, own_mask_ref, open_ref, near_codes_ref, near_mask_ref = refs[:6]
+    near_tiles_ref, own_real_ref, own_imag_ref, open_ref, near_codes_ref, near_mask_ref = refs[:6]
     outs, made_ref = refs[6:-1], refs[-1]
     core, chip, row = me_ref[0], me_ref[1], me_ref[2]
     half = plan.row_dev // 2
@@ -159,17 +163,27 @@
         if owner == 1:
             for k in range(plan.row_dev // TILE_R):
                 before = before + jnp.where(first >= k * TILE_R, near_tiles_ref[k : k + 1], 0)
-        codes, mask = ((own_codes_ref, own_mask_ref), (near_codes_ref, near_mask_ref))[owner]
+        pistons = [jnp.broadcast_to(before[:, i : i + 1], (SUBS, LANES)) for i in range(before.shape[1])]
+        turns = []
+        if owner == 0:
+            for piston in pistons:
+                cos, sin, minus_cos, minus_sin = unit_phase(piston & (LEVELS - 1))
+                turns.append((jnp.where(minus_cos, -cos, cos), jnp.where(minus_sin, -sin, sin)))
         for t in range(half // SUBS):
             rows = pl.ds(t * SUBS, SUBS) if owner == 0 else pl.ds(pl.multiple_of(first + t * SUBS, SUBS), SUBS)
             for j in range(plan.pupil_dev // LANES):
                 lanes = slice(j * LANES, (j + 1) * LANES)
                 column = j * LANES // TILE_C
-                piston = jnp.broadcast_to(before[:, column : column + 1], (SUBS, LANES))
-                cos, sin, minus_cos, minus_sin = unit_phase((codes[rows, lanes] + piston) & (LEVELS - 1))
-                amplitude = mask[rows, lanes].astype(jnp.float32)
-                real = cos * jnp.where(minus_cos, -amplitude, amplitude)
-                imag = sin * jnp.where(minus_sin, -amplitude, amplitude)
+                if owner == 0:
+                    turn_cos, turn_sin = turns[column]
+                    own_real, own_imag = own_real_ref[rows, lanes], own_imag_ref[rows, lanes]
+                    real = own_real * turn_cos - own_imag * turn_sin
+                    imag = own_real * turn_sin + own_imag * turn_cos
+                else:
+                    cos, sin, minus_cos, minus_sin = unit_phase((near_codes_ref[rows, lanes] + pistons[column]) & (LEVELS - 1))
+                    amplitude = near_mask_ref[rows, lanes].astype(jnp.float32)
+                    real = cos * jnp.where(minus_cos, -amplitude, amplitude)
+                    imag = sin * jnp.where(minus_sin, -amplitude, amplitude)
                 for part, value in enumerate((real, imag)):
                     start = (part * plan.lane_parts + j % plan.lane_parts) * plan.n1_dev + j // plan.lane_parts
                     made_ref[owner, pl.ds(t * SUBS * stride + start, SUBS, stride=stride), :] = value
@@ -376,7 +390,7 @@
     place = jnp.stack([col_index % 2, col_index // 2, row_index])
     own = pl.pallas_call(
         partial(own_kernel, plan),
-        out_shape=[jax.ShapeDtypeStruct((half, plan.pupil_dev), jnp.int32)] * 2
+        out_shape=[jax.ShapeDtypeStruct((half, plan.pupil_dev), jnp.float32)] * 2
         + [jax.ShapeDtypeStruct((SUBS, LANES), jnp.int32)],
         grid_spec=pltpu.PrefetchScalarGridSpec(
             num_scalar_prefetch=1,

time: 64.8 us -> 64.6 us (level)
  no operation moved by 1% of the time
where the time goes in v13:
time: 64.6 us; the launch traced here: 64.4 us
  waiting for transfers between devices  27.2 us (42%)
  starting transfers between devices  25.9 us (40%)
  Pallas kernels  8.31 us (13%)
  local copies, waits for them, and re-layouts  2.8 us (4%)
    ppermute x7, waiting for transfers between devices, per_device(): lax.ppermute(made[b], 'col', [(q, q ^ b) for q in range(n_col)])  18.7 us
    ppermute x7, starting transfers between devices, spectra_by_chip(): lax.ppermute(rows[b], 'col', [(q, q ^ 2 * b) for q in range(n_col)])  14.3 us
    ppermute x7, waiting for transfers between devices, spectra_by_chip(): lax.ppermute(rows[b], 'col', [(q, q ^ 2 * b) for q in range(n_col)])  7.09 us
    ppermute x7, starting transfers between devices, per_device(): lax.ppermute(made[b], 'col', [(q, q ^ b) for q in range(n_col)])  6.72 us
    pallas_call x1, Pallas kernels, spectra_by_chip(): pl.pallas_call(partial(chip_transform_kernel, plan, order), out_shape=spe...  3.2 us
    unnamed x6, local copies, waits for them, and re-layouts  2.8 us
    ppermute x1, starting transfers between devices, spectra_by_chip(): near_others.append(lax.ppermute(tile_offsets, ('row', 'col'), pairs))  2.57 us
    pallas_call x1, Pallas kernels, per_device(): pl.pallas_call(partial(merge_kernel, plan, 2 if by_chip else 1), out_shap...  2.12 us
  transfers between devices with their start and end apart: 20, of which 8 were waited for; matrix products, arithmetic and copies ran while one was open for 0% of the time, Pallas kernels for 3%

profile of v13, /device:TPU:0, one launch (start us, length us, event | category | flops | bytes accessed | tf_op | source)
XLA Modules:
  0.0 64.4 jit_solution(17971088075412527869)
XLA Ops:
  0.0 0.5 collective-permute-start.3
  0.5 2.6 %collective-permute-start.1 = (s32[2,4]{1,0:T(2,128)}, s32[2,4]{1,0:T(2,128)S(1)}, u32[]{:S(2)}, u32[]{:S(2)}) collective-permute-start(s32[2,4]{1,0:T(2,128)} %tiles_ref.1), channel_id=1, source_target_pairs={{0,17},{1,16},{2,19},{3,18},{4,21},{5,20},{6,23},{7,22},{8,25},{9,... | collective-permute-start | bytes 104 | tf_op jit(solution)/shard_map/ppermute | solution.py:388
  3.1 0.4 collective-permute-start
  3.5 0.1 collective-permute-start.2
  3.6 0.1 pad_add_fusion.me_ref
  3.7 1.8 %own.1 = (f32[16,2048]{1,0:T(8,128)S(1)}, f32[16,2048]{1,0:T(8,128)S(1)}, s32[8,128]{1,0:T(8,128)S(1)}) custom-call(s32[3]{0:T(128)S(1)} %pad_add_fusion.me_ref, s32[2,4]{1,0:T(2,128)} %tiles_ref.1, s32[32,2048]{1,0:T(8,128)} %codes_ref.1, s32[32,2048]{1,0:T(8,128)} %mask_ref.1), custom_call_target="tpu_custom_call" | custom-call | tf_op jit(solution)/shard_map/own/pallas_call | solution.py:391
  5.5 1.4 %collective-permute-done.refs_0_ = s32[2,4]{1,0:T(2,128)S(1)} collective-permute-done((s32[2,4]{1,0:T(2,128)}, s32[2,4]{1,0:T(2,128)S(1)}, u32[]{:S(2)}, u32[]{:S(2)}) %collective-permute-start) | collective-permute-done | bytes 64 | tf_op jit(solution)/shard_map/ppermute | solution.py:353
  6.9 1.1 %field.1 = (f32[264,128]{1,0:T(8,128)S(1)}, f32[264,128]{1,0:T(8,128)S(1)}, f32[264,128]{1,0:T(8,128)S(1)}, f32[264,128]{1,0:T(8,128)S(1)}, f32[264,128]{1,0:T(8...) custom-call(s32[3]{0:T(128)S(1)} %pad_add_fusion.me_ref, ...), custom_call_target="tpu_custom_call" | custom-call | tf_op jit(solution)/shard_map/field/pallas_call | solution.py:409
  8.0 2.7 %collective-permute-start.5 = (f32[264,128]{1,0:T(8,128)S(1)}, f32[264,128]{1,0:T(8,128)S(1)}, u32[]{:S(2)}, u32[]{:S(2)}) collective-permute-start(f32[264,128]{1,0:T(8,128)S(1)} %get-tuple-element.33), channel_id=1, source_target_pairs={{0,8},{1,9},{2,10},{3,11},{4,12},{5,13},{6,14},{7,15},{8,0},{9,1},... | collective-permute-start | bytes 405512 | tf_op jit(solution)/shard_map/ppermute | solution.py:419
  10.7 1.5 %collective-permute-start.6 = (f32[264,128]{1,0:T(8,128)S(1)}, f32[264,128]{1,0:T(8,128)S(1)}, u32[]{:S(2)}, u32[]{:S(2)}) collective-permute-start(f32[264,128]{1,0:T(8,128)S(1)} %get-tuple-element.34), channel_id=1, source_target_pairs={{0,2},{1,3},{2,0},{3,1},{4,6},{5,7},{6,4},{7,5},{8,10},{9,11},{10,... | collective-permute-start | bytes 405512 | tf_op jit(solution)/shard_map/ppermute | solution.py:419
  12.2 0.3 collective-permute-start.7
  12.5 2.5 %collective-permute-start.8 = (f32[264,128]{1,0:T(8,128)S(1)}, f32[264,128]{1,0:T(8,128)S(1)}, u32[]{:S(2)}, u32[]{:S(2)}) collective-permute-start(f32[264,128]{1,0:T(8,128)S(1)} %get-tuple-element.36), channel_id=1, source_target_pairs={{0,6},{1,7},{2,4},{3,5},{4,2},{5,3},{6,0},{7,1},{8,14},{9,15},{10,... | collective-permute-start | bytes 405512 | tf_op jit(solution)/shard_map/ppermute | solution.py:419
  15.0 2.5 %collective-permute-start.9 = (f32[264,128]{1,0:T(8,128)S(1)}, f32[264,128]{1,0:T(8,128)S(1)}, u32[]{:S(2)}, u32[]{:S(2)}) collective-permute-start(f32[264,128]{1,0:T(8,128)S(1)} %get-tuple-element.37), channel_id=1, source_target_pairs={{0,12},{1,13},{2,14},{3,15},{4,8},{5,9},{6,10},{7,11},{8,4},{9,5},... | collective-permute-start | bytes 405512 | tf_op jit(solution)/shard_map/ppermute | solution.py:419
  17.5 4.8 %collective-permute-done.5.refs_0_ = f32[264,128]{1,0:T(8,128)S(1)} collective-permute-done((f32[264,128]{1,0:T(8,128)S(1)}, f32[264,128]{1,0:T(8,128)S(1)}, u32[]{:S(2)}, u32[]{:S(2)}) %collective-permute-start.5) | collective-permute-done | bytes 135200 | tf_op jit(solution)/shard_map/ppermute | solution.py:419
  22.3 4.8 %collective-permute-start.11 = (f32[264,128]{1,0:T(8,128)S(1)}, f32[264,128]{1,0:T(8,128)S(1)}, u32[]{:S(2)}, u32[]{:S(2)}) collective-permute-start(f32[264,128]{1,0:T(8,128)S(1)} %get-tuple-element.39), channel_id=1, source_target_pairs={{0,14},{1,15},{2,12},{3,13},{4,10},{5,11},{6,8},{7,9},{8,6},{9,7},... | collective-permute-start | bytes 405512 | tf_op jit(solution)/shard_map/ppermute | solution.py:419
  27.1 0.9 %copy-done = bf16[2,16,2,8,256]{4,3,2,1,0:T(8,128)(2,1)S(1)} copy-done((bf16[2,16,2,8,256]{4,3,2,1,0:T(8,128)(2,1)S(1)}, bf16[2,16,2,8,256]{4,3,2,1,0:T(8,128)(2,1)}, u32[]{:S(2)}) %copy-start) | copy-done | bytes 262168
  28.0 0.9 %copy-done.1 = bf16[2,8,2,2,8,256]{5,4,3,2,1,0:T(8,128)(2,1)S(1)} copy-done((bf16[2,8,2,2,8,256]{5,4,3,2,1,0:T(8,128)(2,1)S(1)}, bf16[2,8,2,2,8,256]{5,4,3,2,1,0:T(8,128)(2,1)}, u32[]{:S(2)}) %copy-start.1) | copy-done | bytes 262168
  29.0 0.9 %copy-done.2 = f32[64,512]{1,0:T(8,128)S(1)} copy-done((f32[64,512]{1,0:T(8,128)S(1)}, f32[64,512]{1,0:T(8,128)}, u32[]{:S(2)}) %copy-start.2) | copy-done | bytes 131096
  29.9 0.1 tables.1
  30.0 2.3 %collective-permute-done.11.refs_6_ = f32[264,128]{1,0:T(8,128)S(1)} collective-permute-done((f32[264,128]{1,0:T(8,128)S(1)}, f32[264,128]{1,0:T(8,128)S(1)}, u32[]{:S(2)}, u32[]{:S(2)}) %collective-permute-start.11) | collective-permute-done | bytes 135200 | tf_op jit(solution)/shard_map/ppermute | solution.py:419
  32.3 3.2 %transform.1 = (f32[4,2,16,512]{3,2,1,0:T(8,128)S(1)}, f32[4,2,16,512]{3,2,1,0:T(8,128)S(1)}, f32[4,2,16,512]{3,2,1,0:T(8,128)S(1)}, f32[4,2,16,512]{3,2,1,0:T(8...) custom-call(f32[264,128]{1,0:T(8,128)S(1)} %collective-permute-done., ...), custom_call_target="tpu_custom_call" | custom-call | tf_op jit(solution)/shard_map/transform/pallas_call | solution.py:420
  35.5 3.5 %collective-permute-start.12 = (f32[4,2,16,512]{3,2,1,0:T(8,128)S(1)}, f32[4,2,16,512]{3,2,1,0:T(8,128)S(1)}, u32[]{:S(2)}, u32[]{:S(2)}) collective-permute-start(f32[4,2,16,512]{3,2,1,0:T(8,128)S(1)} %get-tuple-element.44), channel_id=1, source_target_pairs={{0,6},{1,7},{2,4},{3,5},{4,2},{5,3},{6,0},{7,1},{8,14},{9,15},{10,... | collective-permute-start | bytes 786440 | tf_op jit(solution)/shard_map/ppermute | solution.py:488
  39.0 1.3 %collective-permute-start.14 = (f32[4,2,16,512]{3,2,1,0:T(8,128)S(1)}, f32[4,2,16,512]{3,2,1,0:T(8,128)S(1)}, u32[]{:S(2)}, u32[]{:S(2)}) collective-permute-start(f32[4,2,16,512]{3,2,1,0:T(8,128)S(1)} %get-tuple-element.47), channel_id=1, source_target_pairs={{0,2},{1,3},{2,0},{3,1},{4,6},{5,7},{6,4},{7,5},{8,10},{9,11},{10,... | collective-permute-start | bytes 786440 | tf_op jit(solution)/shard_map/ppermute | solution.py:488
  40.3 1.0 %collective-permute-start.15 = (f32[4,2,16,512]{3,2,1,0:T(8,128)S(1)}, f32[4,2,16,512]{3,2,1,0:T(8,128)S(1)}, u32[]{:S(2)}, u32[]{:S(2)}) collective-permute-start(f32[4,2,16,512]{3,2,1,0:T(8,128)S(1)} %get-tuple-element.49), channel_id=1, source_target_pairs={{0,7},{1,6},{2,5},{3,4},{4,3},{5,2},{6,1},{7,0},{8,15},{9,14},{10,... | collective-permute-start | bytes 786440 | tf_op jit(solution)/shard_map/ppermute | solution.py:488
  41.3 0.9 %collective-permute-start.16 = (f32[4,2,16,512]{3,2,1,0:T(8,128)S(1)}, f32[4,2,16,512]{3,2,1,0:T(8,128)S(1)}, u32[]{:S(2)}, u32[]{:S(2)}) collective-permute-start(f32[4,2,16,512]{3,2,1,0:T(8,128)S(1)} %get-tuple-element.50), channel_id=1, source_target_pairs={{0,5},{1,4},{2,7},{3,6},{4,1},{5,0},{6,3},{7,2},{8,13},{9,12},{10,... | collective-permute-start | bytes 786440 | tf_op jit(solution)/shard_map/ppermute | solution.py:488
  42.2 3.9 %collective-permute-done.12.refs_0_ = f32[4,2,16,512]{3,2,1,0:T(8,128)S(1)} collective-permute-done((f32[4,2,16,512]{3,2,1,0:T(8,128)S(1)}, f32[4,2,16,512]{3,2,1,0:T(8,128)S(1)}, u32[]{:S(2)}, u32[]{:S(2)}) %collective-permute-start.12) | collective-permute-done | bytes 262176 | tf_op jit(solution)/shard_map/ppermute | solution.py:488
  46.2 5.7 %collective-permute-done.14.refs_2_ = f32[4,2,16,512]{3,2,1,0:T(8,128)S(1)} collective-permute-done((f32[4,2,16,512]{3,2,1,0:T(8,128)S(1)}, f32[4,2,16,512]{3,2,1,0:T(8,128)S(1)}, u32[]{:S(2)}, u32[]{:S(2)}) %collective-permute-start.14) | collective-permute-done | bytes 262176 | tf_op jit(solution)/shard_map/ppermute | solution.py:488
  51.9 1.3 %collective-permute-start.19 = (f32[8,128]{1,0:T(8,128)S(1)}, f32[8,128]{1,0:T(8,128)S(1)}, u32[]{:S(2)}, u32[]{:S(2)}) collective-permute-start(f32[8,128]{1,0:T(8,128)S(1)} %get-tuple-element.54.refs_8_), channel_id=1, source_target_pairs={{0,16},{16,0},{1,17},{17,1},{2,18},{18,2},{3,19},{19,3},{4,20},{20... | collective-permute-start | bytes 12296 | tf_op jit(solution)/shard_map/ppermute | solution.py:353
  53.2 3.9 %collective-permute-done.15.refs_3_ = f32[4,2,16,512]{3,2,1,0:T(8,128)S(1)} collective-permute-done((f32[4,2,16,512]{3,2,1,0:T(8,128)S(1)}, f32[4,2,16,512]{3,2,1,0:T(8,128)S(1)}, u32[]{:S(2)}, u32[]{:S(2)}) %collective-permute-start.15) | collective-permute-done | bytes 262176 | tf_op jit(solution)/shard_map/ppermute | solution.py:488
  57.0 4.7 %collective-permute-done.16.refs_4_ = f32[4,2,16,512]{3,2,1,0:T(8,128)S(1)} collective-permute-done((f32[4,2,16,512]{3,2,1,0:T(8,128)S(1)}, f32[4,2,16,512]{3,2,1,0:T(8,128)S(1)}, u32[]{:S(2)}, u32[]{:S(2)}) %collective-permute-start.16) | collective-permute-done | bytes 262176 | tf_op jit(solution)/shard_map/ppermute | solution.py:488
  61.7 0.6 collective-permute-done.17.refs_5_
  62.3 2.1 %merge.1 = f32[2,4,512,128]{3,2,1,0:T(8,128)} custom-call(s32[1]{0:T(128)} %bitcast.me_ref, f32[4,2,16,512]{3,2,1,0:T(8,128)S(1)} %collective-permute-done.12.refs_0_, f32[4,2,16,512]{3,2,1,0:T(8,128)S(1)} %collective-permute-done.13.refs_1_, f32[4,2,16,512]{3,2,1,0:T(8,128)S(1)} %collective-permute-done.14.refs_2_, ...), custom_call_target="tpu_custom_call" | custom-call | tf_op jit(solution)/shard_map/merge/pallas_call | solution.py:494
  (20 shorter events, 0.1 us)
Async XLA Ops:
  0.0 6.9 %collective-permute-start.3 = (s32[32,2048]{1,0:T(8,128)}, s32[32,2048]{1,0:T(8,128)S(1)}, u32[]{:S(2)}, u32[]{:S(2)}) collective-permute-start(s32[32,2048]{1,0:T(8,128)} %codes_ref.1), channel_id=1, source_target_pairs={{0,1},{1,0},{2,3},{3,2},{4,5},{5,4},{6,7},{7,6},{8,9},{9,8},{10,11... | collective-permute-start | bytes 786440 | tf_op jit(solution)/shard_map/ppermute | solution.py:389
  0.5 6.4 %collective-permute-start.4 = (s32[32,2048]{1,0:T(8,128)}, s32[32,2048]{1,0:T(8,128)S(1)}, u32[]{:S(2)}, u32[]{:S(2)}) collective-permute-start(s32[32,2048]{1,0:T(8,128)} %mask_ref.1), channel_id=1, source_target_pairs={{0,1},{1,0},{2,3},{3,2},{4,5},{5,4},{6,7},{7,6},{8,9},{9,8},{10,11... | collective-permute-start | bytes 786440 | tf_op jit(solution)/shard_map/ppermute | solution.py:389
  0.5 4.9 %collective-permute-start.1 = (s32[2,4]{1,0:T(2,128)}, s32[2,4]{1,0:T(2,128)S(1)}, u32[]{:S(2)}, u32[]{:S(2)}) collective-permute-start(s32[2,4]{1,0:T(2,128)} %tiles_ref.1), channel_id=1, source_target_pairs={{0,17},{1,16},{2,19},{3,18},{4,21},{5,20},{6,23},{7,22},{8,25},{9,... | collective-permute-start | bytes 104 | tf_op jit(solution)/shard_map/ppermute | solution.py:388
  3.1 3.8 %collective-permute-start = (s32[2,4]{1,0:T(2,128)}, s32[2,4]{1,0:T(2,128)S(1)}, u32[]{:S(2)}, u32[]{:S(2)}) collective-permute-start(s32[2,4]{1,0:T(2,128)} %tiles_ref.1), channel_id=1, source_target_pairs={{0,16},{16,0},{1,17},{17,1},{2,18},{18,2},{3,19},{19,3},{4,20},{20... | collective-permute-start | bytes 104 | tf_op jit(solution)/shard_map/ppermute | solution.py:353
  3.5 3.4 %collective-permute-start.2 = (s32[2,4]{1,0:T(2,128)}, s32[2,4]{1,0:T(2,128)S(1)}, u32[]{:S(2)}, u32[]{:S(2)}) collective-permute-start(s32[2,4]{1,0:T(2,128)} %tiles_ref.1), channel_id=1, source_target_pairs={{0,1},{1,0},{2,3},{3,2},{4,5},{5,4},{6,7},{7,6},{8,9},{9,8},{10,11... | collective-permute-start | bytes 104 | tf_op jit(solution)/shard_map/ppermute | solution.py:389
  8.0 14.2 %collective-permute-start.5 = (f32[264,128]{1,0:T(8,128)S(1)}, f32[264,128]{1,0:T(8,128)S(1)}, u32[]{:S(2)}, u32[]{:S(2)}) collective-permute-start(f32[264,128]{1,0:T(8,128)S(1)} %get-tuple-element.33), channel_id=1, source_target_pairs={{0,8},{1,9},{2,10},{3,11},{4,12},{5,13},{6,14},{7,15},{8,0},{9,1},... | collective-permute-start | bytes 405512 | tf_op jit(solution)/shard_map/ppermute | solution.py:419
  10.7 11.6 %collective-permute-start.6 = (f32[264,128]{1,0:T(8,128)S(1)}, f32[264,128]{1,0:T(8,128)S(1)}, u32[]{:S(2)}, u32[]{:S(2)}) collective-permute-start(f32[264,128]{1,0:T(8,128)S(1)} %get-tuple-element.34), channel_id=1, source_target_pairs={{0,2},{1,3},{2,0},{3,1},{4,6},{5,7},{6,4},{7,5},{8,10},{9,11},{10,... | collective-permute-start | bytes 405512 | tf_op jit(solution)/shard_map/ppermute | solution.py:419
  12.2 17.8 %collective-permute-start.7 = (f32[264,128]{1,0:T(8,128)S(1)}, f32[264,128]{1,0:T(8,128)S(1)}, u32[]{:S(2)}, u32[]{:S(2)}) collective-permute-start(f32[264,128]{1,0:T(8,128)S(1)} %get-tuple-element.35), channel_id=1, source_target_pairs={{0,10},{1,11},{2,8},{3,9},{4,14},{5,15},{6,12},{7,13},{8,2},{9,3},... | collective-permute-start | bytes 405512 | tf_op jit(solution)/shard_map/ppermute | solution.py:419
  12.5 17.5 %collective-permute-start.8 = (f32[264,128]{1,0:T(8,128)S(1)}, f32[264,128]{1,0:T(8,128)S(1)}, u32[]{:S(2)}, u32[]{:S(2)}) collective-permute-start(f32[264,128]{1,0:T(8,128)S(1)} %get-tuple-element.36), channel_id=1, source_target_pairs={{0,6},{1,7},{2,4},{3,5},{4,2},{5,3},{6,0},{7,1},{8,14},{9,15},{10,... | collective-permute-start | bytes 405512 | tf_op jit(solution)/shard_map/ppermute | solution.py:419
  15.0 15.0 %collective-permute-start.9 = (f32[264,128]{1,0:T(8,128)S(1)}, f32[264,128]{1,0:T(8,128)S(1)}, u32[]{:S(2)}, u32[]{:S(2)}) collective-permute-start(f32[264,128]{1,0:T(8,128)S(1)} %get-tuple-element.37), channel_id=1, source_target_pairs={{0,12},{1,13},{2,14},{3,15},{4,8},{5,9},{6,10},{7,11},{8,4},{9,5},... | collective-permute-start | bytes 405512 | tf_op jit(solution)/shard_map/ppermute | solution.py:419
  22.3 7.8 %collective-permute-start.10 = (f32[264,128]{1,0:T(8,128)S(1)}, f32[264,128]{1,0:T(8,128)S(1)}, u32[]{:S(2)}, u32[]{:S(2)}) collective-permute-start(f32[264,128]{1,0:T(8,128)S(1)} %get-tuple-element.38), channel_id=1, source_target_pairs={{0,4},{1,5},{2,6},{3,7},{4,0},{5,1},{6,2},{7,3},{8,12},{9,13},{10,... | collective-permute-start | bytes 405512 | tf_op jit(solution)/shard_map/ppermute | solution.py:419
  22.3 10.0 %collective-permute-start.11 = (f32[264,128]{1,0:T(8,128)S(1)}, f32[264,128]{1,0:T(8,128)S(1)}, u32[]{:S(2)}, u32[]{:S(2)}) collective-permute-start(f32[264,128]{1,0:T(8,128)S(1)} %get-tuple-element.39), channel_id=1, source_target_pairs={{0,14},{1,15},{2,12},{3,13},{4,10},{5,11},{6,8},{7,9},{8,6},{9,7},... | collective-permute-start | bytes 405512 | tf_op jit(solution)/shard_map/ppermute | solution.py:419
  27.1 0.9 %copy-start = (bf16[2,16,2,8,256]{4,3,2,1,0:T(8,128)(2,1)S(1)}, bf16[2,16,2,8,256]{4,3,2,1,0:T(8,128)(2,1)}, u32[]{:S(2)}) copy-start(bf16[2,16,2,8,256]{4,3,2,1,0:T(8,128)(2,1)} %constant.40.clone.inner_ref) | copy-start | bytes 786436
  28.0 0.9 %copy-start.1 = (bf16[2,8,2,2,8,256]{5,4,3,2,1,0:T(8,128)(2,1)S(1)}, bf16[2,8,2,2,8,256]{5,4,3,2,1,0:T(8,128)(2,1)}, u32[]{:S(2)}) copy-start(bf16[2,8,2,2,8,256]{5,4,3,2,1,0:T(8,128)(2,1)} %constant.39.clone.outer_ref) | copy-start | bytes 786436
  29.0 0.9 %copy-start.2 = (f32[64,512]{1,0:T(8,128)S(1)}, f32[64,512]{1,0:T(8,128)}, u32[]{:S(2)}) copy-start(f32[64,512]{1,0:T(8,128)} %constant.41.clone.twist_ref) | copy-start | bytes 393220
  35.5 10.7 %collective-permute-start.12 = (f32[4,2,16,512]{3,2,1,0:T(8,128)S(1)}, f32[4,2,16,512]{3,2,1,0:T(8,128)S(1)}, u32[]{:S(2)}, u32[]{:S(2)}) collective-permute-start(f32[4,2,16,512]{3,2,1,0:T(8,128)S(1)} %get-tuple-element.44), channel_id=1, source_target_pairs={{0,6},{1,7},{2,4},{3,5},{4,2},{5,3},{6,0},{7,1},{8,14},{9,15},{10,... | collective-permute-start | bytes 786440 | tf_op jit(solution)/shard_map/ppermute | solution.py:488
  39.0 12.8 %collective-permute-start.14 = (f32[4,2,16,512]{3,2,1,0:T(8,128)S(1)}, f32[4,2,16,512]{3,2,1,0:T(8,128)S(1)}, u32[]{:S(2)}, u32[]{:S(2)}) collective-permute-start(f32[4,2,16,512]{3,2,1,0:T(8,128)S(1)} %get-tuple-element.47), channel_id=1, source_target_pairs={{0,2},{1,3},{2,0},{3,1},{4,6},{5,7},{6,4},{7,5},{8,10},{9,11},{10,... | collective-permute-start | bytes 786440 | tf_op jit(solution)/shard_map/ppermute | solution.py:488
  40.3 11.5 %collective-permute-start.13 = (f32[4,2,16,512]{3,2,1,0:T(8,128)S(1)}, f32[4,2,16,512]{3,2,1,0:T(8,128)S(1)}, u32[]{:S(2)}, u32[]{:S(2)}) collective-permute-start(f32[4,2,16,512]{3,2,1,0:T(8,128)S(1)} %get-tuple-element.45), channel_id=1, source_target_pairs={{0,4},{1,5},{2,6},{3,7},{4,0},{5,1},{6,2},{7,3},{8,12},{9,13},{10,... | collective-permute-start | bytes 786440 | tf_op jit(solution)/shard_map/ppermute | solution.py:488
  40.3 16.7 %collective-permute-start.15 = (f32[4,2,16,512]{3,2,1,0:T(8,128)S(1)}, f32[4,2,16,512]{3,2,1,0:T(8,128)S(1)}, u32[]{:S(2)}, u32[]{:S(2)}) collective-permute-start(f32[4,2,16,512]{3,2,1,0:T(8,128)S(1)} %get-tuple-element.49), channel_id=1, source_target_pairs={{0,7},{1,6},{2,5},{3,4},{4,3},{5,2},{6,1},{7,0},{8,15},{9,14},{10,... | collective-permute-start | bytes 786440 | tf_op jit(solution)/shard_map/ppermute | solution.py:488
  41.3 20.4 %collective-permute-start.16 = (f32[4,2,16,512]{3,2,1,0:T(8,128)S(1)}, f32[4,2,16,512]{3,2,1,0:T(8,128)S(1)}, u32[]{:S(2)}, u32[]{:S(2)}) collective-permute-start(f32[4,2,16,512]{3,2,1,0:T(8,128)S(1)} %get-tuple-element.50), channel_id=1, source_target_pairs={{0,5},{1,4},{2,7},{3,6},{4,1},{5,0},{6,3},{7,2},{8,13},{9,12},{10,... | collective-permute-start | bytes 786440 | tf_op jit(solution)/shard_map/ppermute | solution.py:488
  46.2 16.1 %collective-permute-start.17 = (f32[4,2,16,512]{3,2,1,0:T(8,128)S(1)}, f32[4,2,16,512]{3,2,1,0:T(8,128)S(1)}, u32[]{:S(2)}, u32[]{:S(2)}) collective-permute-start(f32[4,2,16,512]{3,2,1,0:T(8,128)S(1)} %get-tuple-element.51), channel_id=1, source_target_pairs={{0,3},{1,2},{2,1},{3,0},{4,7},{5,6},{6,5},{7,4},{8,11},{9,10},{10,... | collective-permute-start | bytes 786440 | tf_op jit(solution)/shard_map/ppermute | solution.py:488
  51.8 10.4 %collective-permute-start.18 = (f32[4,2,16,512]{3,2,1,0:T(8,128)S(1)}, f32[4,2,16,512]{3,2,1,0:T(8,128)S(1)}, u32[]{:S(2)}, u32[]{:S(2)}) collective-permute-start(f32[4,2,16,512]{3,2,1,0:T(8,128)S(1)} %get-tuple-element.52), channel_id=1, source_target_pairs={{0,1},{1,0},{2,3},{3,2},{4,5},{5,4},{6,7},{7,6},{8,9},{9,8},{10,11... | collective-permute-start | bytes 786440 | tf_op jit(solution)/shard_map/ppermute | solution.py:488
  51.9 10.4 %collective-permute-start.19 = (f32[8,128]{1,0:T(8,128)S(1)}, f32[8,128]{1,0:T(8,128)S(1)}, u32[]{:S(2)}, u32[]{:S(2)}) collective-permute-start(f32[8,128]{1,0:T(8,128)S(1)} %get-tuple-element.54.refs_8_), channel_id=1, source_target_pairs={{0,16},{16,0},{1,17},{17,1},{2,18},{18,2},{3,19},{19,3},{4,20},{20... | collective-permute-start | bytes 12296 | tf_op jit(solution)/shard_map/ppermute | solution.py:353

commit v14 on v13

--- a/solution.py
+++ b/solution.py
@@ -18,7 +18,7 @@
 INNER = 256
 PAD = 4
 FINE = 16
-CHIP_ORDER = (4, 1, 5, 3, 6, 2, 7)
+CHIP_ORDER = (4, 1, 6, 2, 5, 3, 7)
 ORDER = (6, 4, 2, 7, 5, 3, 1)
 GROUP = 8
 

time: 64.6 us -> 64.6 us (level)
  waiting for transfers between devices: 27.2 us -> 30.3 us
  starting transfers between devices: 25.9 us -> 22.8 us
    ppermute x7, waiting for transfers between devices: 7.09 us -> 9.8 us  [spectra_by_chip(): lax.ppermute(rows[b], 'col', [(q, q ^ 2 * b) for q in range(n_col)])]
    ppermute x7, starting transfers between devices: 14.3 us -> 12.6 us  [spectra_by_chip(): lax.ppermute(rows[b], 'col', [(q, q ^ 2 * b) for q in range(n_col)])]
    ppermute x7, starting transfers between devices: 6.72 us -> 5.67 us  [per_device(): lax.ppermute(made[b], 'col', [(q, q ^ b) for q in range(n_col)])]
where the time goes in v14:
time: 64.6 us; the launch traced here: 64.4 us
  waiting for transfers between devices  30.3 us (47%)
  starting transfers between devices  22.8 us (35%)
  Pallas kernels  8.31 us (13%)
  local copies, waits for them, and re-layouts  2.8 us (4%)
    ppermute x7, waiting for transfers between devices, per_device(): lax.ppermute(made[b], 'col', [(q, q ^ b) for q in range(n_col)])  19.1 us
    ppermute x7, starting transfers between devices, spectra_by_chip(): lax.ppermute(rows[b], 'col', [(q, q ^ 2 * b) for q in range(n_col)])  12.6 us
    ppermute x7, waiting for transfers between devices, spectra_by_chip(): lax.ppermute(rows[b], 'col', [(q, q ^ 2 * b) for q in range(n_col)])  9.8 us
    ppermute x7, starting transfers between devices, per_device(): lax.ppermute(made[b], 'col', [(q, q ^ b) for q in range(n_col)])  5.67 us
    pallas_call x1, Pallas kernels, spectra_by_chip(): pl.pallas_call(partial(chip_transform_kernel, plan, order), out_shape=spe...  3.19 us
    unnamed x6, local copies, waits for them, and re-layouts  2.8 us
    ppermute x1, starting transfers between devices, spectra_by_chip(): near_others.append(lax.ppermute(tile_offsets, ('row', 'col'), pairs))  2.57 us
    pallas_call x1, Pallas kernels, per_device(): pl.pallas_call(partial(merge_kernel, plan, 2 if by_chip else 1), out_shap...  2.12 us
  transfers between devices with their start and end apart: 20, of which 8 were waited for; matrix products, arithmetic and copies ran while one was open for 0% of the time, Pallas kernels for 3%

profile of v14, /device:TPU:0, one launch (start us, length us, event | category | flops | bytes accessed | tf_op | source)
XLA Modules:
  0.0 64.4 jit_solution(864151563773185601)
XLA Ops:
  0.0 0.5 collective-permute-start.3
  0.5 2.6 %collective-permute-start.1 = (s32[2,4]{1,0:T(2,128)}, s32[2,4]{1,0:T(2,128)S(1)}, u32[]{:S(2)}, u32[]{:S(2)}) collective-permute-start(s32[2,4]{1,0:T(2,128)} %tiles_ref.1), channel_id=1, source_target_pairs={{0,17},{1,16},{2,19},{3,18},{4,21},{5,20},{6,23},{7,22},{8,25},{9,... | collective-permute-start | bytes 104 | tf_op jit(solution)/shard_map/ppermute | solution.py:388
  3.1 0.4 collective-permute-start
  3.5 0.1 collective-permute-start.2
  3.7 1.8 %own.1 = (f32[16,2048]{1,0:T(8,128)S(1)}, f32[16,2048]{1,0:T(8,128)S(1)}, s32[8,128]{1,0:T(8,128)S(1)}) custom-call(s32[3]{0:T(128)S(1)} %pad_add_fusion.me_ref, s32[2,4]{1,0:T(2,128)} %tiles_ref.1, s32[32,2048]{1,0:T(8,128)} %codes_ref.1, s32[32,2048]{1,0:T(8,128)} %mask_ref.1), custom_call_target="tpu_custom_call" | custom-call | tf_op jit(solution)/shard_map/own/pallas_call | solution.py:391
  5.5 1.4 %collective-permute-done.refs_0_ = s32[2,4]{1,0:T(2,128)S(1)} collective-permute-done((s32[2,4]{1,0:T(2,128)}, s32[2,4]{1,0:T(2,128)S(1)}, u32[]{:S(2)}, u32[]{:S(2)}) %collective-permute-start) | collective-permute-done | bytes 64 | tf_op jit(solution)/shard_map/ppermute | solution.py:353
  6.9 1.1 %field.1 = (f32[264,128]{1,0:T(8,128)S(1)}, f32[264,128]{1,0:T(8,128)S(1)}, f32[264,128]{1,0:T(8,128)S(1)}, f32[264,128]{1,0:T(8,128)S(1)}, f32[264,128]{1,0:T(8...) custom-call(s32[3]{0:T(128)S(1)} %pad_add_fusion.me_ref, ...), custom_call_target="tpu_custom_call" | custom-call | tf_op jit(solution)/shard_map/field/pallas_call | solution.py:409
  8.0 2.7 %collective-permute-start.5 = (f32[264,128]{1,0:T(8,128)S(1)}, f32[264,128]{1,0:T(8,128)S(1)}, u32[]{:S(2)}, u32[]{:S(2)}) collective-permute-start(f32[264,128]{1,0:T(8,128)S(1)} %get-tuple-element.33), channel_id=1, source_target_pairs={{0,8},{1,9},{2,10},{3,11},{4,12},{5,13},{6,14},{7,15},{8,0},{9,1},... | collective-permute-start | bytes 405512 | tf_op jit(solution)/shard_map/ppermute | solution.py:419
  10.7 1.5 %collective-permute-start.6 = (f32[264,128]{1,0:T(8,128)S(1)}, f32[264,128]{1,0:T(8,128)S(1)}, u32[]{:S(2)}, u32[]{:S(2)}) collective-permute-start(f32[264,128]{1,0:T(8,128)S(1)} %get-tuple-element.34), channel_id=1, source_target_pairs={{0,2},{1,3},{2,0},{3,1},{4,6},{5,7},{6,4},{7,5},{8,10},{9,11},{10,... | collective-permute-start | bytes 405512 | tf_op jit(solution)/shard_map/ppermute | solution.py:419
  12.2 1.4 %collective-permute-start.7 = (f32[264,128]{1,0:T(8,128)S(1)}, f32[264,128]{1,0:T(8,128)S(1)}, u32[]{:S(2)}, u32[]{:S(2)}) collective-permute-start(f32[264,128]{1,0:T(8,128)S(1)} %get-tuple-element.35), channel_id=1, source_target_pairs={{0,12},{1,13},{2,14},{3,15},{4,8},{5,9},{6,10},{7,11},{8,4},{9,5},... | collective-permute-start | bytes 405512 | tf_op jit(solution)/shard_map/ppermute | solution.py:419
  13.5 0.2 collective-permute-start.8
  13.8 2.8 %collective-permute-start.9 = (f32[264,128]{1,0:T(8,128)S(1)}, f32[264,128]{1,0:T(8,128)S(1)}, u32[]{:S(2)}, u32[]{:S(2)}) collective-permute-start(f32[264,128]{1,0:T(8,128)S(1)} %get-tuple-element.37), channel_id=1, source_target_pairs={{0,10},{1,11},{2,8},{3,9},{4,14},{5,15},{6,12},{7,13},{8,2},{9,3},... | collective-permute-start | bytes 405512 | tf_op jit(solution)/shard_map/ppermute | solution.py:419
  16.5 5.8 %collective-permute-done.5.refs_0_ = f32[264,128]{1,0:T(8,128)S(1)} collective-permute-done((f32[264,128]{1,0:T(8,128)S(1)}, f32[264,128]{1,0:T(8,128)S(1)}, u32[]{:S(2)}, u32[]{:S(2)}) %collective-permute-start.5) | collective-permute-done | bytes 135200 | tf_op jit(solution)/shard_map/ppermute | solution.py:419
  22.3 0.4 collective-permute-start.10
  22.7 3.7 %collective-permute-start.11 = (f32[264,128]{1,0:T(8,128)S(1)}, f32[264,128]{1,0:T(8,128)S(1)}, u32[]{:S(2)}, u32[]{:S(2)}) collective-permute-start(f32[264,128]{1,0:T(8,128)S(1)} %get-tuple-element.39), channel_id=1, source_target_pairs={{0,14},{1,15},{2,12},{3,13},{4,10},{5,11},{6,8},{7,9},{8,6},{9,7},... | collective-permute-start | bytes 405512 | tf_op jit(solution)/shard_map/ppermute | solution.py:419
  26.5 0.9 %copy-done = bf16[2,16,2,8,256]{4,3,2,1,0:T(8,128)(2,1)S(1)} copy-done((bf16[2,16,2,8,256]{4,3,2,1,0:T(8,128)(2,1)S(1)}, bf16[2,16,2,8,256]{4,3,2,1,0:T(8,128)(2,1)}, u32[]{:S(2)}) %copy-start) | copy-done | bytes 262168
  27.4 0.9 %copy-done.1 = bf16[2,8,2,2,8,256]{5,4,3,2,1,0:T(8,128)(2,1)S(1)} copy-done((bf16[2,8,2,2,8,256]{5,4,3,2,1,0:T(8,128)(2,1)S(1)}, bf16[2,8,2,2,8,256]{5,4,3,2,1,0:T(8,128)(2,1)}, u32[]{:S(2)}) %copy-start.1) | copy-done | bytes 262168
  28.4 0.9 %copy-done.2 = f32[64,512]{1,0:T(8,128)S(1)} copy-done((f32[64,512]{1,0:T(8,128)S(1)}, f32[64,512]{1,0:T(8,128)}, u32[]{:S(2)}) %copy-start.2) | copy-done | bytes 131096
  29.3 0.1 tables.1
  29.4 4.0 %collective-permute-done.9.refs_4_ = f32[264,128]{1,0:T(8,128)S(1)} collective-permute-done((f32[264,128]{1,0:T(8,128)S(1)}, f32[264,128]{1,0:T(8,128)S(1)}, u32[]{:S(2)}, u32[]{:S(2)}) %collective-permute-start.9) | collective-permute-done | bytes 135200 | tf_op jit(solution)/shard_map/ppermute | solution.py:419
  33.4 3.2 %transform.1 = (f32[4,2,16,512]{3,2,1,0:T(8,128)S(1)}, f32[4,2,16,512]{3,2,1,0:T(8,128)S(1)}, f32[4,2,16,512]{3,2,1,0:T(8,128)S(1)}, f32[4,2,16,512]{3,2,1,0:T(8...) custom-call(f32[264,128]{1,0:T(8,128)S(1)} %collective-permute-done., ...), custom_call_target="tpu_custom_call" | custom-call | tf_op jit(solution)/shard_map/transform/pallas_call | solution.py:420
  36.6 2.5 %collective-permute-start.12 = (f32[4,2,16,512]{3,2,1,0:T(8,128)S(1)}, f32[4,2,16,512]{3,2,1,0:T(8,128)S(1)}, u32[]{:S(2)}, u32[]{:S(2)}) collective-permute-start(f32[4,2,16,512]{3,2,1,0:T(8,128)S(1)} %get-tuple-element.44), channel_id=1, source_target_pairs={{0,6},{1,7},{2,4},{3,5},{4,2},{5,3},{6,0},{7,1},{8,14},{9,15},{10,... | collective-permute-start | bytes 786440 | tf_op jit(solution)/shard_map/ppermute | solution.py:488
  39.0 1.3 %collective-permute-start.14 = (f32[4,2,16,512]{3,2,1,0:T(8,128)S(1)}, f32[4,2,16,512]{3,2,1,0:T(8,128)S(1)}, u32[]{:S(2)}, u32[]{:S(2)}) collective-permute-start(f32[4,2,16,512]{3,2,1,0:T(8,128)S(1)} %get-tuple-element.47), channel_id=1, source_target_pairs={{0,2},{1,3},{2,0},{3,1},{4,6},{5,7},{6,4},{7,5},{8,10},{9,11},{10,... | collective-permute-start | bytes 786440 | tf_op jit(solution)/shard_map/ppermute | solution.py:488
  40.4 0.9 %collective-permute-start.15 = (f32[4,2,16,512]{3,2,1,0:T(8,128)S(1)}, f32[4,2,16,512]{3,2,1,0:T(8,128)S(1)}, u32[]{:S(2)}, u32[]{:S(2)}) collective-permute-start(f32[4,2,16,512]{3,2,1,0:T(8,128)S(1)} %get-tuple-element.49), channel_id=1, source_target_pairs={{0,7},{1,6},{2,5},{3,4},{4,3},{5,2},{6,1},{7,0},{8,15},{9,14},{10,... | collective-permute-start | bytes 786440 | tf_op jit(solution)/shard_map/ppermute | solution.py:488
  41.3 0.9 %collective-permute-start.16 = (f32[4,2,16,512]{3,2,1,0:T(8,128)S(1)}, f32[4,2,16,512]{3,2,1,0:T(8,128)S(1)}, u32[]{:S(2)}, u32[]{:S(2)}) collective-permute-start(f32[4,2,16,512]{3,2,1,0:T(8,128)S(1)} %get-tuple-element.50), channel_id=1, source_target_pairs={{0,5},{1,4},{2,7},{3,6},{4,1},{5,0},{6,3},{7,2},{8,13},{9,12},{10,... | collective-permute-start | bytes 786440 | tf_op jit(solution)/shard_map/ppermute | solution.py:488
  42.2 4.5 %collective-permute-done.12.refs_0_ = f32[4,2,16,512]{3,2,1,0:T(8,128)S(1)} collective-permute-done((f32[4,2,16,512]{3,2,1,0:T(8,128)S(1)}, f32[4,2,16,512]{3,2,1,0:T(8,128)S(1)}, u32[]{:S(2)}, u32[]{:S(2)}) %collective-permute-start.12) | collective-permute-done | bytes 262176 | tf_op jit(solution)/shard_map/ppermute | solution.py:488
  46.8 5.7 %collective-permute-done.14.refs_2_ = f32[4,2,16,512]{3,2,1,0:T(8,128)S(1)} collective-permute-done((f32[4,2,16,512]{3,2,1,0:T(8,128)S(1)}, f32[4,2,16,512]{3,2,1,0:T(8,128)S(1)}, u32[]{:S(2)}, u32[]{:S(2)}) %collective-permute-start.14) | collective-permute-done | bytes 262176 | tf_op jit(solution)/shard_map/ppermute | solution.py:488
  52.5 0.9 %collective-permute-start.19 = (f32[8,128]{1,0:T(8,128)S(1)}, f32[8,128]{1,0:T(8,128)S(1)}, u32[]{:S(2)}, u32[]{:S(2)}) collective-permute-start(f32[8,128]{1,0:T(8,128)S(1)} %get-tuple-element.54.refs_8_), channel_id=1, source_target_pairs={{0,16},{16,0},{1,17},{17,1},{2,18},{18,2},{3,19},{19,3},{4,20},{20... | collective-permute-start | bytes 12296 | tf_op jit(solution)/shard_map/ppermute | solution.py:353
  53.4 3.6 %collective-permute-done.15.refs_3_ = f32[4,2,16,512]{3,2,1,0:T(8,128)S(1)} collective-permute-done((f32[4,2,16,512]{3,2,1,0:T(8,128)S(1)}, f32[4,2,16,512]{3,2,1,0:T(8,128)S(1)}, u32[]{:S(2)}, u32[]{:S(2)}) %collective-permute-start.15) | collective-permute-done | bytes 262176 | tf_op jit(solution)/shard_map/ppermute | solution.py:488
  57.0 4.7 %collective-permute-done.16.refs_4_ = f32[4,2,16,512]{3,2,1,0:T(8,128)S(1)} collective-permute-done((f32[4,2,16,512]{3,2,1,0:T(8,128)S(1)}, f32[4,2,16,512]{3,2,1,0:T(8,128)S(1)}, u32[]{:S(2)}, u32[]{:S(2)}) %collective-permute-start.16) | collective-permute-done | bytes 262176 | tf_op jit(solution)/shard_map/ppermute | solution.py:488
  61.7 0.6 collective-permute-done.17.refs_5_
  62.3 2.1 %merge.1 = f32[2,4,512,128]{3,2,1,0:T(8,128)} custom-call(s32[1]{0:T(128)} %bitcast.me_ref, f32[4,2,16,512]{3,2,1,0:T(8,128)S(1)} %collective-permute-done.12.refs_0_, f32[4,2,16,512]{3,2,1,0:T(8,128)S(1)} %collective-permute-done.13.refs_1_, f32[4,2,16,512]{3,2,1,0:T(8,128)S(1)} %collective-permute-done.14.refs_2_, ...), custom_call_target="tpu_custom_call" | custom-call | tf_op jit(solution)/shard_map/merge/pallas_call | solution.py:494
  (20 shorter events, 0.2 us)
Async XLA Ops:
  0.0 6.9 %collective-permute-start.3 = (s32[32,2048]{1,0:T(8,128)}, s32[32,2048]{1,0:T(8,128)S(1)}, u32[]{:S(2)}, u32[]{:S(2)}) collective-permute-start(s32[32,2048]{1,0:T(8,128)} %codes_ref.1), channel_id=1, source_target_pairs={{0,1},{1,0},{2,3},{3,2},{4,5},{5,4},{6,7},{7,6},{8,9},{9,8},{10,11... | collective-permute-start | bytes 786440 | tf_op jit(solution)/shard_map/ppermute | solution.py:389
  0.5 6.4 %collective-permute-start.4 = (s32[32,2048]{1,0:T(8,128)}, s32[32,2048]{1,0:T(8,128)S(1)}, u32[]{:S(2)}, u32[]{:S(2)}) collective-permute-start(s32[32,2048]{1,0:T(8,128)} %mask_ref.1), channel_id=1, source_target_pairs={{0,1},{1,0},{2,3},{3,2},{4,5},{5,4},{6,7},{7,6},{8,9},{9,8},{10,11... | collective-permute-start | bytes 786440 | tf_op jit(solution)/shard_map/ppermute | solution.py:389
  0.5 4.9 %collective-permute-start.1 = (s32[2,4]{1,0:T(2,128)}, s32[2,4]{1,0:T(2,128)S(1)}, u32[]{:S(2)}, u32[]{:S(2)}) collective-permute-start(s32[2,4]{1,0:T(2,128)} %tiles_ref.1), channel_id=1, source_target_pairs={{0,17},{1,16},{2,19},{3,18},{4,21},{5,20},{6,23},{7,22},{8,25},{9,... | collective-permute-start | bytes 104 | tf_op jit(solution)/shard_map/ppermute | solution.py:388
  3.1 3.8 %collective-permute-start = (s32[2,4]{1,0:T(2,128)}, s32[2,4]{1,0:T(2,128)S(1)}, u32[]{:S(2)}, u32[]{:S(2)}) collective-permute-start(s32[2,4]{1,0:T(2,128)} %tiles_ref.1), channel_id=1, source_target_pairs={{0,16},{16,0},{1,17},{17,1},{2,18},{18,2},{3,19},{19,3},{4,20},{20... | collective-permute-start | bytes 104 | tf_op jit(solution)/shard_map/ppermute | solution.py:353
  3.5 3.4 %collective-permute-start.2 = (s32[2,4]{1,0:T(2,128)}, s32[2,4]{1,0:T(2,128)S(1)}, u32[]{:S(2)}, u32[]{:S(2)}) collective-permute-start(s32[2,4]{1,0:T(2,128)} %tiles_ref.1), channel_id=1, source_target_pairs={{0,1},{1,0},{2,3},{3,2},{4,5},{5,4},{6,7},{7,6},{8,9},{9,8},{10,11... | collective-permute-start | bytes 104 | tf_op jit(solution)/shard_map/ppermute | solution.py:389
  8.0 14.3 %collective-permute-start.5 = (f32[264,128]{1,0:T(8,128)S(1)}, f32[264,128]{1,0:T(8,128)S(1)}, u32[]{:S(2)}, u32[]{:S(2)}) collective-permute-start(f32[264,128]{1,0:T(8,128)S(1)} %get-tuple-element.33), channel_id=1, source_target_pairs={{0,8},{1,9},{2,10},{3,11},{4,12},{5,13},{6,14},{7,15},{8,0},{9,1},... | collective-permute-start | bytes 405512 | tf_op jit(solution)/shard_map/ppermute | solution.py:419
  10.7 12.0 %collective-permute-start.6 = (f32[264,128]{1,0:T(8,128)S(1)}, f32[264,128]{1,0:T(8,128)S(1)}, u32[]{:S(2)}, u32[]{:S(2)}) collective-permute-start(f32[264,128]{1,0:T(8,128)S(1)} %get-tuple-element.34), channel_id=1, source_target_pairs={{0,2},{1,3},{2,0},{3,1},{4,6},{5,7},{6,4},{7,5},{8,10},{9,11},{10,... | collective-permute-start | bytes 405512 | tf_op jit(solution)/shard_map/ppermute | solution.py:419
  12.2 17.2 %collective-permute-start.7 = (f32[264,128]{1,0:T(8,128)S(1)}, f32[264,128]{1,0:T(8,128)S(1)}, u32[]{:S(2)}, u32[]{:S(2)}) collective-permute-start(f32[264,128]{1,0:T(8,128)S(1)} %get-tuple-element.35), channel_id=1, source_target_pairs={{0,12},{1,13},{2,14},{3,15},{4,8},{5,9},{6,10},{7,11},{8,4},{9,5},... | collective-permute-start | bytes 405512 | tf_op jit(solution)/shard_map/ppermute | solution.py:419
  13.5 15.8 %collective-permute-start.8 = (f32[264,128]{1,0:T(8,128)S(1)}, f32[264,128]{1,0:T(8,128)S(1)}, u32[]{:S(2)}, u32[]{:S(2)}) collective-permute-start(f32[264,128]{1,0:T(8,128)S(1)} %get-tuple-element.36), channel_id=1, source_target_pairs={{0,4},{1,5},{2,6},{3,7},{4,0},{5,1},{6,2},{7,3},{8,12},{9,13},{10,... | collective-permute-start | bytes 405512 | tf_op jit(solution)/shard_map/ppermute | solution.py:419
  13.8 19.6 %collective-permute-start.9 = (f32[264,128]{1,0:T(8,128)S(1)}, f32[264,128]{1,0:T(8,128)S(1)}, u32[]{:S(2)}, u32[]{:S(2)}) collective-permute-start(f32[264,128]{1,0:T(8,128)S(1)} %get-tuple-element.37), channel_id=1, source_target_pairs={{0,10},{1,11},{2,8},{3,9},{4,14},{5,15},{6,12},{7,13},{8,2},{9,3},... | collective-permute-start | bytes 405512 | tf_op jit(solution)/shard_map/ppermute | solution.py:419
  22.3 11.1 %collective-permute-start.10 = (f32[264,128]{1,0:T(8,128)S(1)}, f32[264,128]{1,0:T(8,128)S(1)}, u32[]{:S(2)}, u32[]{:S(2)}) collective-permute-start(f32[264,128]{1,0:T(8,128)S(1)} %get-tuple-element.38), channel_id=1, source_target_pairs={{0,6},{1,7},{2,4},{3,5},{4,2},{5,3},{6,0},{7,1},{8,14},{9,15},{10,... | collective-permute-start | bytes 405512 | tf_op jit(solution)/shard_map/ppermute | solution.py:419
  22.7 10.7 %collective-permute-start.11 = (f32[264,128]{1,0:T(8,128)S(1)}, f32[264,128]{1,0:T(8,128)S(1)}, u32[]{:S(2)}, u32[]{:S(2)}) collective-permute-start(f32[264,128]{1,0:T(8,128)S(1)} %get-tuple-element.39), channel_id=1, source_target_pairs={{0,14},{1,15},{2,12},{3,13},{4,10},{5,11},{6,8},{7,9},{8,6},{9,7},... | collective-permute-start | bytes 405512 | tf_op jit(solution)/shard_map/ppermute | solution.py:419
  26.5 0.9 %copy-start = (bf16[2,16,2,8,256]{4,3,2,1,0:T(8,128)(2,1)S(1)}, bf16[2,16,2,8,256]{4,3,2,1,0:T(8,128)(2,1)}, u32[]{:S(2)}) copy-start(bf16[2,16,2,8,256]{4,3,2,1,0:T(8,128)(2,1)} %constant.40.clone.inner_ref) | copy-start | bytes 786436
  27.4 0.9 %copy-start.1 = (bf16[2,8,2,2,8,256]{5,4,3,2,1,0:T(8,128)(2,1)S(1)}, bf16[2,8,2,2,8,256]{5,4,3,2,1,0:T(8,128)(2,1)}, u32[]{:S(2)}) copy-start(bf16[2,8,2,2,8,256]{5,4,3,2,1,0:T(8,128)(2,1)} %constant.39.clone.outer_ref) | copy-start | bytes 786436
  28.4 0.9 %copy-start.2 = (f32[64,512]{1,0:T(8,128)S(1)}, f32[64,512]{1,0:T(8,128)}, u32[]{:S(2)}) copy-start(f32[64,512]{1,0:T(8,128)} %constant.41.clone.twist_ref) | copy-start | bytes 393220
  36.6 10.2 %collective-permute-start.12 = (f32[4,2,16,512]{3,2,1,0:T(8,128)S(1)}, f32[4,2,16,512]{3,2,1,0:T(8,128)S(1)}, u32[]{:S(2)}, u32[]{:S(2)}) collective-permute-start(f32[4,2,16,512]{3,2,1,0:T(8,128)S(1)} %get-tuple-element.44), channel_id=1, source_target_pairs={{0,6},{1,7},{2,4},{3,5},{4,2},{5,3},{6,0},{7,1},{8,14},{9,15},{10,... | collective-permute-start | bytes 786440 | tf_op jit(solution)/shard_map/ppermute | solution.py:488
  39.0 13.4 %collective-permute-start.14 = (f32[4,2,16,512]{3,2,1,0:T(8,128)S(1)}, f32[4,2,16,512]{3,2,1,0:T(8,128)S(1)}, u32[]{:S(2)}, u32[]{:S(2)}) collective-permute-start(f32[4,2,16,512]{3,2,1,0:T(8,128)S(1)} %get-tuple-element.47), channel_id=1, source_target_pairs={{0,2},{1,3},{2,0},{3,1},{4,6},{5,7},{6,4},{7,5},{8,10},{9,11},{10,... | collective-permute-start | bytes 786440 | tf_op jit(solution)/shard_map/ppermute | solution.py:488
  40.4 12.1 %collective-permute-start.13 = (f32[4,2,16,512]{3,2,1,0:T(8,128)S(1)}, f32[4,2,16,512]{3,2,1,0:T(8,128)S(1)}, u32[]{:S(2)}, u32[]{:S(2)}) collective-permute-start(f32[4,2,16,512]{3,2,1,0:T(8,128)S(1)} %get-tuple-element.45), channel_id=1, source_target_pairs={{0,4},{1,5},{2,6},{3,7},{4,0},{5,1},{6,2},{7,3},{8,12},{9,13},{10,... | collective-permute-start | bytes 786440 | tf_op jit(solution)/shard_map/ppermute | solution.py:488
  40.4 16.7 %collective-permute-start.15 = (f32[4,2,16,512]{3,2,1,0:T(8,128)S(1)}, f32[4,2,16,512]{3,2,1,0:T(8,128)S(1)}, u32[]{:S(2)}, u32[]{:S(2)}) collective-permute-start(f32[4,2,16,512]{3,2,1,0:T(8,128)S(1)} %get-tuple-element.49), channel_id=1, source_target_pairs={{0,7},{1,6},{2,5},{3,4},{4,3},{5,2},{6,1},{7,0},{8,15},{9,14},{10,... | collective-permute-start | bytes 786440 | tf_op jit(solution)/shard_map/ppermute | solution.py:488
  41.3 20.4 %collective-permute-start.16 = (f32[4,2,16,512]{3,2,1,0:T(8,128)S(1)}, f32[4,2,16,512]{3,2,1,0:T(8,128)S(1)}, u32[]{:S(2)}, u32[]{:S(2)}) collective-permute-start(f32[4,2,16,512]{3,2,1,0:T(8,128)S(1)} %get-tuple-element.50), channel_id=1, source_target_pairs={{0,5},{1,4},{2,7},{3,6},{4,1},{5,0},{6,3},{7,2},{8,13},{9,12},{10,... | collective-permute-start | bytes 786440 | tf_op jit(solution)/shard_map/ppermute | solution.py:488
  46.8 15.5 %collective-permute-start.17 = (f32[4,2,16,512]{3,2,1,0:T(8,128)S(1)}, f32[4,2,16,512]{3,2,1,0:T(8,128)S(1)}, u32[]{:S(2)}, u32[]{:S(2)}) collective-permute-start(f32[4,2,16,512]{3,2,1,0:T(8,128)S(1)} %get-tuple-element.51), channel_id=1, source_target_pairs={{0,3},{1,2},{2,1},{3,0},{4,7},{5,6},{6,5},{7,4},{8,11},{9,10},{10,... | collective-permute-start | bytes 786440 | tf_op jit(solution)/shard_map/ppermute | solution.py:488
  52.5 9.8 %collective-permute-start.18 = (f32[4,2,16,512]{3,2,1,0:T(8,128)S(1)}, f32[4,2,16,512]{3,2,1,0:T(8,128)S(1)}, u32[]{:S(2)}, u32[]{:S(2)}) collective-permute-start(f32[4,2,16,512]{3,2,1,0:T(8,128)S(1)} %get-tuple-element.52), channel_id=1, source_target_pairs={{0,1},{1,0},{2,3},{3,2},{4,5},{5,4},{6,7},{7,6},{8,9},{9,8},{10,11... | collective-permute-start | bytes 786440 | tf_op jit(solution)/shard_map/ppermute | solution.py:488
  52.5 9.8 %collective-permute-start.19 = (f32[8,128]{1,0:T(8,128)S(1)}, f32[8,128]{1,0:T(8,128)S(1)}, u32[]{:S(2)}, u32[]{:S(2)}) collective-permute-start(f32[8,128]{1,0:T(8,128)S(1)} %get-tuple-element.54.refs_8_), channel_id=1, source_target_pairs={{0,16},{16,0},{1,17},{17,1},{2,18},{18,2},{3,19},{19,3},{4,20},{20... | collective-permute-start | bytes 12296 | tf_op jit(solution)/shard_map/ppermute | solution.py:353
